TPU v7x, 256 devices: a whole 4x4x8 slice. The times are simulated.
256 devices in a mesh: outer: 16 (over x_hi, z), inner: 16 (over y, x_lo, core).
Axes of the slice: x: 4 (x_hi: 2, x_lo: 2; x = x_hi * 2 + x_lo), y: 4, z: 8, core: 2. Of those that a mesh axis runs over, the one named last changes fastest.
Arguments:
- activations: bfloat16 [65536, 8192], P(('outer', 'inner')), may hold values from -24 to 24
- output_grads: bfloat16 [65536, 512], P(('outer', 'inner')), may hold values from -0.0234375 to 0.0234375
- master_weights: float32 [8192, 512], P(('inner', 'outer')), may hold values from -0.0625 to 0.0625
- first_moment: float32 [8192, 512], P(('inner', 'outer')), may hold values from -5 to 5
- second_moment: float32 [8192, 512], P(('inner', 'outer')), may hold values from 0.1 to 2
- next_tokens: bfloat16 [65536, 8192], P(('outer', 'inner')), may hold values from -6 to 6
Outputs:
- new_master: float32 [8192, 512], P(('inner', 'outer'))
- new_first_moment: float32 [8192, 512], P(('inner', 'outer'))
- new_second_moment: float32 [8192, 512], P(('inner', 'outer'))
- kept_weights: bfloat16 [8192, 512], P('inner')
- projection: bfloat16 [65536, 512], P(('outer', 'inner'))
All inputs are finite; a program needn't handle non-finite values.
Results may differ from a plain program's by a relative error of at most 0.012.
Values may be sent and summed in bfloat16 or wider, within the bound.
No kernel may reach another device: no remote copies, remote signals or barrier semaphores. Data moves between devices by JAX's collectives and lax.ppermute only.
A program may use at most 128 MiB of HBM per device.

v0:
```python
import jax
import jax.numpy as jnp
from jax import lax
from jax.sharding import PartitionSpec as P

ADAM_STEP = 10


beta_first = 0.9
beta_second = 0.95
learn_rate = 0.002
decay_rate = 0.1
adam_eps = 1e-08


def adamw_update(gradient, master_weights, first_moment, second_moment):
    new_first = beta_first * first_moment + (1.0 - beta_first) * gradient
    new_second = beta_second * second_moment + (1.0 - beta_second) * gradient * gradient
    first_hat = new_first / (1.0 - beta_first**ADAM_STEP)
    second_hat = new_second / (1.0 - beta_second**ADAM_STEP)
    new_master = master_weights - learn_rate * (
        first_hat / (jnp.sqrt(second_hat) + adam_eps) + decay_rate * master_weights
    )
    return (new_master, new_first, new_second)


def rounded_term(columns, output_grads):
    contrib = jnp.einsum(
        "tr,tc->rc", columns, output_grads, preferred_element_type=jnp.float32
    ).astype(jnp.bfloat16)
    contrib = lax.optimization_barrier(contrib)
    return contrib.astype(jnp.float32)


def regroup_features(activations, outer_count, inner_count):
    tok_rows, width = activations.shape
    shard_rows = width // (outer_count * inner_count)
    split_view = activations.reshape(tok_rows, inner_count, outer_count, shard_rows)
    return split_view.transpose(0, 2, 1, 3).reshape(tok_rows, width)


def local(activations, output_grads, master_weights, first_moment, second_moment, next_tokens):
    outer_count = lax.axis_size("outer")
    inner_count = lax.axis_size("inner")
    regrouped = regroup_features(activations, outer_count, inner_count)
    columns = regrouped
    gradient = lax.psum_scatter(
        rounded_term(columns, output_grads), ("outer", "inner"), scatter_dimension=0, tiled=True
    )
    new_master, new_first, new_second = adamw_update(
        gradient, master_weights, first_moment, second_moment
    )
    kept_shard = new_master.astype(jnp.bfloat16)
    kept_weights = lax.all_gather(kept_shard, "outer", axis=0, tiled=True)
    columns = next_tokens
    projected = jnp.dot(
        columns,
        lax.all_gather(kept_weights, "inner", axis=0, tiled=True),
        preferred_element_type=jnp.float32,
    )
    return (new_master, new_first, new_second, kept_weights, projected.astype(jnp.bfloat16))


def solution(mesh):
    placed = (
        P(("outer", "inner"), None),
        P(("outer", "inner"), None),
        P(("inner", "outer"), None),
        P(("inner", "outer"), None),
        P(("inner", "outer"), None),
        P(("outer", "inner"), None),
    )
    return jax.shard_map(
        local,
        mesh=mesh,
        in_specs=placed,
        out_specs=(
            P(("inner", "outer"), None),
            P(("inner", "outer"), None),
            P(("inner", "outer"), None),
            P("inner", None),
            P(("outer", "inner"), None),
        ),
        check_vma=False,
    )
```

profile of v0, /device:TPU:1, one launch (start us, length us, event | category | flops | bytes accessed | tf_op | source)
XLA Modules:
  0.0 1438.1 jit_solution(3119426075619440255)
XLA Ops:
  7.2 0.0 copy-start
  7.2 0.0 reduce-scatter.2.cloned.1.call-start
  7.2 6.4 copy.12
  13.6 2.8 copy.13
  16.5 0.0 copy-done
  16.5 5.6 convolution_convert_fusion
  22.0 11.5 convert_element_type.16
  33.6 0.0 copy-start.2
  33.6 0.0 copy-start.3
  33.6 0.0 copy-start.4
  33.6 0.0 reduce-scatter.2.cloned.1.call-update
  33.6 0.0 all-gather.2.cloned.1.call-start
  33.6 1294.2 %reduce-scatter.2.cloned.1.call-done = f32[32,512]{1,0:T(8,128)} async-done(((f32[8192,512]{1,0:T(8,128)}), f32[32,512]{1,0:T(8,128)}) %reduce-scatter.2.cloned.1.call-update) | async-done | bytes 65552 | tf_op jit(solution)/shard_map/reduce_scatter | solution.py:47
  1327.9 0.0 copy-done.2
  1327.9 0.0 copy-done.3
  1327.9 0.0 copy-done.4
  1327.9 1.5 fusion.2
  1329.4 33.8 %all_gather.6 = bf16[512,512]{1,0:T(8,128)(2,1)} all-gather(bf16[32,512]{1,0:T(8,128)(2,1)S(1)} %get-tuple-element.15), channel_id=1, replica_groups=mesh['outer'=16,'inner'=16] {'outer'}, dimensions={0}, use_global_device_ids=true | all-gather | bytes 557056 | tf_op jit(solution)/shard_map/all_gather | solution.py:54
  1363.2 0.0 all-gather.2.cloned.1.call-update
  1363.2 0.0 copy-start.1
  1363.2 59.4 %all-gather.2.cloned.1.call-done = bf16[8192,512]{1,0:T(8,128)(2,1)} async-done(((bf16[512,512]{1,0:T(8,128)(2,1)}), bf16[8192,512]{1,0:T(8,128)(2,1)}) %all-gather.2.cloned.1.call-update) | async-done | bytes 8388624 | tf_op jit(solution)/shard_map/all_gather | solution.py:58
  1422.7 6.9 fusion
  1429.6 0.8 copy.14
  1430.5 0.0 copy-done.1
  1430.5 0.8 copy.16
Async XLA Ops:
  7.2 9.3 copy-start
  7.2 1320.7 %reduce-scatter.2.cloned.1.call-start = ((), (), s32[]{:S(2)}) async-start(), calls=%async_computation.1 | async-start | bytes 16842752 | tf_op jit(solution)/shard_map/reduce_scatter | solution.py:47
  33.6 1294.3 %copy-start.2 = (f32[32,512]{1,0:T(8,128)S(1)}, f32[32,512]{1,0:T(8,128)}, u32[]{:S(2)}) copy-start(f32[32,512]{1,0:T(8,128)} %param.8) | copy-start | bytes 196612
  33.6 1294.3 %copy-start.3 = (f32[32,512]{1,0:T(8,128)S(1)}, f32[32,512]{1,0:T(8,128)}, u32[]{:S(2)}) copy-start(f32[32,512]{1,0:T(8,128)} %param.9) | copy-start | bytes 196612
  33.6 1294.3 %copy-start.4 = (f32[32,512]{1,0:T(8,128)S(1)}, f32[32,512]{1,0:T(8,128)}, u32[]{:S(2)}) copy-start(f32[32,512]{1,0:T(8,128)} %param.10) | copy-start | bytes 196612
  33.6 1389.1 %all-gather.2.cloned.1.call-start = ((), (), s32[]{:S(2)}) async-start(), calls=%async_computation.2 | async-start | bytes 8912896 | tf_op jit(solution)/shard_map/all_gather | solution.py:58
  1363.2 67.2 %copy-start.1 = (bf16[512,512]{1,0:T(8,128)(2,1)S(1)}, bf16[512,512]{1,0:T(8,128)(2,1)}, u32[]{:S(2)}) copy-start(bf16[512,512]{1,0:T(8,128)(2,1)} %all_gather.6) | copy-start | bytes 1572868
Sparse Core Ops, SparseCore 0:
  33.7 1294.1 reduce-scatter.1
  1363.4 59.2 all-gather.1
where the time goes:
time: 1440 us
  waiting for transfers between devices  1350 us (94%)
  blocking collectives  33.8 us (2%)
    reduce_scatter x1, waiting for transfers between devices, local(): lax.psum_scatter(rounded_term(columns, output_grads), ('outer', 'inner'),...  1290 us
    all_gather x1, waiting for transfers between devices, local(): lax.all_gather(kept_weights, 'inner', axis=0, tiled=True)  59.4 us
    all_gather x1, blocking collectives, local(): kept_weights = lax.all_gather(kept_shard, 'outer', axis=0, tiled=True)  33.8 us
  transfers between devices with their start and end apart: 2, of which 2 were waited for; matrix products, arithmetic and copies ran while one was open for 0% of the time, Pallas kernels for 0%

commit v1 on v0

v1 whole, which is shorter than its diff:
```python
import itertools

import jax
import jax.numpy as jnp
from jax import lax
from jax.experimental import pallas as pl
from jax.experimental.pallas import tpu as pltpu
from jax.sharding import PartitionSpec as P

ADAM_STEP = 10
beta_first = 0.9
beta_second = 0.95
learn_rate = 0.002
decay_rate = 0.1
adam_eps = 1e-08

AXES = ("outer", "inner")
SIZES = (2, 8, 4, 2, 2)
TOK = 256
COLS = 512
WIDTH = 8192
HALF = WIDTH // 2
PARTS = 4
BLOCKS = 16
ROWS = 64

ORDERS = ((0, 2, 1, 3), (1, 3, 0, 2), (2, 0, 3, 1), (3, 1, 2, 0))
Z_STEPS = (1, 2, 4)


def moves(change):
    pairs = []
    for here in itertools.product(*(range(n) for n in SIZES)):
        source = target = 0
        for n, i, j in zip(SIZES, here, change(*here)):
            source, target = source * n + i, target * n + j
        pairs.append((source, target))
    return pairs


def pair_x(odd):
    def change(xh, z, y, xl, c):
        x = xh * 2 + xl
        x = ((x ^ 1) if not odd else ((x + 1) % 4 if x % 2 else (x - 1) % 4))
        return x // 2, z, y, x % 2, c

    return change


def pair_y(odd):
    def change(xh, z, y, xl, c):
        y = (y ^ 1) if not odd else ((y + 1) % 4 if y % 2 else (y - 1) % 4)
        return xh, z, y, xl, c

    return change


PAIRINGS = (moves(pair_x(0)), moves(pair_x(1)), moves(pair_y(0)), moves(pair_y(1)))


def across(array, pairing):
    return lax.ppermute(array, AXES, PAIRINGS[pairing])


def z_swap(array, mask):
    return lax.ppermute(array, AXES, moves(lambda xh, z, y, xl, c: (xh, z ^ mask, y, xl, c)))


def core_swap(array):
    return lax.ppermute(array, AXES, moves(lambda xh, z, y, xl, c: (xh, z, y, xl, 1 - c)))


def place():
    outer, inner = lax.axis_index("outer"), lax.axis_index("inner")
    xh, z = outer // 8, outer % 8
    y, xl, c = inner // 4, (inner // 2) % 2, inner % 2
    return xh, z, y, xl, c


def block_table(xh, y, xl, core):
    r = jnp.arange(BLOCKS, dtype=jnp.int32)
    a, b, c, d = (r >> 3) & 1, (r >> 2) & 1, (r >> 1) & 1, r & 1
    to_xh, to_xl = xh ^ b, xl ^ a ^ b
    to_y = y ^ (2 * d) ^ (c ^ d)
    return ((to_y * 2 + to_xl) * 2 + core) * 2 + to_xh


def pack_kernel(table, source, packed):
    packed[...] = source[...]


def pack(array, table):
    return pl.pallas_call(
        pack_kernel,
        out_shape=jax.ShapeDtypeStruct((TOK, HALF), jnp.bfloat16),
        grid_spec=pltpu.PrefetchScalarGridSpec(
            num_scalar_prefetch=1,
            grid=(BLOCKS,),
            in_specs=[pl.BlockSpec((TOK, 256), lambda r, t: (0, t[r]))],
            out_specs=pl.BlockSpec((TOK, 256), lambda r, t: (0, r)),
        ),
        name="pack",
    )(table, array)


def term_kernel(table, own, other, grads_own, grads_other, term):
    dims = (((0,), (0,)), ((), ()))
    total = lax.dot_general(own[...], grads_own[...], dims, preferred_element_type=jnp.float32)
    total += lax.dot_general(other[...], grads_other[...], dims, preferred_element_type=jnp.float32)
    term[...] = total.astype(jnp.bfloat16).reshape(term.shape)


def gradient_term(table, own, other, grads_own, grads_other):
    whole = pl.BlockSpec((TOK, COLS), lambda r, t: (0, 0))
    return pl.pallas_call(
        term_kernel,
        out_shape=jax.ShapeDtypeStruct((PARTS, BLOCKS, ROWS, COLS), jnp.bfloat16),
        grid_spec=pltpu.PrefetchScalarGridSpec(
            num_scalar_prefetch=1,
            grid=(BLOCKS,),
            in_specs=[
                pl.BlockSpec((TOK, 256), lambda r, t: (0, t[r])),
                pl.BlockSpec((TOK, 256), lambda r, t: (0, r)),
                whole,
                whole,
            ],
            out_specs=pl.BlockSpec((PARTS, 1, ROWS, COLS), lambda r, t: (0, r, 0, 0)),
        ),
        name="gradient_term",
    )(table, own, other, grads_own, grads_other)


def project_kernel(table, own, other, *refs):
    parts, (mine, theirs, total_mine, total_theirs) = refs[:PARTS], refs[PARTS:]
    step = pl.program_id(0)

    @pl.when(step == 0)
    def _():
        total_mine[...] = jnp.zeros_like(total_mine)
        total_theirs[...] = jnp.zeros_like(total_theirs)

    weights = jnp.concatenate([p[...].reshape(ROWS, COLS) for p in parts], axis=0)
    total_mine[...] += jnp.dot(own[...], weights, preferred_element_type=jnp.float32)
    total_theirs[...] += jnp.dot(other[...], weights, preferred_element_type=jnp.float32)

    @pl.when(step == BLOCKS - 1)
    def _():
        mine[...] = total_mine[...]
        theirs[...] = total_theirs[...]


def project(table, own, other, parts):
    out = pl.BlockSpec((TOK, COLS), lambda r, t: (0, 0))
    shape = jax.ShapeDtypeStruct((TOK, COLS), jnp.float32)
    return pl.pallas_call(
        project_kernel,
        out_shape=(shape, shape),
        grid_spec=pltpu.PrefetchScalarGridSpec(
            num_scalar_prefetch=1,
            grid=(BLOCKS,),
            in_specs=[
                pl.BlockSpec((TOK, 256), lambda r, t: (0, t[r])),
                pl.BlockSpec((TOK, 256), lambda r, t: (0, r)),
            ]
            + [pl.BlockSpec((1, ROWS, COLS), lambda r, t: (r, 0, 0))] * PARTS,
            out_specs=(out, out),
            scratch_shapes=[pltpu.VMEM((TOK, COLS), jnp.float32)] * 2,
        ),
        name="project",
    )(table, own, other, *parts)


def adamw_update(gradient, master_weights, first_moment, second_moment):
    new_first = beta_first * first_moment + (1.0 - beta_first) * gradient
    new_second = beta_second * second_moment + (1.0 - beta_second) * gradient * gradient
    first_hat = new_first / (1.0 - beta_first**ADAM_STEP)
    second_hat = new_second / (1.0 - beta_second**ADAM_STEP)
    new_master = master_weights - learn_rate * (
        first_hat / (jnp.sqrt(second_hat) + adam_eps) + decay_rate * master_weights
    )
    return (new_master, new_first, new_second)


def wide(array):
    return array.astype(jnp.float32)


def half_of(array, dim, index):
    return lax.index_in_dim(array, index, dim, keepdims=True)


def reduce_parts(term):
    parts = [term[i].reshape(2, 2, 2, 2, ROWS, COLS) for i in range(PARTS)]
    for step in range(4):
        later = []
        for i in range(PARTS):
            v = ORDERS[i][step]
            got = across(half_of(parts[i], v, 1), v)
            later.append((wide(half_of(parts[i], v, 0)) + wide(got)).astype(jnp.bfloat16))
        parts = later
    return jnp.concatenate([p.reshape(ROWS, COLS) for p in parts], axis=0)


def reduce_z(rows, z):
    total = rows.reshape(2, 2, 2, 32, COLS)
    for mask, bit_dim in ((1, 2), (2, 1), (4, 0)):
        bit = (z & mask) != 0
        low, high = half_of(total, bit_dim, 0), half_of(total, bit_dim, 1)
        got = z_swap(jnp.where(bit, low, high), mask)
        total = wide(jnp.where(bit, high, low)) + wide(got)
        if mask != 4:
            total = total.astype(jnp.bfloat16)
    return total.reshape(32, COLS)


def gather_z(shard, z):
    rows = shard[None]
    for mask in (4, 2, 1):
        got = z_swap(rows, mask)
        bit = (z & mask) != 0
        rows = jnp.stack([jnp.where(bit, got, rows), jnp.where(bit, rows, got)], axis=1)
        rows = rows.reshape(-1, 32, COLS)
    return rows.reshape(2, 2, 2, 32, COLS)


def gather_parts(rows):
    parts = [rows[i * ROWS : (i + 1) * ROWS].reshape(1, 1, 1, 1, ROWS, COLS) for i in range(PARTS)]
    for step in range(4):
        later = []
        for i in range(PARTS):
            v = ORDERS[i][3 - step]
            got = across(parts[i], v)
            later.append(jnp.concatenate([parts[i], got], axis=v))
        parts = later
    return [p.reshape(BLOCKS, ROWS, COLS) for p in parts]


def local(activations, output_grads, master_weights, first_moment, second_moment, next_tokens):
    xh, z, y, xl, core = place()
    table = block_table(xh, y, xl, core)
    other_table = block_table(xh, y, xl, 1 - core)

    got_acts = core_swap(pack(activations, other_table))
    got_grads = core_swap(output_grads)
    got_tokens = core_swap(pack(next_tokens, other_table))

    term = gradient_term(table, activations, got_acts, output_grads, got_grads)
    gradient = reduce_z(reduce_parts(term), z)
    new_master, new_first, new_second = adamw_update(
        gradient, master_weights, first_moment, second_moment
    )
    rows = gather_z(new_master.astype(jnp.bfloat16), z).reshape(256, COLS)
    parts = gather_parts(rows)

    far = jnp.concatenate([p[12] for p in parts], axis=0)
    low = xh == 0
    kept_weights = jnp.concatenate([jnp.where(low, rows, far), jnp.where(low, far, rows)], axis=0)

    mine, theirs = project(table, next_tokens, got_tokens, parts)
    projection = (mine + core_swap(theirs)).astype(jnp.bfloat16)
    return (new_master, new_first, new_second, kept_weights, projection)


def solution(mesh):
    placed = (
        P(("outer", "inner"), None),
        P(("outer", "inner"), None),
        P(("inner", "outer"), None),
        P(("inner", "outer"), None),
        P(("inner", "outer"), None),
        P(("outer", "inner"), None),
    )
    return jax.shard_map(
        local,
        mesh=mesh,
        in_specs=placed,
        out_specs=(
            P(("inner", "outer"), None),
            P(("inner", "outer"), None),
            P(("inner", "outer"), None),
            P("inner", None),
            P(("outer", "inner"), None),
        ),
        check_vma=False,
    )
```

time: 1440 us -> 197 us (0.14)
  waiting for transfers between devices: 1350 us -> 54.3 us
  starting transfers between devices: 0.08 us -> 67.2 us
  Pallas kernels: 0 us -> 47.3 us
  blocking collectives: 33.8 us -> 0 us
    reduce_scatter x1 -> x0, waiting for transfers between devices: 1290 us -> none  [local(): lax.psum_scatter(rounded_term(columns, output_grads), ('outer', 'inner'),...]
    ppermute x0 -> x42, starting transfers between devices: none -> 67.2 us  [the longest x32 29.6 us: across(): return lax.ppermute(array, AXES, PAIRINGS[pairing])]
    all_gather x1 -> x0, waiting for transfers between devices: 59.4 us -> none  [local(): lax.all_gather(kept_weights, 'inner', axis=0, tiled=True)]
    ppermute x0 -> x42, waiting for transfers between devices: none -> 54.3 us  [the longest x32 36.1 us: across(): return lax.ppermute(array, AXES, PAIRINGS[pairing])]
    pallas_call x0 -> x4, Pallas kernels: none -> 47.3 us  [the longest x2 20.5 us: pack(): pl.pallas_call(pack_kernel, out_shape=jax.ShapeDtypeStruct((TOK, HALF), j...]
    all_gather x1 -> x0, blocking collectives: 33.8 us -> none  [local(): kept_weights = lax.all_gather(kept_shard, 'outer', axis=0, tiled=True)]
  transfers between devices with their start and end apart: 2 -> 42, of which waited for: 2 -> 25; matrix products, arithmetic and copies ran while one was open for 0% -> 9% of each run, Pallas kernels for 0% -> 5%
where the time goes in v1:
time: 197 us; the launch traced here: 195 us
  starting transfers between devices  67.2 us (34%)
  waiting for transfers between devices  54.3 us (28%)
  Pallas kernels  47.3 us (24%)
  other arithmetic  17 us (9%)
  local copies, waits for them, and re-layouts  8.15 us (4%)
    ppermute x32, waiting for transfers between devices, across(): return lax.ppermute(array, AXES, PAIRINGS[pairing])  36.1 us
    ppermute x32, starting transfers between devices, across(): return lax.ppermute(array, AXES, PAIRINGS[pairing])  29.6 us
    pallas_call x2, Pallas kernels, pack(): pl.pallas_call(pack_kernel, out_shape=jax.ShapeDtypeStruct((TOK, HALF), j...  20.5 us
    ppermute x4, starting transfers between devices, core_swap(): lax.ppermute(array, AXES, moves(lambda xh, z, y, xl, c: (xh, z, y, xl, 1...  18.9 us
    ppermute x6, starting transfers between devices, z_swap(): lax.ppermute(array, AXES, moves(lambda xh, z, y, xl, c: (xh, z ^ mask, y,...  18.7 us
    ppermute x6, waiting for transfers between devices, z_swap(): lax.ppermute(array, AXES, moves(lambda xh, z, y, xl, c: (xh, z ^ mask, y,...  14.4 us
    pallas_call x1, Pallas kernels, gradient_term(): pl.pallas_call(term_kernel, out_shape=jax.ShapeDtypeStruct((PARTS, BLOCKS...  13.6 us
    pallas_call x1, Pallas kernels, project(): pl.pallas_call(project_kernel, out_shape=(shape, shape), grid_spec=pltpu....  13.3 us
  transfers between devices with their start and end apart: 42, of which 25 were waited for; matrix products, arithmetic and copies ran while one was open for 9% of the time, Pallas kernels for 5%

profile of v1, /device:TPU:1, one launch (start us, length us, event | category | flops | bytes accessed | tf_op | source)
XLA Modules:
  0.0 195.2 jit_solution(15746129888277018717)
XLA Ops:
  1.3 10.3 %pack.2 = bf16[256,4096]{1,0:T(8,128)(2,1)} custom-call(s32[16]{0:T(128)} %multiply_add_fusion.table, bf16[256,8192]{1,0:T(8,128)(2,1)} %own.2), custom_call_target="tpu_custom_call" | custom-call | tf_op jit(solution)/shard_map/pack/pallas_call | solution.py:93
  11.6 3.2 %collective-permute-start = (bf16[256,4096]{1,0:T(8,128)(2,1)}, bf16[256,4096]{1,0:T(8,128)(2,1)S(1)}, u32[]{:S(2)}, u32[]{:S(2)}) collective-permute-start(bf16[256,4096]{1,0:T(8,128)(2,1)} %pack.2), channel_id=1, source_target_pairs={{0,1},{1,0},{2,3},{3,2},{4,5},{5,4},{6,7},{7,6},{8,9},{9,8},{10,11... | collective-permute-start | bytes 6291464 | tf_op jit(solution)/shard_map/ppermute | solution.py:70
  15.4 3.4 %collective-permute-done.1.grads_other = bf16[256,512]{1,0:T(8,128)(2,1)S(1)} collective-permute-done((bf16[256,512]{1,0:T(8,128)(2,1)S(1)}, bf16[256,512]{1,0:T(8,128)(2,1)S(1)}, u32[]{:S(2)}, u32[]{:S(2)}) %collective-permute-start.1) | collective-permute-done | bytes 262176 | tf_op jit(solution)/shard_map/ppermute | solution.py:70
  20.9 13.6 %gradient_term.1 = bf16[4,16,64,512]{3,2,1,0:T(8,128)(2,1)} custom-call(s32[16]{0:T(128)} %multiply_add_fusion.1.table, bf16[256,8192]{1,0:T(8,128)(2,1)} %own.2, bf16[256,4096]{1,0:T(8,128)(2,1)} %copy-done.2, bf16[256,512]{1,0:T(8,128)(2,1)} %grads_own.1, bf16[256,512]{1,0:T(8,128)(2,1)} %copy-done.7), custom_call_target="tpu_custom_call" | custom-call | tf_op jit(solution)/shard_map/gradient_term/pallas_call | solution.py:115
  34.5 2.3 %fusion.14 = (bf16[1,8,64,512]{3,2,1,0:T(8,128)(2,1)}, bf16[1,8,64,512]{3,2,1,0:T(8,128)(2,1)}) fusion(bf16[4,16,64,512]{3,2,1,0:T(8,128)(2,1)} %gradient_term.1), kind=kLoop, calls=%fused_computation.86 | loop fusion | bytes 2097152 | tf_op jit(solution)/shard_map/slice | solution.py:189
  36.8 2.1 %fusion.15 = (bf16[1,16,64,512]{3,2,1,0:T(8,128)(2,1)S(1)}, bf16[1,16,64,512]{3,2,1,0:T(8,128)(2,1)S(1)}, bf16[1,16,64,512]{3,2,1,0:T(8,128)(2,1)S(1)}) fusion(bf16[4,16,64,512]{3,2,1,0:T(8,128)(2,1)} %gradient_term.1), kind=kLoop, calls=%fused_computation.87 | loop fusion | bytes 6291456 | tf_op jit(solution)/shard_map/slice | solution.py:193
  42.5 2.0 %collective-permute-start.14 = (bf16[2,2,2,1,64,512]{5,4,3,2,1,0:T(8,128)(2,1)S(1)}, bf16[2,2,2,1,64,512]{5,4,3,2,1,0:T(8,128)(2,1)S(1)}, u32[]{:S(2)}, u32[]{:S(2)}) collective-permute-start(bf16[2,2,2,1,64,512]{5,4,3,2,1,0:T(8,128)(2,1)S(1)} %slice.236), channel_id=1, source_target_pairs={{0,12},{1,13},{2,14},{3,15},{4,8},{5,9},{6,10},{7,11},{8,4},{9,5},... | collective-permute-start | bytes 1572872 | tf_op jit(solution)/shard_map/ppermute | solution.py:62
  44.5 6.0 %collective-permute-done.2 = bf16[1,2,2,2,64,512]{5,4,3,2,1,0:T(8,128)(2,1)} collective-permute-done((bf16[1,2,2,2,64,512]{5,4,3,2,1,0:T(8,128)(2,1)}, bf16[1,2,2,2,64,512]{5,4,3,2,1,0:T(8,128)(2,1)}, u32[]{:S(2)}, u32[]{:S(2)}) %collective-permute-start.2) | collective-permute-done | bytes 524320 | tf_op jit(solution)/shard_map/ppermute | solution.py:62
  52.0 2.7 %collective-permute-done.6 = bf16[2,1,2,2,64,512]{5,4,3,2,1,0:T(8,128)(2,1)} collective-permute-done((bf16[2,1,2,2,64,512]{5,4,3,2,1,0:T(8,128)(2,1)}, bf16[2,1,2,2,64,512]{5,4,3,2,1,0:T(8,128)(2,1)}, u32[]{:S(2)}, u32[]{:S(2)}) %collective-permute-start.6) | collective-permute-done | bytes 524320 | tf_op jit(solution)/shard_map/ppermute | solution.py:62
  55.8 2.0 %collective-permute-start.7 = (bf16[2,1,2,1,64,512]{5,4,3,2,1,0:T(8,128)(2,1)S(1)}, bf16[2,1,2,1,64,512]{5,4,3,2,1,0:T(8,128)(2,1)S(1)}, u32[]{:S(2)}, u32[]{:S(2)}) collective-permute-start(bf16[2,1,2,1,64,512]{5,4,3,2,1,0:T(8,128)(2,1)S(1)} %slice.220), channel_id=1, source_target_pairs={{0,12},{1,13},{2,14},{3,15},{4,8},{5,9},{6,10},{7,11},{8,4},{9,5},... | collective-permute-start | bytes 786440 | tf_op jit(solution)/shard_map/ppermute | solution.py:62
  58.3 1.9 collective-permute-start.15
  61.4 2.6 %collective-permute-done.7 = bf16[2,1,2,1,64,512]{5,4,3,2,1,0:T(8,128)(2,1)S(1)} collective-permute-done((bf16[2,1,2,1,64,512]{5,4,3,2,1,0:T(8,128)(2,1)S(1)}, bf16[2,1,2,1,64,512]{5,4,3,2,1,0:T(8,128)(2,1)S(1)}, u32[]{:S(2)}, u32[]{:S(2)}) %collective-permute-start.7) | collective-permute-done | bytes 262176 | tf_op jit(solution)/shard_map/ppermute | solution.py:62
  66.2 2.4 %collective-permute-done.4 = bf16[1,1,1,2,64,512]{5,4,3,2,1,0:T(8,128)(2,1)S(1)} collective-permute-done((bf16[1,1,1,2,64,512]{5,4,3,2,1,0:T(8,128)(2,1)S(1)}, bf16[1,1,1,2,64,512]{5,4,3,2,1,0:T(8,128)(2,1)S(1)}, u32[]{:S(2)}, u32[]{:S(2)}) %collective-permute-start.4) | collective-permute-done | bytes 131104 | tf_op jit(solution)/shard_map/ppermute | solution.py:62
  69.9 1.9 collective-permute-start.13
  75.3 2.0 %collective-permute-start.18 = (bf16[2,2,1,32,512]{4,3,2,1,0:T(8,128)(2,1)S(1)}, bf16[2,2,1,32,512]{4,3,2,1,0:T(8,128)(2,1)S(1)}, u32[]{:S(2)}, u32[]{:S(2)}) collective-permute-start(bf16[2,2,1,32,512]{4,3,2,1,0:T(8,128)(2,1)S(1)} %broadcast_select_fusion), channel_id=1, source_target_pairs={{0,16},{1,17},{2,18},{3,19},{4,20},{5,21},{6,22},{7,23},{8,24},{9,... | collective-permute-start | bytes 393224 | tf_op jit(solution)/shard_map/ppermute | solution.py:66
  77.3 2.4 %collective-permute-done.18 = bf16[2,2,1,32,512]{4,3,2,1,0:T(8,128)(2,1)S(1)} collective-permute-done((bf16[2,2,1,32,512]{4,3,2,1,0:T(8,128)(2,1)S(1)}, bf16[2,2,1,32,512]{4,3,2,1,0:T(8,128)(2,1)S(1)}, u32[]{:S(2)}, u32[]{:S(2)}) %collective-permute-start.18) | collective-permute-done | bytes 131104 | tf_op jit(solution)/shard_map/ppermute | solution.py:66
  79.7 3.1 %collective-permute-start.19 = (bf16[2,1,1,32,512]{4,3,2,1,0:T(8,128)(2,1)S(1)}, bf16[2,1,1,32,512]{4,3,2,1,0:T(8,128)(2,1)S(1)}, u32[]{:S(2)}, u32[]{:S(2)}) collective-permute-start(bf16[2,1,1,32,512]{4,3,2,1,0:T(8,128)(2,1)S(1)} %broadcast_select_fusion.1), channel_id=1, source_target_pairs={{0,32},{1,33},{2,34},{3,35},{4,36},{5,37},{6,38},{7,39},{8,40},{9,... | collective-permute-start | bytes 196616 | tf_op jit(solution)/shard_map/ppermute | solution.py:66
  84.6 7.0 %collective-permute-start.20 = (bf16[1,1,1,32,512]{4,3,2,1,0:T(8,128)(2,1)S(1)}, bf16[1,1,1,32,512]{4,3,2,1,0:T(8,128)(2,1)S(1)}, u32[]{:S(2)}, u32[]{:S(2)}) collective-permute-start(bf16[1,1,1,32,512]{4,3,2,1,0:T(8,128)(2,1)S(1)} %broadcast_select_fusion.2), channel_id=1, source_target_pairs={{0,64},{1,65},{2,66},{3,67},{4,68},{5,69},{6,70},{7,71},{8,72},{9,... | collective-permute-start | bytes 98312 | tf_op jit(solution)/shard_map/ppermute | solution.py:66
  93.5 5.4 %collective-permute-start.21 = (bf16[1,32,512]{2,1,0:T(8,128)(2,1)S(1)}, bf16[1,32,512]{2,1,0:T(8,128)(2,1)S(1)}, u32[]{:S(2)}, u32[]{:S(2)}) collective-permute-start(bf16[1,32,512]{2,1,0:T(8,128)(2,1)S(1)} %get-tuple-element.9), channel_id=1, source_target_pairs={{0,64},{1,65},{2,66},{3,67},{4,68},{5,69},{6,70},{7,71},{8,72},{9,... | collective-permute-start | bytes 98312 | tf_op jit(solution)/shard_map/ppermute | solution.py:66
  101.5 3.6 %collective-permute-done.22 = bf16[2,32,512]{2,1,0:T(8,128)(2,1)S(1)} collective-permute-done((bf16[2,32,512]{2,1,0:T(8,128)(2,1)S(1)}, bf16[2,32,512]{2,1,0:T(8,128)(2,1)S(1)}, u32[]{:S(2)}, u32[]{:S(2)}) %collective-permute-start.22) | collective-permute-done | bytes 65568 | tf_op jit(solution)/shard_map/ppermute | solution.py:66
  105.2 4.1 %collective-permute-done.23 = bf16[4,32,512]{2,1,0:T(8,128)(2,1)S(1)} collective-permute-done((bf16[4,32,512]{2,1,0:T(8,128)(2,1)S(1)}, bf16[4,32,512]{2,1,0:T(8,128)(2,1)S(1)}, u32[]{:S(2)}, u32[]{:S(2)}) %collective-permute-start.23) | collective-permute-done | bytes 131104 | tf_op jit(solution)/shard_map/ppermute | solution.py:66
  110.5 10.3 %pack.3 = bf16[256,4096]{1,0:T(8,128)(2,1)} custom-call(s32[16]{0:T(128)} %multiply_add_fusion.table, bf16[256,8192]{1,0:T(8,128)(2,1)} %own.3), custom_call_target="tpu_custom_call" | custom-call | tf_op jit(solution)/shard_map/pack/pallas_call | solution.py:93
  120.8 12.7 %collective-permute-start.40 = (bf16[256,4096]{1,0:T(8,128)(2,1)}, bf16[256,4096]{1,0:T(8,128)(2,1)}, u32[]{:S(2)}, u32[]{:S(2)}) collective-permute-start(bf16[256,4096]{1,0:T(8,128)(2,1)} %pack.3), channel_id=1, source_target_pairs={{0,1},{1,0},{2,3},{3,2},{4,5},{5,4},{6,7},{7,6},{8,9},{9,8},{10,11... | collective-permute-start | bytes 6291464 | tf_op jit(solution)/shard_map/ppermute | solution.py:70
  134.5 2.4 %collective-permute-start.25 = (bf16[1,1,1,2,64,512]{5,4,3,2,1,0:T(8,128)(2,1)S(1)}, bf16[1,1,1,2,64,512]{5,4,3,2,1,0:T(8,128)(2,1)S(1)}, u32[]{:S(2)}, u32[]{:S(2)}) collective-permute-start(bf16[1,1,1,2,64,512]{5,4,3,2,1,0:T(8,128)(2,1)S(1)} %pad_maximum_fusion.17), channel_id=1, source_target_pairs={{0,130},{1,131},{2,128},{3,129},{4,134},{5,135},{6,132},{7,133},{8... | collective-permute-start | bytes 393224 | tf_op jit(solution)/shard_map/ppermute | solution.py:62
  144.6 3.7 %collective-permute-done.26 = bf16[1,2,1,2,64,512]{5,4,3,2,1,0:T(8,128)(2,1)S(1)} collective-permute-done((bf16[1,2,1,2,64,512]{5,4,3,2,1,0:T(8,128)(2,1)S(1)}, bf16[1,2,1,2,64,512]{5,4,3,2,1,0:T(8,128)(2,1)S(1)}, u32[]{:S(2)}, u32[]{:S(2)}) %collective-permute-start.26) | collective-permute-done | bytes 262176 | tf_op jit(solution)/shard_map/ppermute | solution.py:62
  148.4 2.6 %collective-permute-done.37 = bf16[2,1,1,1,64,512]{5,4,3,2,1,0:T(8,128)(2,1)S(1)} collective-permute-done((bf16[2,1,1,1,64,512]{5,4,3,2,1,0:T(8,128)(2,1)S(1)}, bf16[2,1,1,1,64,512]{5,4,3,2,1,0:T(8,128)(2,1)S(1)}, u32[]{:S(2)}, u32[]{:S(2)}) %collective-permute-start.37) | collective-permute-done | bytes 131104 | tf_op jit(solution)/shard_map/ppermute | solution.py:62
  153.5 1.9 collective-permute-start.31
  157.2 1.8 collective-permute-done.38
  163.2 7.1 %collective-permute-done.31 = bf16[2,1,2,2,64,512]{5,4,3,2,1,0:T(8,128)(2,1)} collective-permute-done((bf16[2,1,2,2,64,512]{5,4,3,2,1,0:T(8,128)(2,1)}, bf16[2,1,2,2,64,512]{5,4,3,2,1,0:T(8,128)(2,1)}, u32[]{:S(2)}, u32[]{:S(2)}) %collective-permute-start.31) | collective-permute-done | bytes 524320 | tf_op jit(solution)/shard_map/ppermute | solution.py:62
  171.6 2.5 %pad_maximum_fusion.2 = bf16[2,2,2,2,64,512]{5,4,3,2,1,0:T(8,128)(2,1)} fusion(bf16[2,2,1,2,64,512]{5,4,3,2,1,0:T(8,128)(2,1)} %collective-permute-done.35, bf16[1,2,1,2,64,512]{5,4,3,2,1,0:T(8,128)(2,1)S(1)} %collective-permute-done.34, bf16[1,2,1,1,64,512]{5,4,3,2,1,0:T(8,128)(2,1)S(1)} %collective-permute-done.33, ...), kind=kLoop, calls=%fused_computation.2 | loop fusion | flops 2097152 | bytes 2097152 | tf_op jit(solution)/shard_map/concatenate | solution.py:233
  175.4 13.3 %project.1 = (f32[256,512]{1,0:T(8,128)}, f32[256,512]{1,0:T(8,128)}) custom-call(s32[16]{0:T(128)} %multiply_add_fusion.1.table, bf16[256,8192]{1,0:T(8,128)(2,1)} %own.3, bf16[256,4096]{1,0:T(8,128)(2,1)} %collective-permute-done.40.other, bf16[16,64,512]{2,1,0:T(8,128)(2,1)} %bitcast.67, bf16[16,64,512]{2,1,0:T(8,128)(2,1)} %bitcast.69, ...), custom_call_target="tpu_custom_call" | custom-call | tf_op jit(solution)/shard_map/project/pallas_call | solution.py:155
  188.6 2.9 %collective-permute-start.41 = (f32[256,512]{1,0:T(8,128)}, f32[256,512]{1,0:T(8,128)S(1)}, u32[]{:S(2)}, u32[]{:S(2)}) collective-permute-start(f32[256,512]{1,0:T(8,128)} %get-tuple-element.8), channel_id=1, source_target_pairs={{0,1},{1,0},{2,3},{3,2},{4,5},{5,4},{6,7},{7,6},{8,9},{9,8},{10,11... | collective-permute-start | bytes 1572872 | tf_op jit(solution)/shard_map/ppermute | solution.py:70
  (149 shorter events, 48.8 us)
Async XLA Ops:
  11.6 7.6 %collective-permute-start = (bf16[256,4096]{1,0:T(8,128)(2,1)}, bf16[256,4096]{1,0:T(8,128)(2,1)S(1)}, u32[]{:S(2)}, u32[]{:S(2)}) collective-permute-start(bf16[256,4096]{1,0:T(8,128)(2,1)} %pack.2), channel_id=1, source_target_pairs={{0,1},{1,0},{2,3},{3,2},{4,5},{5,4},{6,7},{7,6},{8,9},{9,8},{10,11... | collective-permute-start | bytes 6291464 | tf_op jit(solution)/shard_map/ppermute | solution.py:70
  36.8 13.7 %collective-permute-start.2 = (bf16[1,2,2,2,64,512]{5,4,3,2,1,0:T(8,128)(2,1)}, bf16[1,2,2,2,64,512]{5,4,3,2,1,0:T(8,128)(2,1)}, u32[]{:S(2)}, u32[]{:S(2)}) collective-permute-start(bf16[1,2,2,2,64,512]{5,4,3,2,1,0:T(8,128)(2,1)} %bitcast.1), channel_id=1, source_target_pairs={{0,2},{1,3},{2,0},{3,1},{4,6},{5,7},{6,4},{7,5},{8,10},{9,11},{10,... | collective-permute-start | bytes 1572872 | tf_op jit(solution)/shard_map/ppermute | solution.py:62
  39.7 14.9 %collective-permute-start.6 = (bf16[2,1,2,2,64,512]{5,4,3,2,1,0:T(8,128)(2,1)}, bf16[2,1,2,2,64,512]{5,4,3,2,1,0:T(8,128)(2,1)}, u32[]{:S(2)}, u32[]{:S(2)}) collective-permute-start(bf16[2,1,2,2,64,512]{5,4,3,2,1,0:T(8,128)(2,1)} %slice.218), channel_id=1, source_target_pairs={{0,130},{1,131},{2,128},{3,129},{4,134},{5,135},{6,132},{7,133},{8... | collective-permute-start | bytes 1572872 | tf_op jit(solution)/shard_map/ppermute | solution.py:62
  41.1 16.8 %collective-permute-start.10 = (bf16[2,2,1,2,64,512]{5,4,3,2,1,0:T(8,128)(2,1)S(1)}, bf16[2,2,1,2,64,512]{5,4,3,2,1,0:T(8,128)(2,1)S(1)}, u32[]{:S(2)}, u32[]{:S(2)}) collective-permute-start(bf16[2,2,1,2,64,512]{5,4,3,2,1,0:T(8,128)(2,1)S(1)} %slice.227), channel_id=1, source_target_pairs={{0,4},{1,5},{2,6},{3,7},{4,0},{5,1},{6,2},{7,3},{8,12},{9,13},{10,... | collective-permute-start | bytes 1572872 | tf_op jit(solution)/shard_map/ppermute | solution.py:62
  42.5 15.6 %collective-permute-start.14 = (bf16[2,2,2,1,64,512]{5,4,3,2,1,0:T(8,128)(2,1)S(1)}, bf16[2,2,2,1,64,512]{5,4,3,2,1,0:T(8,128)(2,1)S(1)}, u32[]{:S(2)}, u32[]{:S(2)}) collective-permute-start(bf16[2,2,2,1,64,512]{5,4,3,2,1,0:T(8,128)(2,1)S(1)} %slice.236), channel_id=1, source_target_pairs={{0,12},{1,13},{2,14},{3,15},{4,8},{5,9},{6,10},{7,11},{8,4},{9,5},... | collective-permute-start | bytes 1572872 | tf_op jit(solution)/shard_map/ppermute | solution.py:62
  51.9 8.3 %collective-permute-start.3 = (bf16[1,2,1,2,64,512]{5,4,3,2,1,0:T(8,128)(2,1)S(1)}, bf16[1,2,1,2,64,512]{5,4,3,2,1,0:T(8,128)(2,1)S(1)}, u32[]{:S(2)}, u32[]{:S(2)}) collective-permute-start(bf16[1,2,1,2,64,512]{5,4,3,2,1,0:T(8,128)(2,1)S(1)} %slice.211), channel_id=1, source_target_pairs={{0,4},{1,5},{2,6},{3,7},{4,0},{5,1},{6,2},{7,3},{8,12},{9,13},{10,... | collective-permute-start | bytes 786440 | tf_op jit(solution)/shard_map/ppermute | solution.py:62
  55.8 8.2 %collective-permute-start.7 = (bf16[2,1,2,1,64,512]{5,4,3,2,1,0:T(8,128)(2,1)S(1)}, bf16[2,1,2,1,64,512]{5,4,3,2,1,0:T(8,128)(2,1)S(1)}, u32[]{:S(2)}, u32[]{:S(2)}) collective-permute-start(bf16[2,1,2,1,64,512]{5,4,3,2,1,0:T(8,128)(2,1)S(1)} %slice.220), channel_id=1, source_target_pairs={{0,12},{1,13},{2,14},{3,15},{4,8},{5,9},{6,10},{7,11},{8,4},{9,5},... | collective-permute-start | bytes 786440 | tf_op jit(solution)/shard_map/ppermute | solution.py:62
  58.0 6.3 %collective-permute-start.11 = (bf16[1,2,1,2,64,512]{5,4,3,2,1,0:T(8,128)(2,1)S(1)}, bf16[1,2,1,2,64,512]{5,4,3,2,1,0:T(8,128)(2,1)S(1)}, u32[]{:S(2)}, u32[]{:S(2)}) collective-permute-start(bf16[1,2,1,2,64,512]{5,4,3,2,1,0:T(8,128)(2,1)S(1)} %slice.229), channel_id=1, source_target_pairs={{0,2},{1,3},{2,0},{3,1},{4,6},{5,7},{6,4},{7,5},{8,10},{9,11},{10,... | collective-permute-start | bytes 786440 | tf_op jit(solution)/shard_map/ppermute | solution.py:62
  58.3 7.7 %collective-permute-start.15 = (bf16[2,1,2,1,64,512]{5,4,3,2,1,0:T(8,128)(2,1)S(1)}, bf16[2,1,2,1,64,512]{5,4,3,2,1,0:T(8,128)(2,1)S(1)}, u32[]{:S(2)}, u32[]{:S(2)}) collective-permute-start(bf16[2,1,2,1,64,512]{5,4,3,2,1,0:T(8,128)(2,1)S(1)} %slice.238), channel_id=1, source_target_pairs={{0,130},{1,131},{2,128},{3,129},{4,134},{5,135},{6,132},{7,133},{8... | collective-permute-start | bytes 786440 | tf_op jit(solution)/shard_map/ppermute | solution.py:62
  60.3 8.3 %collective-permute-start.4 = (bf16[1,1,1,2,64,512]{5,4,3,2,1,0:T(8,128)(2,1)S(1)}, bf16[1,1,1,2,64,512]{5,4,3,2,1,0:T(8,128)(2,1)S(1)}, u32[]{:S(2)}, u32[]{:S(2)}) collective-permute-start(bf16[1,1,1,2,64,512]{5,4,3,2,1,0:T(8,128)(2,1)S(1)} %slice.213), channel_id=1, source_target_pairs={{0,130},{1,131},{2,128},{3,129},{4,134},{5,135},{6,132},{7,133},{8... | collective-permute-start | bytes 393224 | tf_op jit(solution)/shard_map/ppermute | solution.py:62
  64.1 5.3 %collective-permute-start.8 = (bf16[1,1,2,1,64,512]{5,4,3,2,1,0:T(8,128)(2,1)S(1)}, bf16[1,1,2,1,64,512]{5,4,3,2,1,0:T(8,128)(2,1)S(1)}, u32[]{:S(2)}, u32[]{:S(2)}) collective-permute-start(bf16[1,1,2,1,64,512]{5,4,3,2,1,0:T(8,128)(2,1)S(1)} %slice.222), channel_id=1, source_target_pairs={{0,2},{1,3},{2,0},{3,1},{4,6},{5,7},{6,4},{7,5},{8,10},{9,11},{10,... | collective-permute-start | bytes 393224 | tf_op jit(solution)/shard_map/ppermute | solution.py:62
  64.4 5.4 %collective-permute-start.12 = (bf16[1,2,1,1,64,512]{5,4,3,2,1,0:T(8,128)(2,1)S(1)}, bf16[1,2,1,1,64,512]{5,4,3,2,1,0:T(8,128)(2,1)S(1)}, u32[]{:S(2)}, u32[]{:S(2)}) collective-permute-start(bf16[1,2,1,1,64,512]{5,4,3,2,1,0:T(8,128)(2,1)S(1)} %slice.231), channel_id=1, source_target_pairs={{0,12},{1,13},{2,14},{3,15},{4,8},{5,9},{6,10},{7,11},{8,4},{9,5},... | collective-permute-start | bytes 393224 | tf_op jit(solution)/shard_map/ppermute | solution.py:62
  66.1 5.7 %collective-permute-start.16 = (bf16[2,1,1,1,64,512]{5,4,3,2,1,0:T(8,128)(2,1)S(1)}, bf16[2,1,1,1,64,512]{5,4,3,2,1,0:T(8,128)(2,1)S(1)}, u32[]{:S(2)}, u32[]{:S(2)}) collective-permute-start(bf16[2,1,1,1,64,512]{5,4,3,2,1,0:T(8,128)(2,1)S(1)} %slice.240), channel_id=1, source_target_pairs={{0,4},{1,5},{2,6},{3,7},{4,0},{5,1},{6,2},{7,3},{8,12},{9,13},{10,... | collective-permute-start | bytes 393224 | tf_op jit(solution)/shard_map/ppermute | solution.py:62
  79.7 4.8 %collective-permute-start.19 = (bf16[2,1,1,32,512]{4,3,2,1,0:T(8,128)(2,1)S(1)}, bf16[2,1,1,32,512]{4,3,2,1,0:T(8,128)(2,1)S(1)}, u32[]{:S(2)}, u32[]{:S(2)}) collective-permute-start(bf16[2,1,1,32,512]{4,3,2,1,0:T(8,128)(2,1)S(1)} %broadcast_select_fusion.1), channel_id=1, source_target_pairs={{0,32},{1,33},{2,34},{3,35},{4,36},{5,37},{6,38},{7,39},{8,40},{9,... | collective-permute-start | bytes 196616 | tf_op jit(solution)/shard_map/ppermute | solution.py:66
  84.6 8.3 %collective-permute-start.20 = (bf16[1,1,1,32,512]{4,3,2,1,0:T(8,128)(2,1)S(1)}, bf16[1,1,1,32,512]{4,3,2,1,0:T(8,128)(2,1)S(1)}, u32[]{:S(2)}, u32[]{:S(2)}) collective-permute-start(bf16[1,1,1,32,512]{4,3,2,1,0:T(8,128)(2,1)S(1)} %broadcast_select_fusion.2), channel_id=1, source_target_pairs={{0,64},{1,65},{2,66},{3,67},{4,68},{5,69},{6,70},{7,71},{8,72},{9,... | collective-permute-start | bytes 98312 | tf_op jit(solution)/shard_map/ppermute | solution.py:66
  93.5 6.8 %collective-permute-start.21 = (bf16[1,32,512]{2,1,0:T(8,128)(2,1)S(1)}, bf16[1,32,512]{2,1,0:T(8,128)(2,1)S(1)}, u32[]{:S(2)}, u32[]{:S(2)}) collective-permute-start(bf16[1,32,512]{2,1,0:T(8,128)(2,1)S(1)} %get-tuple-element.9), channel_id=1, source_target_pairs={{0,64},{1,65},{2,66},{3,67},{4,68},{5,69},{6,70},{7,71},{8,72},{9,... | collective-permute-start | bytes 98312 | tf_op jit(solution)/shard_map/ppermute | solution.py:66
  109.4 25.0 %collective-permute-start.24 = (bf16[1,1,1,1,64,512]{5,4,3,2,1,0:T(8,128)(2,1)S(1)}, bf16[1,1,1,1,64,512]{5,4,3,2,1,0:T(8,128)(2,1)S(1)}, u32[]{:S(2)}, u32[]{:S(2)}) collective-permute-start(bf16[1,1,1,1,64,512]{5,4,3,2,1,0:T(8,128)(2,1)S(1)} %bitcast.98), channel_id=1, source_target_pairs={{0,12},{1,13},{2,14},{3,15},{4,8},{5,9},{6,10},{7,11},{8,4},{9,5},... | collective-permute-start | bytes 196616 | tf_op jit(solution)/shard_map/ppermute | solution.py:62
  120.8 54.5 %collective-permute-start.40 = (bf16[256,4096]{1,0:T(8,128)(2,1)}, bf16[256,4096]{1,0:T(8,128)(2,1)}, u32[]{:S(2)}, u32[]{:S(2)}) collective-permute-start(bf16[256,4096]{1,0:T(8,128)(2,1)} %pack.3), channel_id=1, source_target_pairs={{0,1},{1,0},{2,3},{3,2},{4,5},{5,4},{6,7},{7,6},{8,9},{9,8},{10,11... | collective-permute-start | bytes 6291464 | tf_op jit(solution)/shard_map/ppermute | solution.py:70
  134.4 8.1 %collective-permute-start.36 = (bf16[1,1,1,1,64,512]{5,4,3,2,1,0:T(8,128)(2,1)S(1)}, bf16[1,1,1,1,64,512]{5,4,3,2,1,0:T(8,128)(2,1)S(1)}, u32[]{:S(2)}, u32[]{:S(2)}) collective-permute-start(bf16[1,1,1,1,64,512]{5,4,3,2,1,0:T(8,128)(2,1)S(1)} %bitcast.83), channel_id=1, source_target_pairs={{0,2},{1,3},{2,0},{3,1},{4,6},{5,7},{6,4},{7,5},{8,10},{9,11},{10,... | collective-permute-start | bytes 196616 | tf_op jit(solution)/shard_map/ppermute | solution.py:62
  134.5 7.0 %collective-permute-start.25 = (bf16[1,1,1,2,64,512]{5,4,3,2,1,0:T(8,128)(2,1)S(1)}, bf16[1,1,1,2,64,512]{5,4,3,2,1,0:T(8,128)(2,1)S(1)}, u32[]{:S(2)}, u32[]{:S(2)}) collective-permute-start(bf16[1,1,1,2,64,512]{5,4,3,2,1,0:T(8,128)(2,1)S(1)} %pad_maximum_fusion.17), channel_id=1, source_target_pairs={{0,130},{1,131},{2,128},{3,129},{4,134},{5,135},{6,132},{7,133},{8... | collective-permute-start | bytes 393224 | tf_op jit(solution)/shard_map/ppermute | solution.py:62
  137.2 6.0 %collective-permute-start.29 = (bf16[1,1,2,1,64,512]{5,4,3,2,1,0:T(8,128)(2,1)S(1)}, bf16[1,1,2,1,64,512]{5,4,3,2,1,0:T(8,128)(2,1)S(1)}, u32[]{:S(2)}, u32[]{:S(2)}) collective-permute-start(bf16[1,1,2,1,64,512]{5,4,3,2,1,0:T(8,128)(2,1)S(1)} %pad_maximum_fusion.18), channel_id=1, source_target_pairs={{0,2},{1,3},{2,0},{3,1},{4,6},{5,7},{6,4},{7,5},{8,10},{9,11},{10,... | collective-permute-start | bytes 393224 | tf_op jit(solution)/shard_map/ppermute | solution.py:62
  138.4 6.1 %collective-permute-start.33 = (bf16[1,2,1,1,64,512]{5,4,3,2,1,0:T(8,128)(2,1)S(1)}, bf16[1,2,1,1,64,512]{5,4,3,2,1,0:T(8,128)(2,1)S(1)}, u32[]{:S(2)}, u32[]{:S(2)}) collective-permute-start(bf16[1,2,1,1,64,512]{5,4,3,2,1,0:T(8,128)(2,1)S(1)} %pad_maximum_fusion.19), channel_id=1, source_target_pairs={{0,12},{1,13},{2,14},{3,15},{4,8},{5,9},{6,10},{7,11},{8,4},{9,5},... | collective-permute-start | bytes 393224 | tf_op jit(solution)/shard_map/ppermute | solution.py:62
  141.5 6.8 %collective-permute-start.26 = (bf16[1,2,1,2,64,512]{5,4,3,2,1,0:T(8,128)(2,1)S(1)}, bf16[1,2,1,2,64,512]{5,4,3,2,1,0:T(8,128)(2,1)S(1)}, u32[]{:S(2)}, u32[]{:S(2)}) collective-permute-start(bf16[1,2,1,2,64,512]{5,4,3,2,1,0:T(8,128)(2,1)S(1)} %pad_maximum_fusion.11), channel_id=1, source_target_pairs={{0,4},{1,5},{2,6},{3,7},{4,0},{5,1},{6,2},{7,3},{8,12},{9,13},{10,... | collective-permute-start | bytes 786440 | tf_op jit(solution)/shard_map/ppermute | solution.py:62
  142.5 8.6 %collective-permute-start.37 = (bf16[2,1,1,1,64,512]{5,4,3,2,1,0:T(8,128)(2,1)S(1)}, bf16[2,1,1,1,64,512]{5,4,3,2,1,0:T(8,128)(2,1)S(1)}, u32[]{:S(2)}, u32[]{:S(2)}) collective-permute-start(bf16[2,1,1,1,64,512]{5,4,3,2,1,0:T(8,128)(2,1)S(1)} %pad_maximum_fusion.20), channel_id=1, source_target_pairs={{0,4},{1,5},{2,6},{3,7},{4,0},{5,1},{6,2},{7,3},{8,12},{9,13},{10,... | collective-permute-start | bytes 393224 | tf_op jit(solution)/shard_map/ppermute | solution.py:62
  143.2 9.4 %collective-permute-start.30 = (bf16[2,1,2,1,64,512]{5,4,3,2,1,0:T(8,128)(2,1)S(1)}, bf16[2,1,2,1,64,512]{5,4,3,2,1,0:T(8,128)(2,1)S(1)}, u32[]{:S(2)}, u32[]{:S(2)}) collective-permute-start(bf16[2,1,2,1,64,512]{5,4,3,2,1,0:T(8,128)(2,1)S(1)} %pad_maximum_fusion.12), channel_id=1, source_target_pairs={{0,12},{1,13},{2,14},{3,15},{4,8},{5,9},{6,10},{7,11},{8,4},{9,5},... | collective-permute-start | bytes 786440 | tf_op jit(solution)/shard_map/ppermute | solution.py:62
  144.5 10.9 %collective-permute-start.34 = (bf16[1,2,1,2,64,512]{5,4,3,2,1,0:T(8,128)(2,1)S(1)}, bf16[1,2,1,2,64,512]{5,4,3,2,1,0:T(8,128)(2,1)S(1)}, u32[]{:S(2)}, u32[]{:S(2)}) collective-permute-start(bf16[1,2,1,2,64,512]{5,4,3,2,1,0:T(8,128)(2,1)S(1)} %pad_maximum_fusion.13), channel_id=1, source_target_pairs={{0,2},{1,3},{2,0},{3,1},{4,6},{5,7},{6,4},{7,5},{8,10},{9,11},{10,... | collective-permute-start | bytes 786440 | tf_op jit(solution)/shard_map/ppermute | solution.py:62
  148.3 13.7 %collective-permute-start.27 = (bf16[1,2,2,2,64,512]{5,4,3,2,1,0:T(8,128)(2,1)S(1)}, bf16[1,2,2,2,64,512]{5,4,3,2,1,0:T(8,128)(2,1)}, u32[]{:S(2)}, u32[]{:S(2)}) collective-permute-start(bf16[1,2,2,2,64,512]{5,4,3,2,1,0:T(8,128)(2,1)S(1)} %pad_maximum_fusion.4), channel_id=1, source_target_pairs={{0,2},{1,3},{2,0},{3,1},{4,6},{5,7},{6,4},{7,5},{8,10},{9,11},{10,... | collective-permute-start | bytes 1572872 | tf_op jit(solution)/shard_map/ppermute | solution.py:62
  151.8 7.2 %collective-permute-start.38 = (bf16[2,1,2,1,64,512]{5,4,3,2,1,0:T(8,128)(2,1)}, bf16[2,1,2,1,64,512]{5,4,3,2,1,0:T(8,128)(2,1)S(1)}, u32[]{:S(2)}, u32[]{:S(2)}) collective-permute-start(bf16[2,1,2,1,64,512]{5,4,3,2,1,0:T(8,128)(2,1)} %pad_maximum_fusion.14), channel_id=1, source_target_pairs={{0,130},{1,131},{2,128},{3,129},{4,134},{5,135},{6,132},{7,133},{8... | collective-permute-start | bytes 786440 | tf_op jit(solution)/shard_map/ppermute | solution.py:62
  153.5 16.9 %collective-permute-start.31 = (bf16[2,1,2,2,64,512]{5,4,3,2,1,0:T(8,128)(2,1)}, bf16[2,1,2,2,64,512]{5,4,3,2,1,0:T(8,128)(2,1)}, u32[]{:S(2)}, u32[]{:S(2)}) collective-permute-start(bf16[2,1,2,2,64,512]{5,4,3,2,1,0:T(8,128)(2,1)} %pad_maximum_fusion.5), channel_id=1, source_target_pairs={{0,130},{1,131},{2,128},{3,129},{4,134},{5,135},{6,132},{7,133},{8... | collective-permute-start | bytes 1572872 | tf_op jit(solution)/shard_map/ppermute | solution.py:62
  156.3 15.3 %collective-permute-start.35 = (bf16[2,2,1,2,64,512]{5,4,3,2,1,0:T(8,128)(2,1)}, bf16[2,2,1,2,64,512]{5,4,3,2,1,0:T(8,128)(2,1)}, u32[]{:S(2)}, u32[]{:S(2)}) collective-permute-start(bf16[2,2,1,2,64,512]{5,4,3,2,1,0:T(8,128)(2,1)} %pad_maximum_fusion.6), channel_id=1, source_target_pairs={{0,4},{1,5},{2,6},{3,7},{4,0},{5,1},{6,2},{7,3},{8,12},{9,13},{10,... | collective-permute-start | bytes 1572872 | tf_op jit(solution)/shard_map/ppermute | solution.py:62
  159.1 15.0 %collective-permute-start.39 = (bf16[2,2,2,1,64,512]{5,4,3,2,1,0:T(8,128)(2,1)S(1)}, bf16[2,2,2,1,64,512]{5,4,3,2,1,0:T(8,128)(2,1)S(1)}, u32[]{:S(2)}, u32[]{:S(2)}) collective-permute-start(bf16[2,2,2,1,64,512]{5,4,3,2,1,0:T(8,128)(2,1)S(1)} %pad_maximum_fusion.7), channel_id=1, source_target_pairs={{0,12},{1,13},{2,14},{3,15},{4,8},{5,9},{6,10},{7,11},{8,4},{9,5},... | collective-permute-start | bytes 1572872 | tf_op jit(solution)/shard_map/ppermute | solution.py:62
  188.6 4.8 %collective-permute-start.41 = (f32[256,512]{1,0:T(8,128)}, f32[256,512]{1,0:T(8,128)S(1)}, u32[]{:S(2)}, u32[]{:S(2)}) collective-permute-start(f32[256,512]{1,0:T(8,128)} %get-tuple-element.8), channel_id=1, source_target_pairs={{0,1},{1,0},{2,3},{3,2},{4,5},{5,4},{6,7},{7,6},{8,9},{9,8},{10,11... | collective-permute-start | bytes 1572872 | tf_op jit(solution)/shard_map/ppermute | solution.py:70
  (21 other events, 192.8 us)

commit v2 on v0

v2 whole, which is shorter than its diff:
```python
import functools
import itertools

import jax
import jax.numpy as jnp
from jax import lax
from jax.experimental import pallas as pl
from jax.experimental.pallas import tpu as pltpu
from jax.sharding import PartitionSpec as P

ADAM_STEP = 10
beta_first = 0.9
beta_second = 0.95
learn_rate = 0.002
decay_rate = 0.1
adam_eps = 1e-08

AXES = ("outer", "inner")
SIZES = (2, 8, 4, 2, 2)
TOK = 256
COLS = 512
HALF = 4096
BLOCK = 256
BLOCKS = 16
PARTS = 4
ROWS = 64

ORDERS = ((0, 2, 1, 3), (1, 3, 0, 2), (2, 0, 3, 1), (3, 1, 2, 0))


def moves(change):
    pairs = []
    for here in itertools.product(*(range(n) for n in SIZES)):
        source = target = 0
        for n, i, j in zip(SIZES, here, change(*here)):
            source, target = source * n + i, target * n + j
        pairs.append((source, target))
    return pairs


def paired(i, odd):
    if odd:
        return (i + 1) % 4 if i % 2 else (i - 1) % 4
    return i ^ 1


def pair_x(odd, xh, z, y, xl, c):
    x = paired(xh * 2 + xl, odd)
    return x // 2, z, y, x % 2, c


def pair_y(odd, xh, z, y, xl, c):
    return xh, z, paired(y, odd), xl, c


PAIRINGS = tuple(moves(functools.partial(f, odd)) for f in (pair_x, pair_y) for odd in (0, 1))


def across(array, pairing):
    return lax.ppermute(array, AXES, PAIRINGS[pairing])


def z_swap(array, mask):
    return lax.ppermute(array, AXES, moves(lambda xh, z, y, xl, c: (xh, z ^ mask, y, xl, c)))


def core_swap(array):
    return lax.ppermute(array, AXES, moves(lambda xh, z, y, xl, c: (xh, z, y, xl, 1 - c)))


def place():
    outer, inner = lax.axis_index("outer"), lax.axis_index("inner")
    return outer // 8, outer % 8, inner // 4, (inner // 2) % 2, inner % 2


def columns_of(where, r, core):
    xh, _, y, xl, _ = where
    a, b, c, d = (r >> 3) & 1, (r >> 2) & 1, (r >> 1) & 1, r & 1
    to_xh, to_xl, to_y = xh ^ b, xl ^ (a ^ b), y ^ (2 * d + (c ^ d))
    block = ((to_y * 2 + to_xl) * 2 + core) * 2 + to_xh
    return pl.ds(pl.multiple_of(block * BLOCK, BLOCK), BLOCK)


def side_and_slot(m, r):
    bits = [(r >> (3 - v)) & 1 for v in range(4)]
    side = bits.pop(ORDERS[m][0])
    return side, bits[0] * 4 + bits[1] * 2 + bits[2]


def pair_rows(where, m):
    z = where[1]
    first = jnp.where(z < 4, z, 7 - z) ^ m
    return (
        pl.ds(pl.multiple_of(first * 32, 32), 32),
        pl.ds(pl.multiple_of((7 - first) * 32, 32), 32),
    )


ANY = pl.BlockSpec(memory_space=pl.ANY)
VMEM = pl.BlockSpec(memory_space=pltpu.VMEM)
PARAMS = pltpu.CompilerParams(vmem_limit_bytes=40 * 1024 * 1024)


def pack_kernel(acts, master, first, second, packed, state, sems):
    where = place()
    copies = [
        pltpu.make_async_copy(
            acts.at[:, columns_of(where, r, 1 - where[4])],
            packed.at[:, pl.ds(r * BLOCK, BLOCK)],
            sems.at[r],
        )
        for r in range(BLOCKS)
    ] + [
        pltpu.make_async_copy(source, state.at[i], sems.at[BLOCKS + i])
        for i, source in enumerate((master, first, second))
    ]
    for copy in copies:
        copy.start()
    for copy in copies:
        copy.wait()


def pack(acts, master, first, second):
    return pl.pallas_call(
        pack_kernel,
        out_shape=(
            jax.ShapeDtypeStruct((TOK, HALF), jnp.bfloat16),
            jax.ShapeDtypeStruct((3, 32, COLS), jnp.float32),
        ),
        in_specs=[ANY] * 4,
        out_specs=(ANY, ANY),
        scratch_shapes=[pltpu.SemaphoreType.DMA((BLOCKS + 3,))],
        compiler_params=PARAMS,
        name="pack",
    )(acts, master, first, second)


def term_kernel(acts, got, grads, got_grads, tokens, *refs):
    halves, packed, both, grads_both, term, sems = (
        refs[: 2 * PARTS],
        *refs[2 * PARTS :],
    )
    where = place()
    own, other, pack_copies = [], [], []
    for r in range(BLOCKS):
        here = pl.ds(r * BLOCK, BLOCK)
        own.append(
            pltpu.make_async_copy(
                acts.at[:, columns_of(where, r, where[4])], both.at[:TOK, here], sems.at[r]
            )
        )
        other.append(
            pltpu.make_async_copy(got.at[:, here], both.at[TOK:, here], sems.at[BLOCKS + r])
        )
        pack_copies.append(
            pltpu.make_async_copy(
                tokens.at[:, columns_of(where, r, 1 - where[4])],
                packed.at[:, here],
                sems.at[2 * BLOCKS + r],
            )
        )
    for r in range(BLOCKS):
        own[r].start()
        other[r].start()
    grads_both[:TOK] = grads[...]
    grads_both[TOK:] = got_grads[...]
    rows = [pair_rows(where, m) for m in range(PARTS)]
    for r in range(BLOCKS):
        own[r].wait()
        other[r].wait()
        pack_copies[r].start()
        term[r % 2] = lax.dot_general(
            both[:, r * BLOCK : (r + 1) * BLOCK],
            grads_both[...],
            (((0,), (0,)), ((), ())),
            preferred_element_type=jnp.float32,
        ).astype(jnp.bfloat16)
        for m in range(PARTS):
            side, slot = side_and_slot(m, r)
            out = halves[2 * m + side]
            out[slot, :32] = term[r % 2, rows[m][0]]
            out[slot, 32:] = term[r % 2, rows[m][1]]
    for copy in pack_copies:
        copy.wait()


def gradient_term(acts, got, grads, got_grads, tokens):
    half = jax.ShapeDtypeStruct((8, ROWS, COLS), jnp.bfloat16)
    return pl.pallas_call(
        term_kernel,
        out_shape=(half,) * (2 * PARTS) + (jax.ShapeDtypeStruct((TOK, HALF), jnp.bfloat16),),
        in_specs=[ANY, ANY, VMEM, VMEM, ANY],
        out_specs=(VMEM,) * (2 * PARTS) + (ANY,),
        scratch_shapes=[
            pltpu.VMEM((2 * TOK, HALF), jnp.bfloat16),
            pltpu.VMEM((2 * TOK, COLS), jnp.bfloat16),
            pltpu.VMEM((2, BLOCK, COLS), jnp.bfloat16),
            pltpu.SemaphoreType.DMA((3 * BLOCKS,)),
        ],
        compiler_params=PARAMS,
        name="gradient_term",
    )(acts, got, grads, got_grads, tokens)


STRIPE = 1024


def project_kernel(tokens, got, *refs):
    halves = refs[: 2 * PARTS]
    kept, mine, theirs, both, held, weights, total, sems = refs[2 * PARTS :]
    where = place()
    weight_copies = [
        pltpu.make_async_copy(halves[i], held.at[i], sems.at[i]) for i in range(2 * PARTS)
    ]
    token_copies = [
        pltpu.make_async_copy(
            tokens.at[:, columns_of(where, r, where[4])],
            both.at[:TOK, pl.ds(r * BLOCK, BLOCK)],
            sems.at[8 + r],
        )
        for r in range(BLOCKS)
    ]
    got_copies = [
        pltpu.make_async_copy(
            got.at[:, pl.ds(s * STRIPE, STRIPE)],
            both.at[TOK:, pl.ds(s * STRIPE, STRIPE)],
            sems.at[8 + BLOCKS + s],
        )
        for s in range(HALF // STRIPE)
    ]
    for copy in weight_copies + token_copies + got_copies:
        copy.start()
    rows = [pair_rows(where, m) for m in range(PARTS)]
    for copy in weight_copies:
        copy.wait()
    per = STRIPE // BLOCK
    for s in range(HALF // STRIPE):
        for k in range(per):
            r = s * per + k
            for m in range(PARTS):
                side, slot = side_and_slot(m, r)
                for j in range(2):
                    at = pl.ds(pl.multiple_of(k * BLOCK + rows[m][j].start, 32), 32)
                    weights[s % 2, at] = held[2 * m + side, slot, j * 32 : j * 32 + 32]
            token_copies[r].wait()
        got_copies[s].wait()
        if s == 0:
            kept[pl.ds(pl.multiple_of(where[0] * BLOCK, BLOCK), BLOCK)] = weights[0, :BLOCK]
        if s == 3:
            kept[pl.ds(pl.multiple_of((1 - where[0]) * BLOCK, BLOCK), BLOCK)] = weights[1, :BLOCK]
        product = jnp.dot(
            both[:, s * STRIPE : (s + 1) * STRIPE],
            weights[s % 2],
            preferred_element_type=jnp.float32,
        )
        if s == 0:
            total[...] = product
        elif s < HALF // STRIPE - 1:
            total[...] += product
        else:
            product += total[...]
            mine[...] = product[:TOK]
            theirs[...] = product[TOK:].astype(jnp.bfloat16)


def project(tokens, got, halves):
    return pl.pallas_call(
        project_kernel,
        out_shape=(
            jax.ShapeDtypeStruct((2 * BLOCK, COLS), jnp.bfloat16),
            jax.ShapeDtypeStruct((TOK, COLS), jnp.float32),
            jax.ShapeDtypeStruct((TOK, COLS), jnp.bfloat16),
        ),
        in_specs=[ANY] * (2 + 2 * PARTS),
        out_specs=(VMEM,) * 3,
        scratch_shapes=[
            pltpu.VMEM((2 * TOK, HALF), jnp.bfloat16),
            pltpu.VMEM((2 * PARTS, 8, ROWS, COLS), jnp.bfloat16),
            pltpu.VMEM((2, STRIPE, COLS), jnp.bfloat16),
            pltpu.VMEM((2 * TOK, COLS), jnp.float32),
            pltpu.SemaphoreType.DMA((8 + BLOCKS + HALF // STRIPE,)),
        ],
        compiler_params=PARAMS,
        name="project",
    )(tokens, got, *halves)


def adamw_update(gradient, master_weights, first_moment, second_moment):
    new_first = beta_first * first_moment + (1.0 - beta_first) * gradient
    new_second = beta_second * second_moment + (1.0 - beta_second) * gradient * gradient
    first_hat = new_first / (1.0 - beta_first**ADAM_STEP)
    second_hat = new_second / (1.0 - beta_second**ADAM_STEP)
    new_master = master_weights - learn_rate * (
        first_hat / (jnp.sqrt(second_hat) + adam_eps) + decay_rate * master_weights
    )
    return (new_master, new_first, new_second)


def wide(array):
    return array.astype(jnp.float32)


def reduce_parts(halves):
    parts = []
    left = []
    for m in range(PARTS):
        keep, send = halves[2 * m], halves[2 * m + 1]
        left.append([v for v in range(4) if v != ORDERS[m][0]])
        got = across(send, ORDERS[m][0])
        parts.append((wide(keep) + wide(got)).astype(jnp.bfloat16).reshape(2, 2, 2, ROWS, COLS))
    for step in range(1, 4):
        for m in range(PARTS):
            v = ORDERS[m][step]
            dim = left[m].index(v)
            left[m].remove(v)
            keep = lax.index_in_dim(parts[m], 0, dim, keepdims=False)
            got = across(lax.index_in_dim(parts[m], 1, dim, keepdims=False), v)
            total = wide(keep) + wide(got)
            parts[m] = total if step == 3 and m == 0 else total.astype(jnp.bfloat16)
    return parts


def reduce_z(parts):
    total = parts[0]
    for m in range(1, PARTS):
        total = total + wide(z_swap(parts[m], m))
    total = total.astype(jnp.bfloat16)
    return (wide(total) + wide(z_swap(total, 7))).reshape(2, 32, COLS)


def gather_parts(pair):
    parts = [pair] + [z_swap(pair, m) for m in range(1, PARTS)]
    known = [[] for _ in range(PARTS)]
    for step in range(3, 0, -1):
        for m in range(PARTS):
            v = ORDERS[m][step]
            known[m] = sorted(known[m] + [v])
            parts[m] = jnp.stack([parts[m], across(parts[m], v)], axis=known[m].index(v))
    halves = []
    for m in range(PARTS):
        keep = parts[m].reshape(8, ROWS, COLS)
        halves += [keep, across(keep, ORDERS[m][0])]
    return halves


def local(activations, output_grads, master_weights, first_moment, second_moment, next_tokens):
    low = lax.axis_index("outer") % 8 < 4
    packed, state = pack(activations, master_weights, first_moment, second_moment)
    got_acts = core_swap(packed)
    got_grads = core_swap(output_grads)
    got_state = z_swap(state, 7)
    *halves, packed_tokens = gradient_term(
        activations, got_acts, output_grads, got_grads, next_tokens
    )
    got_tokens = core_swap(packed_tokens)

    gradient = reduce_z(reduce_parts(halves))
    pairs = jnp.stack([jnp.where(low, state, got_state), jnp.where(low, got_state, state)], axis=1)
    updated = adamw_update(gradient, *pairs)
    new_master, new_first, new_second = (jnp.where(low, u[0], u[1]) for u in updated)
    pair = updated[0].astype(jnp.bfloat16).reshape(ROWS, COLS)

    kept_weights, mine, theirs = project(next_tokens, got_tokens, gather_parts(pair))
    projection = (mine + wide(core_swap(theirs))).astype(jnp.bfloat16)
    return (new_master, new_first, new_second, kept_weights, projection)


def solution(mesh):
    placed = (
        P(("outer", "inner"), None),
        P(("outer", "inner"), None),
        P(("inner", "outer"), None),
        P(("inner", "outer"), None),
        P(("inner", "outer"), None),
        P(("outer", "inner"), None),
    )
    return jax.shard_map(
        local,
        mesh=mesh,
        in_specs=placed,
        out_specs=(
            P(("inner", "outer"), None),
            P(("inner", "outer"), None),
            P(("inner", "outer"), None),
            P("inner", None),
            P(("outer", "inner"), None),
        ),
        check_vma=False,
    )
```

time: 1440 us -> 128 us (0.09)
  waiting for transfers between devices: 1350 us -> 34.1 us
  starting transfers between devices: 0.08 us -> 70.9 us
  blocking collectives: 33.8 us -> 0 us
    reduce_scatter x1 -> x0, waiting for transfers between devices: 1290 us -> none  [local(): lax.psum_scatter(rounded_term(columns, output_grads), ('outer', 'inner'),...]
    ppermute x0 -> x44, starting transfers between devices: none -> 70.9 us  [the longest x32 34.8 us: across(): return lax.ppermute(array, AXES, PAIRINGS[pairing])]
    all_gather x1 -> x0, waiting for transfers between devices: 59.4 us -> none  [local(): lax.all_gather(kept_weights, 'inner', axis=0, tiled=True)]
    ppermute x0 -> x44, waiting for transfers between devices: none -> 34.1 us  [the longest x32 27.2 us: across(): return lax.ppermute(array, AXES, PAIRINGS[pairing])]
    all_gather x1 -> x0, blocking collectives: 33.8 us -> none  [local(): kept_weights = lax.all_gather(kept_shard, 'outer', axis=0, tiled=True)]
  transfers between devices with their start and end apart: 2 -> 44, of which waited for: 2 -> 17; matrix products, arithmetic and copies ran while one was open for 0% -> 3% of each run, Pallas kernels for 0% -> 0%
where the time goes in v2:
time: 128 us
  starting transfers between devices  70.9 us (55%)
  waiting for transfers between devices  34.1 us (27%)
  Pallas kernels  13 us (10%)
  local copies, waits for them, and re-layouts  5.03 us (4%)
  other arithmetic  3.85 us (3%)
    ppermute x32, starting transfers between devices, across(): return lax.ppermute(array, AXES, PAIRINGS[pairing])  34.8 us
    ppermute x32, waiting for transfers between devices, across(): return lax.ppermute(array, AXES, PAIRINGS[pairing])  27.2 us
    ppermute x4, starting transfers between devices, core_swap(): lax.ppermute(array, AXES, moves(lambda xh, z, y, xl, c: (xh, z, y, xl, 1...  19.9 us
    ppermute x8, starting transfers between devices, z_swap(): lax.ppermute(array, AXES, moves(lambda xh, z, y, xl, c: (xh, z ^ mask, y,...  16.1 us
    pallas_call x1, Pallas kernels, gradient_term(): pl.pallas_call(term_kernel, out_shape=(half,) * (2 * PARTS) + (jax.ShapeD...  7.46 us
    unnamed x13, local copies, waits for them, and re-layouts  4.72 us
    pallas_call x1, Pallas kernels, project(): pl.pallas_call(project_kernel, out_shape=(jax.ShapeDtypeStruct((2 * BLOCK...  4.67 us
    ppermute x4, waiting for transfers between devices, core_swap(): lax.ppermute(array, AXES, moves(lambda xh, z, y, xl, c: (xh, z, y, xl, 1...  4.06 us
  transfers between devices with their start and end apart: 44, of which 17 were waited for; matrix products, arithmetic and copies ran while one was open for 3% of the time, Pallas kernels for 0%

profile of v2, /device:TPU:1, one launch (start us, length us, event | category | flops | bytes accessed | tf_op | source)
XLA Modules:
  0.0 127.9 jit_solution(1212238552892552911)
XLA Ops:
  0.6 2.2 %copy-done = bf16[256,8192]{1,0:T(8,128)(2,1)S(1)} copy-done((bf16[256,8192]{1,0:T(8,128)(2,1)S(1)}, bf16[256,8192]{1,0:T(8,128)(2,1)}, u32[]{:S(2)}) %copy-start) | copy-done | bytes 4194328
  6.2 3.3 %collective-permute-start.1 = (bf16[256,4096]{1,0:T(8,128)(2,1)S(1)}, bf16[256,4096]{1,0:T(8,128)(2,1)S(1)}, u32[]{:S(2)}, u32[]{:S(2)}) collective-permute-start(bf16[256,4096]{1,0:T(8,128)(2,1)S(1)} %get-tuple-element.20), channel_id=1, source_target_pairs={{0,1},{1,0},{2,3},{3,2},{4,5},{5,4},{6,7},{7,6},{8,9},{9,8},{10,11... | collective-permute-start | bytes 6291464 | tf_op jit(solution)/shard_map/ppermute | solution.py:68
  9.6 4.1 %collective-permute-done.2.got_grads = bf16[256,512]{1,0:T(8,128)(2,1)S(1)} collective-permute-done((bf16[256,512]{1,0:T(8,128)(2,1)S(1)}, bf16[256,512]{1,0:T(8,128)(2,1)S(1)}, u32[]{:S(2)}, u32[]{:S(2)}) %collective-permute-start.2) | collective-permute-done | bytes 262176 | tf_op jit(solution)/shard_map/ppermute | solution.py:68
  13.7 7.5 %gradient_term.1 = (bf16[8,64,512]{2,1,0:T(8,128)(2,1)S(1)}, bf16[8,64,512]{2,1,0:T(8,128)(2,1)S(1)}, bf16[8,64,512]{2,1,0:T(8,128)(2,1)S(1)}, bf16[8,64,512]{2,...) custom-call(bf16[256,8192]{1,0:T(8,128)(2,1)S(1)} %copy-done, ...), custom_call_target="tpu_custom_call" | custom-call | tf_op jit(solution)/shard_map/gradient_term/pallas_call | solution.py:189
  23.3 1.9 %collective-permute-start.17 = (bf16[8,64,512]{2,1,0:T(8,128)(2,1)S(1)}, bf16[8,64,512]{2,1,0:T(8,128)(2,1)S(1)}, u32[]{:S(2)}, u32[]{:S(2)}) collective-permute-start(bf16[8,64,512]{2,1,0:T(8,128)(2,1)S(1)} %get-tuple-element.28), channel_id=1, source_target_pairs={{0,12},{1,13},{2,14},{3,15},{4,8},{5,9},{6,10},{7,11},{8,4},{9,5},... | collective-permute-start | bytes 1572872 | tf_op jit(solution)/shard_map/ppermute | solution.py:60
  25.2 10.4 %collective-permute-done.7 = bf16[8,64,512]{2,1,0:T(8,128)(2,1)S(1)} collective-permute-done((bf16[8,64,512]{2,1,0:T(8,128)(2,1)S(1)}, bf16[8,64,512]{2,1,0:T(8,128)(2,1)S(1)}, u32[]{:S(2)}, u32[]{:S(2)}) %collective-permute-start.7) | collective-permute-done | bytes 524320 | tf_op jit(solution)/shard_map/ppermute | solution.py:60
  37.4 2.6 %collective-permute-start.18 = (bf16[2,2,64,512]{3,2,0,1:T(8,128)(2,1)S(1)}, bf16[2,2,64,512]{3,2,0,1:T(8,128)(2,1)S(1)}, u32[]{:S(2)}, u32[]{:S(2)}) collective-permute-start(bf16[2,2,64,512]{3,2,0,1:T(8,128)(2,1)S(1)} %bitcast.203), channel_id=1, source_target_pairs={{0,130},{1,131},{2,128},{3,129},{4,134},{5,135},{6,132},{7,133},{8... | collective-permute-start | bytes 786440 | tf_op jit(solution)/shard_map/ppermute | solution.py:60
  40.2 3.4 %collective-permute-done.8 = bf16[2,2,64,512]{3,2,1,0:T(8,128)(2,1)S(1)} collective-permute-done((bf16[2,2,64,512]{3,2,1,0:T(8,128)(2,1)S(1)}, bf16[2,2,64,512]{3,2,1,0:T(8,128)(2,1)S(1)}, u32[]{:S(2)}, u32[]{:S(2)}) %collective-permute-start.8) | collective-permute-done | bytes 262176 | tf_op jit(solution)/shard_map/ppermute | solution.py:60
  43.9 1.6 %collective-permute-start.14 = (bf16[2,64,512]{2,1,0:T(8,128)(2,1)S(1)}, bf16[2,64,512]{2,1,0:T(8,128)(2,1)S(1)}, u32[]{:S(2)}, u32[]{:S(2)}) collective-permute-start(bf16[2,64,512]{2,1,0:T(8,128)(2,1)S(1)} %slice_bitcast_fusion.6), channel_id=1, source_target_pairs={{0,12},{1,13},{2,14},{3,15},{4,8},{5,9},{6,10},{7,11},{8,4},{9,5},... | collective-permute-start | bytes 393224 | tf_op jit(solution)/shard_map/ppermute | solution.py:60
  46.3 1.7 %collective-permute-start.5 = (bf16[2,64,512]{2,1,0:T(8,128)(2,1)S(1)}, bf16[2,64,512]{2,1,0:T(8,128)(2,1)S(1)}, u32[]{:S(2)}, u32[]{:S(2)}) collective-permute-start(bf16[2,64,512]{2,1,0:T(8,128)(2,1)S(1)} %slice_bitcast_fusion.10), channel_id=1, source_target_pairs={{0,130},{1,131},{2,128},{3,129},{4,134},{5,135},{6,132},{7,133},{8... | collective-permute-start | bytes 393224 | tf_op jit(solution)/shard_map/ppermute | solution.py:60
  48.1 1.5 %collective-permute-start.10 = (bf16[64,512]{1,0:T(8,128)(2,1)S(1)}, bf16[64,512]{1,0:T(8,128)(2,1)S(1)}, u32[]{:S(2)}, u32[]{:S(2)}) collective-permute-start(bf16[64,512]{1,0:T(8,128)(2,1)S(1)} %slice_bitcast_fusion.16), channel_id=1, source_target_pairs={{0,4},{1,5},{2,6},{3,7},{4,0},{5,1},{6,2},{7,3},{8,12},{9,13},{10,... | collective-permute-start | bytes 196616 | tf_op jit(solution)/shard_map/ppermute | solution.py:60
  49.7 1.8 %collective-permute-start.15 = (bf16[64,512]{1,0:T(8,128)(2,1)S(1)}, bf16[64,512]{1,0:T(8,128)(2,1)S(1)}, u32[]{:S(2)}, u32[]{:S(2)}) collective-permute-start(bf16[64,512]{1,0:T(8,128)(2,1)S(1)} %slice_bitcast_fusion.14), channel_id=1, source_target_pairs={{0,130},{1,131},{2,128},{3,129},{4,134},{5,135},{6,132},{7,133},{8... | collective-permute-start | bytes 196616 | tf_op jit(solution)/shard_map/ppermute | solution.py:60
  51.8 2.2 %collective-permute-start.6 = (bf16[64,512]{1,0:T(8,128)(2,1)S(1)}, bf16[64,512]{1,0:T(8,128)(2,1)S(1)}, u32[]{:S(2)}, u32[]{:S(2)}) collective-permute-start(bf16[64,512]{1,0:T(8,128)(2,1)S(1)} %slice_bitcast_fusion.18), channel_id=1, source_target_pairs={{0,12},{1,13},{2,14},{3,15},{4,8},{5,9},{6,10},{7,11},{8,4},{9,5},... | collective-permute-start | bytes 196616 | tf_op jit(solution)/shard_map/ppermute | solution.py:60
  54.0 1.7 %collective-permute-start.11 = (bf16[64,512]{1,0:T(8,128)(2,1)S(1)}, bf16[64,512]{1,0:T(8,128)(2,1)S(1)}, u32[]{:S(2)}, u32[]{:S(2)}) collective-permute-start(bf16[64,512]{1,0:T(8,128)(2,1)S(1)} %fusion.25), channel_id=1, source_target_pairs={{0,16},{1,17},{2,18},{3,19},{4,20},{5,21},{6,22},{7,23},{8,24},{9,... | collective-permute-start | bytes 196616 | tf_op jit(solution)/shard_map/ppermute | solution.py:64
  55.7 3.1 %collective-permute-start.16 = (bf16[64,512]{1,0:T(8,128)(2,1)S(1)}, bf16[64,512]{1,0:T(8,128)(2,1)S(1)}, u32[]{:S(2)}, u32[]{:S(2)}) collective-permute-start(bf16[64,512]{1,0:T(8,128)(2,1)S(1)} %fusion.24), channel_id=1, source_target_pairs={{0,32},{1,33},{2,34},{3,35},{4,36},{5,37},{6,38},{7,39},{8,40},{9,... | collective-permute-start | bytes 196616 | tf_op jit(solution)/shard_map/ppermute | solution.py:64
  59.5 4.0 %collective-permute-start = (f32[3,32,512]{2,1,0:T(8,128)S(1)}, f32[3,32,512]{2,1,0:T(8,128)S(1)}, u32[]{:S(2)}, u32[]{:S(2)}) collective-permute-start(f32[3,32,512]{2,1,0:T(8,128)S(1)} %get-tuple-element.19), channel_id=1, source_target_pairs={{0,112},{1,113},{2,114},{3,115},{4,116},{5,117},{6,118},{7,119},{8... | collective-permute-start | bytes 589832 | tf_op jit(solution)/shard_map/ppermute | solution.py:64
  63.9 3.1 %collective-permute-start.22 = (bf16[64,512]{1,0:T(8,128)(2,1)S(1)}, bf16[64,512]{1,0:T(8,128)(2,1)S(1)}, u32[]{:S(2)}, u32[]{:S(2)}) collective-permute-start(bf16[64,512]{1,0:T(8,128)(2,1)S(1)} %fusion.29), channel_id=1, source_target_pairs={{0,112},{1,113},{2,114},{3,115},{4,116},{5,117},{6,118},{7,119},{8... | collective-permute-start | bytes 196616 | tf_op jit(solution)/shard_map/ppermute | solution.py:64
  67.0 1.9 %collective-permute-done = f32[3,32,512]{2,1,0:T(8,128)S(1)} collective-permute-done((f32[3,32,512]{2,1,0:T(8,128)S(1)}, f32[3,32,512]{2,1,0:T(8,128)S(1)}, u32[]{:S(2)}, u32[]{:S(2)}) %collective-permute-start) | collective-permute-done | bytes 196640 | tf_op jit(solution)/shard_map/ppermute | solution.py:64
  69.0 6.1 %collective-permute-start.23 = (bf16[256,4096]{1,0:T(8,128)(2,1)S(1)}, bf16[256,4096]{1,0:T(8,128)(2,1)S(1)}, u32[]{:S(2)}, u32[]{:S(2)}) collective-permute-start(bf16[256,4096]{1,0:T(8,128)(2,1)S(1)} %get-tuple-element.29), channel_id=1, source_target_pairs={{0,1},{1,0},{2,3},{3,2},{4,5},{5,4},{6,7},{7,6},{8,9},{9,8},{10,11... | collective-permute-start | bytes 6291464 | tf_op jit(solution)/shard_map/ppermute | solution.py:68
  75.4 1.7 %collective-permute-start.38 = (bf16[64,512]{1,0:T(8,128)(2,1)S(1)}, bf16[64,512]{1,0:T(8,128)(2,1)S(1)}, u32[]{:S(2)}, u32[]{:S(2)}) collective-permute-start(bf16[64,512]{1,0:T(8,128)(2,1)S(1)} %fusion.20), channel_id=1, source_target_pairs={{0,48},{1,49},{2,50},{3,51},{4,52},{5,53},{6,54},{7,55},{8,56},{9,... | collective-permute-start | bytes 196616 | tf_op jit(solution)/shard_map/ppermute | solution.py:64
  78.1 1.8 %collective-permute-start.28 = (bf16[64,512]{1,0:T(8,128)(2,1)S(1)}, bf16[64,512]{1,0:T(8,128)(2,1)S(1)}, u32[]{:S(2)}, u32[]{:S(2)}) collective-permute-start(bf16[64,512]{1,0:T(8,128)(2,1)S(1)} %fusion.20), channel_id=1, source_target_pairs={{0,16},{1,17},{2,18},{3,19},{4,20},{5,21},{6,22},{7,23},{8,24},{9,... | collective-permute-start | bytes 196616 | tf_op jit(solution)/shard_map/ppermute | solution.py:64
  81.4 2.2 %collective-permute-start.25 = (bf16[2,64,512]{2,1,0:T(8,128)(2,1)S(1)}, bf16[2,64,512]{2,1,0:T(8,128)(2,1)S(1)}, u32[]{:S(2)}, u32[]{:S(2)}) collective-permute-start(bf16[2,64,512]{2,1,0:T(8,128)(2,1)S(1)} %get-tuple-element.60), channel_id=1, source_target_pairs={{0,130},{1,131},{2,128},{3,129},{4,134},{5,135},{6,132},{7,133},{8... | collective-permute-start | bytes 393224 | tf_op jit(solution)/shard_map/ppermute | solution.py:60
  83.6 2.7 %collective-permute-start.34 = (bf16[64,512]{1,0:T(8,128)(2,1)S(1)}, bf16[64,512]{1,0:T(8,128)(2,1)S(1)}, u32[]{:S(2)}, u32[]{:S(2)}) collective-permute-start(bf16[64,512]{1,0:T(8,128)(2,1)S(1)} %collective-permute-done.33), channel_id=1, source_target_pairs={{0,130},{1,131},{2,128},{3,129},{4,134},{5,135},{6,132},{7,133},{8... | collective-permute-start | bytes 196616 | tf_op jit(solution)/shard_map/ppermute | solution.py:60
  86.4 1.8 %collective-permute-start.40 = (bf16[2,64,512]{2,1,0:T(8,128)(2,1)S(1)}, bf16[2,64,512]{2,1,0:T(8,128)(2,1)S(1)}, u32[]{:S(2)}, u32[]{:S(2)}) collective-permute-start(bf16[2,64,512]{2,1,0:T(8,128)(2,1)S(1)} %get-tuple-element.54), channel_id=1, source_target_pairs={{0,4},{1,5},{2,6},{3,7},{4,0},{5,1},{6,2},{7,3},{8,12},{9,13},{10,... | collective-permute-start | bytes 393224 | tf_op jit(solution)/shard_map/ppermute | solution.py:60
  88.2 1.9 %collective-permute-start.35 = (bf16[2,64,512]{2,1,0:T(8,128)(2,1)S(1)}, bf16[2,64,512]{2,1,0:T(8,128)(2,1)S(1)}, u32[]{:S(2)}, u32[]{:S(2)}) collective-permute-start(bf16[2,64,512]{2,1,0:T(8,128)(2,1)S(1)} %get-tuple-element.56), channel_id=1, source_target_pairs={{0,12},{1,13},{2,14},{3,15},{4,8},{5,9},{6,10},{7,11},{8,4},{9,5},... | collective-permute-start | bytes 393224 | tf_op jit(solution)/shard_map/ppermute | solution.py:60
  94.0 1.8 %collective-permute-start.31 = (bf16[2,2,64,512]{3,2,1,0:T(8,128)(2,1)S(1)}, bf16[2,2,64,512]{3,2,1,0:T(8,128)(2,1)S(1)}, u32[]{:S(2)}, u32[]{:S(2)}) collective-permute-start(bf16[2,2,64,512]{3,2,1,0:T(8,128)(2,1)S(1)} %get-tuple-element.50), channel_id=1, source_target_pairs={{0,12},{1,13},{2,14},{3,15},{4,8},{5,9},{6,10},{7,11},{8,4},{9,5},... | collective-permute-start | bytes 786440 | tf_op jit(solution)/shard_map/ppermute | solution.py:60
  95.9 1.6 %collective-permute-start.27 = (bf16[8,64,512]{2,1,0:T(8,128)(2,1)S(1)}, bf16[8,64,512]{2,1,0:T(8,128)(2,1)S(1)}, u32[]{:S(2)}, u32[]{:S(2)}) collective-permute-start(bf16[8,64,512]{2,1,0:T(8,128)(2,1)S(1)} %bitcast.187), channel_id=1, source_target_pairs={{0,2},{1,3},{2,0},{3,1},{4,6},{5,7},{6,4},{7,5},{8,10},{9,11},{10,... | collective-permute-start | bytes 1572872 | tf_op jit(solution)/shard_map/ppermute | solution.py:60
  98.9 1.4 %collective-permute-done.36 = bf16[2,2,64,512]{3,2,0,1:T(8,128)(2,1)S(1)} collective-permute-done((bf16[2,2,64,512]{3,2,0,1:T(8,128)(2,1)S(1)}, bf16[2,2,64,512]{3,2,0,1:T(8,128)(2,1)S(1)}, u32[]{:S(2)}, u32[]{:S(2)}) %collective-permute-start.36) | collective-permute-done | bytes 262176 | tf_op jit(solution)/shard_map/ppermute | solution.py:60
  100.9 2.6 %collective-permute-start.32 = (bf16[8,64,512]{2,1,0:T(8,128)(2,1)S(1)}, bf16[8,64,512]{2,1,0:T(8,128)(2,1)S(1)}, u32[]{:S(2)}, u32[]{:S(2)}) collective-permute-start(bf16[8,64,512]{2,1,0:T(8,128)(2,1)S(1)} %bitcast.193), channel_id=1, source_target_pairs={{0,130},{1,131},{2,128},{3,129},{4,134},{5,135},{6,132},{7,133},{8... | collective-permute-start | bytes 1572872 | tf_op jit(solution)/shard_map/ppermute | solution.py:60
  103.5 6.9 %collective-permute-done.27.refs_1_ = bf16[8,64,512]{2,1,0:T(8,128)(2,1)S(1)} collective-permute-done((bf16[8,64,512]{2,1,0:T(8,128)(2,1)S(1)}, bf16[8,64,512]{2,1,0:T(8,128)(2,1)S(1)}, u32[]{:S(2)}, u32[]{:S(2)}) %collective-permute-start.27) | collective-permute-done | bytes 524320 | tf_op jit(solution)/shard_map/ppermute | solution.py:60
  110.7 4.7 %project.1 = (bf16[512,512]{1,0:T(8,128)(2,1)}, f32[256,512]{1,0:T(8,128)S(1)}, bf16[256,512]{1,0:T(8,128)(2,1)S(1)}) custom-call(bf16[256,8192]{1,0:T(8,128)(2,1)S(1)} %copy-done.1, bf16[256,4096]{1,0:T(8,128)(2,1)S(1)} %collective-permute-done.23.got, bf16[8,64,512]{2,1,0:T(8,128)(2,1)S(1)} %bitcast.188, ...), custom_call_target="tpu_custom_call" | custom-call | tf_op jit(solution)/shard_map/project/pallas_call | solution.py:267
  115.4 10.4 %collective-permute-start.43 = (bf16[256,512]{1,0:T(8,128)(2,1)S(1)}, bf16[256,512]{1,0:T(8,128)(2,1)S(1)}, u32[]{:S(2)}, u32[]{:S(2)}) collective-permute-start(bf16[256,512]{1,0:T(8,128)(2,1)S(1)} %get-tuple-element.32), channel_id=1, source_target_pairs={{0,1},{1,0},{2,3},{3,2},{4,5},{5,4},{6,7},{7,6},{8,9},{9,8},{10,11... | collective-permute-start | bytes 786440 | tf_op jit(solution)/shard_map/ppermute | solution.py:68
  (123 shorter events, 21.3 us)
Async XLA Ops:
  6.2 7.5 %collective-permute-start.1 = (bf16[256,4096]{1,0:T(8,128)(2,1)S(1)}, bf16[256,4096]{1,0:T(8,128)(2,1)S(1)}, u32[]{:S(2)}, u32[]{:S(2)}) collective-permute-start(bf16[256,4096]{1,0:T(8,128)(2,1)S(1)} %get-tuple-element.20), channel_id=1, source_target_pairs={{0,1},{1,0},{2,3},{3,2},{4,5},{5,4},{6,7},{7,6},{8,9},{9,8},{10,11... | collective-permute-start | bytes 6291464 | tf_op jit(solution)/shard_map/ppermute | solution.py:68
  21.1 14.4 %collective-permute-start.7 = (bf16[8,64,512]{2,1,0:T(8,128)(2,1)S(1)}, bf16[8,64,512]{2,1,0:T(8,128)(2,1)S(1)}, u32[]{:S(2)}, u32[]{:S(2)}) collective-permute-start(bf16[8,64,512]{2,1,0:T(8,128)(2,1)S(1)} %get-tuple-element.24), channel_id=1, source_target_pairs={{0,130},{1,131},{2,128},{3,129},{4,134},{5,135},{6,132},{7,133},{8... | collective-permute-start | bytes 1572872 | tf_op jit(solution)/shard_map/ppermute | solution.py:60
  22.0 14.9 %collective-permute-start.12 = (bf16[8,64,512]{2,1,0:T(8,128)(2,1)S(1)}, bf16[8,64,512]{2,1,0:T(8,128)(2,1)S(1)}, u32[]{:S(2)}, u32[]{:S(2)}) collective-permute-start(bf16[8,64,512]{2,1,0:T(8,128)(2,1)S(1)} %get-tuple-element.26), channel_id=1, source_target_pairs={{0,4},{1,5},{2,6},{3,7},{4,0},{5,1},{6,2},{7,3},{8,12},{9,13},{10,... | collective-permute-start | bytes 1572872 | tf_op jit(solution)/shard_map/ppermute | solution.py:60
  23.3 13.9 %collective-permute-start.17 = (bf16[8,64,512]{2,1,0:T(8,128)(2,1)S(1)}, bf16[8,64,512]{2,1,0:T(8,128)(2,1)S(1)}, u32[]{:S(2)}, u32[]{:S(2)}) collective-permute-start(bf16[8,64,512]{2,1,0:T(8,128)(2,1)S(1)} %get-tuple-element.28), channel_id=1, source_target_pairs={{0,12},{1,13},{2,14},{3,15},{4,8},{5,9},{6,10},{7,11},{8,4},{9,5},... | collective-permute-start | bytes 1572872 | tf_op jit(solution)/shard_map/ppermute | solution.py:60
  25.2 14.8 %collective-permute-start.3 = (bf16[8,64,512]{2,1,0:T(8,128)(2,1)S(1)}, bf16[8,64,512]{2,1,0:T(8,128)(2,1)S(1)}, u32[]{:S(2)}, u32[]{:S(2)}) collective-permute-start(bf16[8,64,512]{2,1,0:T(8,128)(2,1)S(1)} %get-tuple-element.22), channel_id=1, source_target_pairs={{0,2},{1,3},{2,0},{3,1},{4,6},{5,7},{6,4},{7,5},{8,10},{9,11},{10,... | collective-permute-start | bytes 1572872 | tf_op jit(solution)/shard_map/ppermute | solution.py:60
  35.8 7.9 %collective-permute-start.8 = (bf16[2,2,64,512]{3,2,1,0:T(8,128)(2,1)S(1)}, bf16[2,2,64,512]{3,2,1,0:T(8,128)(2,1)S(1)}, u32[]{:S(2)}, u32[]{:S(2)}) collective-permute-start(bf16[2,2,64,512]{3,2,1,0:T(8,128)(2,1)S(1)} %slice_bitcast_fusion), channel_id=1, source_target_pairs={{0,12},{1,13},{2,14},{3,15},{4,8},{5,9},{6,10},{7,11},{8,4},{9,5},... | collective-permute-start | bytes 786440 | tf_op jit(solution)/shard_map/ppermute | solution.py:60
  37.1 6.8 %collective-permute-start.13 = (bf16[2,2,64,512]{3,2,0,1:T(8,128)(2,1)S(1)}, bf16[2,2,64,512]{3,2,0,1:T(8,128)(2,1)S(1)}, u32[]{:S(2)}, u32[]{:S(2)}) collective-permute-start(bf16[2,2,64,512]{3,2,0,1:T(8,128)(2,1)S(1)} %copy.17), channel_id=1, source_target_pairs={{0,2},{1,3},{2,0},{3,1},{4,6},{5,7},{6,4},{7,5},{8,10},{9,11},{10,... | collective-permute-start | bytes 786440 | tf_op jit(solution)/shard_map/ppermute | solution.py:60
  37.4 8.1 %collective-permute-start.18 = (bf16[2,2,64,512]{3,2,0,1:T(8,128)(2,1)S(1)}, bf16[2,2,64,512]{3,2,0,1:T(8,128)(2,1)S(1)}, u32[]{:S(2)}, u32[]{:S(2)}) collective-permute-start(bf16[2,2,64,512]{3,2,0,1:T(8,128)(2,1)S(1)} %bitcast.203), channel_id=1, source_target_pairs={{0,130},{1,131},{2,128},{3,129},{4,134},{5,135},{6,132},{7,133},{8... | collective-permute-start | bytes 786440 | tf_op jit(solution)/shard_map/ppermute | solution.py:60
  40.1 6.1 %collective-permute-start.4 = (bf16[2,2,64,512]{3,2,1,0:T(8,128)(2,1)S(1)}, bf16[2,2,64,512]{3,2,1,0:T(8,128)(2,1)S(1)}, u32[]{:S(2)}, u32[]{:S(2)}) collective-permute-start(bf16[2,2,64,512]{3,2,1,0:T(8,128)(2,1)S(1)} %slice_bitcast_fusion.2), channel_id=1, source_target_pairs={{0,4},{1,5},{2,6},{3,7},{4,0},{5,1},{6,2},{7,3},{8,12},{9,13},{10,... | collective-permute-start | bytes 786440 | tf_op jit(solution)/shard_map/ppermute | solution.py:60
  43.9 5.7 %collective-permute-start.14 = (bf16[2,64,512]{2,1,0:T(8,128)(2,1)S(1)}, bf16[2,64,512]{2,1,0:T(8,128)(2,1)S(1)}, u32[]{:S(2)}, u32[]{:S(2)}) collective-permute-start(bf16[2,64,512]{2,1,0:T(8,128)(2,1)S(1)} %slice_bitcast_fusion.6), channel_id=1, source_target_pairs={{0,12},{1,13},{2,14},{3,15},{4,8},{5,9},{6,10},{7,11},{8,4},{9,5},... | collective-permute-start | bytes 393224 | tf_op jit(solution)/shard_map/ppermute | solution.py:60
  45.6 5.9 %collective-permute-start.19 = (bf16[2,64,512]{2,1,0:T(8,128)(2,1)S(1)}, bf16[2,64,512]{2,1,0:T(8,128)(2,1)S(1)}, u32[]{:S(2)}, u32[]{:S(2)}) collective-permute-start(bf16[2,64,512]{2,1,0:T(8,128)(2,1)S(1)} %slice_bitcast_fusion.4), channel_id=1, source_target_pairs={{0,4},{1,5},{2,6},{3,7},{4,0},{5,1},{6,2},{7,3},{8,12},{9,13},{10,... | collective-permute-start | bytes 393224 | tf_op jit(solution)/shard_map/ppermute | solution.py:60
  48.1 5.9 %collective-permute-start.10 = (bf16[64,512]{1,0:T(8,128)(2,1)S(1)}, bf16[64,512]{1,0:T(8,128)(2,1)S(1)}, u32[]{:S(2)}, u32[]{:S(2)}) collective-permute-start(bf16[64,512]{1,0:T(8,128)(2,1)S(1)} %slice_bitcast_fusion.16), channel_id=1, source_target_pairs={{0,4},{1,5},{2,6},{3,7},{4,0},{5,1},{6,2},{7,3},{8,12},{9,13},{10,... | collective-permute-start | bytes 196616 | tf_op jit(solution)/shard_map/ppermute | solution.py:60
  49.7 6.0 %collective-permute-start.15 = (bf16[64,512]{1,0:T(8,128)(2,1)S(1)}, bf16[64,512]{1,0:T(8,128)(2,1)S(1)}, u32[]{:S(2)}, u32[]{:S(2)}) collective-permute-start(bf16[64,512]{1,0:T(8,128)(2,1)S(1)} %slice_bitcast_fusion.14), channel_id=1, source_target_pairs={{0,130},{1,131},{2,128},{3,129},{4,134},{5,135},{6,132},{7,133},{8... | collective-permute-start | bytes 196616 | tf_op jit(solution)/shard_map/ppermute | solution.py:60
  51.5 7.3 %collective-permute-start.20 = (bf16[64,512]{1,0:T(8,128)(2,1)S(1)}, bf16[64,512]{1,0:T(8,128)(2,1)S(1)}, u32[]{:S(2)}, u32[]{:S(2)}) collective-permute-start(bf16[64,512]{1,0:T(8,128)(2,1)S(1)} %slice_bitcast_fusion.12), channel_id=1, source_target_pairs={{0,2},{1,3},{2,0},{3,1},{4,6},{5,7},{6,4},{7,5},{8,10},{9,11},{10,... | collective-permute-start | bytes 196616 | tf_op jit(solution)/shard_map/ppermute | solution.py:60
  51.8 11.7 %collective-permute-start.6 = (bf16[64,512]{1,0:T(8,128)(2,1)S(1)}, bf16[64,512]{1,0:T(8,128)(2,1)S(1)}, u32[]{:S(2)}, u32[]{:S(2)}) collective-permute-start(bf16[64,512]{1,0:T(8,128)(2,1)S(1)} %slice_bitcast_fusion.18), channel_id=1, source_target_pairs={{0,12},{1,13},{2,14},{3,15},{4,8},{5,9},{6,10},{7,11},{8,4},{9,5},... | collective-permute-start | bytes 196616 | tf_op jit(solution)/shard_map/ppermute | solution.py:60
  54.0 9.5 %collective-permute-start.11 = (bf16[64,512]{1,0:T(8,128)(2,1)S(1)}, bf16[64,512]{1,0:T(8,128)(2,1)S(1)}, u32[]{:S(2)}, u32[]{:S(2)}) collective-permute-start(bf16[64,512]{1,0:T(8,128)(2,1)S(1)} %fusion.25), channel_id=1, source_target_pairs={{0,16},{1,17},{2,18},{3,19},{4,20},{5,21},{6,22},{7,23},{8,24},{9,... | collective-permute-start | bytes 196616 | tf_op jit(solution)/shard_map/ppermute | solution.py:64
  55.7 7.8 %collective-permute-start.16 = (bf16[64,512]{1,0:T(8,128)(2,1)S(1)}, bf16[64,512]{1,0:T(8,128)(2,1)S(1)}, u32[]{:S(2)}, u32[]{:S(2)}) collective-permute-start(bf16[64,512]{1,0:T(8,128)(2,1)S(1)} %fusion.24), channel_id=1, source_target_pairs={{0,32},{1,33},{2,34},{3,35},{4,36},{5,37},{6,38},{7,39},{8,40},{9,... | collective-permute-start | bytes 196616 | tf_op jit(solution)/shard_map/ppermute | solution.py:64
  59.5 9.5 %collective-permute-start = (f32[3,32,512]{2,1,0:T(8,128)S(1)}, f32[3,32,512]{2,1,0:T(8,128)S(1)}, u32[]{:S(2)}, u32[]{:S(2)}) collective-permute-start(f32[3,32,512]{2,1,0:T(8,128)S(1)} %get-tuple-element.19), channel_id=1, source_target_pairs={{0,112},{1,113},{2,114},{3,115},{4,116},{5,117},{6,118},{7,119},{8... | collective-permute-start | bytes 589832 | tf_op jit(solution)/shard_map/ppermute | solution.py:64
  63.9 11.2 %collective-permute-start.22 = (bf16[64,512]{1,0:T(8,128)(2,1)S(1)}, bf16[64,512]{1,0:T(8,128)(2,1)S(1)}, u32[]{:S(2)}, u32[]{:S(2)}) collective-permute-start(bf16[64,512]{1,0:T(8,128)(2,1)S(1)} %fusion.29), channel_id=1, source_target_pairs={{0,112},{1,113},{2,114},{3,115},{4,116},{5,117},{6,118},{7,119},{8... | collective-permute-start | bytes 196616 | tf_op jit(solution)/shard_map/ppermute | solution.py:64
  69.0 41.5 %collective-permute-start.23 = (bf16[256,4096]{1,0:T(8,128)(2,1)S(1)}, bf16[256,4096]{1,0:T(8,128)(2,1)S(1)}, u32[]{:S(2)}, u32[]{:S(2)}) collective-permute-start(bf16[256,4096]{1,0:T(8,128)(2,1)S(1)} %get-tuple-element.29), channel_id=1, source_target_pairs={{0,1},{1,0},{2,3},{3,2},{4,5},{5,4},{6,7},{7,6},{8,9},{9,8},{10,11... | collective-permute-start | bytes 6291464 | tf_op jit(solution)/shard_map/ppermute | solution.py:68
  78.1 8.3 %collective-permute-start.28 = (bf16[64,512]{1,0:T(8,128)(2,1)S(1)}, bf16[64,512]{1,0:T(8,128)(2,1)S(1)}, u32[]{:S(2)}, u32[]{:S(2)}) collective-permute-start(bf16[64,512]{1,0:T(8,128)(2,1)S(1)} %fusion.20), channel_id=1, source_target_pairs={{0,16},{1,17},{2,18},{3,19},{4,20},{5,21},{6,22},{7,23},{8,24},{9,... | collective-permute-start | bytes 196616 | tf_op jit(solution)/shard_map/ppermute | solution.py:64
  80.4 6.0 %collective-permute-start.39 = (bf16[64,512]{1,0:T(8,128)(2,1)S(1)}, bf16[64,512]{1,0:T(8,128)(2,1)S(1)}, u32[]{:S(2)}, u32[]{:S(2)}) collective-permute-start(bf16[64,512]{1,0:T(8,128)(2,1)S(1)} %collective-permute-done.38), channel_id=1, source_target_pairs={{0,2},{1,3},{2,0},{3,1},{4,6},{5,7},{6,4},{7,5},{8,10},{9,11},{10,... | collective-permute-start | bytes 196616 | tf_op jit(solution)/shard_map/ppermute | solution.py:60
  81.4 8.8 %collective-permute-start.25 = (bf16[2,64,512]{2,1,0:T(8,128)(2,1)S(1)}, bf16[2,64,512]{2,1,0:T(8,128)(2,1)S(1)}, u32[]{:S(2)}, u32[]{:S(2)}) collective-permute-start(bf16[2,64,512]{2,1,0:T(8,128)(2,1)S(1)} %get-tuple-element.60), channel_id=1, source_target_pairs={{0,130},{1,131},{2,128},{3,129},{4,134},{5,135},{6,132},{7,133},{8... | collective-permute-start | bytes 393224 | tf_op jit(solution)/shard_map/ppermute | solution.py:60
  90.2 5.6 %collective-permute-start.26 = (bf16[2,2,64,512]{3,2,1,0:T(8,128)(2,1)S(1)}, bf16[2,2,64,512]{3,2,1,0:T(8,128)(2,1)S(1)}, u32[]{:S(2)}, u32[]{:S(2)}) collective-permute-start(bf16[2,2,64,512]{3,2,1,0:T(8,128)(2,1)S(1)} %get-tuple-element.52), channel_id=1, source_target_pairs={{0,4},{1,5},{2,6},{3,7},{4,0},{5,1},{6,2},{7,3},{8,12},{9,13},{10,... | collective-permute-start | bytes 786440 | tf_op jit(solution)/shard_map/ppermute | solution.py:60
  91.4 6.5 %collective-permute-start.41 = (bf16[2,2,64,512]{3,2,1,0:T(8,128)(2,1)S(1)}, bf16[2,2,64,512]{3,2,1,0:T(8,128)(2,1)S(1)}, u32[]{:S(2)}, u32[]{:S(2)}) collective-permute-start(bf16[2,2,64,512]{3,2,1,0:T(8,128)(2,1)S(1)} %get-tuple-element.46), channel_id=1, source_target_pairs={{0,130},{1,131},{2,128},{3,129},{4,134},{5,135},{6,132},{7,133},{8... | collective-permute-start | bytes 786440 | tf_op jit(solution)/shard_map/ppermute | solution.py:60
  93.3 7.0 %collective-permute-start.36 = (bf16[2,2,64,512]{3,2,0,1:T(8,128)(2,1)S(1)}, bf16[2,2,64,512]{3,2,0,1:T(8,128)(2,1)S(1)}, u32[]{:S(2)}, u32[]{:S(2)}) collective-permute-start(bf16[2,2,64,512]{3,2,0,1:T(8,128)(2,1)S(1)} %get-tuple-element.48), channel_id=1, source_target_pairs={{0,2},{1,3},{2,0},{3,1},{4,6},{5,7},{6,4},{7,5},{8,10},{9,11},{10,... | collective-permute-start | bytes 786440 | tf_op jit(solution)/shard_map/ppermute | solution.py:60
  94.0 6.8 %collective-permute-start.31 = (bf16[2,2,64,512]{3,2,1,0:T(8,128)(2,1)S(1)}, bf16[2,2,64,512]{3,2,1,0:T(8,128)(2,1)S(1)}, u32[]{:S(2)}, u32[]{:S(2)}) collective-permute-start(bf16[2,2,64,512]{3,2,1,0:T(8,128)(2,1)S(1)} %get-tuple-element.50), channel_id=1, source_target_pairs={{0,12},{1,13},{2,14},{3,15},{4,8},{5,9},{6,10},{7,11},{8,4},{9,5},... | collective-permute-start | bytes 786440 | tf_op jit(solution)/shard_map/ppermute | solution.py:60
  95.9 14.5 %collective-permute-start.27 = (bf16[8,64,512]{2,1,0:T(8,128)(2,1)S(1)}, bf16[8,64,512]{2,1,0:T(8,128)(2,1)S(1)}, u32[]{:S(2)}, u32[]{:S(2)}) collective-permute-start(bf16[8,64,512]{2,1,0:T(8,128)(2,1)S(1)} %bitcast.187), channel_id=1, source_target_pairs={{0,2},{1,3},{2,0},{3,1},{4,6},{5,7},{6,4},{7,5},{8,10},{9,11},{10,... | collective-permute-start | bytes 1572872 | tf_op jit(solution)/shard_map/ppermute | solution.py:60
  98.0 12.7 %collective-permute-start.42 = (bf16[8,64,512]{2,1,0:T(8,128)(2,1)S(1)}, bf16[8,64,512]{2,1,0:T(8,128)(2,1)S(1)}, u32[]{:S(2)}, u32[]{:S(2)}) collective-permute-start(bf16[8,64,512]{2,1,0:T(8,128)(2,1)S(1)} %bitcast.189), channel_id=1, source_target_pairs={{0,12},{1,13},{2,14},{3,15},{4,8},{5,9},{6,10},{7,11},{8,4},{9,5},... | collective-permute-start | bytes 1572872 | tf_op jit(solution)/shard_map/ppermute | solution.py:60
  100.4 10.2 %collective-permute-start.37 = (bf16[8,64,512]{2,1,0:T(8,128)(2,1)S(1)}, bf16[8,64,512]{2,1,0:T(8,128)(2,1)S(1)}, u32[]{:S(2)}, u32[]{:S(2)}) collective-permute-start(bf16[8,64,512]{2,1,0:T(8,128)(2,1)S(1)} %bitcast.191), channel_id=1, source_target_pairs={{0,4},{1,5},{2,6},{3,7},{4,0},{5,1},{6,2},{7,3},{8,12},{9,13},{10,... | collective-permute-start | bytes 1572872 | tf_op jit(solution)/shard_map/ppermute | solution.py:60
  100.9 9.7 %collective-permute-start.32 = (bf16[8,64,512]{2,1,0:T(8,128)(2,1)S(1)}, bf16[8,64,512]{2,1,0:T(8,128)(2,1)S(1)}, u32[]{:S(2)}, u32[]{:S(2)}) collective-permute-start(bf16[8,64,512]{2,1,0:T(8,128)(2,1)S(1)} %bitcast.193), channel_id=1, source_target_pairs={{0,130},{1,131},{2,128},{3,129},{4,134},{5,135},{6,132},{7,133},{8... | collective-permute-start | bytes 1572872 | tf_op jit(solution)/shard_map/ppermute | solution.py:60
  115.4 11.7 %collective-permute-start.43 = (bf16[256,512]{1,0:T(8,128)(2,1)S(1)}, bf16[256,512]{1,0:T(8,128)(2,1)S(1)}, u32[]{:S(2)}, u32[]{:S(2)}) collective-permute-start(bf16[256,512]{1,0:T(8,128)(2,1)S(1)} %get-tuple-element.32), channel_id=1, source_target_pairs={{0,1},{1,0},{2,3},{3,2},{4,5},{5,4},{6,7},{7,6},{8,9},{9,8},{10,11... | collective-permute-start | bytes 786440 | tf_op jit(solution)/shard_map/ppermute | solution.py:68
  (18 other events, 75.3 us)

commit v3 on v2

--- a/solution.py
+++ b/solution.py
@@ -25,7 +25,8 @@
 PARTS = 4
 ROWS = 64
 
-ORDERS = ((0, 2, 1, 3), (1, 3, 0, 2), (2, 0, 3, 1), (3, 1, 2, 0))
+ORDERS = ((0, 2, 1, 3), (1, 3, 0, 2), (2, 0, 1, 3), (3, 1, 0, 2))
+COUPLES = ((0, 2), (1, 3))
 
 
 def moves(change):
@@ -97,21 +98,23 @@
 
 
 ANY = pl.BlockSpec(memory_space=pl.ANY)
+HBM = pl.BlockSpec(memory_space=pltpu.HBM)
 VMEM = pl.BlockSpec(memory_space=pltpu.VMEM)
 PARAMS = pltpu.CompilerParams(vmem_limit_bytes=40 * 1024 * 1024)
 
 
-def pack_kernel(acts, master, first, second, packed, state, sems):
+def pack_kernel(acts, tokens, master, first, second, packed, packed_tokens, state, sems):
     where = place()
     copies = [
         pltpu.make_async_copy(
-            acts.at[:, columns_of(where, r, 1 - where[4])],
-            packed.at[:, pl.ds(r * BLOCK, BLOCK)],
-            sems.at[r],
-        )
+            source.at[:, columns_of(where, r, 1 - where[4])],
+            target.at[:, pl.ds(r * BLOCK, BLOCK)],
+            sems.at[i * BLOCKS + r],
+        )
+        for i, (source, target) in enumerate(((acts, packed), (tokens, packed_tokens)))
         for r in range(BLOCKS)
     ] + [
-        pltpu.make_async_copy(source, state.at[i], sems.at[BLOCKS + i])
+        pltpu.make_async_copy(source, state.at[i], sems.at[2 * BLOCKS + i])
         for i, source in enumerate((master, first, second))
     ]
     for copy in copies:
@@ -120,28 +123,24 @@
         copy.wait()
 
 
-def pack(acts, master, first, second):
+def pack(acts, tokens, master, first, second):
+    half = jax.ShapeDtypeStruct((TOK, HALF), jnp.bfloat16)
     return pl.pallas_call(
         pack_kernel,
-        out_shape=(
-            jax.ShapeDtypeStruct((TOK, HALF), jnp.bfloat16),
-            jax.ShapeDtypeStruct((3, 32, COLS), jnp.float32),
-        ),
-        in_specs=[ANY] * 4,
-        out_specs=(ANY, ANY),
-        scratch_shapes=[pltpu.SemaphoreType.DMA((BLOCKS + 3,))],
+        out_shape=(half, half, jax.ShapeDtypeStruct((3, 32, COLS), jnp.float32)),
+        in_specs=[HBM] * 5,
+        out_specs=(ANY,) * 3,
+        scratch_shapes=[pltpu.SemaphoreType.DMA((2 * BLOCKS + 3,))],
         compiler_params=PARAMS,
         name="pack",
-    )(acts, master, first, second)
-
-
-def term_kernel(acts, got, grads, got_grads, tokens, *refs):
-    halves, packed, both, grads_both, term, sems = (
-        refs[: 2 * PARTS],
-        *refs[2 * PARTS :],
-    )
+    )(acts, tokens, master, first, second)
+
+
+def term_kernel(acts, got, grads, got_grads, _tokens, _state, *refs):
+    halves = refs[: 2 * PARTS]
+    both, grads_both, term, sems = refs[2 * PARTS :]
     where = place()
-    own, other, pack_copies = [], [], []
+    own, other = [], []
     for r in range(BLOCKS):
         here = pl.ds(r * BLOCK, BLOCK)
         own.append(
@@ -151,13 +150,6 @@
         )
         other.append(
             pltpu.make_async_copy(got.at[:, here], both.at[TOK:, here], sems.at[BLOCKS + r])
-        )
-        pack_copies.append(
-            pltpu.make_async_copy(
-                tokens.at[:, columns_of(where, r, 1 - where[4])],
-                packed.at[:, here],
-                sems.at[2 * BLOCKS + r],
-            )
         )
     for r in range(BLOCKS):
         own[r].start()
@@ -168,7 +160,6 @@
     for r in range(BLOCKS):
         own[r].wait()
         other[r].wait()
-        pack_copies[r].start()
         term[r % 2] = lax.dot_general(
             both[:, r * BLOCK : (r + 1) * BLOCK],
             grads_both[...],
@@ -180,26 +171,24 @@
             out = halves[2 * m + side]
             out[slot, :32] = term[r % 2, rows[m][0]]
             out[slot, 32:] = term[r % 2, rows[m][1]]
-    for copy in pack_copies:
-        copy.wait()
-
-
-def gradient_term(acts, got, grads, got_grads, tokens):
+
+
+def gradient_term(acts, got, grads, got_grads, got_tokens, got_state):
     half = jax.ShapeDtypeStruct((8, ROWS, COLS), jnp.bfloat16)
     return pl.pallas_call(
         term_kernel,
-        out_shape=(half,) * (2 * PARTS) + (jax.ShapeDtypeStruct((TOK, HALF), jnp.bfloat16),),
-        in_specs=[ANY, ANY, VMEM, VMEM, ANY],
-        out_specs=(VMEM,) * (2 * PARTS) + (ANY,),
+        out_shape=(half,) * (2 * PARTS),
+        in_specs=[HBM, ANY, VMEM, VMEM, ANY, ANY],
+        out_specs=(VMEM,) * (2 * PARTS),
         scratch_shapes=[
             pltpu.VMEM((2 * TOK, HALF), jnp.bfloat16),
             pltpu.VMEM((2 * TOK, COLS), jnp.bfloat16),
             pltpu.VMEM((2, BLOCK, COLS), jnp.bfloat16),
-            pltpu.SemaphoreType.DMA((3 * BLOCKS,)),
+            pltpu.SemaphoreType.DMA((2 * BLOCKS,)),
         ],
         compiler_params=PARAMS,
         name="gradient_term",
-    )(acts, got, grads, got_grads, tokens)
+    )(acts, got, grads, got_grads, got_tokens, got_state)
 
 
 STRIPE = 1024
@@ -271,7 +260,7 @@
             jax.ShapeDtypeStruct((TOK, COLS), jnp.float32),
             jax.ShapeDtypeStruct((TOK, COLS), jnp.bfloat16),
         ),
-        in_specs=[ANY] * (2 + 2 * PARTS),
+        in_specs=[HBM] + [ANY] * (1 + 2 * PARTS),
         out_specs=(VMEM,) * 3,
         scratch_shapes=[
             pltpu.VMEM((2 * TOK, HALF), jnp.bfloat16),
@@ -300,59 +289,65 @@
     return array.astype(jnp.float32)
 
 
+def add(keep, got):
+    return (wide(keep) + wide(got)).astype(jnp.bfloat16)
+
+
+def halve(array, dim, pairing):
+    keep = lax.index_in_dim(array, 0, dim, keepdims=False)
+    return add(keep, across(lax.index_in_dim(array, 1, dim, keepdims=False), pairing))
+
+
 def reduce_parts(halves):
-    parts = []
-    left = []
-    for m in range(PARTS):
-        keep, send = halves[2 * m], halves[2 * m + 1]
-        left.append([v for v in range(4) if v != ORDERS[m][0]])
-        got = across(send, ORDERS[m][0])
-        parts.append((wide(keep) + wide(got)).astype(jnp.bfloat16).reshape(2, 2, 2, ROWS, COLS))
-    for step in range(1, 4):
-        for m in range(PARTS):
-            v = ORDERS[m][step]
-            dim = left[m].index(v)
-            left[m].remove(v)
-            keep = lax.index_in_dim(parts[m], 0, dim, keepdims=False)
-            got = across(lax.index_in_dim(parts[m], 1, dim, keepdims=False), v)
-            total = wide(keep) + wide(got)
-            parts[m] = total if step == 3 and m == 0 else total.astype(jnp.bfloat16)
+    parts = [None] * PARTS
+    for m, (v, w, _, _) in enumerate(ORDERS):
+        got = across(halves[2 * m + 1], v)
+        part = add(halves[2 * m], got).reshape(2, 2, 2, ROWS, COLS)
+        parts[m] = halve(part, w - (v < w), w)
+    for m, n in COUPLES:
+        v, w = ORDERS[m][2:]
+        couple = halve(halve(jnp.stack([parts[m], parts[n]]), 1, v), 1, w)
+        parts[m], parts[n] = couple[0], couple[1]
     return parts
 
 
 def reduce_z(parts):
-    total = parts[0]
+    total = wide(parts[0])
     for m in range(1, PARTS):
         total = total + wide(z_swap(parts[m], m))
     total = total.astype(jnp.bfloat16)
     return (wide(total) + wide(z_swap(total, 7))).reshape(2, 32, COLS)
 
 
+def double(array, dim, pairing):
+    return jnp.stack([array, across(array, pairing)], axis=dim)
+
+
 def gather_parts(pair):
     parts = [pair] + [z_swap(pair, m) for m in range(1, PARTS)]
-    known = [[] for _ in range(PARTS)]
-    for step in range(3, 0, -1):
-        for m in range(PARTS):
-            v = ORDERS[m][step]
-            known[m] = sorted(known[m] + [v])
-            parts[m] = jnp.stack([parts[m], across(parts[m], v)], axis=known[m].index(v))
+    for m, n in COUPLES:
+        v, w = ORDERS[m][2:]
+        couple = double(double(jnp.stack([parts[m], parts[n]]), 1, w), 1, v)
+        parts[m], parts[n] = couple[0], couple[1]
     halves = []
-    for m in range(PARTS):
-        keep = parts[m].reshape(8, ROWS, COLS)
-        halves += [keep, across(keep, ORDERS[m][0])]
+    for m, (v, w, _, _) in enumerate(ORDERS):
+        keep = double(parts[m], w - (v < w), w).reshape(8, ROWS, COLS)
+        halves += [keep, across(keep, v)]
     return halves
 
 
 def local(activations, output_grads, master_weights, first_moment, second_moment, next_tokens):
     low = lax.axis_index("outer") % 8 < 4
-    packed, state = pack(activations, master_weights, first_moment, second_moment)
+    packed, packed_tokens, state = pack(
+        activations, next_tokens, master_weights, first_moment, second_moment
+    )
     got_acts = core_swap(packed)
     got_grads = core_swap(output_grads)
     got_state = z_swap(state, 7)
-    *halves, packed_tokens = gradient_term(
-        activations, got_acts, output_grads, got_grads, next_tokens
-    )
     got_tokens = core_swap(packed_tokens)
+    halves = gradient_term(
+        activations, got_acts, output_grads, got_grads, got_tokens, got_state
+    )
 
     gradient = reduce_z(reduce_parts(halves))
     pairs = jnp.stack([jnp.where(low, state, got_state), jnp.where(low, got_state, state)], axis=1)

time: 128 us -> 140 us (1.094)
  waiting for transfers between devices: 34.1 us -> 55.7 us
  starting transfers between devices: 70.9 us -> 59.8 us
  local copies, waits for them, and re-layouts: 5.03 us -> 7.13 us
    ppermute x8, waiting for transfers between devices: 2.77 us -> 19.6 us  [z_swap(): lax.ppermute(array, AXES, moves(lambda xh, z, y, xl, c: (xh, z ^ mask, y,...]
    ppermute x32 -> x24, waiting for transfers between devices: 27.2 us -> 36.1 us  [across(): return lax.ppermute(array, AXES, PAIRINGS[pairing])]
    ppermute x8, starting transfers between devices: 16.1 us -> 11.8 us  [z_swap(): lax.ppermute(array, AXES, moves(lambda xh, z, y, xl, c: (xh, z ^ mask, y,...]
    ppermute x4, waiting for transfers between devices: 4.06 us -> 0.01 us  [core_swap(): lax.ppermute(array, AXES, moves(lambda xh, z, y, xl, c: (xh, z, y, xl, 1...]
    ppermute x32 -> x24, starting transfers between devices: 34.8 us -> 31.1 us  [across(): return lax.ppermute(array, AXES, PAIRINGS[pairing])]
    ppermute x4, starting transfers between devices: 19.9 us -> 16.8 us  [core_swap(): lax.ppermute(array, AXES, moves(lambda xh, z, y, xl, c: (xh, z, y, xl, 1...]
    unnamed x13 -> x14, local copies, waits for them, and re-layouts: 4.72 us -> 6.89 us
  transfers between devices with their start and end apart: 44 -> 36, of which waited for: 17 -> 25; matrix products, arithmetic and copies ran while one was open for 3% -> 2% of each run, Pallas kernels for 0% -> 0%
where the time goes in v3:
time: 140 us
  starting transfers between devices  59.8 us (43%)
  waiting for transfers between devices  55.7 us (40%)
  Pallas kernels  12.7 us (9%)
  local copies, waits for them, and re-layouts  7.13 us (5%)
  other arithmetic  3.91 us (3%)
    ppermute x24, waiting for transfers between devices, across(): return lax.ppermute(array, AXES, PAIRINGS[pairing])  36.1 us
    ppermute x24, starting transfers between devices, across(): return lax.ppermute(array, AXES, PAIRINGS[pairing])  31.1 us
    ppermute x8, waiting for transfers between devices, z_swap(): lax.ppermute(array, AXES, moves(lambda xh, z, y, xl, c: (xh, z ^ mask, y,...  19.6 us
    ppermute x4, starting transfers between devices, core_swap(): lax.ppermute(array, AXES, moves(lambda xh, z, y, xl, c: (xh, z, y, xl, 1...  16.8 us
    ppermute x8, starting transfers between devices, z_swap(): lax.ppermute(array, AXES, moves(lambda xh, z, y, xl, c: (xh, z ^ mask, y,...  11.8 us
    unnamed x14, local copies, waits for them, and re-layouts  6.89 us
    pallas_call x1, Pallas kernels, gradient_term(): pl.pallas_call(term_kernel, out_shape=(half,) * (2 * PARTS), in_specs=[HB...  6.77 us
    pallas_call x1, Pallas kernels, project(): pl.pallas_call(project_kernel, out_shape=(jax.ShapeDtypeStruct((2 * BLOCK...  4.55 us
  transfers between devices with their start and end apart: 36, of which 25 were waited for; matrix products, arithmetic and copies ran while one was open for 2% of the time, Pallas kernels for 0%

profile of v3, /device:TPU:1, one launch (start us, length us, event | category | flops | bytes accessed | tf_op | source)
XLA Modules:
  0.0 140.1 jit_solution(17624590002007107002)
XLA Ops:
  0.6 2.2 %copy-done = bf16[256,8192]{1,0:T(8,128)(2,1)S(1)} copy-done((bf16[256,8192]{1,0:T(8,128)(2,1)S(1)}, bf16[256,8192]{1,0:T(8,128)(2,1)}, u32[]{:S(2)}) %copy-start) | copy-done | bytes 4194328
  2.8 2.2 %copy-done.1 = bf16[256,8192]{1,0:T(8,128)(2,1)S(1)} copy-done((bf16[256,8192]{1,0:T(8,128)(2,1)S(1)}, bf16[256,8192]{1,0:T(8,128)(2,1)}, u32[]{:S(2)}) %copy-start.1) | copy-done | bytes 4194328
  8.9 3.3 %collective-permute-start.3 = (bf16[256,4096]{1,0:T(8,128)(2,1)S(1)}, bf16[256,4096]{1,0:T(8,128)(2,1)S(1)}, u32[]{:S(2)}, u32[]{:S(2)}) collective-permute-start(bf16[256,4096]{1,0:T(8,128)(2,1)S(1)} %get-tuple-element.21), channel_id=1, source_target_pairs={{0,1},{1,0},{2,3},{3,2},{4,5},{5,4},{6,7},{7,6},{8,9},{9,8},{10,11... | collective-permute-start | bytes 6291464 | tf_op jit(solution)/shard_map/ppermute | solution.py:69
  12.7 3.9 %collective-permute-start = (f32[3,32,512]{2,1,0:T(8,128)S(1)}, f32[3,32,512]{2,1,0:T(8,128)S(1)}, u32[]{:S(2)}, u32[]{:S(2)}) collective-permute-start(f32[3,32,512]{2,1,0:T(8,128)S(1)} %get-tuple-element.19), channel_id=1, source_target_pairs={{0,112},{1,113},{2,114},{3,115},{4,116},{5,117},{6,118},{7,119},{8... | collective-permute-start | bytes 589832 | tf_op jit(solution)/shard_map/ppermute | solution.py:65
  16.6 9.4 %collective-permute-done._state = f32[3,32,512]{2,1,0:T(8,128)S(1)} collective-permute-done((f32[3,32,512]{2,1,0:T(8,128)S(1)}, f32[3,32,512]{2,1,0:T(8,128)S(1)}, u32[]{:S(2)}, u32[]{:S(2)}) %collective-permute-start) | collective-permute-done | bytes 196640 | tf_op jit(solution)/shard_map/ppermute | solution.py:65
  26.0 6.8 %gradient_term.1 = (bf16[8,64,512]{2,1,0:T(8,128)(2,1)S(1)}, bf16[8,64,512]{2,1,0:T(8,128)(2,1)S(1)}, bf16[8,64,512]{2,1,0:T(8,128)(2,1)S(1)}, bf16[8,64,512]{2,...) custom-call(bf16[256,8192]{1,0:T(8,128)(2,1)S(1)} %copy-done, ...), custom_call_target="tpu_custom_call" | custom-call | tf_op jit(solution)/shard_map/gradient_term/pallas_call | solution.py:178
  35.4 1.8 %collective-permute-start.10 = (bf16[8,64,512]{2,1,0:T(8,128)(2,1)S(1)}, bf16[8,64,512]{2,1,0:T(8,128)(2,1)S(1)}, u32[]{:S(2)}, u32[]{:S(2)}) collective-permute-start(bf16[8,64,512]{2,1,0:T(8,128)(2,1)S(1)} %get-tuple-element.27), channel_id=1, source_target_pairs={{0,130},{1,131},{2,128},{3,129},{4,134},{5,135},{6,132},{7,133},{8... | collective-permute-start | bytes 1572872 | tf_op jit(solution)/shard_map/ppermute | solution.py:61
  37.2 1.9 %collective-permute-start.12 = (bf16[8,64,512]{2,1,0:T(8,128)(2,1)S(1)}, bf16[8,64,512]{2,1,0:T(8,128)(2,1)S(1)}, u32[]{:S(2)}, u32[]{:S(2)}) collective-permute-start(bf16[8,64,512]{2,1,0:T(8,128)(2,1)S(1)} %get-tuple-element.29), channel_id=1, source_target_pairs={{0,12},{1,13},{2,14},{3,15},{4,8},{5,9},{6,10},{7,11},{8,4},{9,5},... | collective-permute-start | bytes 1572872 | tf_op jit(solution)/shard_map/ppermute | solution.py:61
  39.1 6.6 %collective-permute-done.4 = bf16[8,64,512]{2,1,0:T(8,128)(2,1)S(1)} collective-permute-done((bf16[8,64,512]{2,1,0:T(8,128)(2,1)S(1)}, bf16[8,64,512]{2,1,0:T(8,128)(2,1)S(1)}, u32[]{:S(2)}, u32[]{:S(2)}) %collective-permute-start.4) | collective-permute-done | bytes 524320 | tf_op jit(solution)/shard_map/ppermute | solution.py:61
  48.9 2.0 %collective-permute-start.11 = (bf16[2,2,64,512]{3,2,1,0:T(8,128)(2,1)S(1)}, bf16[2,2,64,512]{3,2,1,0:T(8,128)(2,1)S(1)}, u32[]{:S(2)}, u32[]{:S(2)}) collective-permute-start(bf16[2,2,64,512]{3,2,1,0:T(8,128)(2,1)S(1)} %slice_bitcast_fusion.2), channel_id=1, source_target_pairs={{0,12},{1,13},{2,14},{3,15},{4,8},{5,9},{6,10},{7,11},{8,4},{9,5},... | collective-permute-start | bytes 786440 | tf_op jit(solution)/shard_map/ppermute | solution.py:61
  51.1 2.1 %collective-permute-start.13 = (bf16[2,2,64,512]{3,2,1,0:T(8,128)(2,1)S(1)}, bf16[2,2,64,512]{3,2,1,0:T(8,128)(2,1)S(1)}, u32[]{:S(2)}, u32[]{:S(2)}) collective-permute-start(bf16[2,2,64,512]{3,2,1,0:T(8,128)(2,1)S(1)} %slice_bitcast_fusion), channel_id=1, source_target_pairs={{0,130},{1,131},{2,128},{3,129},{4,134},{5,135},{6,132},{7,133},{8... | collective-permute-start | bytes 786440 | tf_op jit(solution)/shard_map/ppermute | solution.py:61
  53.6 2.6 %collective-permute-start.8 = (bf16[2,2,64,512]{3,2,0,1:T(8,128)(2,1)S(1)}, bf16[2,2,64,512]{3,2,0,1:T(8,128)(2,1)S(1)}, u32[]{:S(2)}, u32[]{:S(2)}) collective-permute-start(bf16[2,2,64,512]{3,2,0,1:T(8,128)(2,1)S(1)} %fusion.17), channel_id=1, source_target_pairs={{0,130},{1,131},{2,128},{3,129},{4,134},{5,135},{6,132},{7,133},{8... | collective-permute-start | bytes 786440 | tf_op jit(solution)/shard_map/ppermute | solution.py:61
  56.2 1.9 %collective-permute-done.13 = bf16[2,2,64,512]{3,2,1,0:T(8,128)(2,1)S(1)} collective-permute-done((bf16[2,2,64,512]{3,2,1,0:T(8,128)(2,1)S(1)}, bf16[2,2,64,512]{3,2,1,0:T(8,128)(2,1)S(1)}, u32[]{:S(2)}, u32[]{:S(2)}) %collective-permute-start.13) | collective-permute-done | bytes 262176 | tf_op jit(solution)/shard_map/ppermute | solution.py:61
  58.3 5.2 %collective-permute-done.8 = bf16[2,2,64,512]{3,2,0,1:T(8,128)(2,1)S(1)} collective-permute-done((bf16[2,2,64,512]{3,2,0,1:T(8,128)(2,1)S(1)}, bf16[2,2,64,512]{3,2,0,1:T(8,128)(2,1)S(1)}, u32[]{:S(2)}, u32[]{:S(2)}) %collective-permute-start.8) | collective-permute-done | bytes 262176 | tf_op jit(solution)/shard_map/ppermute | solution.py:61
  63.6 1.8 %collective-permute-start.9 = (bf16[2,64,512]{2,1,0:T(8,128)(2,1)S(1)}, bf16[2,64,512]{2,1,0:T(8,128)(2,1)S(1)}, u32[]{:S(2)}, u32[]{:S(2)}) collective-permute-start(bf16[2,64,512]{2,1,0:T(8,128)(2,1)S(1)} %slice_bitcast_fusion.8), channel_id=1, source_target_pairs={{0,12},{1,13},{2,14},{3,15},{4,8},{5,9},{6,10},{7,11},{8,4},{9,5},... | collective-permute-start | bytes 393224 | tf_op jit(solution)/shard_map/ppermute | solution.py:61
  65.7 3.0 %collective-permute-done.9 = bf16[2,64,512]{2,1,0:T(8,128)(2,1)S(1)} collective-permute-done((bf16[2,64,512]{2,1,0:T(8,128)(2,1)S(1)}, bf16[2,64,512]{2,1,0:T(8,128)(2,1)S(1)}, u32[]{:S(2)}, u32[]{:S(2)}) %collective-permute-start.9) | collective-permute-done | bytes 131104 | tf_op jit(solution)/shard_map/ppermute | solution.py:61
  70.8 1.7 %collective-permute-start.18 = (bf16[64,512]{1,0:T(8,128)(2,1)S(1)}, bf16[64,512]{1,0:T(8,128)(2,1)S(1)}, u32[]{:S(2)}, u32[]{:S(2)}) collective-permute-start(bf16[64,512]{1,0:T(8,128)(2,1)S(1)} %get-tuple-element.59), channel_id=1, source_target_pairs={{0,48},{1,49},{2,50},{3,51},{4,52},{5,53},{6,54},{7,55},{8,56},{9,... | collective-permute-start | bytes 196616 | tf_op jit(solution)/shard_map/ppermute | solution.py:65
  73.6 2.2 %collective-permute-done.18 = bf16[64,512]{1,0:T(8,128)(2,1)S(1)} collective-permute-done((bf16[64,512]{1,0:T(8,128)(2,1)S(1)}, bf16[64,512]{1,0:T(8,128)(2,1)S(1)}, u32[]{:S(2)}, u32[]{:S(2)}) %collective-permute-start.18) | collective-permute-done | bytes 65568 | tf_op jit(solution)/shard_map/ppermute | solution.py:65
  75.8 2.3 %collective-permute-start.19 = (bf16[64,512]{1,0:T(8,128)(2,1)S(1)}, bf16[64,512]{1,0:T(8,128)(2,1)S(1)}, u32[]{:S(2)}, u32[]{:S(2)}) collective-permute-start(bf16[64,512]{1,0:T(8,128)(2,1)S(1)} %fusion.37), channel_id=1, source_target_pairs={{0,112},{1,113},{2,114},{3,115},{4,116},{5,117},{6,118},{7,119},{8... | collective-permute-start | bytes 196616 | tf_op jit(solution)/shard_map/ppermute | solution.py:65
  78.1 2.3 %collective-permute-done.19 = bf16[64,512]{1,0:T(8,128)(2,1)S(1)} collective-permute-done((bf16[64,512]{1,0:T(8,128)(2,1)S(1)}, bf16[64,512]{1,0:T(8,128)(2,1)S(1)}, u32[]{:S(2)}, u32[]{:S(2)}) %collective-permute-start.19) | collective-permute-done | bytes 65568 | tf_op jit(solution)/shard_map/ppermute | solution.py:65
  83.9 2.9 %collective-permute-done.26 = bf16[64,512]{1,0:T(8,128)(2,1)S(1)} collective-permute-done((bf16[64,512]{1,0:T(8,128)(2,1)S(1)}, bf16[64,512]{1,0:T(8,128)(2,1)S(1)}, u32[]{:S(2)}, u32[]{:S(2)}) %collective-permute-start.26) | collective-permute-done | bytes 65568 | tf_op jit(solution)/shard_map/ppermute | solution.py:65
  88.3 1.5 %collective-permute-start.21 = (bf16[2,64,512]{2,1,0:T(8,128)(2,1)S(1)}, bf16[2,64,512]{2,1,0:T(8,128)(2,1)S(1)}, u32[]{:S(2)}, u32[]{:S(2)}) collective-permute-start(bf16[2,64,512]{2,1,0:T(8,128)(2,1)S(1)} %get-tuple-element.57), channel_id=1, source_target_pairs={{0,12},{1,13},{2,14},{3,15},{4,8},{5,9},{6,10},{7,11},{8,4},{9,5},... | collective-permute-start | bytes 393224 | tf_op jit(solution)/shard_map/ppermute | solution.py:61
  90.8 2.6 %collective-permute-done.21 = bf16[2,64,512]{2,1,0:T(8,128)(2,1)S(1)} collective-permute-done((bf16[2,64,512]{2,1,0:T(8,128)(2,1)S(1)}, bf16[2,64,512]{2,1,0:T(8,128)(2,1)S(1)}, u32[]{:S(2)}, u32[]{:S(2)}) %collective-permute-start.21) | collective-permute-done | bytes 131104 | tf_op jit(solution)/shard_map/ppermute | solution.py:61
  93.4 2.4 %collective-permute-start.22 = (bf16[2,2,64,512]{3,2,0,1:T(8,128)(2,1)S(1)}, bf16[2,2,64,512]{3,2,0,1:T(8,128)(2,1)S(1)}, u32[]{:S(2)}, u32[]{:S(2)}) collective-permute-start(bf16[2,2,64,512]{3,2,0,1:T(8,128)(2,1)S(1)} %get-tuple-element.53), channel_id=1, source_target_pairs={{0,130},{1,131},{2,128},{3,129},{4,134},{5,135},{6,132},{7,133},{8... | collective-permute-start | bytes 786440 | tf_op jit(solution)/shard_map/ppermute | solution.py:61
  96.4 2.3 %collective-permute-start.33 = (bf16[2,2,64,512]{3,2,1,0:T(8,128)(2,1)S(1)}, bf16[2,2,64,512]{3,2,1,0:T(8,128)(2,1)S(1)}, u32[]{:S(2)}, u32[]{:S(2)}) collective-permute-start(bf16[2,2,64,512]{3,2,1,0:T(8,128)(2,1)S(1)} %get-tuple-element.41), channel_id=1, source_target_pairs={{0,130},{1,131},{2,128},{3,129},{4,134},{5,135},{6,132},{7,133},{8... | collective-permute-start | bytes 786440 | tf_op jit(solution)/shard_map/ppermute | solution.py:61
  100.1 1.8 %collective-permute-start.29 = (bf16[2,2,64,512]{3,2,1,0:T(8,128)(2,1)S(1)}, bf16[2,2,64,512]{3,2,1,0:T(8,128)(2,1)S(1)}, u32[]{:S(2)}, u32[]{:S(2)}) collective-permute-start(bf16[2,2,64,512]{3,2,1,0:T(8,128)(2,1)S(1)} %get-tuple-element.40), channel_id=1, source_target_pairs={{0,12},{1,13},{2,14},{3,15},{4,8},{5,9},{6,10},{7,11},{8,4},{9,5},... | collective-permute-start | bytes 786440 | tf_op jit(solution)/shard_map/ppermute | solution.py:61
  103.3 1.9 %collective-permute-start.34 = (bf16[8,64,512]{2,1,0:T(8,128)(2,1)S(1)}, bf16[8,64,512]{2,1,0:T(8,128)(2,1)S(1)}, u32[]{:S(2)}, u32[]{:S(2)}) collective-permute-start(bf16[8,64,512]{2,1,0:T(8,128)(2,1)S(1)} %bitcast.184), channel_id=1, source_target_pairs={{0,12},{1,13},{2,14},{3,15},{4,8},{5,9},{6,10},{7,11},{8,4},{9,5},... | collective-permute-start | bytes 1572872 | tf_op jit(solution)/shard_map/ppermute | solution.py:61
  106.9 2.4 %collective-permute-start.30 = (bf16[8,64,512]{2,1,0:T(8,128)(2,1)S(1)}, bf16[8,64,512]{2,1,0:T(8,128)(2,1)S(1)}, u32[]{:S(2)}, u32[]{:S(2)}) collective-permute-start(bf16[8,64,512]{2,1,0:T(8,128)(2,1)S(1)} %bitcast.188), channel_id=1, source_target_pairs={{0,130},{1,131},{2,128},{3,129},{4,134},{5,135},{6,132},{7,133},{8... | collective-permute-start | bytes 1572872 | tf_op jit(solution)/shard_map/ppermute | solution.py:61
  110.1 3.0 %collective-permute-done.34.refs_7_ = bf16[8,64,512]{2,1,0:T(8,128)(2,1)S(1)} collective-permute-done((bf16[8,64,512]{2,1,0:T(8,128)(2,1)S(1)}, bf16[8,64,512]{2,1,0:T(8,128)(2,1)S(1)}, u32[]{:S(2)}, u32[]{:S(2)}) %collective-permute-start.34) | collective-permute-done | bytes 524320 | tf_op jit(solution)/shard_map/ppermute | solution.py:61
  114.3 6.2 %collective-permute-done.30.refs_3_ = bf16[8,64,512]{2,1,0:T(8,128)(2,1)S(1)} collective-permute-done((bf16[8,64,512]{2,1,0:T(8,128)(2,1)S(1)}, bf16[8,64,512]{2,1,0:T(8,128)(2,1)S(1)}, u32[]{:S(2)}, u32[]{:S(2)}) %collective-permute-start.30) | collective-permute-done | bytes 524320 | tf_op jit(solution)/shard_map/ppermute | solution.py:61
  120.5 4.5 %project.1 = (bf16[512,512]{1,0:T(8,128)(2,1)}, f32[256,512]{1,0:T(8,128)S(1)}, bf16[256,512]{1,0:T(8,128)(2,1)S(1)}) custom-call(bf16[256,8192]{1,0:T(8,128)(2,1)S(1)} %copy-done.2, bf16[256,4096]{1,0:T(8,128)(2,1)S(1)} %collective-permute-done.3._tokens.got, bf16[8,64,512]{2,1,0:T(8,128)(2,1)S(1)} %bitcast.191, ...), custom_call_target="tpu_custom_call" | custom-call | tf_op jit(solution)/shard_map/project/pallas_call | solution.py:256
  125.0 13.0 %collective-permute-start.35 = (bf16[256,512]{1,0:T(8,128)(2,1)S(1)}, bf16[256,512]{1,0:T(8,128)(2,1)S(1)}, u32[]{:S(2)}, u32[]{:S(2)}) collective-permute-start(bf16[256,512]{1,0:T(8,128)(2,1)S(1)} %get-tuple-element.32), channel_id=1, source_target_pairs={{0,1},{1,0},{2,3},{3,2},{4,5},{5,4},{6,7},{7,6},{8,9},{9,8},{10,11... | collective-permute-start | bytes 786440 | tf_op jit(solution)/shard_map/ppermute | solution.py:69
  (100 shorter events, 29.7 us)
Async XLA Ops:
  8.9 17.1 %collective-permute-start.3 = (bf16[256,4096]{1,0:T(8,128)(2,1)S(1)}, bf16[256,4096]{1,0:T(8,128)(2,1)S(1)}, u32[]{:S(2)}, u32[]{:S(2)}) collective-permute-start(bf16[256,4096]{1,0:T(8,128)(2,1)S(1)} %get-tuple-element.21), channel_id=1, source_target_pairs={{0,1},{1,0},{2,3},{3,2},{4,5},{5,4},{6,7},{7,6},{8,9},{9,8},{10,11... | collective-permute-start | bytes 6291464 | tf_op jit(solution)/shard_map/ppermute | solution.py:69
  12.2 13.8 %collective-permute-start.1 = (bf16[256,4096]{1,0:T(8,128)(2,1)S(1)}, bf16[256,4096]{1,0:T(8,128)(2,1)S(1)}, u32[]{:S(2)}, u32[]{:S(2)}) collective-permute-start(bf16[256,4096]{1,0:T(8,128)(2,1)S(1)} %get-tuple-element.20), channel_id=1, source_target_pairs={{0,1},{1,0},{2,3},{3,2},{4,5},{5,4},{6,7},{7,6},{8,9},{9,8},{10,11... | collective-permute-start | bytes 6291464 | tf_op jit(solution)/shard_map/ppermute | solution.py:69
  12.3 13.6 %collective-permute-start.2 = (bf16[256,512]{1,0:T(8,128)(2,1)S(1)}, bf16[256,512]{1,0:T(8,128)(2,1)S(1)}, u32[]{:S(2)}, u32[]{:S(2)}) collective-permute-start(bf16[256,512]{1,0:T(8,128)(2,1)S(1)} %copy-done.3), channel_id=1, source_target_pairs={{0,1},{1,0},{2,3},{3,2},{4,5},{5,4},{6,7},{7,6},{8,9},{9,8},{10,11... | collective-permute-start | bytes 786440 | tf_op jit(solution)/shard_map/ppermute | solution.py:69
  12.7 13.2 %collective-permute-start = (f32[3,32,512]{2,1,0:T(8,128)S(1)}, f32[3,32,512]{2,1,0:T(8,128)S(1)}, u32[]{:S(2)}, u32[]{:S(2)}) collective-permute-start(f32[3,32,512]{2,1,0:T(8,128)S(1)} %get-tuple-element.19), channel_id=1, source_target_pairs={{0,112},{1,113},{2,114},{3,115},{4,116},{5,117},{6,118},{7,119},{8... | collective-permute-start | bytes 589832 | tf_op jit(solution)/shard_map/ppermute | solution.py:65
  32.8 12.9 %collective-permute-start.4 = (bf16[8,64,512]{2,1,0:T(8,128)(2,1)S(1)}, bf16[8,64,512]{2,1,0:T(8,128)(2,1)S(1)}, u32[]{:S(2)}, u32[]{:S(2)}) collective-permute-start(bf16[8,64,512]{2,1,0:T(8,128)(2,1)S(1)} %get-tuple-element.23), channel_id=1, source_target_pairs={{0,2},{1,3},{2,0},{3,1},{4,6},{5,7},{6,4},{7,5},{8,10},{9,11},{10,... | collective-permute-start | bytes 1572872 | tf_op jit(solution)/shard_map/ppermute | solution.py:61
  34.1 13.1 %collective-permute-start.6 = (bf16[8,64,512]{2,1,0:T(8,128)(2,1)S(1)}, bf16[8,64,512]{2,1,0:T(8,128)(2,1)S(1)}, u32[]{:S(2)}, u32[]{:S(2)}) collective-permute-start(bf16[8,64,512]{2,1,0:T(8,128)(2,1)S(1)} %get-tuple-element.25), channel_id=1, source_target_pairs={{0,4},{1,5},{2,6},{3,7},{4,0},{5,1},{6,2},{7,3},{8,12},{9,13},{10,... | collective-permute-start | bytes 1572872 | tf_op jit(solution)/shard_map/ppermute | solution.py:61
  35.4 13.4 %collective-permute-start.10 = (bf16[8,64,512]{2,1,0:T(8,128)(2,1)S(1)}, bf16[8,64,512]{2,1,0:T(8,128)(2,1)S(1)}, u32[]{:S(2)}, u32[]{:S(2)}) collective-permute-start(bf16[8,64,512]{2,1,0:T(8,128)(2,1)S(1)} %get-tuple-element.27), channel_id=1, source_target_pairs={{0,130},{1,131},{2,128},{3,129},{4,134},{5,135},{6,132},{7,133},{8... | collective-permute-start | bytes 1572872 | tf_op jit(solution)/shard_map/ppermute | solution.py:61
  37.2 13.7 %collective-permute-start.12 = (bf16[8,64,512]{2,1,0:T(8,128)(2,1)S(1)}, bf16[8,64,512]{2,1,0:T(8,128)(2,1)S(1)}, u32[]{:S(2)}, u32[]{:S(2)}) collective-permute-start(bf16[8,64,512]{2,1,0:T(8,128)(2,1)S(1)} %get-tuple-element.29), channel_id=1, source_target_pairs={{0,12},{1,13},{2,14},{3,15},{4,8},{5,9},{6,10},{7,11},{8,4},{9,5},... | collective-permute-start | bytes 1572872 | tf_op jit(solution)/shard_map/ppermute | solution.py:61
  45.8 7.4 %collective-permute-start.5 = (bf16[2,2,64,512]{3,2,1,0:T(8,128)(2,1)S(1)}, bf16[2,2,64,512]{3,2,1,0:T(8,128)(2,1)S(1)}, u32[]{:S(2)}, u32[]{:S(2)}) collective-permute-start(bf16[2,2,64,512]{3,2,1,0:T(8,128)(2,1)S(1)} %slice_bitcast_fusion.4), channel_id=1, source_target_pairs={{0,4},{1,5},{2,6},{3,7},{4,0},{5,1},{6,2},{7,3},{8,12},{9,13},{10,... | collective-permute-start | bytes 786440 | tf_op jit(solution)/shard_map/ppermute | solution.py:61
  47.4 6.1 %collective-permute-start.7 = (bf16[2,2,64,512]{3,2,1,0:T(8,128)(2,1)S(1)}, bf16[2,2,64,512]{3,2,1,0:T(8,128)(2,1)S(1)}, u32[]{:S(2)}, u32[]{:S(2)}) collective-permute-start(bf16[2,2,64,512]{3,2,1,0:T(8,128)(2,1)S(1)} %bitcast.204), channel_id=1, source_target_pairs={{0,2},{1,3},{2,0},{3,1},{4,6},{5,7},{6,4},{7,5},{8,10},{9,11},{10,... | collective-permute-start | bytes 786440 | tf_op jit(solution)/shard_map/ppermute | solution.py:61
  48.9 7.2 %collective-permute-start.11 = (bf16[2,2,64,512]{3,2,1,0:T(8,128)(2,1)S(1)}, bf16[2,2,64,512]{3,2,1,0:T(8,128)(2,1)S(1)}, u32[]{:S(2)}, u32[]{:S(2)}) collective-permute-start(bf16[2,2,64,512]{3,2,1,0:T(8,128)(2,1)S(1)} %slice_bitcast_fusion.2), channel_id=1, source_target_pairs={{0,12},{1,13},{2,14},{3,15},{4,8},{5,9},{6,10},{7,11},{8,4},{9,5},... | collective-permute-start | bytes 786440 | tf_op jit(solution)/shard_map/ppermute | solution.py:61
  51.1 7.0 %collective-permute-start.13 = (bf16[2,2,64,512]{3,2,1,0:T(8,128)(2,1)S(1)}, bf16[2,2,64,512]{3,2,1,0:T(8,128)(2,1)S(1)}, u32[]{:S(2)}, u32[]{:S(2)}) collective-permute-start(bf16[2,2,64,512]{3,2,1,0:T(8,128)(2,1)S(1)} %slice_bitcast_fusion), channel_id=1, source_target_pairs={{0,130},{1,131},{2,128},{3,129},{4,134},{5,135},{6,132},{7,133},{8... | collective-permute-start | bytes 786440 | tf_op jit(solution)/shard_map/ppermute | solution.py:61
  53.6 10.0 %collective-permute-start.8 = (bf16[2,2,64,512]{3,2,0,1:T(8,128)(2,1)S(1)}, bf16[2,2,64,512]{3,2,0,1:T(8,128)(2,1)S(1)}, u32[]{:S(2)}, u32[]{:S(2)}) collective-permute-start(bf16[2,2,64,512]{3,2,0,1:T(8,128)(2,1)S(1)} %fusion.17), channel_id=1, source_target_pairs={{0,130},{1,131},{2,128},{3,129},{4,134},{5,135},{6,132},{7,133},{8... | collective-permute-start | bytes 786440 | tf_op jit(solution)/shard_map/ppermute | solution.py:61
  58.2 7.2 %collective-permute-start.14 = (bf16[2,2,64,512]{3,2,0,1:T(8,128)(2,1)S(1)}, bf16[2,2,64,512]{3,2,0,1:T(8,128)(2,1)S(1)}, u32[]{:S(2)}, u32[]{:S(2)}) collective-permute-start(bf16[2,2,64,512]{3,2,0,1:T(8,128)(2,1)S(1)} %fusion.16), channel_id=1, source_target_pairs={{0,2},{1,3},{2,0},{3,1},{4,6},{5,7},{6,4},{7,5},{8,10},{9,11},{10,... | collective-permute-start | bytes 786440 | tf_op jit(solution)/shard_map/ppermute | solution.py:61
  63.6 5.1 %collective-permute-start.9 = (bf16[2,64,512]{2,1,0:T(8,128)(2,1)S(1)}, bf16[2,64,512]{2,1,0:T(8,128)(2,1)S(1)}, u32[]{:S(2)}, u32[]{:S(2)}) collective-permute-start(bf16[2,64,512]{2,1,0:T(8,128)(2,1)S(1)} %slice_bitcast_fusion.8), channel_id=1, source_target_pairs={{0,12},{1,13},{2,14},{3,15},{4,8},{5,9},{6,10},{7,11},{8,4},{9,5},... | collective-permute-start | bytes 393224 | tf_op jit(solution)/shard_map/ppermute | solution.py:61
  65.5 4.2 %collective-permute-start.15 = (bf16[2,64,512]{2,1,0:T(8,128)(2,1)S(1)}, bf16[2,64,512]{2,1,0:T(8,128)(2,1)S(1)}, u32[]{:S(2)}, u32[]{:S(2)}) collective-permute-start(bf16[2,64,512]{2,1,0:T(8,128)(2,1)S(1)} %slice_bitcast_fusion.6), channel_id=1, source_target_pairs={{0,4},{1,5},{2,6},{3,7},{4,0},{5,1},{6,2},{7,3},{8,12},{9,13},{10,... | collective-permute-start | bytes 393224 | tf_op jit(solution)/shard_map/ppermute | solution.py:61
  70.8 4.9 %collective-permute-start.18 = (bf16[64,512]{1,0:T(8,128)(2,1)S(1)}, bf16[64,512]{1,0:T(8,128)(2,1)S(1)}, u32[]{:S(2)}, u32[]{:S(2)}) collective-permute-start(bf16[64,512]{1,0:T(8,128)(2,1)S(1)} %get-tuple-element.59), channel_id=1, source_target_pairs={{0,48},{1,49},{2,50},{3,51},{4,52},{5,53},{6,54},{7,55},{8,56},{9,... | collective-permute-start | bytes 196616 | tf_op jit(solution)/shard_map/ppermute | solution.py:65
  75.8 4.6 %collective-permute-start.19 = (bf16[64,512]{1,0:T(8,128)(2,1)S(1)}, bf16[64,512]{1,0:T(8,128)(2,1)S(1)}, u32[]{:S(2)}, u32[]{:S(2)}) collective-permute-start(bf16[64,512]{1,0:T(8,128)(2,1)S(1)} %fusion.37), channel_id=1, source_target_pairs={{0,112},{1,113},{2,114},{3,115},{4,116},{5,117},{6,118},{7,119},{8... | collective-permute-start | bytes 196616 | tf_op jit(solution)/shard_map/ppermute | solution.py:65
  81.8 4.9 %collective-permute-start.26 = (bf16[64,512]{1,0:T(8,128)(2,1)S(1)}, bf16[64,512]{1,0:T(8,128)(2,1)S(1)}, u32[]{:S(2)}, u32[]{:S(2)}) collective-permute-start(bf16[64,512]{1,0:T(8,128)(2,1)S(1)} %fusion.32), channel_id=1, source_target_pairs={{0,48},{1,49},{2,50},{3,51},{4,52},{5,53},{6,54},{7,55},{8,56},{9,... | collective-permute-start | bytes 196616 | tf_op jit(solution)/shard_map/ppermute | solution.py:65
  83.3 4.9 %collective-permute-start.20 = (bf16[64,512]{1,0:T(8,128)(2,1)S(1)}, bf16[64,512]{1,0:T(8,128)(2,1)S(1)}, u32[]{:S(2)}, u32[]{:S(2)}) collective-permute-start(bf16[64,512]{1,0:T(8,128)(2,1)S(1)} %fusion.32), channel_id=1, source_target_pairs={{0,32},{1,33},{2,34},{3,35},{4,36},{5,37},{6,38},{7,39},{8,40},{9,... | collective-permute-start | bytes 196616 | tf_op jit(solution)/shard_map/ppermute | solution.py:65
  88.3 5.1 %collective-permute-start.21 = (bf16[2,64,512]{2,1,0:T(8,128)(2,1)S(1)}, bf16[2,64,512]{2,1,0:T(8,128)(2,1)S(1)}, u32[]{:S(2)}, u32[]{:S(2)}) collective-permute-start(bf16[2,64,512]{2,1,0:T(8,128)(2,1)S(1)} %get-tuple-element.57), channel_id=1, source_target_pairs={{0,12},{1,13},{2,14},{3,15},{4,8},{5,9},{6,10},{7,11},{8,4},{9,5},... | collective-permute-start | bytes 393224 | tf_op jit(solution)/shard_map/ppermute | solution.py:61
  90.7 5.6 %collective-permute-start.28 = (bf16[2,2,64,512]{3,2,1,0:T(8,128)(2,1)S(1)}, bf16[2,2,64,512]{3,2,1,0:T(8,128)(2,1)S(1)}, u32[]{:S(2)}, u32[]{:S(2)}) collective-permute-start(bf16[2,2,64,512]{3,2,1,0:T(8,128)(2,1)S(1)} %get-tuple-element.51), channel_id=1, source_target_pairs={{0,2},{1,3},{2,0},{3,1},{4,6},{5,7},{6,4},{7,5},{8,10},{9,11},{10,... | collective-permute-start | bytes 786440 | tf_op jit(solution)/shard_map/ppermute | solution.py:61
  93.4 6.5 %collective-permute-start.22 = (bf16[2,2,64,512]{3,2,0,1:T(8,128)(2,1)S(1)}, bf16[2,2,64,512]{3,2,0,1:T(8,128)(2,1)S(1)}, u32[]{:S(2)}, u32[]{:S(2)}) collective-permute-start(bf16[2,2,64,512]{3,2,0,1:T(8,128)(2,1)S(1)} %get-tuple-element.53), channel_id=1, source_target_pairs={{0,130},{1,131},{2,128},{3,129},{4,134},{5,135},{6,132},{7,133},{8... | collective-permute-start | bytes 786440 | tf_op jit(solution)/shard_map/ppermute | solution.py:61
  96.4 6.8 %collective-permute-start.33 = (bf16[2,2,64,512]{3,2,1,0:T(8,128)(2,1)S(1)}, bf16[2,2,64,512]{3,2,1,0:T(8,128)(2,1)S(1)}, u32[]{:S(2)}, u32[]{:S(2)}) collective-permute-start(bf16[2,2,64,512]{3,2,1,0:T(8,128)(2,1)S(1)} %get-tuple-element.41), channel_id=1, source_target_pairs={{0,130},{1,131},{2,128},{3,129},{4,134},{5,135},{6,132},{7,133},{8... | collective-permute-start | bytes 786440 | tf_op jit(solution)/shard_map/ppermute | solution.py:61
  100.0 5.8 %collective-permute-start.31 = (bf16[2,2,64,512]{3,2,1,0:T(8,128)(2,1)S(1)}, bf16[2,2,64,512]{3,2,1,0:T(8,128)(2,1)S(1)}, u32[]{:S(2)}, u32[]{:S(2)}) collective-permute-start(bf16[2,2,64,512]{3,2,1,0:T(8,128)(2,1)S(1)} %bitcast.199), channel_id=1, source_target_pairs={{0,2},{1,3},{2,0},{3,1},{4,6},{5,7},{6,4},{7,5},{8,10},{9,11},{10,... | collective-permute-start | bytes 786440 | tf_op jit(solution)/shard_map/ppermute | solution.py:61
  100.1 6.7 %collective-permute-start.29 = (bf16[2,2,64,512]{3,2,1,0:T(8,128)(2,1)S(1)}, bf16[2,2,64,512]{3,2,1,0:T(8,128)(2,1)S(1)}, u32[]{:S(2)}, u32[]{:S(2)}) collective-permute-start(bf16[2,2,64,512]{3,2,1,0:T(8,128)(2,1)S(1)} %get-tuple-element.40), channel_id=1, source_target_pairs={{0,12},{1,13},{2,14},{3,15},{4,8},{5,9},{6,10},{7,11},{8,4},{9,5},... | collective-permute-start | bytes 786440 | tf_op jit(solution)/shard_map/ppermute | solution.py:61
  101.9 7.4 %collective-permute-start.23 = (bf16[2,2,64,512]{3,2,1,0:T(8,128)(2,1)S(1)}, bf16[2,2,64,512]{3,2,1,0:T(8,128)(2,1)S(1)}, u32[]{:S(2)}, u32[]{:S(2)}) collective-permute-start(bf16[2,2,64,512]{3,2,1,0:T(8,128)(2,1)S(1)} %get-tuple-element.44), channel_id=1, source_target_pairs={{0,4},{1,5},{2,6},{3,7},{4,0},{5,1},{6,2},{7,3},{8,12},{9,13},{10,... | collective-permute-start | bytes 786440 | tf_op jit(solution)/shard_map/ppermute | solution.py:61
  103.3 9.8 %collective-permute-start.34 = (bf16[8,64,512]{2,1,0:T(8,128)(2,1)S(1)}, bf16[8,64,512]{2,1,0:T(8,128)(2,1)S(1)}, u32[]{:S(2)}, u32[]{:S(2)}) collective-permute-start(bf16[8,64,512]{2,1,0:T(8,128)(2,1)S(1)} %bitcast.184), channel_id=1, source_target_pairs={{0,12},{1,13},{2,14},{3,15},{4,8},{5,9},{6,10},{7,11},{8,4},{9,5},... | collective-permute-start | bytes 1572872 | tf_op jit(solution)/shard_map/ppermute | solution.py:61
  105.9 8.4 %collective-permute-start.32 = (bf16[8,64,512]{2,1,0:T(8,128)(2,1)S(1)}, bf16[8,64,512]{2,1,0:T(8,128)(2,1)S(1)}, u32[]{:S(2)}, u32[]{:S(2)}) collective-permute-start(bf16[8,64,512]{2,1,0:T(8,128)(2,1)S(1)} %bitcast.186), channel_id=1, source_target_pairs={{0,4},{1,5},{2,6},{3,7},{4,0},{5,1},{6,2},{7,3},{8,12},{9,13},{10,... | collective-permute-start | bytes 1572872 | tf_op jit(solution)/shard_map/ppermute | solution.py:61
  106.9 13.6 %collective-permute-start.30 = (bf16[8,64,512]{2,1,0:T(8,128)(2,1)S(1)}, bf16[8,64,512]{2,1,0:T(8,128)(2,1)S(1)}, u32[]{:S(2)}, u32[]{:S(2)}) collective-permute-start(bf16[8,64,512]{2,1,0:T(8,128)(2,1)S(1)} %bitcast.188), channel_id=1, source_target_pairs={{0,130},{1,131},{2,128},{3,129},{4,134},{5,135},{6,132},{7,133},{8... | collective-permute-start | bytes 1572872 | tf_op jit(solution)/shard_map/ppermute | solution.py:61
  109.3 11.2 %collective-permute-start.24 = (bf16[8,64,512]{2,1,0:T(8,128)(2,1)S(1)}, bf16[8,64,512]{2,1,0:T(8,128)(2,1)S(1)}, u32[]{:S(2)}, u32[]{:S(2)}) collective-permute-start(bf16[8,64,512]{2,1,0:T(8,128)(2,1)S(1)} %bitcast.190), channel_id=1, source_target_pairs={{0,2},{1,3},{2,0},{3,1},{4,6},{5,7},{6,4},{7,5},{8,10},{9,11},{10,... | collective-permute-start | bytes 1572872 | tf_op jit(solution)/shard_map/ppermute | solution.py:61
  125.0 14.3 %collective-permute-start.35 = (bf16[256,512]{1,0:T(8,128)(2,1)S(1)}, bf16[256,512]{1,0:T(8,128)(2,1)S(1)}, u32[]{:S(2)}, u32[]{:S(2)}) collective-permute-start(bf16[256,512]{1,0:T(8,128)(2,1)S(1)} %get-tuple-element.32), channel_id=1, source_target_pairs={{0,1},{1,0},{2,3},{3,2},{4,5},{5,4},{6,7},{7,6},{8,9},{9,8},{10,11... | collective-permute-start | bytes 786440 | tf_op jit(solution)/shard_map/ppermute | solution.py:69
  (11 other events, 40.6 us)

commit v4 on v3

v4 whole, which is shorter than its diff:
```python
import functools
import itertools

import jax
import jax.numpy as jnp
from jax import lax
from jax.experimental import pallas as pl
from jax.experimental.pallas import tpu as pltpu
from jax.sharding import PartitionSpec as P

ADAM_STEP = 10
beta_first = 0.9
beta_second = 0.95
learn_rate = 0.002
decay_rate = 0.1
adam_eps = 1e-08

AXES = ("outer", "inner")
SIZES = (2, 8, 4, 2, 2)
TOK = 256
COLS = 512
HALF = 4096
BLOCK = 256
BLOCKS = 16
PARTS = 2
ROWS = 128
PAIRS = 4

ORDERS = ((0, 2, 1, 3), (1, 3, 0, 2))


def moves(change):
    pairs = []
    for here in itertools.product(*(range(n) for n in SIZES)):
        source = target = 0
        for n, i, j in zip(SIZES, here, change(*here)):
            source, target = source * n + i, target * n + j
        pairs.append((source, target))
    return pairs


def paired(i, odd):
    if odd:
        return (i + 1) % 4 if i % 2 else (i - 1) % 4
    return i ^ 1


def pair(v, xh, z, y, xl, c):
    v = v ^ (2 * c)
    if v < 2:
        x = paired(xh * 2 + xl, v)
        return x // 2, z, y, x % 2, c
    return xh, z, paired(y, v - 2), xl, c


PAIRINGS = tuple(moves(functools.partial(pair, v)) for v in range(4))


def across(array, pairing):
    return lax.ppermute(array, AXES, PAIRINGS[pairing])


def z_swap(array, mask):
    return lax.ppermute(array, AXES, moves(lambda xh, z, y, xl, c: (xh, z ^ mask, y, xl, c)))


def core_swap(array):
    return lax.ppermute(array, AXES, moves(lambda xh, z, y, xl, c: (xh, z, y, xl, 1 - c)))


def place():
    outer, inner = lax.axis_index("outer"), lax.axis_index("inner")
    return outer // 8, outer % 8, inner // 4, (inner // 2) % 2, inner % 2


def columns_of(where, r, core):
    xh, _, y, xl, _ = where
    bits = [(r >> (3 - v)) & 1 for v in range(4)]
    a, b, c, d = (bits[v] + core * (bits[v ^ 2] - bits[v]) for v in range(4))
    to_xh, to_xl, to_y = xh ^ b, xl ^ (a ^ b), y ^ (2 * d + (c ^ d))
    block = ((to_y * 2 + to_xl) * 2 + core) * 2 + to_xh
    return pl.ds(pl.multiple_of(block * BLOCK, BLOCK), BLOCK)


def side_and_slot(m, r):
    bits = [(r >> (3 - v)) & 1 for v in range(4)]
    side = bits.pop(ORDERS[m][0])
    return side, bits[0] * 4 + bits[1] * 2 + bits[2]


def pair_starts(where, m):
    z = where[1]
    first = jnp.where(z < 4, z, 7 - z) ^ m
    return first * 32, (7 - first) * 32


ANY = pl.BlockSpec(memory_space=pl.ANY)
VMEM = pl.BlockSpec(memory_space=pltpu.VMEM)
PARAMS = pltpu.CompilerParams(vmem_limit_bytes=40 * 1024 * 1024)
WHOLE = pltpu.CompilerParams(vmem_limit_bytes=60 * 1024 * 1024)


def cost(flops, size):
    return pl.CostEstimate(flops=flops, bytes_accessed=size, transcendentals=0)


def run_all(copies):
    for copy in copies:
        copy.start()
    for copy in copies:
        copy.wait()


def theirs_of(source, packed, sems):
    where = place()
    return [
        pltpu.make_async_copy(
            source.at[:, columns_of(where, r, 1 - where[4])],
            packed.at[:, pl.ds(r * BLOCK, BLOCK)],
            sems.at[r],
        )
        for r in range(BLOCKS)
    ]


PACKED = jax.ShapeDtypeStruct((TOK, HALF), jnp.bfloat16)


DONE = jax.ShapeDtypeStruct((8, 128), jnp.float32)


def pack_acts_kernel(acts, packed, done, sems):
    done[...] = jnp.zeros_like(done)
    run_all(theirs_of(acts, packed, sems))


def pack_acts(acts):
    return pl.pallas_call(
        pack_acts_kernel,
        out_shape=(PACKED, DONE),
        in_specs=[ANY],
        out_specs=(ANY, VMEM),
        scratch_shapes=[pltpu.SemaphoreType.DMA((BLOCKS,))],
        compiler_params=WHOLE,
        cost_estimate=cost(0, 4 << 20),
        name="pack_acts",
    )(acts)


def pack_rest_kernel(tokens, master, first, second, _after, packed, state, done, sems):
    done[...] = jnp.zeros_like(done)
    run_all(
        theirs_of(tokens, packed, sems)
        + [
            pltpu.make_async_copy(source, state.at[i], sems.at[BLOCKS + i])
            for i, source in enumerate((master, first, second))
        ]
    )


def pack_rest(tokens, master, first, second, after):
    return pl.pallas_call(
        pack_rest_kernel,
        out_shape=(
            PACKED,
            jax.ShapeDtypeStruct((3, 32, COLS), jnp.float32),
            DONE,
        ),
        in_specs=[ANY] * 4 + [VMEM],
        out_specs=(ANY, ANY, VMEM),
        scratch_shapes=[pltpu.SemaphoreType.DMA((BLOCKS + 3,))],
        compiler_params=PARAMS,
        cost_estimate=cost(0, 5 << 20),
        name="pack_rest",
    )(tokens, master, first, second, after)


def term_kernel(acts, got, grads, got_grads, _after, *refs):
    halves = refs[: 2 * PARTS]
    both, grads_both, term, sems = refs[2 * PARTS :]
    where = place()
    own, other = [], []
    for r in range(BLOCKS):
        here = pl.ds(r * BLOCK, BLOCK)
        own.append(
            pltpu.make_async_copy(
                acts.at[:, columns_of(where, r, where[4])], both.at[:TOK, here], sems.at[r]
            )
        )
        other.append(
            pltpu.make_async_copy(got.at[:, here], both.at[TOK:, here], sems.at[BLOCKS + r])
        )
    for r in range(BLOCKS):
        own[r].start()
        other[r].start()
    grads_both[:TOK] = grads[...]
    grads_both[TOK:] = got_grads[...]
    starts = [pair_starts(where, m) for m in range(PAIRS)]
    for r in range(BLOCKS):
        own[r].wait()
        other[r].wait()
        term[r % 2] = lax.dot_general(
            both[:, r * BLOCK : (r + 1) * BLOCK],
            grads_both[...],
            (((0,), (0,)), ((), ())),
            preferred_element_type=jnp.float32,
        ).astype(jnp.bfloat16)
        for m in range(PAIRS):
            side, slot = side_and_slot(m // 2, r)
            for j in range(2):
                to = (m % 2) * 64 + j * 32
                halves[2 * (m // 2) + side][slot, to : to + 32] = term[
                    r % 2, pl.ds(pl.multiple_of(starts[m][j], 32), 32)
                ]


def gradient_term(acts, got, grads, got_grads, after):
    half = jax.ShapeDtypeStruct((8, ROWS, COLS), jnp.bfloat16)
    return pl.pallas_call(
        term_kernel,
        out_shape=(half,) * (2 * PARTS),
        in_specs=[ANY, ANY, VMEM, VMEM, VMEM],
        out_specs=(VMEM,) * (2 * PARTS),
        scratch_shapes=[
            pltpu.VMEM((2 * TOK, HALF), jnp.bfloat16),
            pltpu.VMEM((2 * TOK, COLS), jnp.bfloat16),
            pltpu.VMEM((2, BLOCK, COLS), jnp.bfloat16),
            pltpu.SemaphoreType.DMA((2 * BLOCKS,)),
        ],
        compiler_params=PARAMS,
        cost_estimate=cost(2 * 2 * TOK * HALF * COLS, 9 << 20),
        name="gradient_term",
    )(acts, got, grads, got_grads, after)


def add_kernel(dim, keep, got, *refs):
    next_keep, next_send = refs[-2:]
    blocks = keep.shape[0]
    inner = blocks >> (dim + 1)
    for slot in range(blocks):
        side = (slot // inner) % 2
        out = next_send if side else next_keep
        out[slot // (2 * inner) * inner + slot % inner] = (
            keep[slot].astype(jnp.float32) + got[slot].astype(jnp.float32)
        ).astype(jnp.bfloat16)


def add_halves(keep, got, dim, after=()):
    blocks = keep.shape[0]
    half = jax.ShapeDtypeStruct((blocks // 2, ROWS, COLS), jnp.bfloat16)
    return pl.pallas_call(
        functools.partial(add_kernel, dim),
        out_shape=(half, half),
        in_specs=[VMEM, VMEM] + [ANY] * len(after),
        out_specs=(VMEM, VMEM),
        compiler_params=PARAMS,
        cost_estimate=cost(blocks << 16, blocks * 3 << 17),
        name="add_halves",
    )(keep, got, *after)


def join_kernel(dim, here, got, both):
    blocks = here.shape[0]
    inner = blocks >> dim
    for slot in range(2 * blocks):
        source = got if (slot // inner) % 2 else here
        both[slot] = source[slot // (2 * inner) * inner + slot % inner]


def join(here, got, dim):
    blocks = here.shape[0]
    return pl.pallas_call(
        functools.partial(join_kernel, dim),
        out_shape=jax.ShapeDtypeStruct((2 * blocks, ROWS, COLS), jnp.bfloat16),
        in_specs=[VMEM, VMEM],
        out_specs=VMEM,
        compiler_params=PARAMS,
        cost_estimate=cost(0, blocks * 4 << 17),
        name="join",
    )(here, got)


STRIPE = 1024


def project_kernel(tokens, got, *refs):
    halves = refs[: 2 * PARTS]
    kept, mine, theirs, both, weights, total, sems = refs[2 * PARTS :]
    where = place()
    token_copies = [
        pltpu.make_async_copy(
            tokens.at[:, columns_of(where, r, where[4])],
            both.at[:TOK, pl.ds(r * BLOCK, BLOCK)],
            sems.at[r],
        )
        for r in range(BLOCKS)
    ]
    got_copies = [
        pltpu.make_async_copy(
            got.at[:, pl.ds(s * STRIPE, STRIPE)],
            both.at[TOK:, pl.ds(s * STRIPE, STRIPE)],
            sems.at[BLOCKS + s],
        )
        for s in range(HALF // STRIPE)
    ]
    per = STRIPE // BLOCK
    for s in range(HALF // STRIPE):
        for k in range(per):
            token_copies[s * per + k].start()
        got_copies[s].start()
    starts = [pair_starts(where, m) for m in range(PAIRS)]

    def keep_block(x_hi, block):
        kept[pl.ds(pl.multiple_of(x_hi * BLOCK, BLOCK), BLOCK)] = block

    for s in range(HALF // STRIPE):
        for k in range(per):
            for m in range(PAIRS):
                side, slot = side_and_slot(m // 2, s * per + k)
                for j in range(2):
                    at = pl.ds(pl.multiple_of(k * BLOCK + starts[m][j], 32), 32)
                    of = (m % 2) * 64 + j * 32
                    weights[s % 2, at] = halves[2 * (m // 2) + side][slot, of : of + 32]
            token_copies[s * per + k].wait()
        got_copies[s].wait()
        if s == 0:
            keep_block(where[0], weights[0, :BLOCK])

            @pl.when(where[4] == 1)
            def _():
                keep_block(1 - where[0], weights[0, 3 * BLOCK :])

        if s == 3:

            @pl.when(where[4] == 0)
            def _():
                keep_block(1 - where[0], weights[1, :BLOCK])

        product = jnp.dot(
            both[:, s * STRIPE : (s + 1) * STRIPE],
            weights[s % 2],
            preferred_element_type=jnp.float32,
        )
        if s == 0:
            total[...] = product
        elif s < HALF // STRIPE - 1:
            total[...] += product
        else:
            product += total[...]
            mine[...] = product[:TOK]
            theirs[...] = product[TOK:].astype(jnp.bfloat16)


def project(tokens, got, halves):
    return pl.pallas_call(
        project_kernel,
        out_shape=(
            jax.ShapeDtypeStruct((2 * BLOCK, COLS), jnp.bfloat16),
            jax.ShapeDtypeStruct((TOK, COLS), jnp.float32),
            jax.ShapeDtypeStruct((TOK, COLS), jnp.bfloat16),
        ),
        in_specs=[ANY, ANY] + [VMEM] * (2 * PARTS),
        out_specs=(VMEM,) * 3,
        scratch_shapes=[
            pltpu.VMEM((2 * TOK, HALF), jnp.bfloat16),
            pltpu.VMEM((2, STRIPE, COLS), jnp.bfloat16),
            pltpu.VMEM((2 * TOK, COLS), jnp.float32),
            pltpu.SemaphoreType.DMA((BLOCKS + HALF // STRIPE,)),
        ],
        compiler_params=PARAMS,
        cost_estimate=cost(2 * 2 * TOK * HALF * COLS, 9 << 20),
        name="project",
    )(tokens, got, *halves)


def adamw_update(gradient, master_weights, first_moment, second_moment):
    new_first = beta_first * first_moment + (1.0 - beta_first) * gradient
    new_second = beta_second * second_moment + (1.0 - beta_second) * gradient * gradient
    first_hat = new_first / (1.0 - beta_first**ADAM_STEP)
    second_hat = new_second / (1.0 - beta_second**ADAM_STEP)
    new_master = master_weights - learn_rate * (
        first_hat / (jnp.sqrt(second_hat) + adam_eps) + decay_rate * master_weights
    )
    return (new_master, new_first, new_second)


def wide(array):
    return array.astype(jnp.float32)


def add(keep, got):
    return (wide(keep) + wide(got)).astype(jnp.bfloat16)


def halve(array, dim, pairing):
    keep = lax.index_in_dim(array, 0, dim, keepdims=False)
    return add(keep, across(lax.index_in_dim(array, 1, dim, keepdims=False), pairing))


def reduce_parts(halves, tokens, state):
    parts = []
    for i, (v, w, p, q) in enumerate(ORDERS):
        keep, got = halves[2 * i], across(halves[2 * i + 1], v)
        keep, send = add_halves(keep, got, w - (v < w), (tokens,) if i else ())
        got = across(send, w)
        keep, send = add_halves(keep, got, sorted((p, q)).index(p), (state,) if i else ())
        got = across(send, p)
        keep, send = add_halves(keep, got, 0)
        parts.append((wide(keep) + wide(across(send, q))).astype(jnp.bfloat16).reshape(ROWS, COLS))
    return parts


def reduce_z(parts):
    total = wide(parts[0][:64])
    for m in range(1, PAIRS):
        rows = parts[m // 2][(m % 2) * 64 : (m % 2) * 64 + 64]
        total = total + wide(z_swap(rows, m))
    total = total.astype(jnp.bfloat16)
    return (wide(total) + wide(z_swap(total, 7))).reshape(2, 32, COLS)


def gather_parts(pair):
    pairs = [pair] + [z_swap(pair, m) for m in range(1, PAIRS)]
    halves = []
    for i, (v, w, p, q) in enumerate(ORDERS):
        part = jnp.concatenate(pairs[2 * i : 2 * i + 2], axis=0)[None]
        for bit, dim in ((q, 0), (p, sorted((p, q)).index(p)), (w, w - (v < w))):
            part = join(part, across(part, bit), dim)
        halves += [part, across(part, v)]
    return halves


def local(activations, output_grads, master_weights, first_moment, second_moment, next_tokens):
    low = lax.axis_index("outer") % 8 < 4
    packed, packed_acts = pack_acts(activations)
    packed_tokens, state, packed_all = pack_rest(
        next_tokens, master_weights, first_moment, second_moment, packed_acts
    )
    got_acts, got_grads = core_swap(packed), core_swap(output_grads)
    halves = gradient_term(
        activations, got_acts, output_grads, got_grads, packed_all
    )
    got_state = z_swap(state, 7)
    got_tokens = core_swap(packed_tokens)

    gradient = reduce_z(reduce_parts(halves, got_tokens, got_state))
    pairs = jnp.stack([jnp.where(low, state, got_state), jnp.where(low, got_state, state)], axis=1)
    updated = adamw_update(gradient, *pairs)
    new_master, new_first, new_second = (jnp.where(low, u[0], u[1]) for u in updated)
    rows = updated[0].astype(jnp.bfloat16).reshape(64, COLS)

    kept_weights, mine, theirs = project(next_tokens, got_tokens, gather_parts(rows))
    projection = (mine + wide(core_swap(theirs))).astype(jnp.bfloat16)
    return (new_master, new_first, new_second, kept_weights, projection)


def solution(mesh):
    placed = (
        P(("outer", "inner"), None),
        P(("outer", "inner"), None),
        P(("inner", "outer"), None),
        P(("inner", "outer"), None),
        P(("inner", "outer"), None),
        P(("outer", "inner"), None),
    )
    return jax.shard_map(
        local,
        mesh=mesh,
        in_specs=placed,
        out_specs=(
            P(("inner", "outer"), None),
            P(("inner", "outer"), None),
            P(("inner", "outer"), None),
            P("inner", None),
            P(("outer", "inner"), None),
        ),
        check_vma=False,
    )
```

time: 140 us -> 204 us (1.46)
  Pallas kernels: 12.7 us -> 77.6 us
  waiting for transfers between devices: 55.7 us -> 73 us
  starting transfers between devices: 59.8 us -> 47.1 us
  local copies, waits for them, and re-layouts: 7.13 us -> 2.91 us
    pallas_call x2 -> x15, Pallas kernels: 8.14 us -> 73.9 us  [the longest x1 65.4 us: pack_acts(): pl.pallas_call(pack_acts_kernel, out_shape=(PACKED, DONE), in_specs=[ANY]...]
    ppermute x24 -> x16, waiting for transfers between devices: 36.1 us -> 51.3 us  [across(): return lax.ppermute(array, AXES, PAIRINGS[pairing])]
    ppermute x24 -> x16, starting transfers between devices: 31.1 us -> 18.3 us  [across(): return lax.ppermute(array, AXES, PAIRINGS[pairing])]
    ppermute x4, waiting for transfers between devices: 0.01 us -> 4.03 us  [core_swap(): lax.ppermute(array, AXES, moves(lambda xh, z, y, xl, c: (xh, z, y, xl, 1...]
    unnamed x14 -> x16, local copies, waits for them, and re-layouts: 6.89 us -> 2.89 us
    ppermute x8, starting transfers between devices: 11.8 us -> 14.7 us  [z_swap(): lax.ppermute(array, AXES, moves(lambda xh, z, y, xl, c: (xh, z ^ mask, y,...]
    ppermute x4, starting transfers between devices: 16.8 us -> 14 us  [core_swap(): lax.ppermute(array, AXES, moves(lambda xh, z, y, xl, c: (xh, z, y, xl, 1...]
  transfers between devices with their start and end apart: 36 -> 28, of which waited for: 25 -> 20; matrix products, arithmetic and copies ran while one was open for 2% -> 1% of each run, Pallas kernels for 0% -> 4%
where the time goes in v4:
time: 204 us
  Pallas kernels  77.6 us (38%)
  waiting for transfers between devices  73 us (36%)
  starting transfers between devices  47.1 us (23%)
  local copies, waits for them, and re-layouts  2.91 us (1%)
  other arithmetic  2.49 us (1%)
    pallas_call x1, Pallas kernels, pack_acts(): pl.pallas_call(pack_acts_kernel, out_shape=(PACKED, DONE), in_specs=[ANY]...  65.4 us
    ppermute x16, waiting for transfers between devices, across(): return lax.ppermute(array, AXES, PAIRINGS[pairing])  51.3 us
    ppermute x16, starting transfers between devices, across(): return lax.ppermute(array, AXES, PAIRINGS[pairing])  18.3 us
    ppermute x8, waiting for transfers between devices, z_swap(): lax.ppermute(array, AXES, moves(lambda xh, z, y, xl, c: (xh, z ^ mask, y,...  17.6 us
    ppermute x8, starting transfers between devices, z_swap(): lax.ppermute(array, AXES, moves(lambda xh, z, y, xl, c: (xh, z ^ mask, y,...  14.7 us
    ppermute x4, starting transfers between devices, core_swap(): lax.ppermute(array, AXES, moves(lambda xh, z, y, xl, c: (xh, z, y, xl, 1...  14 us
    pallas_call x1, Pallas kernels, gradient_term(): pl.pallas_call(term_kernel, out_shape=(half,) * (2 * PARTS), in_specs=[AN...  6.59 us
  transfers between devices with their start and end apart: 28, of which 20 were waited for; matrix products, arithmetic and copies ran while one was open for 1% of the time, Pallas kernels for 4%

profile of v4, /device:TPU:1, one launch (start us, length us, event | category | flops | bytes accessed | tf_op | source)
XLA Modules:
  0.0 203.9 jit_solution(14087376692215693907)
XLA Ops:
  0.7 65.4 %pack_acts.1 = (bf16[256,4096]{1,0:T(8,128)(2,1)}, f32[8,128]{1,0:T(8,128)}) custom-call(bf16[256,8192]{1,0:T(8,128)(2,1)} %acts.3), custom_call_target="tpu_custom_call" | custom-call | bytes 4194304 | tf_op jit(solution)/shard_map/pack_acts/pallas_call | solution.py:138
  66.1 3.3 %collective-permute-start.1 = (bf16[256,4096]{1,0:T(8,128)(2,1)}, bf16[256,4096]{1,0:T(8,128)(2,1)S(1)}, u32[]{:S(2)}, u32[]{:S(2)}) collective-permute-start(bf16[256,4096]{1,0:T(8,128)(2,1)} %get-tuple-element.31), channel_id=1, source_target_pairs={{0,1},{1,0},{2,3},{3,2},{4,5},{5,4},{6,7},{7,6},{8,9},{9,8},{10,11... | collective-permute-start | bytes 6291464 | tf_op jit(solution)/shard_map/ppermute | solution.py:68
  69.4 2.2 %copy-done = bf16[256,8192]{1,0:T(8,128)(2,1)S(1)} copy-done((bf16[256,8192]{1,0:T(8,128)(2,1)S(1)}, bf16[256,8192]{1,0:T(8,128)(2,1)}, u32[]{:S(2)}) %copy-start) | copy-done | bytes 4194328
  73.8 4.0 %collective-permute-done.2.got_grads = bf16[256,512]{1,0:T(8,128)(2,1)S(1)} collective-permute-done((bf16[256,512]{1,0:T(8,128)(2,1)S(1)}, bf16[256,512]{1,0:T(8,128)(2,1)S(1)}, u32[]{:S(2)}, u32[]{:S(2)}) %collective-permute-start.2) | collective-permute-done | bytes 262176 | tf_op jit(solution)/shard_map/ppermute | solution.py:68
  77.8 6.6 %gradient_term.1 = (bf16[8,128,512]{2,1,0:T(8,128)(2,1)S(1)}, bf16[8,128,512]{2,1,0:T(8,128)(2,1)S(1)}, bf16[8,128,512]{2,1,0:T(8,128)(2,1)S(1)}, bf16[8,128,512]{2,1,0:T(8,128)(2,1)S(1)}) custom-call(bf16[256,8192]{1,0:T(8,128)(2,1)S(1)} %copy-done.2, bf16[256,4096]{1,0:T(8,128)(2,1)S(1)} %collective-permute-done.1.got, bf16[256,512]{1,0:T(8,128)(2,1)S(1)} %copy-done.7, ...), custom_call_target="tpu_custom_call" | custom-call | flops 2147483648 | bytes 9437184 | tf_op jit(solution)/shard_map/gradient_term/pallas_call | solution.py:219
  85.5 14.2 %collective-permute-done.8.got = bf16[8,128,512]{2,1,0:T(8,128)(2,1)S(1)} collective-permute-done((bf16[8,128,512]{2,1,0:T(8,128)(2,1)S(1)}, bf16[8,128,512]{2,1,0:T(8,128)(2,1)S(1)}, u32[]{:S(2)}, u32[]{:S(2)}) %collective-permute-start.8) | collective-permute-done | bytes 1048608 | tf_op jit(solution)/shard_map/ppermute | solution.py:60
  101.1 5.7 %collective-permute-start = (f32[3,32,512]{2,1,0:T(8,128)S(1)}, f32[3,32,512]{2,1,0:T(8,128)S(1)}, u32[]{:S(2)}, u32[]{:S(2)}) collective-permute-start(f32[3,32,512]{2,1,0:T(8,128)S(1)} %get-tuple-element.30), channel_id=1, source_target_pairs={{0,112},{1,113},{2,114},{3,115},{4,116},{5,117},{6,118},{7,119},{8... | collective-permute-start | bytes 589832 | tf_op jit(solution)/shard_map/ppermute | solution.py:64
  106.8 9.1 %collective-permute-done.refs_0_ = f32[3,32,512]{2,1,0:T(8,128)S(1)} collective-permute-done((f32[3,32,512]{2,1,0:T(8,128)S(1)}, f32[3,32,512]{2,1,0:T(8,128)S(1)}, u32[]{:S(2)}, u32[]{:S(2)}) %collective-permute-start) | collective-permute-done | bytes 196640 | tf_op jit(solution)/shard_map/ppermute | solution.py:64
  116.3 2.9 %collective-permute-start.5 = (bf16[2,128,512]{2,1,0:T(8,128)(2,1)S(1)}, bf16[2,128,512]{2,1,0:T(8,128)(2,1)S(1)}, u32[]{:S(2)}, u32[]{:S(2)}) collective-permute-start(bf16[2,128,512]{2,1,0:T(8,128)(2,1)S(1)} %get-tuple-element.38), channel_id=1, source_target_pairs={{0,130},{1,13},{2,128},{3,15},{4,134},{5,9},{6,132},{7,11},{8,138}... | collective-permute-start | bytes 786440 | tf_op jit(solution)/shard_map/ppermute | solution.py:60
  119.1 2.5 %collective-permute-done.11.got = bf16[2,128,512]{2,1,0:T(8,128)(2,1)S(1)} collective-permute-done((bf16[2,128,512]{2,1,0:T(8,128)(2,1)S(1)}, bf16[2,128,512]{2,1,0:T(8,128)(2,1)S(1)}, u32[]{:S(2)}, u32[]{:S(2)}) %collective-permute-start.11) | collective-permute-done | bytes 262176 | tf_op jit(solution)/shard_map/ppermute | solution.py:60
  121.7 1.7 collective-permute-start.12
  124.3 1.7 collective-permute-done.12
  126.2 1.6 collective-permute-start.14
  129.0 1.2 collective-permute-done.13
  130.2 1.1 collective-permute-done.14
  132.4 2.5 %collective-permute-start.15 = (bf16[64,512]{1,0:T(8,128)(2,1)S(1)}, bf16[64,512]{1,0:T(8,128)(2,1)S(1)}, u32[]{:S(2)}, u32[]{:S(2)}) collective-permute-start(bf16[64,512]{1,0:T(8,128)(2,1)S(1)} %fusion.17), channel_id=1, source_target_pairs={{0,112},{1,113},{2,114},{3,115},{4,116},{5,117},{6,118},{7,119},{8... | collective-permute-start | bytes 196616 | tf_op jit(solution)/shard_map/ppermute | solution.py:64
  134.9 1.9 collective-permute-done.15
  137.1 3.0 %collective-permute-start.21 = (bf16[64,512]{1,0:T(8,128)(2,1)S(1)}, bf16[64,512]{1,0:T(8,128)(2,1)S(1)}, u32[]{:S(2)}, u32[]{:S(2)}) collective-permute-start(bf16[64,512]{1,0:T(8,128)(2,1)S(1)} %fusion.12), channel_id=1, source_target_pairs={{0,32},{1,33},{2,34},{3,35},{4,36},{5,37},{6,38},{7,39},{8,40},{9,... | collective-permute-start | bytes 196616 | tf_op jit(solution)/shard_map/ppermute | solution.py:64
  140.0 1.7 collective-permute-start.22
  142.0 3.1 %collective-permute-done.22 = bf16[64,512]{1,0:T(8,128)(2,1)S(1)} collective-permute-done((bf16[64,512]{1,0:T(8,128)(2,1)S(1)}, bf16[64,512]{1,0:T(8,128)(2,1)S(1)}, u32[]{:S(2)}, u32[]{:S(2)}) %collective-permute-start.22) | collective-permute-done | bytes 65568 | tf_op jit(solution)/shard_map/ppermute | solution.py:64
  145.1 1.4 collective-permute-start.23
  146.5 1.1 collective-permute-start.17
  147.6 1.4 collective-permute-done.23.got
  150.0 1.6 collective-permute-done.17.got
  151.6 2.1 %collective-permute-start.18 = (bf16[2,128,512]{2,1,0:T(8,128)(2,1)S(1)}, bf16[2,128,512]{2,1,0:T(8,128)(2,1)S(1)}, u32[]{:S(2)}, u32[]{:S(2)}) collective-permute-start(bf16[2,128,512]{2,1,0:T(8,128)(2,1)S(1)} %join.6.here), channel_id=1, source_target_pairs={{0,130},{1,13},{2,128},{3,15},{4,134},{5,9},{6,132},{7,11},{8,138}... | collective-permute-start | bytes 786440 | tf_op jit(solution)/shard_map/ppermute | solution.py:60
  155.4 4.4 %collective-permute-done.18.got = bf16[2,128,512]{2,1,0:T(8,128)(2,1)S(1)} collective-permute-done((bf16[2,128,512]{2,1,0:T(8,128)(2,1)S(1)}, bf16[2,128,512]{2,1,0:T(8,128)(2,1)S(1)}, u32[]{:S(2)}, u32[]{:S(2)}) %collective-permute-start.18) | collective-permute-done | bytes 262176 | tf_op jit(solution)/shard_map/ppermute | solution.py:60
  160.0 3.7 %collective-permute-done.25.got = bf16[4,128,512]{2,1,0:T(8,128)(2,1)S(1)} collective-permute-done((bf16[4,128,512]{2,1,0:T(8,128)(2,1)S(1)}, bf16[4,128,512]{2,1,0:T(8,128)(2,1)S(1)}, u32[]{:S(2)}, u32[]{:S(2)}) %collective-permute-start.25) | collective-permute-done | bytes 524320 | tf_op jit(solution)/shard_map/ppermute | solution.py:60
  163.8 3.8 %collective-permute-start.26 = (bf16[8,128,512]{2,1,0:T(8,128)(2,1)S(1)}, bf16[8,128,512]{2,1,0:T(8,128)(2,1)S(1)}, u32[]{:S(2)}, u32[]{:S(2)}) collective-permute-start(bf16[8,128,512]{2,1,0:T(8,128)(2,1)S(1)} %join.11.refs_2_), channel_id=1, source_target_pairs={{0,130},{1,13},{2,128},{3,15},{4,134},{5,9},{6,132},{7,11},{8,138}... | collective-permute-start | bytes 3145736 | tf_op jit(solution)/shard_map/ppermute | solution.py:60
  168.9 16.2 %collective-permute-done.26.refs_3_ = bf16[8,128,512]{2,1,0:T(8,128)(2,1)S(1)} collective-permute-done((bf16[8,128,512]{2,1,0:T(8,128)(2,1)S(1)}, bf16[8,128,512]{2,1,0:T(8,128)(2,1)S(1)}, u32[]{:S(2)}, u32[]{:S(2)}) %collective-permute-start.26) | collective-permute-done | bytes 1048608 | tf_op jit(solution)/shard_map/ppermute | solution.py:60
  185.0 3.0 %collective-permute-done.20.refs_1_ = bf16[8,128,512]{2,1,0:T(8,128)(2,1)S(1)} collective-permute-done((bf16[8,128,512]{2,1,0:T(8,128)(2,1)S(1)}, bf16[8,128,512]{2,1,0:T(8,128)(2,1)S(1)}, u32[]{:S(2)}, u32[]{:S(2)}) %collective-permute-start.20) | collective-permute-done | bytes 1048608 | tf_op jit(solution)/shard_map/ppermute | solution.py:60
  188.1 3.6 %project.1 = (bf16[512,512]{1,0:T(8,128)(2,1)}, f32[256,512]{1,0:T(8,128)S(1)}, bf16[256,512]{1,0:T(8,128)(2,1)S(1)}) custom-call(bf16[256,8192]{1,0:T(8,128)(2,1)S(1)} %copy-done.1, bf16[256,4096]{1,0:T(8,128)(2,1)S(1)} %collective-permute-done.9.refs_0_.got, bf16[8,128,512]{2,1,0:T(8,128)(2,1)S(1)} %join.8.refs_0_, ...), custom_call_target="tpu_custom_call" | custom-call | flops 2147483648 | bytes 9437184 | tf_op jit(solution)/shard_map/project/pallas_call | solution.py:355
  191.7 10.1 %collective-permute-start.27 = (bf16[256,512]{1,0:T(8,128)(2,1)S(1)}, bf16[256,512]{1,0:T(8,128)(2,1)S(1)}, u32[]{:S(2)}, u32[]{:S(2)}) collective-permute-start(bf16[256,512]{1,0:T(8,128)(2,1)S(1)} %get-tuple-element.52), channel_id=1, source_target_pairs={{0,1},{1,0},{2,3},{3,2},{4,5},{5,4},{6,7},{7,6},{8,9},{9,8},{10,11... | collective-permute-start | bytes 786440 | tf_op jit(solution)/shard_map/ppermute | solution.py:68
  (70 shorter events, 15.2 us)
Async XLA Ops:
  0.6 68.8 %copy-start.5 = (f32[32,512]{1,0:T(8,128)S(1)}, f32[32,512]{1,0:T(8,128)}, u32[]{:S(2)}) copy-start(f32[32,512]{1,0:T(8,128)} %second.1) | copy-start | bytes 196612
  0.6 68.8 %copy-start.3 = (f32[32,512]{1,0:T(8,128)S(1)}, f32[32,512]{1,0:T(8,128)}, u32[]{:S(2)}) copy-start(f32[32,512]{1,0:T(8,128)} %master.1) | copy-start | bytes 196612
  0.7 68.8 %copy-start.4 = (f32[32,512]{1,0:T(8,128)S(1)}, f32[32,512]{1,0:T(8,128)}, u32[]{:S(2)}) copy-start(f32[32,512]{1,0:T(8,128)} %first.1) | copy-start | bytes 196612
  0.7 72.6 %copy-start.7 = (bf16[256,512]{1,0:T(8,128)(2,1)S(1)}, bf16[256,512]{1,0:T(8,128)(2,1)}, u32[]{:S(2)}) copy-start(bf16[256,512]{1,0:T(8,128)(2,1)} %grads.1) | copy-start | bytes 786436
  66.1 11.7 %collective-permute-start.1 = (bf16[256,4096]{1,0:T(8,128)(2,1)}, bf16[256,4096]{1,0:T(8,128)(2,1)S(1)}, u32[]{:S(2)}, u32[]{:S(2)}) collective-permute-start(bf16[256,4096]{1,0:T(8,128)(2,1)} %get-tuple-element.31), channel_id=1, source_target_pairs={{0,1},{1,0},{2,3},{3,2},{4,5},{5,4},{6,7},{7,6},{8,9},{9,8},{10,11... | collective-permute-start | bytes 6291464 | tf_op jit(solution)/shard_map/ppermute | solution.py:68
  73.2 12.3 %collective-permute-start.9 = (bf16[256,4096]{1,0:T(8,128)(2,1)S(1)}, bf16[256,4096]{1,0:T(8,128)(2,1)S(1)}, u32[]{:S(2)}, u32[]{:S(2)}) collective-permute-start(bf16[256,4096]{1,0:T(8,128)(2,1)S(1)} %get-tuple-element.43), channel_id=1, source_target_pairs={{0,1},{1,0},{2,3},{3,2},{4,5},{5,4},{6,7},{7,6},{8,9},{9,8},{10,11... | collective-permute-start | bytes 6291464 | tf_op jit(solution)/shard_map/ppermute | solution.py:68
  73.3 4.5 %collective-permute-start.2 = (bf16[256,512]{1,0:T(8,128)(2,1)S(1)}, bf16[256,512]{1,0:T(8,128)(2,1)S(1)}, u32[]{:S(2)}, u32[]{:S(2)}) collective-permute-start(bf16[256,512]{1,0:T(8,128)(2,1)S(1)} %copy-done.7), channel_id=1, source_target_pairs={{0,1},{1,0},{2,3},{3,2},{4,5},{5,4},{6,7},{7,6},{8,9},{9,8},{10,11... | collective-permute-start | bytes 786440 | tf_op jit(solution)/shard_map/ppermute | solution.py:68
  84.4 15.2 %collective-permute-start.8 = (bf16[8,128,512]{2,1,0:T(8,128)(2,1)S(1)}, bf16[8,128,512]{2,1,0:T(8,128)(2,1)S(1)}, u32[]{:S(2)}, u32[]{:S(2)}) collective-permute-start(bf16[8,128,512]{2,1,0:T(8,128)(2,1)S(1)} %get-tuple-element.42), channel_id=1, source_target_pairs={{0,130},{1,13},{2,128},{3,15},{4,134},{5,9},{6,132},{7,11},{8,138}... | collective-permute-start | bytes 3145736 | tf_op jit(solution)/shard_map/ppermute | solution.py:60
  85.5 15.3 %collective-permute-start.3 = (bf16[8,128,512]{2,1,0:T(8,128)(2,1)S(1)}, bf16[8,128,512]{2,1,0:T(8,128)(2,1)S(1)}, u32[]{:S(2)}, u32[]{:S(2)}) collective-permute-start(bf16[8,128,512]{2,1,0:T(8,128)(2,1)S(1)} %get-tuple-element.34), channel_id=1, source_target_pairs={{0,2},{1,5},{2,0},{3,7},{4,6},{5,1},{6,4},{7,3},{8,10},{9,13},{10,... | collective-permute-start | bytes 3145736 | tf_op jit(solution)/shard_map/ppermute | solution.py:60
  99.9 16.0 %collective-permute-start.10 = (bf16[4,128,512]{2,1,0:T(8,128)(2,1)S(1)}, bf16[4,128,512]{2,1,0:T(8,128)(2,1)S(1)}, u32[]{:S(2)}, u32[]{:S(2)}) collective-permute-start(bf16[4,128,512]{2,1,0:T(8,128)(2,1)S(1)} %get-tuple-element.45), channel_id=1, source_target_pairs={{0,12},{1,131},{2,14},{3,129},{4,8},{5,135},{6,10},{7,133},{8,4},{... | collective-permute-start | bytes 1572872 | tf_op jit(solution)/shard_map/ppermute | solution.py:60
  101.0 15.1 %collective-permute-start.4 = (bf16[4,128,512]{2,1,0:T(8,128)(2,1)S(1)}, bf16[4,128,512]{2,1,0:T(8,128)(2,1)S(1)}, u32[]{:S(2)}, u32[]{:S(2)}) collective-permute-start(bf16[4,128,512]{2,1,0:T(8,128)(2,1)S(1)} %get-tuple-element.36), channel_id=1, source_target_pairs={{0,4},{1,3},{2,6},{3,1},{4,0},{5,7},{6,2},{7,5},{8,12},{9,11},{10,... | collective-permute-start | bytes 1572872 | tf_op jit(solution)/shard_map/ppermute | solution.py:60
  101.1 14.7 %collective-permute-start = (f32[3,32,512]{2,1,0:T(8,128)S(1)}, f32[3,32,512]{2,1,0:T(8,128)S(1)}, u32[]{:S(2)}, u32[]{:S(2)}) collective-permute-start(f32[3,32,512]{2,1,0:T(8,128)S(1)} %get-tuple-element.30), channel_id=1, source_target_pairs={{0,112},{1,113},{2,114},{3,115},{4,116},{5,117},{6,118},{7,119},{8... | collective-permute-start | bytes 589832 | tf_op jit(solution)/shard_map/ppermute | solution.py:64
  116.0 5.6 %collective-permute-start.11 = (bf16[2,128,512]{2,1,0:T(8,128)(2,1)S(1)}, bf16[2,128,512]{2,1,0:T(8,128)(2,1)S(1)}, u32[]{:S(2)}, u32[]{:S(2)}) collective-permute-start(bf16[2,128,512]{2,1,0:T(8,128)(2,1)S(1)} %get-tuple-element.47), channel_id=1, source_target_pairs={{0,2},{1,5},{2,0},{3,7},{4,6},{5,1},{6,4},{7,3},{8,10},{9,13},{10,... | collective-permute-start | bytes 786440 | tf_op jit(solution)/shard_map/ppermute | solution.py:60
  116.3 7.2 %collective-permute-start.5 = (bf16[2,128,512]{2,1,0:T(8,128)(2,1)S(1)}, bf16[2,128,512]{2,1,0:T(8,128)(2,1)S(1)}, u32[]{:S(2)}, u32[]{:S(2)}) collective-permute-start(bf16[2,128,512]{2,1,0:T(8,128)(2,1)S(1)} %get-tuple-element.38), channel_id=1, source_target_pairs={{0,130},{1,13},{2,128},{3,15},{4,134},{5,9},{6,132},{7,11},{8,138}... | collective-permute-start | bytes 786440 | tf_op jit(solution)/shard_map/ppermute | solution.py:60
  121.7 4.4 %collective-permute-start.12 = (bf16[1,128,512]{2,1,0:T(8,128)(2,1)S(1)}, bf16[1,128,512]{2,1,0:T(8,128)(2,1)S(1)}, u32[]{:S(2)}, u32[]{:S(2)}) collective-permute-start(bf16[1,128,512]{2,1,0:T(8,128)(2,1)S(1)} %get-tuple-element.49), channel_id=1, source_target_pairs={{0,4},{1,3},{2,6},{3,1},{4,0},{5,7},{6,2},{7,5},{8,12},{9,11},{10,... | collective-permute-start | bytes 393224 | tf_op jit(solution)/shard_map/ppermute | solution.py:60
  123.5 5.3 %collective-permute-start.6 = (bf16[1,128,512]{2,1,0:T(8,128)(2,1)S(1)}, bf16[1,128,512]{2,1,0:T(8,128)(2,1)S(1)}, u32[]{:S(2)}, u32[]{:S(2)}) collective-permute-start(bf16[1,128,512]{2,1,0:T(8,128)(2,1)S(1)} %get-tuple-element.40), channel_id=1, source_target_pairs={{0,12},{1,131},{2,14},{3,129},{4,8},{5,135},{6,10},{7,133},{8,4},{... | collective-permute-start | bytes 393224 | tf_op jit(solution)/shard_map/ppermute | solution.py:60
  126.1 4.1 %collective-permute-start.13 = (bf16[64,512]{1,0:T(8,128)(2,1)S(1)}, bf16[64,512]{1,0:T(8,128)(2,1)S(1)}, u32[]{:S(2)}, u32[]{:S(2)}) collective-permute-start(bf16[64,512]{1,0:T(8,128)(2,1)S(1)} %get-tuple-element.61), channel_id=1, source_target_pairs={{0,32},{1,33},{2,34},{3,35},{4,36},{5,37},{6,38},{7,39},{8,40},{9,... | collective-permute-start | bytes 196616 | tf_op jit(solution)/shard_map/ppermute | solution.py:64
  126.2 5.1 %collective-permute-start.14 = (bf16[64,512]{1,0:T(8,128)(2,1)S(1)}, bf16[64,512]{1,0:T(8,128)(2,1)S(1)}, u32[]{:S(2)}, u32[]{:S(2)}) collective-permute-start(bf16[64,512]{1,0:T(8,128)(2,1)S(1)} %get-tuple-element.62), channel_id=1, source_target_pairs={{0,48},{1,49},{2,50},{3,51},{4,52},{5,53},{6,54},{7,55},{8,56},{9,... | collective-permute-start | bytes 196616 | tf_op jit(solution)/shard_map/ppermute | solution.py:64
  128.8 3.5 %collective-permute-start.7 = (bf16[64,512]{1,0:T(8,128)(2,1)S(1)}, bf16[64,512]{1,0:T(8,128)(2,1)S(1)}, u32[]{:S(2)}, u32[]{:S(2)}) collective-permute-start(bf16[64,512]{1,0:T(8,128)(2,1)S(1)} %slice_bitcast_fusion.2), channel_id=1, source_target_pairs={{0,16},{1,17},{2,18},{3,19},{4,20},{5,21},{6,22},{7,23},{8,24},{9,... | collective-permute-start | bytes 196616 | tf_op jit(solution)/shard_map/ppermute | solution.py:64
  132.4 4.4 %collective-permute-start.15 = (bf16[64,512]{1,0:T(8,128)(2,1)S(1)}, bf16[64,512]{1,0:T(8,128)(2,1)S(1)}, u32[]{:S(2)}, u32[]{:S(2)}) collective-permute-start(bf16[64,512]{1,0:T(8,128)(2,1)S(1)} %fusion.17), channel_id=1, source_target_pairs={{0,112},{1,113},{2,114},{3,115},{4,116},{5,117},{6,118},{7,119},{8... | collective-permute-start | bytes 196616 | tf_op jit(solution)/shard_map/ppermute | solution.py:64
  137.1 4.9 %collective-permute-start.21 = (bf16[64,512]{1,0:T(8,128)(2,1)S(1)}, bf16[64,512]{1,0:T(8,128)(2,1)S(1)}, u32[]{:S(2)}, u32[]{:S(2)}) collective-permute-start(bf16[64,512]{1,0:T(8,128)(2,1)S(1)} %fusion.12), channel_id=1, source_target_pairs={{0,32},{1,33},{2,34},{3,35},{4,36},{5,37},{6,38},{7,39},{8,40},{9,... | collective-permute-start | bytes 196616 | tf_op jit(solution)/shard_map/ppermute | solution.py:64
  140.0 5.0 %collective-permute-start.22 = (bf16[64,512]{1,0:T(8,128)(2,1)S(1)}, bf16[64,512]{1,0:T(8,128)(2,1)S(1)}, u32[]{:S(2)}, u32[]{:S(2)}) collective-permute-start(bf16[64,512]{1,0:T(8,128)(2,1)S(1)} %fusion.12), channel_id=1, source_target_pairs={{0,48},{1,49},{2,50},{3,51},{4,52},{5,53},{6,54},{7,55},{8,56},{9,... | collective-permute-start | bytes 196616 | tf_op jit(solution)/shard_map/ppermute | solution.py:64
  141.7 4.7 %collective-permute-start.16 = (bf16[64,512]{1,0:T(8,128)(2,1)S(1)}, bf16[64,512]{1,0:T(8,128)(2,1)S(1)}, u32[]{:S(2)}, u32[]{:S(2)}) collective-permute-start(bf16[64,512]{1,0:T(8,128)(2,1)S(1)} %fusion.12), channel_id=1, source_target_pairs={{0,16},{1,17},{2,18},{3,19},{4,20},{5,21},{6,22},{7,23},{8,24},{9,... | collective-permute-start | bytes 196616 | tf_op jit(solution)/shard_map/ppermute | solution.py:64
  145.1 3.9 %collective-permute-start.23 = (bf16[1,128,512]{2,1,0:T(8,128)(2,1)S(1)}, bf16[1,128,512]{2,1,0:T(8,128)(2,1)S(1)}, u32[]{:S(2)}, u32[]{:S(2)}) collective-permute-start(bf16[1,128,512]{2,1,0:T(8,128)(2,1)S(1)} %maximum_bitcast_fusion.1.here), channel_id=1, source_target_pairs={{0,4},{1,3},{2,6},{3,1},{4,0},{5,7},{6,2},{7,5},{8,12},{9,11},{10,... | collective-permute-start | bytes 393224 | tf_op jit(solution)/shard_map/ppermute | solution.py:60
  146.5 5.1 %collective-permute-start.17 = (bf16[1,128,512]{2,1,0:T(8,128)(2,1)S(1)}, bf16[1,128,512]{2,1,0:T(8,128)(2,1)S(1)}, u32[]{:S(2)}, u32[]{:S(2)}) collective-permute-start(bf16[1,128,512]{2,1,0:T(8,128)(2,1)S(1)} %maximum_bitcast_fusion.here), channel_id=1, source_target_pairs={{0,12},{1,131},{2,14},{3,129},{4,8},{5,135},{6,10},{7,133},{8,4},{... | collective-permute-start | bytes 393224 | tf_op jit(solution)/shard_map/ppermute | solution.py:60
  149.0 5.3 %collective-permute-start.24 = (bf16[2,128,512]{2,1,0:T(8,128)(2,1)S(1)}, bf16[2,128,512]{2,1,0:T(8,128)(2,1)S(1)}, u32[]{:S(2)}, u32[]{:S(2)}) collective-permute-start(bf16[2,128,512]{2,1,0:T(8,128)(2,1)S(1)} %join.9.here), channel_id=1, source_target_pairs={{0,2},{1,5},{2,0},{3,7},{4,6},{5,1},{6,4},{7,3},{8,10},{9,13},{10,... | collective-permute-start | bytes 786440 | tf_op jit(solution)/shard_map/ppermute | solution.py:60
  151.6 8.2 %collective-permute-start.18 = (bf16[2,128,512]{2,1,0:T(8,128)(2,1)S(1)}, bf16[2,128,512]{2,1,0:T(8,128)(2,1)S(1)}, u32[]{:S(2)}, u32[]{:S(2)}) collective-permute-start(bf16[2,128,512]{2,1,0:T(8,128)(2,1)S(1)} %join.6.here), channel_id=1, source_target_pairs={{0,130},{1,13},{2,128},{3,15},{4,134},{5,9},{6,132},{7,11},{8,138}... | collective-permute-start | bytes 786440 | tf_op jit(solution)/shard_map/ppermute | solution.py:60
  154.3 9.3 %collective-permute-start.25 = (bf16[4,128,512]{2,1,0:T(8,128)(2,1)S(1)}, bf16[4,128,512]{2,1,0:T(8,128)(2,1)S(1)}, u32[]{:S(2)}, u32[]{:S(2)}) collective-permute-start(bf16[4,128,512]{2,1,0:T(8,128)(2,1)S(1)} %join.10.here), channel_id=1, source_target_pairs={{0,12},{1,131},{2,14},{3,129},{4,8},{5,135},{6,10},{7,133},{8,4},{... | collective-permute-start | bytes 1572872 | tf_op jit(solution)/shard_map/ppermute | solution.py:60
  159.9 8.8 %collective-permute-start.19 = (bf16[4,128,512]{2,1,0:T(8,128)(2,1)S(1)}, bf16[4,128,512]{2,1,0:T(8,128)(2,1)S(1)}, u32[]{:S(2)}, u32[]{:S(2)}) collective-permute-start(bf16[4,128,512]{2,1,0:T(8,128)(2,1)S(1)} %join.7.here), channel_id=1, source_target_pairs={{0,4},{1,3},{2,6},{3,1},{4,0},{5,7},{6,2},{7,5},{8,12},{9,11},{10,... | collective-permute-start | bytes 1572872 | tf_op jit(solution)/shard_map/ppermute | solution.py:60
  163.8 21.3 %collective-permute-start.26 = (bf16[8,128,512]{2,1,0:T(8,128)(2,1)S(1)}, bf16[8,128,512]{2,1,0:T(8,128)(2,1)S(1)}, u32[]{:S(2)}, u32[]{:S(2)}) collective-permute-start(bf16[8,128,512]{2,1,0:T(8,128)(2,1)S(1)} %join.11.refs_2_), channel_id=1, source_target_pairs={{0,130},{1,13},{2,128},{3,15},{4,134},{5,9},{6,132},{7,11},{8,138}... | collective-permute-start | bytes 3145736 | tf_op jit(solution)/shard_map/ppermute | solution.py:60
  168.7 19.4 %collective-permute-start.20 = (bf16[8,128,512]{2,1,0:T(8,128)(2,1)S(1)}, bf16[8,128,512]{2,1,0:T(8,128)(2,1)S(1)}, u32[]{:S(2)}, u32[]{:S(2)}) collective-permute-start(bf16[8,128,512]{2,1,0:T(8,128)(2,1)S(1)} %join.8.refs_0_), channel_id=1, source_target_pairs={{0,2},{1,5},{2,0},{3,7},{4,6},{5,1},{6,4},{7,3},{8,10},{9,13},{10,... | collective-permute-start | bytes 3145736 | tf_op jit(solution)/shard_map/ppermute | solution.py:60
  191.7 11.4 %collective-permute-start.27 = (bf16[256,512]{1,0:T(8,128)(2,1)S(1)}, bf16[256,512]{1,0:T(8,128)(2,1)S(1)}, u32[]{:S(2)}, u32[]{:S(2)}) collective-permute-start(bf16[256,512]{1,0:T(8,128)(2,1)S(1)} %get-tuple-element.52), channel_id=1, source_target_pairs={{0,1},{1,0},{2,3},{3,2},{4,5},{5,4},{6,7},{7,6},{8,9},{9,8},{10,11... | collective-permute-start | bytes 786440 | tf_op jit(solution)/shard_map/ppermute | solution.py:68
  (4 other events, 36.6 us)

commit v5 on v4

--- a/solution.py
+++ b/solution.py
@@ -22,11 +22,10 @@
 HALF = 4096
 BLOCK = 256
 BLOCKS = 16
-PARTS = 2
-ROWS = 128
-PAIRS = 4
-
-ORDERS = ((0, 2, 1, 3), (1, 3, 0, 2))
+PARTS = 4
+ROWS = 64
+
+ORDERS = ((0, 2, 1, 3), (1, 3, 0, 2), (2, 0, 3, 1), (3, 1, 2, 0))
 
 
 def moves(change):
@@ -129,22 +128,25 @@
 DONE = jax.ShapeDtypeStruct((8, 128), jnp.float32)
 
 
-def pack_acts_kernel(acts, packed, done, sems):
+def pack_acts_kernel(acts, grads, packed, done, sems):
     done[...] = jnp.zeros_like(done)
-    run_all(theirs_of(acts, packed, sems))
-
-
-def pack_acts(acts):
+    run_all(
+        theirs_of(acts, packed, sems)
+        + [pltpu.make_async_copy(grads, packed.at[:, pl.ds(HALF, COLS)], sems.at[BLOCKS])]
+    )
+
+
+def pack_acts(acts, grads):
     return pl.pallas_call(
         pack_acts_kernel,
-        out_shape=(PACKED, DONE),
-        in_specs=[ANY],
-        out_specs=(ANY, VMEM),
-        scratch_shapes=[pltpu.SemaphoreType.DMA((BLOCKS,))],
+        out_shape=(jax.ShapeDtypeStruct((TOK, HALF + COLS), jnp.bfloat16), DONE),
+        in_specs=[ANY, ANY],
+        out_specs=(VMEM, VMEM),
+        scratch_shapes=[pltpu.SemaphoreType.DMA((BLOCKS + 1,))],
         compiler_params=WHOLE,
         cost_estimate=cost(0, 4 << 20),
         name="pack_acts",
-    )(acts)
+    )(acts, grads)
 
 
 def pack_rest_kernel(tokens, master, first, second, _after, packed, state, done, sems):
@@ -167,7 +169,7 @@
             DONE,
         ),
         in_specs=[ANY] * 4 + [VMEM],
-        out_specs=(ANY, ANY, VMEM),
+        out_specs=(VMEM, VMEM, VMEM),
         scratch_shapes=[pltpu.SemaphoreType.DMA((BLOCKS + 3,))],
         compiler_params=PARAMS,
         cost_estimate=cost(0, 5 << 20),
@@ -175,7 +177,7 @@
     )(tokens, master, first, second, after)
 
 
-def term_kernel(acts, got, grads, got_grads, _after, *refs):
+def term_kernel(acts, got, grads, _after, *refs):
     halves = refs[: 2 * PARTS]
     both, grads_both, term, sems = refs[2 * PARTS :]
     where = place()
@@ -193,9 +195,13 @@
     for r in range(BLOCKS):
         own[r].start()
         other[r].start()
+    got_grads = pltpu.make_async_copy(
+        got.at[:, pl.ds(HALF, COLS)], grads_both.at[TOK:], sems.at[2 * BLOCKS]
+    )
+    got_grads.start()
     grads_both[:TOK] = grads[...]
-    grads_both[TOK:] = got_grads[...]
-    starts = [pair_starts(where, m) for m in range(PAIRS)]
+    got_grads.wait()
+    starts = [pair_starts(where, m) for m in range(PARTS)]
     for r in range(BLOCKS):
         own[r].wait()
         other[r].wait()
@@ -205,32 +211,31 @@
             (((0,), (0,)), ((), ())),
             preferred_element_type=jnp.float32,
         ).astype(jnp.bfloat16)
-        for m in range(PAIRS):
-            side, slot = side_and_slot(m // 2, r)
+        for m in range(PARTS):
+            side, slot = side_and_slot(m, r)
             for j in range(2):
-                to = (m % 2) * 64 + j * 32
-                halves[2 * (m // 2) + side][slot, to : to + 32] = term[
+                halves[2 * m + side][slot, j * 32 : j * 32 + 32] = term[
                     r % 2, pl.ds(pl.multiple_of(starts[m][j], 32), 32)
                 ]
 
 
-def gradient_term(acts, got, grads, got_grads, after):
+def gradient_term(acts, got, grads, after):
     half = jax.ShapeDtypeStruct((8, ROWS, COLS), jnp.bfloat16)
     return pl.pallas_call(
         term_kernel,
         out_shape=(half,) * (2 * PARTS),
-        in_specs=[ANY, ANY, VMEM, VMEM, VMEM],
+        in_specs=[ANY, ANY, VMEM, VMEM],
         out_specs=(VMEM,) * (2 * PARTS),
         scratch_shapes=[
             pltpu.VMEM((2 * TOK, HALF), jnp.bfloat16),
             pltpu.VMEM((2 * TOK, COLS), jnp.bfloat16),
             pltpu.VMEM((2, BLOCK, COLS), jnp.bfloat16),
-            pltpu.SemaphoreType.DMA((2 * BLOCKS,)),
+            pltpu.SemaphoreType.DMA((2 * BLOCKS + 1,)),
         ],
         compiler_params=PARAMS,
         cost_estimate=cost(2 * 2 * TOK * HALF * COLS, 9 << 20),
         name="gradient_term",
-    )(acts, got, grads, got_grads, after)
+    )(acts, got, grads, after)
 
 
 def add_kernel(dim, keep, got, *refs):
@@ -308,19 +313,18 @@
         for k in range(per):
             token_copies[s * per + k].start()
         got_copies[s].start()
-    starts = [pair_starts(where, m) for m in range(PAIRS)]
+    starts = [pair_starts(where, m) for m in range(PARTS)]
 
     def keep_block(x_hi, block):
         kept[pl.ds(pl.multiple_of(x_hi * BLOCK, BLOCK), BLOCK)] = block
 
     for s in range(HALF // STRIPE):
         for k in range(per):
-            for m in range(PAIRS):
-                side, slot = side_and_slot(m // 2, s * per + k)
+            for m in range(PARTS):
+                side, slot = side_and_slot(m, s * per + k)
                 for j in range(2):
                     at = pl.ds(pl.multiple_of(k * BLOCK + starts[m][j], 32), 32)
-                    of = (m % 2) * 64 + j * 32
-                    weights[s % 2, at] = halves[2 * (m // 2) + side][slot, of : of + 32]
+                    weights[s % 2, at] = halves[2 * m + side][slot, j * 32 : j * 32 + 32]
             token_copies[s * per + k].wait()
         got_copies[s].wait()
         if s == 0:
@@ -397,33 +401,30 @@
     return add(keep, across(lax.index_in_dim(array, 1, dim, keepdims=False), pairing))
 
 
-def reduce_parts(halves, tokens, state):
+def reduce_parts(halves, after):
     parts = []
-    for i, (v, w, p, q) in enumerate(ORDERS):
-        keep, got = halves[2 * i], across(halves[2 * i + 1], v)
-        keep, send = add_halves(keep, got, w - (v < w), (tokens,) if i else ())
-        got = across(send, w)
-        keep, send = add_halves(keep, got, sorted((p, q)).index(p), (state,) if i else ())
-        got = across(send, p)
-        keep, send = add_halves(keep, got, 0)
-        parts.append((wide(keep) + wide(across(send, q))).astype(jnp.bfloat16).reshape(ROWS, COLS))
+    for m, (v, w, p, q) in enumerate(ORDERS):
+        keep, got = halves[2 * m], across(halves[2 * m + 1], v)
+        keep, send = add_halves(keep, got, w - (v < w), () if m else after)
+        keep, send = add_halves(keep, across(send, w), sorted((p, q)).index(p))
+        keep, send = add_halves(keep, across(send, p), 0)
+        total = wide(keep[0]) + wide(across(send[0], q))
+        parts.append(total.astype(jnp.bfloat16) if m else total)
     return parts
 
 
 def reduce_z(parts):
-    total = wide(parts[0][:64])
-    for m in range(1, PAIRS):
-        rows = parts[m // 2][(m % 2) * 64 : (m % 2) * 64 + 64]
-        total = total + wide(z_swap(rows, m))
+    total = parts[0]
+    for m in range(1, PARTS):
+        total = total + wide(z_swap(parts[m], m))
     total = total.astype(jnp.bfloat16)
     return (wide(total) + wide(z_swap(total, 7))).reshape(2, 32, COLS)
 
 
-def gather_parts(pair):
-    pairs = [pair] + [z_swap(pair, m) for m in range(1, PAIRS)]
+def gather_parts(rows):
     halves = []
-    for i, (v, w, p, q) in enumerate(ORDERS):
-        part = jnp.concatenate(pairs[2 * i : 2 * i + 2], axis=0)[None]
+    for m, (v, w, p, q) in enumerate(ORDERS):
+        part = (z_swap(rows, m) if m else rows)[None]
         for bit, dim in ((q, 0), (p, sorted((p, q)).index(p)), (w, w - (v < w))):
             part = join(part, across(part, bit), dim)
         halves += [part, across(part, v)]
@@ -432,18 +433,15 @@
 
 def local(activations, output_grads, master_weights, first_moment, second_moment, next_tokens):
     low = lax.axis_index("outer") % 8 < 4
-    packed, packed_acts = pack_acts(activations)
+    packed, packed_acts = pack_acts(activations, output_grads)
     packed_tokens, state, packed_all = pack_rest(
         next_tokens, master_weights, first_moment, second_moment, packed_acts
     )
-    got_acts, got_grads = core_swap(packed), core_swap(output_grads)
-    halves = gradient_term(
-        activations, got_acts, output_grads, got_grads, packed_all
-    )
+    halves = gradient_term(activations, core_swap(packed), output_grads, packed_all)
     got_state = z_swap(state, 7)
     got_tokens = core_swap(packed_tokens)
 
-    gradient = reduce_z(reduce_parts(halves, got_tokens, got_state))
+    gradient = reduce_z(reduce_parts(halves, (got_tokens, got_state)))
     pairs = jnp.stack([jnp.where(low, state, got_state), jnp.where(low, got_state, state)], axis=1)
     updated = adamw_update(gradient, *pairs)
     new_master, new_first, new_second = (jnp.where(low, u[0], u[1]) for u in updated)

time: 204 us -> 129 us (0.63)
  Pallas kernels: 77.6 us -> 15.5 us
  waiting for transfers between devices: 73 us -> 37.6 us
  starting transfers between devices: 47.1 us -> 68.6 us
    pallas_call x1, Pallas kernels: 65.4 us -> 3.4 us  [pack_acts(): pl.pallas_call(pack_acts_kernel, out_shape=(jax.ShapeDtypeStruct((TOK, HA...]
    ppermute x16 -> x32, waiting for transfers between devices: 51.3 us -> 24.5 us  [across(): return lax.ppermute(array, AXES, PAIRINGS[pairing])]
    ppermute x16 -> x32, starting transfers between devices: 18.3 us -> 41.7 us  [across(): return lax.ppermute(array, AXES, PAIRINGS[pairing])]
    ppermute x8, waiting for transfers between devices: 17.6 us -> 12.6 us  [z_swap(): lax.ppermute(array, AXES, moves(lambda xh, z, y, xl, c: (xh, z ^ mask, y,...]
    ppermute x4 -> x3, waiting for transfers between devices: 4.03 us -> 0.49 us  [core_swap(): lax.ppermute(array, AXES, moves(lambda xh, z, y, xl, c: (xh, z, y, xl, 1...]
    ppermute x8, starting transfers between devices: 14.7 us -> 12.1 us  [z_swap(): lax.ppermute(array, AXES, moves(lambda xh, z, y, xl, c: (xh, z ^ mask, y,...]
    ppermute x4 -> x3, starting transfers between devices: 14 us -> 14.9 us  [core_swap(): lax.ppermute(array, AXES, moves(lambda xh, z, y, xl, c: (xh, z, y, xl, 1...]
  transfers between devices with their start and end apart: 28 -> 43, of which waited for: 20 -> 19; matrix products, arithmetic and copies ran while one was open for 1% -> 1% of each run, Pallas kernels for 4% -> 7%
where the time goes in v5:
time: 129 us
  starting transfers between devices  68.6 us (53%)
  waiting for transfers between devices  37.6 us (29%)
  Pallas kernels  15.5 us (12%)
  local copies, waits for them, and re-layouts  3.59 us (3%)
  other arithmetic  2.46 us (2%)
    ppermute x32, starting transfers between devices, across(): return lax.ppermute(array, AXES, PAIRINGS[pairing])  41.7 us
    ppermute x32, waiting for transfers between devices, across(): return lax.ppermute(array, AXES, PAIRINGS[pairing])  24.5 us
    ppermute x3, starting transfers between devices, core_swap(): lax.ppermute(array, AXES, moves(lambda xh, z, y, xl, c: (xh, z, y, xl, 1...  14.9 us
    ppermute x8, waiting for transfers between devices, z_swap(): lax.ppermute(array, AXES, moves(lambda xh, z, y, xl, c: (xh, z ^ mask, y,...  12.6 us
    ppermute x8, starting transfers between devices, z_swap(): lax.ppermute(array, AXES, moves(lambda xh, z, y, xl, c: (xh, z ^ mask, y,...  12.1 us
    pallas_call x1, Pallas kernels, gradient_term(): pl.pallas_call(term_kernel, out_shape=(half,) * (2 * PARTS), in_specs=[AN...  6.51 us
    pallas_call x1, Pallas kernels, project(): pl.pallas_call(project_kernel, out_shape=(jax.ShapeDtypeStruct((2 * BLOCK...  3.61 us
    unnamed x16, local copies, waits for them, and re-layouts  3.59 us
  transfers between devices with their start and end apart: 43, of which 19 were waited for; matrix products, arithmetic and copies ran while one was open for 1% of the time, Pallas kernels for 7%

profile of v5, /device:TPU:1, one launch (start us, length us, event | category | flops | bytes accessed | tf_op | source)
XLA Modules:
  0.0 128.8 jit_solution(1329157822610617159)
XLA Ops:
  0.7 3.4 %pack_acts.1 = (bf16[256,4608]{1,0:T(8,128)(2,1)}, f32[8,128]{1,0:T(8,128)}) custom-call(bf16[256,8192]{1,0:T(8,128)(2,1)} %acts.3, bf16[256,512]{1,0:T(8,128)(2,1)} %grads.3), custom_call_target="tpu_custom_call" | custom-call | bytes 4194304 | tf_op jit(solution)/shard_map/pack_acts/pallas_call | solution.py:140
  4.1 3.3 %collective-permute-start.1 = (bf16[256,4608]{1,0:T(8,128)(2,1)}, bf16[256,4608]{1,0:T(8,128)(2,1)S(1)}, u32[]{:S(2)}, u32[]{:S(2)}) collective-permute-start(bf16[256,4608]{1,0:T(8,128)(2,1)} %get-tuple-element.47), channel_id=1, source_target_pairs={{0,1},{1,0},{2,3},{3,2},{4,5},{5,4},{6,7},{7,6},{8,9},{9,8},{10,11... | collective-permute-start | bytes 7077896 | tf_op jit(solution)/shard_map/ppermute | solution.py:67
  7.4 2.2 %copy-done = bf16[256,8192]{1,0:T(8,128)(2,1)S(1)} copy-done((bf16[256,8192]{1,0:T(8,128)(2,1)S(1)}, bf16[256,8192]{1,0:T(8,128)(2,1)}, u32[]{:S(2)}) %copy-start) | copy-done | bytes 4194328
  12.5 6.5 %gradient_term.1 = (bf16[8,64,512]{2,1,0:T(8,128)(2,1)S(1)}, bf16[8,64,512]{2,1,0:T(8,128)(2,1)S(1)}, bf16[8,64,512]{2,1,0:T(8,128)(2,1)S(1)}, bf16[8,64,512]{2,...) custom-call(bf16[256,8192]{1,0:T(8,128)(2,1)S(1)} %copy-done.2, ...), custom_call_target="tpu_custom_call" | custom-call | flops 2147483648 | bytes 9437184 | tf_op jit(solution)/shard_map/gradient_term/pallas_call | solution.py:224
  21.3 1.9 %collective-permute-start.17 = (bf16[8,64,512]{2,1,0:T(8,128)(2,1)S(1)}, bf16[8,64,512]{2,1,0:T(8,128)(2,1)S(1)}, u32[]{:S(2)}, u32[]{:S(2)}) collective-permute-start(bf16[8,64,512]{2,1,0:T(8,128)(2,1)S(1)} %get-tuple-element.75), channel_id=1, source_target_pairs={{0,12},{1,131},{2,14},{3,129},{4,8},{5,135},{6,10},{7,133},{8,4},{... | collective-permute-start | bytes 1572872 | tf_op jit(solution)/shard_map/ppermute | solution.py:59
  23.2 7.9 %collective-permute-done.7.got = bf16[8,64,512]{2,1,0:T(8,128)(2,1)S(1)} collective-permute-done((bf16[8,64,512]{2,1,0:T(8,128)(2,1)S(1)}, bf16[8,64,512]{2,1,0:T(8,128)(2,1)S(1)}, u32[]{:S(2)}, u32[]{:S(2)}) %collective-permute-start.7) | collective-permute-done | bytes 524320 | tf_op jit(solution)/shard_map/ppermute | solution.py:59
  31.1 2.3 %collective-permute-start = (f32[3,32,512]{2,1,0:T(8,128)S(1)}, f32[3,32,512]{2,1,0:T(8,128)S(1)}, u32[]{:S(2)}, u32[]{:S(2)}) collective-permute-start(f32[3,32,512]{2,1,0:T(8,128)S(1)} %get-tuple-element.46), channel_id=1, source_target_pairs={{0,112},{1,113},{2,114},{3,115},{4,116},{5,117},{6,118},{7,119},{8... | collective-permute-start | bytes 589832 | tf_op jit(solution)/shard_map/ppermute | solution.py:63
  33.5 4.9 %collective-permute-start.8 = (bf16[4,64,512]{2,1,0:T(8,128)(2,1)S(1)}, bf16[4,64,512]{2,1,0:T(8,128)(2,1)S(1)}, u32[]{:S(2)}, u32[]{:S(2)}) collective-permute-start(bf16[4,64,512]{2,1,0:T(8,128)(2,1)S(1)} %get-tuple-element.61), channel_id=1, source_target_pairs={{0,12},{1,131},{2,14},{3,129},{4,8},{5,135},{6,10},{7,133},{8,4},{... | collective-permute-start | bytes 786440 | tf_op jit(solution)/shard_map/ppermute | solution.py:59
  39.4 3.7 %collective-permute-done.refs_1_ = f32[3,32,512]{2,1,0:T(8,128)S(1)} collective-permute-done((f32[3,32,512]{2,1,0:T(8,128)S(1)}, f32[3,32,512]{2,1,0:T(8,128)S(1)}, u32[]{:S(2)}, u32[]{:S(2)}) %collective-permute-start) | collective-permute-done | bytes 196640 | tf_op jit(solution)/shard_map/ppermute | solution.py:63
  43.2 5.3 %collective-permute-start.4 = (bf16[4,64,512]{2,1,0:T(8,128)(2,1)S(1)}, bf16[4,64,512]{2,1,0:T(8,128)(2,1)S(1)}, u32[]{:S(2)}, u32[]{:S(2)}) collective-permute-start(bf16[4,64,512]{2,1,0:T(8,128)(2,1)S(1)} %get-tuple-element.53), channel_id=1, source_target_pairs={{0,4},{1,3},{2,6},{3,1},{4,0},{5,7},{6,2},{7,5},{8,12},{9,11},{10,... | collective-permute-start | bytes 786440 | tf_op jit(solution)/shard_map/ppermute | solution.py:59
  48.8 3.2 %collective-permute-start.14 = (bf16[2,64,512]{2,1,0:T(8,128)(2,1)S(1)}, bf16[2,64,512]{2,1,0:T(8,128)(2,1)S(1)}, u32[]{:S(2)}, u32[]{:S(2)}) collective-permute-start(bf16[2,64,512]{2,1,0:T(8,128)(2,1)S(1)} %get-tuple-element.71), channel_id=1, source_target_pairs={{0,12},{1,131},{2,14},{3,129},{4,8},{5,135},{6,10},{7,133},{8,4},{... | collective-permute-start | bytes 393224 | tf_op jit(solution)/shard_map/ppermute | solution.py:59
  53.0 2.1 %collective-permute-start.5 = (bf16[2,64,512]{2,1,0:T(8,128)(2,1)S(1)}, bf16[2,64,512]{2,1,0:T(8,128)(2,1)S(1)}, u32[]{:S(2)}, u32[]{:S(2)}) collective-permute-start(bf16[2,64,512]{2,1,0:T(8,128)(2,1)S(1)} %get-tuple-element.55), channel_id=1, source_target_pairs={{0,130},{1,13},{2,128},{3,15},{4,134},{5,9},{6,132},{7,11},{8,138}... | collective-permute-start | bytes 393224 | tf_op jit(solution)/shard_map/ppermute | solution.py:59
  55.4 2.7 %collective-permute-start.15 = (bf16[64,512]{1,0:T(8,128)(2,1)S(1)}, bf16[64,512]{1,0:T(8,128)(2,1)S(1)}, u32[]{:S(2)}, u32[]{:S(2)}) collective-permute-start(bf16[64,512]{1,0:T(8,128)(2,1)S(1)} %bitcast.85), channel_id=1, source_target_pairs={{0,130},{1,13},{2,128},{3,15},{4,134},{5,9},{6,132},{7,11},{8,138}... | collective-permute-start | bytes 196616 | tf_op jit(solution)/shard_map/ppermute | solution.py:59
  58.4 4.2 %collective-permute-start.6 = (bf16[64,512]{1,0:T(8,128)(2,1)S(1)}, bf16[64,512]{1,0:T(8,128)(2,1)S(1)}, u32[]{:S(2)}, u32[]{:S(2)}) collective-permute-start(bf16[64,512]{1,0:T(8,128)(2,1)S(1)} %bitcast.83), channel_id=1, source_target_pairs={{0,12},{1,131},{2,14},{3,129},{4,8},{5,135},{6,10},{7,133},{8,4},{... | collective-permute-start | bytes 196616 | tf_op jit(solution)/shard_map/ppermute | solution.py:59
  62.7 1.9 %collective-permute-start.16 = (bf16[64,512]{1,0:T(8,128)(2,1)S(1)}, bf16[64,512]{1,0:T(8,128)(2,1)S(1)}, u32[]{:S(2)}, u32[]{:S(2)}) collective-permute-start(bf16[64,512]{1,0:T(8,128)(2,1)S(1)} %fusion.16), channel_id=1, source_target_pairs={{0,32},{1,33},{2,34},{3,35},{4,36},{5,37},{6,38},{7,39},{8,40},{9,... | collective-permute-start | bytes 196616 | tf_op jit(solution)/shard_map/ppermute | solution.py:63
  64.7 1.8 %collective-permute-start.21 = (bf16[64,512]{1,0:T(8,128)(2,1)S(1)}, bf16[64,512]{1,0:T(8,128)(2,1)S(1)}, u32[]{:S(2)}, u32[]{:S(2)}) collective-permute-start(bf16[64,512]{1,0:T(8,128)(2,1)S(1)} %fusion.15), channel_id=1, source_target_pairs={{0,48},{1,49},{2,50},{3,51},{4,52},{5,53},{6,54},{7,55},{8,56},{9,... | collective-permute-start | bytes 196616 | tf_op jit(solution)/shard_map/ppermute | solution.py:63
  67.1 3.1 %collective-permute-done.21 = bf16[64,512]{1,0:T(8,128)(2,1)S(1)} collective-permute-done((bf16[64,512]{1,0:T(8,128)(2,1)S(1)}, bf16[64,512]{1,0:T(8,128)(2,1)S(1)}, u32[]{:S(2)}, u32[]{:S(2)}) %collective-permute-start.21) | collective-permute-done | bytes 65568 | tf_op jit(solution)/shard_map/ppermute | solution.py:63
  70.3 2.4 %collective-permute-start.22 = (bf16[64,512]{1,0:T(8,128)(2,1)S(1)}, bf16[64,512]{1,0:T(8,128)(2,1)S(1)}, u32[]{:S(2)}, u32[]{:S(2)}) collective-permute-start(bf16[64,512]{1,0:T(8,128)(2,1)S(1)} %fusion.21), channel_id=1, source_target_pairs={{0,112},{1,113},{2,114},{3,115},{4,116},{5,117},{6,118},{7,119},{8... | collective-permute-start | bytes 196616 | tf_op jit(solution)/shard_map/ppermute | solution.py:63
  72.7 2.0 %collective-permute-done.22 = bf16[64,512]{1,0:T(8,128)(2,1)S(1)} collective-permute-done((bf16[64,512]{1,0:T(8,128)(2,1)S(1)}, bf16[64,512]{1,0:T(8,128)(2,1)S(1)}, u32[]{:S(2)}, u32[]{:S(2)}) %collective-permute-start.22) | collective-permute-done | bytes 65568 | tf_op jit(solution)/shard_map/ppermute | solution.py:63
  74.9 1.8 %collective-permute-start.37 = (bf16[64,512]{1,0:T(8,128)(2,1)S(1)}, bf16[64,512]{1,0:T(8,128)(2,1)S(1)}, u32[]{:S(2)}, u32[]{:S(2)}) collective-permute-start(bf16[64,512]{1,0:T(8,128)(2,1)S(1)} %fusion.12), channel_id=1, source_target_pairs={{0,48},{1,49},{2,50},{3,51},{4,52},{5,53},{6,54},{7,55},{8,56},{9,... | collective-permute-start | bytes 196616 | tf_op jit(solution)/shard_map/ppermute | solution.py:63
  76.7 1.9 %collective-permute-start.27 = (bf16[64,512]{1,0:T(8,128)(2,1)S(1)}, bf16[64,512]{1,0:T(8,128)(2,1)S(1)}, u32[]{:S(2)}, u32[]{:S(2)}) collective-permute-start(bf16[64,512]{1,0:T(8,128)(2,1)S(1)} %fusion.12), channel_id=1, source_target_pairs={{0,16},{1,17},{2,18},{3,19},{4,20},{5,21},{6,22},{7,23},{8,24},{9,... | collective-permute-start | bytes 196616 | tf_op jit(solution)/shard_map/ppermute | solution.py:63
  78.6 2.2 %collective-permute-done.37 = bf16[64,512]{1,0:T(8,128)(2,1)S(1)} collective-permute-done((bf16[64,512]{1,0:T(8,128)(2,1)S(1)}, bf16[64,512]{1,0:T(8,128)(2,1)S(1)}, u32[]{:S(2)}, u32[]{:S(2)}) %collective-permute-start.37) | collective-permute-done | bytes 65568 | tf_op jit(solution)/shard_map/ppermute | solution.py:63
  82.9 1.6 %collective-permute-start.24 = (bf16[2,64,512]{2,1,0:T(8,128)(2,1)S(1)}, bf16[2,64,512]{2,1,0:T(8,128)(2,1)S(1)}, u32[]{:S(2)}, u32[]{:S(2)}) collective-permute-start(bf16[2,64,512]{2,1,0:T(8,128)(2,1)S(1)} %join.12.here), channel_id=1, source_target_pairs={{0,130},{1,13},{2,128},{3,15},{4,134},{5,9},{6,132},{7,11},{8,138}... | collective-permute-start | bytes 393224 | tf_op jit(solution)/shard_map/ppermute | solution.py:59
  84.5 1.5 %collective-permute-start.39 = (bf16[2,64,512]{2,1,0:T(8,128)(2,1)S(1)}, bf16[2,64,512]{2,1,0:T(8,128)(2,1)S(1)}, u32[]{:S(2)}, u32[]{:S(2)}) collective-permute-start(bf16[2,64,512]{2,1,0:T(8,128)(2,1)S(1)} %join.21.here), channel_id=1, source_target_pairs={{0,4},{1,3},{2,6},{3,1},{4,0},{5,7},{6,2},{7,5},{8,12},{9,11},{10,... | collective-permute-start | bytes 393224 | tf_op jit(solution)/shard_map/ppermute | solution.py:59
  88.8 2.6 %collective-permute-start.40 = (bf16[4,64,512]{2,1,0:T(8,128)(2,1)S(1)}, bf16[4,64,512]{2,1,0:T(8,128)(2,1)S(1)}, u32[]{:S(2)}, u32[]{:S(2)}) collective-permute-start(bf16[4,64,512]{2,1,0:T(8,128)(2,1)S(1)} %join.22.here), channel_id=1, source_target_pairs={{0,130},{1,13},{2,128},{3,15},{4,134},{5,9},{6,132},{7,11},{8,138}... | collective-permute-start | bytes 786440 | tf_op jit(solution)/shard_map/ppermute | solution.py:59
  91.6 1.7 %collective-permute-start.30 = (bf16[4,64,512]{2,1,0:T(8,128)(2,1)S(1)}, bf16[4,64,512]{2,1,0:T(8,128)(2,1)S(1)}, u32[]{:S(2)}, u32[]{:S(2)}) collective-permute-start(bf16[4,64,512]{2,1,0:T(8,128)(2,1)S(1)} %join.16.here), channel_id=1, source_target_pairs={{0,12},{1,131},{2,14},{3,129},{4,8},{5,135},{6,10},{7,133},{8,4},{... | collective-permute-start | bytes 786440 | tf_op jit(solution)/shard_map/ppermute | solution.py:59
  95.4 1.9 %collective-permute-start.41 = (bf16[8,64,512]{2,1,0:T(8,128)(2,1)S(1)}, bf16[8,64,512]{2,1,0:T(8,128)(2,1)S(1)}, u32[]{:S(2)}, u32[]{:S(2)}) collective-permute-start(bf16[8,64,512]{2,1,0:T(8,128)(2,1)S(1)} %join.23.refs_6_), channel_id=1, source_target_pairs={{0,12},{1,131},{2,14},{3,129},{4,8},{5,135},{6,10},{7,133},{8,4},{... | collective-permute-start | bytes 1572872 | tf_op jit(solution)/shard_map/ppermute | solution.py:59
  100.3 5.1 %collective-permute-done.26.refs_1_ = bf16[8,64,512]{2,1,0:T(8,128)(2,1)S(1)} collective-permute-done((bf16[8,64,512]{2,1,0:T(8,128)(2,1)S(1)}, bf16[8,64,512]{2,1,0:T(8,128)(2,1)S(1)}, u32[]{:S(2)}, u32[]{:S(2)}) %collective-permute-start.26) | collective-permute-done | bytes 524320 | tf_op jit(solution)/shard_map/ppermute | solution.py:59
  106.0 1.8 %collective-permute-done.36.refs_5_ = bf16[8,64,512]{2,1,0:T(8,128)(2,1)S(1)} collective-permute-done((bf16[8,64,512]{2,1,0:T(8,128)(2,1)S(1)}, bf16[8,64,512]{2,1,0:T(8,128)(2,1)S(1)}, u32[]{:S(2)}, u32[]{:S(2)}) %collective-permute-start.36) | collective-permute-done | bytes 524320 | tf_op jit(solution)/shard_map/ppermute | solution.py:59
  107.8 3.8 %collective-permute-done.31.refs_3_ = bf16[8,64,512]{2,1,0:T(8,128)(2,1)S(1)} collective-permute-done((bf16[8,64,512]{2,1,0:T(8,128)(2,1)S(1)}, bf16[8,64,512]{2,1,0:T(8,128)(2,1)S(1)}, u32[]{:S(2)}, u32[]{:S(2)}) %collective-permute-start.31) | collective-permute-done | bytes 524320 | tf_op jit(solution)/shard_map/ppermute | solution.py:59
  111.6 3.6 %project.1 = (bf16[512,512]{1,0:T(8,128)(2,1)}, f32[256,512]{1,0:T(8,128)S(1)}, bf16[256,512]{1,0:T(8,128)(2,1)S(1)}) custom-call(bf16[256,8192]{1,0:T(8,128)(2,1)S(1)} %copy-done.1, bf16[256,4096]{1,0:T(8,128)(2,1)S(1)} %collective-permute-done.3.refs_0_.got, bf16[8,64,512]{2,1,0:T(8,128)(2,1)S(1)} %join.14.refs_0_, ...), custom_call_target="tpu_custom_call" | custom-call | flops 2147483648 | bytes 9437184 | tf_op jit(solution)/shard_map/project/pallas_call | solution.py:359
  115.2 11.5 %collective-permute-start.42 = (bf16[256,512]{1,0:T(8,128)(2,1)S(1)}, bf16[256,512]{1,0:T(8,128)(2,1)S(1)}, u32[]{:S(2)}, u32[]{:S(2)}) collective-permute-start(bf16[256,512]{1,0:T(8,128)(2,1)S(1)} %get-tuple-element.84), channel_id=1, source_target_pairs={{0,1},{1,0},{2,3},{3,2},{4,5},{5,4},{6,7},{7,6},{8,9},{9,8},{10,11... | collective-permute-start | bytes 786440 | tf_op jit(solution)/shard_map/ppermute | solution.py:67
  (109 shorter events, 22.1 us)
Async XLA Ops:
  4.1 7.7 %collective-permute-start.1 = (bf16[256,4608]{1,0:T(8,128)(2,1)}, bf16[256,4608]{1,0:T(8,128)(2,1)S(1)}, u32[]{:S(2)}, u32[]{:S(2)}) collective-permute-start(bf16[256,4608]{1,0:T(8,128)(2,1)} %get-tuple-element.47), channel_id=1, source_target_pairs={{0,1},{1,0},{2,3},{3,2},{4,5},{5,4},{6,7},{7,6},{8,9},{9,8},{10,11... | collective-permute-start | bytes 7077896 | tf_op jit(solution)/shard_map/ppermute | solution.py:67
  11.2 31.9 %collective-permute-start.3 = (bf16[256,4096]{1,0:T(8,128)(2,1)S(1)}, bf16[256,4096]{1,0:T(8,128)(2,1)S(1)}, u32[]{:S(2)}, u32[]{:S(2)}) collective-permute-start(bf16[256,4096]{1,0:T(8,128)(2,1)S(1)} %get-tuple-element.51), channel_id=1, source_target_pairs={{0,1},{1,0},{2,3},{3,2},{4,5},{5,4},{6,7},{7,6},{8,9},{9,8},{10,11... | collective-permute-start | bytes 6291464 | tf_op jit(solution)/shard_map/ppermute | solution.py:67
  19.0 12.1 %collective-permute-start.7 = (bf16[8,64,512]{2,1,0:T(8,128)(2,1)S(1)}, bf16[8,64,512]{2,1,0:T(8,128)(2,1)S(1)}, u32[]{:S(2)}, u32[]{:S(2)}) collective-permute-start(bf16[8,64,512]{2,1,0:T(8,128)(2,1)S(1)} %get-tuple-element.59), channel_id=1, source_target_pairs={{0,130},{1,13},{2,128},{3,15},{4,134},{5,9},{6,132},{7,11},{8,138}... | collective-permute-start | bytes 1572872 | tf_op jit(solution)/shard_map/ppermute | solution.py:59
  20.1 13.4 %collective-permute-start.12 = (bf16[8,64,512]{2,1,0:T(8,128)(2,1)S(1)}, bf16[8,64,512]{2,1,0:T(8,128)(2,1)S(1)}, u32[]{:S(2)}, u32[]{:S(2)}) collective-permute-start(bf16[8,64,512]{2,1,0:T(8,128)(2,1)S(1)} %get-tuple-element.67), channel_id=1, source_target_pairs={{0,4},{1,3},{2,6},{3,1},{4,0},{5,7},{6,2},{7,5},{8,12},{9,11},{10,... | collective-permute-start | bytes 1572872 | tf_op jit(solution)/shard_map/ppermute | solution.py:59
  21.3 17.2 %collective-permute-start.17 = (bf16[8,64,512]{2,1,0:T(8,128)(2,1)S(1)}, bf16[8,64,512]{2,1,0:T(8,128)(2,1)S(1)}, u32[]{:S(2)}, u32[]{:S(2)}) collective-permute-start(bf16[8,64,512]{2,1,0:T(8,128)(2,1)S(1)} %get-tuple-element.75), channel_id=1, source_target_pairs={{0,12},{1,131},{2,14},{3,129},{4,8},{5,135},{6,10},{7,133},{8,4},{... | collective-permute-start | bytes 1572872 | tf_op jit(solution)/shard_map/ppermute | solution.py:59
  23.2 20.0 %collective-permute-start.2 = (bf16[8,64,512]{2,1,0:T(8,128)(2,1)S(1)}, bf16[8,64,512]{2,1,0:T(8,128)(2,1)S(1)}, u32[]{:S(2)}, u32[]{:S(2)}) collective-permute-start(bf16[8,64,512]{2,1,0:T(8,128)(2,1)S(1)} %get-tuple-element.50), channel_id=1, source_target_pairs={{0,2},{1,5},{2,0},{3,7},{4,6},{5,1},{6,4},{7,3},{8,10},{9,13},{10,... | collective-permute-start | bytes 1572872 | tf_op jit(solution)/shard_map/ppermute | solution.py:59
  31.1 12.0 %collective-permute-start = (f32[3,32,512]{2,1,0:T(8,128)S(1)}, f32[3,32,512]{2,1,0:T(8,128)S(1)}, u32[]{:S(2)}, u32[]{:S(2)}) collective-permute-start(f32[3,32,512]{2,1,0:T(8,128)S(1)} %get-tuple-element.46), channel_id=1, source_target_pairs={{0,112},{1,113},{2,114},{3,115},{4,116},{5,117},{6,118},{7,119},{8... | collective-permute-start | bytes 589832 | tf_op jit(solution)/shard_map/ppermute | solution.py:63
  33.5 15.0 %collective-permute-start.8 = (bf16[4,64,512]{2,1,0:T(8,128)(2,1)S(1)}, bf16[4,64,512]{2,1,0:T(8,128)(2,1)S(1)}, u32[]{:S(2)}, u32[]{:S(2)}) collective-permute-start(bf16[4,64,512]{2,1,0:T(8,128)(2,1)S(1)} %get-tuple-element.61), channel_id=1, source_target_pairs={{0,12},{1,131},{2,14},{3,129},{4,8},{5,135},{6,10},{7,133},{8,4},{... | collective-permute-start | bytes 786440 | tf_op jit(solution)/shard_map/ppermute | solution.py:59
  38.5 10.1 %collective-permute-start.13 = (bf16[4,64,512]{2,1,0:T(8,128)(2,1)S(1)}, bf16[4,64,512]{2,1,0:T(8,128)(2,1)S(1)}, u32[]{:S(2)}, u32[]{:S(2)}) collective-permute-start(bf16[4,64,512]{2,1,0:T(8,128)(2,1)S(1)} %get-tuple-element.69), channel_id=1, source_target_pairs={{0,2},{1,5},{2,0},{3,7},{4,6},{5,1},{6,4},{7,3},{8,10},{9,13},{10,... | collective-permute-start | bytes 786440 | tf_op jit(solution)/shard_map/ppermute | solution.py:59
  43.1 8.8 %collective-permute-start.18 = (bf16[4,64,512]{2,1,0:T(8,128)(2,1)S(1)}, bf16[4,64,512]{2,1,0:T(8,128)(2,1)S(1)}, u32[]{:S(2)}, u32[]{:S(2)}) collective-permute-start(bf16[4,64,512]{2,1,0:T(8,128)(2,1)S(1)} %get-tuple-element.77), channel_id=1, source_target_pairs={{0,130},{1,13},{2,128},{3,15},{4,134},{5,9},{6,132},{7,11},{8,138}... | collective-permute-start | bytes 786440 | tf_op jit(solution)/shard_map/ppermute | solution.py:59
  43.2 9.7 %collective-permute-start.4 = (bf16[4,64,512]{2,1,0:T(8,128)(2,1)S(1)}, bf16[4,64,512]{2,1,0:T(8,128)(2,1)S(1)}, u32[]{:S(2)}, u32[]{:S(2)}) collective-permute-start(bf16[4,64,512]{2,1,0:T(8,128)(2,1)S(1)} %get-tuple-element.53), channel_id=1, source_target_pairs={{0,4},{1,3},{2,6},{3,1},{4,0},{5,7},{6,2},{7,5},{8,12},{9,11},{10,... | collective-permute-start | bytes 786440 | tf_op jit(solution)/shard_map/ppermute | solution.py:59
  48.6 6.5 %collective-permute-start.9 = (bf16[2,64,512]{2,1,0:T(8,128)(2,1)S(1)}, bf16[2,64,512]{2,1,0:T(8,128)(2,1)S(1)}, u32[]{:S(2)}, u32[]{:S(2)}) collective-permute-start(bf16[2,64,512]{2,1,0:T(8,128)(2,1)S(1)} %get-tuple-element.63), channel_id=1, source_target_pairs={{0,2},{1,5},{2,0},{3,7},{4,6},{5,1},{6,4},{7,3},{8,10},{9,13},{10,... | collective-permute-start | bytes 393224 | tf_op jit(solution)/shard_map/ppermute | solution.py:59
  48.8 6.6 %collective-permute-start.14 = (bf16[2,64,512]{2,1,0:T(8,128)(2,1)S(1)}, bf16[2,64,512]{2,1,0:T(8,128)(2,1)S(1)}, u32[]{:S(2)}, u32[]{:S(2)}) collective-permute-start(bf16[2,64,512]{2,1,0:T(8,128)(2,1)S(1)} %get-tuple-element.71), channel_id=1, source_target_pairs={{0,12},{1,131},{2,14},{3,129},{4,8},{5,135},{6,10},{7,133},{8,4},{... | collective-permute-start | bytes 393224 | tf_op jit(solution)/shard_map/ppermute | solution.py:59
  52.0 6.2 %collective-permute-start.19 = (bf16[2,64,512]{2,1,0:T(8,128)(2,1)S(1)}, bf16[2,64,512]{2,1,0:T(8,128)(2,1)S(1)}, u32[]{:S(2)}, u32[]{:S(2)}) collective-permute-start(bf16[2,64,512]{2,1,0:T(8,128)(2,1)S(1)} %get-tuple-element.79), channel_id=1, source_target_pairs={{0,4},{1,3},{2,6},{3,1},{4,0},{5,7},{6,2},{7,5},{8,12},{9,11},{10,... | collective-permute-start | bytes 393224 | tf_op jit(solution)/shard_map/ppermute | solution.py:59
  53.0 5.4 %collective-permute-start.5 = (bf16[2,64,512]{2,1,0:T(8,128)(2,1)S(1)}, bf16[2,64,512]{2,1,0:T(8,128)(2,1)S(1)}, u32[]{:S(2)}, u32[]{:S(2)}) collective-permute-start(bf16[2,64,512]{2,1,0:T(8,128)(2,1)S(1)} %get-tuple-element.55), channel_id=1, source_target_pairs={{0,130},{1,13},{2,128},{3,15},{4,134},{5,9},{6,132},{7,11},{8,138}... | collective-permute-start | bytes 393224 | tf_op jit(solution)/shard_map/ppermute | solution.py:59
  55.1 7.5 %collective-permute-start.10 = (bf16[64,512]{1,0:T(8,128)(2,1)S(1)}, bf16[64,512]{1,0:T(8,128)(2,1)S(1)}, u32[]{:S(2)}, u32[]{:S(2)}) collective-permute-start(bf16[64,512]{1,0:T(8,128)(2,1)S(1)} %bitcast.84), channel_id=1, source_target_pairs={{0,4},{1,3},{2,6},{3,1},{4,0},{5,7},{6,2},{7,5},{8,12},{9,11},{10,... | collective-permute-start | bytes 196616 | tf_op jit(solution)/shard_map/ppermute | solution.py:59
  55.4 7.2 %collective-permute-start.15 = (bf16[64,512]{1,0:T(8,128)(2,1)S(1)}, bf16[64,512]{1,0:T(8,128)(2,1)S(1)}, u32[]{:S(2)}, u32[]{:S(2)}) collective-permute-start(bf16[64,512]{1,0:T(8,128)(2,1)S(1)} %bitcast.85), channel_id=1, source_target_pairs={{0,130},{1,13},{2,128},{3,15},{4,134},{5,9},{6,132},{7,11},{8,138}... | collective-permute-start | bytes 196616 | tf_op jit(solution)/shard_map/ppermute | solution.py:59
  58.2 6.4 %collective-permute-start.20 = (bf16[64,512]{1,0:T(8,128)(2,1)S(1)}, bf16[64,512]{1,0:T(8,128)(2,1)S(1)}, u32[]{:S(2)}, u32[]{:S(2)}) collective-permute-start(bf16[64,512]{1,0:T(8,128)(2,1)S(1)} %bitcast.86), channel_id=1, source_target_pairs={{0,2},{1,5},{2,0},{3,7},{4,6},{5,1},{6,4},{7,3},{8,10},{9,13},{10,... | collective-permute-start | bytes 196616 | tf_op jit(solution)/shard_map/ppermute | solution.py:59
  58.4 8.1 %collective-permute-start.6 = (bf16[64,512]{1,0:T(8,128)(2,1)S(1)}, bf16[64,512]{1,0:T(8,128)(2,1)S(1)}, u32[]{:S(2)}, u32[]{:S(2)}) collective-permute-start(bf16[64,512]{1,0:T(8,128)(2,1)S(1)} %bitcast.83), channel_id=1, source_target_pairs={{0,12},{1,131},{2,14},{3,129},{4,8},{5,135},{6,10},{7,133},{8,4},{... | collective-permute-start | bytes 196616 | tf_op jit(solution)/shard_map/ppermute | solution.py:59
  64.7 5.5 %collective-permute-start.21 = (bf16[64,512]{1,0:T(8,128)(2,1)S(1)}, bf16[64,512]{1,0:T(8,128)(2,1)S(1)}, u32[]{:S(2)}, u32[]{:S(2)}) collective-permute-start(bf16[64,512]{1,0:T(8,128)(2,1)S(1)} %fusion.15), channel_id=1, source_target_pairs={{0,48},{1,49},{2,50},{3,51},{4,52},{5,53},{6,54},{7,55},{8,56},{9,... | collective-permute-start | bytes 196616 | tf_op jit(solution)/shard_map/ppermute | solution.py:63
  74.9 5.9 %collective-permute-start.37 = (bf16[64,512]{1,0:T(8,128)(2,1)S(1)}, bf16[64,512]{1,0:T(8,128)(2,1)S(1)}, u32[]{:S(2)}, u32[]{:S(2)}) collective-permute-start(bf16[64,512]{1,0:T(8,128)(2,1)S(1)} %fusion.12), channel_id=1, source_target_pairs={{0,48},{1,49},{2,50},{3,51},{4,52},{5,53},{6,54},{7,55},{8,56},{9,... | collective-permute-start | bytes 196616 | tf_op jit(solution)/shard_map/ppermute | solution.py:63
  76.7 5.3 %collective-permute-start.27 = (bf16[64,512]{1,0:T(8,128)(2,1)S(1)}, bf16[64,512]{1,0:T(8,128)(2,1)S(1)}, u32[]{:S(2)}, u32[]{:S(2)}) collective-permute-start(bf16[64,512]{1,0:T(8,128)(2,1)S(1)} %fusion.12), channel_id=1, source_target_pairs={{0,16},{1,17},{2,18},{3,19},{4,20},{5,21},{6,22},{7,23},{8,24},{9,... | collective-permute-start | bytes 196616 | tf_op jit(solution)/shard_map/ppermute | solution.py:63
  86.5 5.1 %collective-permute-start.29 = (bf16[2,64,512]{2,1,0:T(8,128)(2,1)S(1)}, bf16[2,64,512]{2,1,0:T(8,128)(2,1)S(1)}, u32[]{:S(2)}, u32[]{:S(2)}) collective-permute-start(bf16[2,64,512]{2,1,0:T(8,128)(2,1)S(1)} %join.15.here), channel_id=1, source_target_pairs={{0,2},{1,5},{2,0},{3,7},{4,6},{5,1},{6,4},{7,3},{8,10},{9,13},{10,... | collective-permute-start | bytes 393224 | tf_op jit(solution)/shard_map/ppermute | solution.py:59
  88.0 5.3 %collective-permute-start.25 = (bf16[4,64,512]{2,1,0:T(8,128)(2,1)S(1)}, bf16[4,64,512]{2,1,0:T(8,128)(2,1)S(1)}, u32[]{:S(2)}, u32[]{:S(2)}) collective-permute-start(bf16[4,64,512]{2,1,0:T(8,128)(2,1)S(1)} %join.13.here), channel_id=1, source_target_pairs={{0,4},{1,3},{2,6},{3,1},{4,0},{5,7},{6,2},{7,5},{8,12},{9,11},{10,... | collective-permute-start | bytes 786440 | tf_op jit(solution)/shard_map/ppermute | solution.py:59
  88.8 6.5 %collective-permute-start.40 = (bf16[4,64,512]{2,1,0:T(8,128)(2,1)S(1)}, bf16[4,64,512]{2,1,0:T(8,128)(2,1)S(1)}, u32[]{:S(2)}, u32[]{:S(2)}) collective-permute-start(bf16[4,64,512]{2,1,0:T(8,128)(2,1)S(1)} %join.22.here), channel_id=1, source_target_pairs={{0,130},{1,13},{2,128},{3,15},{4,134},{5,9},{6,132},{7,11},{8,138}... | collective-permute-start | bytes 786440 | tf_op jit(solution)/shard_map/ppermute | solution.py:59
  91.5 6.8 %collective-permute-start.35 = (bf16[4,64,512]{2,1,0:T(8,128)(2,1)S(1)}, bf16[4,64,512]{2,1,0:T(8,128)(2,1)S(1)}, u32[]{:S(2)}, u32[]{:S(2)}) collective-permute-start(bf16[4,64,512]{2,1,0:T(8,128)(2,1)S(1)} %join.19.here), channel_id=1, source_target_pairs={{0,2},{1,5},{2,0},{3,7},{4,6},{5,1},{6,4},{7,3},{8,10},{9,13},{10,... | collective-permute-start | bytes 786440 | tf_op jit(solution)/shard_map/ppermute | solution.py:59
  91.6 8.0 %collective-permute-start.30 = (bf16[4,64,512]{2,1,0:T(8,128)(2,1)S(1)}, bf16[4,64,512]{2,1,0:T(8,128)(2,1)S(1)}, u32[]{:S(2)}, u32[]{:S(2)}) collective-permute-start(bf16[4,64,512]{2,1,0:T(8,128)(2,1)S(1)} %join.16.here), channel_id=1, source_target_pairs={{0,12},{1,131},{2,14},{3,129},{4,8},{5,135},{6,10},{7,133},{8,4},{... | collective-permute-start | bytes 786440 | tf_op jit(solution)/shard_map/ppermute | solution.py:59
  93.4 12.0 %collective-permute-start.26 = (bf16[8,64,512]{2,1,0:T(8,128)(2,1)S(1)}, bf16[8,64,512]{2,1,0:T(8,128)(2,1)S(1)}, u32[]{:S(2)}, u32[]{:S(2)}) collective-permute-start(bf16[8,64,512]{2,1,0:T(8,128)(2,1)S(1)} %join.14.refs_0_), channel_id=1, source_target_pairs={{0,2},{1,5},{2,0},{3,7},{4,6},{5,1},{6,4},{7,3},{8,10},{9,13},{10,... | collective-permute-start | bytes 1572872 | tf_op jit(solution)/shard_map/ppermute | solution.py:59
  95.4 10.6 %collective-permute-start.41 = (bf16[8,64,512]{2,1,0:T(8,128)(2,1)S(1)}, bf16[8,64,512]{2,1,0:T(8,128)(2,1)S(1)}, u32[]{:S(2)}, u32[]{:S(2)}) collective-permute-start(bf16[8,64,512]{2,1,0:T(8,128)(2,1)S(1)} %join.23.refs_6_), channel_id=1, source_target_pairs={{0,12},{1,131},{2,14},{3,129},{4,8},{5,135},{6,10},{7,133},{8,4},{... | collective-permute-start | bytes 1572872 | tf_op jit(solution)/shard_map/ppermute | solution.py:59
  98.3 9.5 %collective-permute-start.36 = (bf16[8,64,512]{2,1,0:T(8,128)(2,1)S(1)}, bf16[8,64,512]{2,1,0:T(8,128)(2,1)S(1)}, u32[]{:S(2)}, u32[]{:S(2)}) collective-permute-start(bf16[8,64,512]{2,1,0:T(8,128)(2,1)S(1)} %join.20.refs_4_), channel_id=1, source_target_pairs={{0,4},{1,3},{2,6},{3,1},{4,0},{5,7},{6,2},{7,5},{8,12},{9,11},{10,... | collective-permute-start | bytes 1572872 | tf_op jit(solution)/shard_map/ppermute | solution.py:59
  99.7 12.0 %collective-permute-start.31 = (bf16[8,64,512]{2,1,0:T(8,128)(2,1)S(1)}, bf16[8,64,512]{2,1,0:T(8,128)(2,1)S(1)}, u32[]{:S(2)}, u32[]{:S(2)}) collective-permute-start(bf16[8,64,512]{2,1,0:T(8,128)(2,1)S(1)} %join.17.refs_2_), channel_id=1, source_target_pairs={{0,130},{1,13},{2,128},{3,15},{4,134},{5,9},{6,132},{7,11},{8,138}... | collective-permute-start | bytes 1572872 | tf_op jit(solution)/shard_map/ppermute | solution.py:59
  115.2 12.8 %collective-permute-start.42 = (bf16[256,512]{1,0:T(8,128)(2,1)S(1)}, bf16[256,512]{1,0:T(8,128)(2,1)S(1)}, u32[]{:S(2)}, u32[]{:S(2)}) collective-permute-start(bf16[256,512]{1,0:T(8,128)(2,1)S(1)} %get-tuple-element.84), channel_id=1, source_target_pairs={{0,1},{1,0},{2,3},{3,2},{4,5},{5,4},{6,7},{7,6},{8,9},{9,8},{10,11... | collective-permute-start | bytes 786440 | tf_op jit(solution)/shard_map/ppermute | solution.py:67
  (19 other events, 105.8 us)

commit v6 on v5

--- a/solution.py
+++ b/solution.py
@@ -110,15 +110,17 @@
         copy.wait()
 
 
-def theirs_of(source, packed, sems):
+def theirs_of(source, packed, sems, pieces=1):
     where = place()
+    rows = TOK // pieces
     return [
         pltpu.make_async_copy(
-            source.at[:, columns_of(where, r, 1 - where[4])],
-            packed.at[:, pl.ds(r * BLOCK, BLOCK)],
-            sems.at[r],
+            source.at[pl.ds(i * rows, rows), columns_of(where, r, 1 - where[4])],
+            packed.at[pl.ds(i * rows, rows), pl.ds(r * BLOCK, BLOCK)],
+            sems.at[r * pieces + i],
         )
         for r in range(BLOCKS)
+        for i in range(pieces)
     ]
 
 
@@ -126,13 +128,16 @@
 
 
 DONE = jax.ShapeDtypeStruct((8, 128), jnp.float32)
+
+
+PIECES = 4
 
 
 def pack_acts_kernel(acts, grads, packed, done, sems):
     done[...] = jnp.zeros_like(done)
     run_all(
-        theirs_of(acts, packed, sems)
-        + [pltpu.make_async_copy(grads, packed.at[:, pl.ds(HALF, COLS)], sems.at[BLOCKS])]
+        theirs_of(acts, packed, sems, PIECES)
+        + [pltpu.make_async_copy(grads, packed.at[:, pl.ds(HALF, COLS)], sems.at[BLOCKS * PIECES])]
     )
 
 
@@ -142,7 +147,7 @@
         out_shape=(jax.ShapeDtypeStruct((TOK, HALF + COLS), jnp.bfloat16), DONE),
         in_specs=[ANY, ANY],
         out_specs=(VMEM, VMEM),
-        scratch_shapes=[pltpu.SemaphoreType.DMA((BLOCKS + 1,))],
+        scratch_shapes=[pltpu.SemaphoreType.DMA((BLOCKS * PIECES + 1,))],
         compiler_params=WHOLE,
         cost_estimate=cost(0, 4 << 20),
         name="pack_acts",
@@ -238,30 +243,32 @@
     )(acts, got, grads, after)
 
 
-def add_kernel(dim, keep, got, *refs):
-    next_keep, next_send = refs[-2:]
-    blocks = keep.shape[0]
-    inner = blocks >> (dim + 1)
-    for slot in range(blocks):
-        side = (slot // inner) % 2
-        out = next_send if side else next_keep
-        out[slot // (2 * inner) * inner + slot % inner] = (
-            keep[slot].astype(jnp.float32) + got[slot].astype(jnp.float32)
-        ).astype(jnp.bfloat16)
-
-
-def add_halves(keep, got, dim, after=()):
-    blocks = keep.shape[0]
+def add_kernel(dims, n_outs, *refs):
+    outs = refs[-n_outs:]
+    for i, dim in enumerate(dims):
+        keep, got = refs[2 * i : 2 * i + 2]
+        blocks = keep.shape[0]
+        inner = blocks >> (dim + 1)
+        for slot in range(blocks):
+            outs[2 * i + (slot // inner) % 2][slot // (2 * inner) * inner + slot % inner] = (
+                keep[slot].astype(jnp.float32) + got[slot].astype(jnp.float32)
+            ).astype(jnp.bfloat16)
+
+
+def add_halves(pairs, dims, after=(), through=()):
+    blocks = pairs[0].shape[0]
     half = jax.ShapeDtypeStruct((blocks // 2, ROWS, COLS), jnp.bfloat16)
-    return pl.pallas_call(
-        functools.partial(add_kernel, dim),
-        out_shape=(half, half),
-        in_specs=[VMEM, VMEM] + [ANY] * len(after),
-        out_specs=(VMEM, VMEM),
+    n, first = len(pairs), len(pairs) + len(after)
+    return pl.pallas_call(
+        functools.partial(add_kernel, dims, n + len(through)),
+        out_shape=(half,) * n + tuple(jax.ShapeDtypeStruct(t.shape, t.dtype) for t in through),
+        in_specs=[VMEM] * n + [ANY] * (len(after) + len(through)),
+        out_specs=(VMEM,) * n + (ANY,) * len(through),
+        input_output_aliases={first + i: n + i for i in range(len(through))},
         compiler_params=PARAMS,
-        cost_estimate=cost(blocks << 16, blocks * 3 << 17),
+        cost_estimate=cost(n * blocks << 15, n * blocks * 3 << 16),
         name="add_halves",
-    )(keep, got, *after)
+    )(*pairs, *after, *through)
 
 
 def join_kernel(dim, here, got, both):
@@ -401,16 +408,21 @@
     return add(keep, across(lax.index_in_dim(array, 1, dim, keepdims=False), pairing))
 
 
-def reduce_parts(halves, after):
+def reduce_parts(halves, packed_tokens, state):
+    pairs, dims = [], []
+    for m, (v, w, _, _) in enumerate(ORDERS):
+        pairs += [halves[2 * m], across(halves[2 * m + 1], v)]
+        dims.append(w - (v < w))
+    *sums, packed_tokens = add_halves(pairs, dims, (state,), (packed_tokens,))
+    tokens = core_swap(packed_tokens)
     parts = []
-    for m, (v, w, p, q) in enumerate(ORDERS):
-        keep, got = halves[2 * m], across(halves[2 * m + 1], v)
-        keep, send = add_halves(keep, got, w - (v < w), () if m else after)
-        keep, send = add_halves(keep, across(send, w), sorted((p, q)).index(p))
-        keep, send = add_halves(keep, across(send, p), 0)
+    for m, (_, w, p, q) in enumerate(ORDERS):
+        keep, send = sums[2 * m : 2 * m + 2]
+        keep, send = add_halves([keep, across(send, w)], [int(p > q)])
+        keep, send = add_halves([keep, across(send, p)], [0], () if m else (tokens,))
         total = wide(keep[0]) + wide(across(send[0], q))
         parts.append(total.astype(jnp.bfloat16) if m else total)
-    return parts
+    return parts, tokens
 
 
 def reduce_z(parts):
@@ -439,9 +451,9 @@
     )
     halves = gradient_term(activations, core_swap(packed), output_grads, packed_all)
     got_state = z_swap(state, 7)
-    got_tokens = core_swap(packed_tokens)
-
-    gradient = reduce_z(reduce_parts(halves, (got_tokens, got_state)))
+
+    parts, got_tokens = reduce_parts(halves, packed_tokens, got_state)
+    gradient = reduce_z(parts)
     pairs = jnp.stack([jnp.where(low, state, got_state), jnp.where(low, got_state, state)], axis=1)
     updated = adamw_update(gradient, *pairs)
     new_master, new_first, new_second = (jnp.where(low, u[0], u[1]) for u in updated)

time: 129 us -> 126 us (0.977)
  starting transfers between devices: 68.6 us -> 60.7 us
  waiting for transfers between devices: 37.6 us -> 41.7 us
    ppermute x32, starting transfers between devices: 41.7 us -> 27.6 us  [across(): return lax.ppermute(array, AXES, PAIRINGS[pairing])]
    ppermute x8, waiting for transfers between devices: 12.6 us -> 15.8 us  [z_swap(): lax.ppermute(array, AXES, moves(lambda xh, z, y, xl, c: (xh, z ^ mask, y,...]
    ppermute x8, starting transfers between devices: 12.1 us -> 15.3 us  [z_swap(): lax.ppermute(array, AXES, moves(lambda xh, z, y, xl, c: (xh, z ^ mask, y,...]
    ppermute x3, starting transfers between devices: 14.9 us -> 17.8 us  [core_swap(): lax.ppermute(array, AXES, moves(lambda xh, z, y, xl, c: (xh, z, y, xl, 1...]
  transfers between devices with their start and end apart: 43 -> 43, of which waited for: 19 -> 25; matrix products, arithmetic and copies ran while one was open for 1% -> 1% of each run, Pallas kernels for 7% -> 1%
where the time goes in v6:
time: 126 us; the launch traced here: 125 us
  starting transfers between devices  60.7 us (48%)
  waiting for transfers between devices  41.7 us (33%)
  Pallas kernels  16 us (13%)
  local copies, waits for them, and re-layouts  3.59 us (3%)
  other arithmetic  2.47 us (2%)
    ppermute x32, starting transfers between devices, across(): return lax.ppermute(array, AXES, PAIRINGS[pairing])  27.6 us
    ppermute x32, waiting for transfers between devices, across(): return lax.ppermute(array, AXES, PAIRINGS[pairing])  25.3 us
    ppermute x3, starting transfers between devices, core_swap(): lax.ppermute(array, AXES, moves(lambda xh, z, y, xl, c: (xh, z, y, xl, 1...  17.8 us
    ppermute x8, waiting for transfers between devices, z_swap(): lax.ppermute(array, AXES, moves(lambda xh, z, y, xl, c: (xh, z ^ mask, y,...  15.8 us
    ppermute x8, starting transfers between devices, z_swap(): lax.ppermute(array, AXES, moves(lambda xh, z, y, xl, c: (xh, z ^ mask, y,...  15.3 us
    pallas_call x1, Pallas kernels, gradient_term(): pl.pallas_call(term_kernel, out_shape=(half,) * (2 * PARTS), in_specs=[AN...  6.54 us
    pallas_call x1, Pallas kernels, pack_acts(): pl.pallas_call(pack_acts_kernel, out_shape=(jax.ShapeDtypeStruct((TOK, HA...  3.85 us
    pallas_call x1, Pallas kernels, project(): pl.pallas_call(project_kernel, out_shape=(jax.ShapeDtypeStruct((2 * BLOCK...  3.61 us
  transfers between devices with their start and end apart: 43, of which 25 were waited for; matrix products, arithmetic and copies ran while one was open for 1% of the time, Pallas kernels for 1%

profile of v6, /device:TPU:1, one launch (start us, length us, event | category | flops | bytes accessed | tf_op | source)
XLA Modules:
  0.0 125.4 jit_solution(8155276477381709970)
XLA Ops:
  0.7 3.8 %pack_acts.1 = (bf16[256,4608]{1,0:T(8,128)(2,1)}, f32[8,128]{1,0:T(8,128)}) custom-call(bf16[256,8192]{1,0:T(8,128)(2,1)} %acts.3, bf16[256,512]{1,0:T(8,128)(2,1)} %grads.3), custom_call_target="tpu_custom_call" | custom-call | bytes 4194304 | tf_op jit(solution)/shard_map/pack_acts/pallas_call | solution.py:145
  4.5 3.3 %collective-permute-start.1 = (bf16[256,4608]{1,0:T(8,128)(2,1)}, bf16[256,4608]{1,0:T(8,128)(2,1)S(1)}, u32[]{:S(2)}, u32[]{:S(2)}) collective-permute-start(bf16[256,4608]{1,0:T(8,128)(2,1)} %get-tuple-element.48), channel_id=1, source_target_pairs={{0,1},{1,0},{2,3},{3,2},{4,5},{5,4},{6,7},{7,6},{8,9},{9,8},{10,11... | collective-permute-start | bytes 7077896 | tf_op jit(solution)/shard_map/ppermute | solution.py:67
  7.9 2.2 %copy-done = bf16[256,8192]{1,0:T(8,128)(2,1)S(1)} copy-done((bf16[256,8192]{1,0:T(8,128)(2,1)S(1)}, bf16[256,8192]{1,0:T(8,128)(2,1)}, u32[]{:S(2)}) %copy-start) | copy-done | bytes 4194328
  12.9 6.5 %gradient_term.1 = (bf16[8,64,512]{2,1,0:T(8,128)(2,1)S(1)}, bf16[8,64,512]{2,1,0:T(8,128)(2,1)S(1)}, bf16[8,64,512]{2,1,0:T(8,128)(2,1)S(1)}, bf16[8,64,512]{2,...) custom-call(bf16[256,8192]{1,0:T(8,128)(2,1)S(1)} %copy-done.2, ...), custom_call_target="tpu_custom_call" | custom-call | flops 2147483648 | bytes 9437184 | tf_op jit(solution)/shard_map/gradient_term/pallas_call | solution.py:229
  19.6 1.4 %collective-permute-start.3 = (bf16[8,64,512]{2,1,0:T(8,128)(2,1)S(1)}, bf16[8,64,512]{2,1,0:T(8,128)(2,1)S(1)}, u32[]{:S(2)}, u32[]{:S(2)}) collective-permute-start(bf16[8,64,512]{2,1,0:T(8,128)(2,1)S(1)} %get-tuple-element.53), channel_id=1, source_target_pairs={{0,130},{1,13},{2,128},{3,15},{4,134},{5,9},{6,132},{7,11},{8,138}... | collective-permute-start | bytes 1572872 | tf_op jit(solution)/shard_map/ppermute | solution.py:59
  22.2 1.9 %collective-permute-start.5 = (bf16[8,64,512]{2,1,0:T(8,128)(2,1)S(1)}, bf16[8,64,512]{2,1,0:T(8,128)(2,1)S(1)}, u32[]{:S(2)}, u32[]{:S(2)}) collective-permute-start(bf16[8,64,512]{2,1,0:T(8,128)(2,1)S(1)} %get-tuple-element.57), channel_id=1, source_target_pairs={{0,12},{1,131},{2,14},{3,129},{4,8},{5,135},{6,10},{7,133},{8,4},{... | collective-permute-start | bytes 1572872 | tf_op jit(solution)/shard_map/ppermute | solution.py:59
  24.1 5.6 %collective-permute-start = (f32[3,32,512]{2,1,0:T(8,128)S(1)}, f32[3,32,512]{2,1,0:T(8,128)S(1)}, u32[]{:S(2)}, u32[]{:S(2)}) collective-permute-start(f32[3,32,512]{2,1,0:T(8,128)S(1)} %get-tuple-element.47), channel_id=1, source_target_pairs={{0,112},{1,113},{2,114},{3,115},{4,116},{5,117},{6,118},{7,119},{8... | collective-permute-start | bytes 589832 | tf_op jit(solution)/shard_map/ppermute | solution.py:63
  29.7 9.1 %collective-permute-done.refs_8_ = f32[3,32,512]{2,1,0:T(8,128)S(1)} collective-permute-done((f32[3,32,512]{2,1,0:T(8,128)S(1)}, f32[3,32,512]{2,1,0:T(8,128)S(1)}, u32[]{:S(2)}, u32[]{:S(2)}) %collective-permute-start) | collective-permute-done | bytes 196640 | tf_op jit(solution)/shard_map/ppermute | solution.py:63
  42.2 5.4 %collective-permute-done.10.refs_1_ = bf16[4,64,512]{2,1,0:T(8,128)(2,1)S(1)} collective-permute-done((bf16[4,64,512]{2,1,0:T(8,128)(2,1)S(1)}, bf16[4,64,512]{2,1,0:T(8,128)(2,1)S(1)}, u32[]{:S(2)}, u32[]{:S(2)}) %collective-permute-start.10) | collective-permute-done | bytes 262176 | tf_op jit(solution)/shard_map/ppermute | solution.py:59
  47.7 1.5 %collective-permute-start.11 = (bf16[2,64,512]{2,1,0:T(8,128)(2,1)S(1)}, bf16[2,64,512]{2,1,0:T(8,128)(2,1)S(1)}, u32[]{:S(2)}, u32[]{:S(2)}) collective-permute-start(bf16[2,64,512]{2,1,0:T(8,128)(2,1)S(1)} %get-tuple-element.69), channel_id=1, source_target_pairs={{0,2},{1,5},{2,0},{3,7},{4,6},{5,1},{6,4},{7,3},{8,10},{9,13},{10,... | collective-permute-start | bytes 393224 | tf_op jit(solution)/shard_map/ppermute | solution.py:59
  56.9 2.5 %collective-permute-done.16 = bf16[64,512]{1,0:T(8,128)(2,1)S(1)} collective-permute-done((bf16[64,512]{1,0:T(8,128)(2,1)S(1)}, bf16[64,512]{1,0:T(8,128)(2,1)S(1)}, u32[]{:S(2)}, u32[]{:S(2)}) %collective-permute-start.16) | collective-permute-done | bytes 65568 | tf_op jit(solution)/shard_map/ppermute | solution.py:59
  59.5 1.7 %collective-permute-start.21 = (bf16[64,512]{1,0:T(8,128)(2,1)S(1)}, bf16[64,512]{1,0:T(8,128)(2,1)S(1)}, u32[]{:S(2)}, u32[]{:S(2)}) collective-permute-start(bf16[64,512]{1,0:T(8,128)(2,1)S(1)} %fusion.15), channel_id=1, source_target_pairs={{0,48},{1,49},{2,50},{3,51},{4,52},{5,53},{6,54},{7,55},{8,56},{9,... | collective-permute-start | bytes 196616 | tf_op jit(solution)/shard_map/ppermute | solution.py:63
  62.3 1.2 collective-permute-done.17
  63.5 1.5 %collective-permute-done.21 = bf16[64,512]{1,0:T(8,128)(2,1)S(1)} collective-permute-done((bf16[64,512]{1,0:T(8,128)(2,1)S(1)}, bf16[64,512]{1,0:T(8,128)(2,1)S(1)}, u32[]{:S(2)}, u32[]{:S(2)}) %collective-permute-start.21) | collective-permute-done | bytes 65568 | tf_op jit(solution)/shard_map/ppermute | solution.py:63
  65.7 3.9 %collective-permute-start.22 = (bf16[64,512]{1,0:T(8,128)(2,1)S(1)}, bf16[64,512]{1,0:T(8,128)(2,1)S(1)}, u32[]{:S(2)}, u32[]{:S(2)}) collective-permute-start(bf16[64,512]{1,0:T(8,128)(2,1)S(1)} %fusion.21), channel_id=1, source_target_pairs={{0,112},{1,113},{2,114},{3,115},{4,116},{5,117},{6,118},{7,119},{8... | collective-permute-start | bytes 196616 | tf_op jit(solution)/shard_map/ppermute | solution.py:63
  69.7 2.1 %collective-permute-done.22 = bf16[64,512]{1,0:T(8,128)(2,1)S(1)} collective-permute-done((bf16[64,512]{1,0:T(8,128)(2,1)S(1)}, bf16[64,512]{1,0:T(8,128)(2,1)S(1)}, u32[]{:S(2)}, u32[]{:S(2)}) %collective-permute-start.22) | collective-permute-done | bytes 65568 | tf_op jit(solution)/shard_map/ppermute | solution.py:63
  72.0 1.7 %collective-permute-start.37 = (bf16[64,512]{1,0:T(8,128)(2,1)S(1)}, bf16[64,512]{1,0:T(8,128)(2,1)S(1)}, u32[]{:S(2)}, u32[]{:S(2)}) collective-permute-start(bf16[64,512]{1,0:T(8,128)(2,1)S(1)} %fusion.12), channel_id=1, source_target_pairs={{0,48},{1,49},{2,50},{3,51},{4,52},{5,53},{6,54},{7,55},{8,56},{9,... | collective-permute-start | bytes 196616 | tf_op jit(solution)/shard_map/ppermute | solution.py:63
  73.7 2.2 %collective-permute-start.32 = (bf16[64,512]{1,0:T(8,128)(2,1)S(1)}, bf16[64,512]{1,0:T(8,128)(2,1)S(1)}, u32[]{:S(2)}, u32[]{:S(2)}) collective-permute-start(bf16[64,512]{1,0:T(8,128)(2,1)S(1)} %fusion.12), channel_id=1, source_target_pairs={{0,32},{1,33},{2,34},{3,35},{4,36},{5,37},{6,38},{7,39},{8,40},{9,... | collective-permute-start | bytes 196616 | tf_op jit(solution)/shard_map/ppermute | solution.py:63
  77.0 1.4 %collective-permute-done.32 = bf16[64,512]{1,0:T(8,128)(2,1)S(1)} collective-permute-done((bf16[64,512]{1,0:T(8,128)(2,1)S(1)}, bf16[64,512]{1,0:T(8,128)(2,1)S(1)}, u32[]{:S(2)}, u32[]{:S(2)}) %collective-permute-start.32) | collective-permute-done | bytes 65568 | tf_op jit(solution)/shard_map/ppermute | solution.py:63
  78.4 1.6 %collective-permute-start.33 = (bf16[1,64,512]{2,1,0:T(8,128)(2,1)S(1)}, bf16[1,64,512]{2,1,0:T(8,128)(2,1)S(1)}, u32[]{:S(2)}, u32[]{:S(2)}) collective-permute-start(bf16[1,64,512]{2,1,0:T(8,128)(2,1)S(1)} %bitcast.79), channel_id=1, source_target_pairs={{0,130},{1,13},{2,128},{3,15},{4,134},{5,9},{6,132},{7,11},{8,138}... | collective-permute-start | bytes 196616 | tf_op jit(solution)/shard_map/ppermute | solution.py:59
  80.2 1.5 %collective-permute-start.24 = (bf16[2,64,512]{2,1,0:T(8,128)(2,1)S(1)}, bf16[2,64,512]{2,1,0:T(8,128)(2,1)S(1)}, u32[]{:S(2)}, u32[]{:S(2)}) collective-permute-start(bf16[2,64,512]{2,1,0:T(8,128)(2,1)S(1)} %join.12.here), channel_id=1, source_target_pairs={{0,130},{1,13},{2,128},{3,15},{4,134},{5,9},{6,132},{7,11},{8,138}... | collective-permute-start | bytes 393224 | tf_op jit(solution)/shard_map/ppermute | solution.py:59
  82.8 1.4 %collective-permute-start.34 = (bf16[2,64,512]{2,1,0:T(8,128)(2,1)S(1)}, bf16[2,64,512]{2,1,0:T(8,128)(2,1)S(1)}, u32[]{:S(2)}, u32[]{:S(2)}) collective-permute-start(bf16[2,64,512]{2,1,0:T(8,128)(2,1)S(1)} %join.18.here), channel_id=1, source_target_pairs={{0,12},{1,131},{2,14},{3,129},{4,8},{5,135},{6,10},{7,133},{8,4},{... | collective-permute-start | bytes 393224 | tf_op jit(solution)/shard_map/ppermute | solution.py:59
  85.4 1.4 %collective-permute-start.25 = (bf16[4,64,512]{2,1,0:T(8,128)(2,1)S(1)}, bf16[4,64,512]{2,1,0:T(8,128)(2,1)S(1)}, u32[]{:S(2)}, u32[]{:S(2)}) collective-permute-start(bf16[4,64,512]{2,1,0:T(8,128)(2,1)S(1)} %join.13.here), channel_id=1, source_target_pairs={{0,4},{1,3},{2,6},{3,1},{4,0},{5,7},{6,2},{7,5},{8,12},{9,11},{10,... | collective-permute-start | bytes 786440 | tf_op jit(solution)/shard_map/ppermute | solution.py:59
  88.5 1.6 %collective-permute-start.30 = (bf16[4,64,512]{2,1,0:T(8,128)(2,1)S(1)}, bf16[4,64,512]{2,1,0:T(8,128)(2,1)S(1)}, u32[]{:S(2)}, u32[]{:S(2)}) collective-permute-start(bf16[4,64,512]{2,1,0:T(8,128)(2,1)S(1)} %join.16.here), channel_id=1, source_target_pairs={{0,12},{1,131},{2,14},{3,129},{4,8},{5,135},{6,10},{7,133},{8,4},{... | collective-permute-start | bytes 786440 | tf_op jit(solution)/shard_map/ppermute | solution.py:59
  90.1 1.3 %collective-permute-done.25.got = bf16[4,64,512]{2,1,0:T(8,128)(2,1)S(1)} collective-permute-done((bf16[4,64,512]{2,1,0:T(8,128)(2,1)S(1)}, bf16[4,64,512]{2,1,0:T(8,128)(2,1)S(1)}, u32[]{:S(2)}, u32[]{:S(2)}) %collective-permute-start.25) | collective-permute-done | bytes 262176 | tf_op jit(solution)/shard_map/ppermute | solution.py:59
  93.4 1.3 collective-permute-start.41
  96.2 1.8 %collective-permute-start.31 = (bf16[8,64,512]{2,1,0:T(8,128)(2,1)S(1)}, bf16[8,64,512]{2,1,0:T(8,128)(2,1)S(1)}, u32[]{:S(2)}, u32[]{:S(2)}) collective-permute-start(bf16[8,64,512]{2,1,0:T(8,128)(2,1)S(1)} %join.17.refs_2_), channel_id=1, source_target_pairs={{0,130},{1,13},{2,128},{3,15},{4,134},{5,9},{6,132},{7,11},{8,138}... | collective-permute-start | bytes 1572872 | tf_op jit(solution)/shard_map/ppermute | solution.py:59
  98.1 4.4 %collective-permute-done.26.refs_1_ = bf16[8,64,512]{2,1,0:T(8,128)(2,1)S(1)} collective-permute-done((bf16[8,64,512]{2,1,0:T(8,128)(2,1)S(1)}, bf16[8,64,512]{2,1,0:T(8,128)(2,1)S(1)}, u32[]{:S(2)}, u32[]{:S(2)}) %collective-permute-start.26) | collective-permute-done | bytes 524320 | tf_op jit(solution)/shard_map/ppermute | solution.py:59
  102.7 2.2 %collective-permute-done.36.refs_5_ = bf16[8,64,512]{2,1,0:T(8,128)(2,1)S(1)} collective-permute-done((bf16[8,64,512]{2,1,0:T(8,128)(2,1)S(1)}, bf16[8,64,512]{2,1,0:T(8,128)(2,1)S(1)}, u32[]{:S(2)}, u32[]{:S(2)}) %collective-permute-start.36) | collective-permute-done | bytes 524320 | tf_op jit(solution)/shard_map/ppermute | solution.py:59
  104.8 1.4 %collective-permute-done.31.refs_3_ = bf16[8,64,512]{2,1,0:T(8,128)(2,1)S(1)} collective-permute-done((bf16[8,64,512]{2,1,0:T(8,128)(2,1)S(1)}, bf16[8,64,512]{2,1,0:T(8,128)(2,1)S(1)}, u32[]{:S(2)}, u32[]{:S(2)}) %collective-permute-start.31) | collective-permute-done | bytes 524320 | tf_op jit(solution)/shard_map/ppermute | solution.py:59
  106.3 3.6 %project.1 = (bf16[512,512]{1,0:T(8,128)(2,1)}, f32[256,512]{1,0:T(8,128)S(1)}, bf16[256,512]{1,0:T(8,128)(2,1)S(1)}) custom-call(bf16[256,8192]{1,0:T(8,128)(2,1)S(1)} %copy-done.1, bf16[256,4096]{1,0:T(8,128)(2,1)S(1)} %collective-permute-done.8.refs_2_.got, bf16[8,64,512]{2,1,0:T(8,128)(2,1)S(1)} %join.14.refs_0_, ...), custom_call_target="tpu_custom_call" | custom-call | flops 2147483648 | bytes 9437184 | tf_op jit(solution)/shard_map/project/pallas_call | solution.py:366
  109.9 13.4 %collective-permute-start.42 = (bf16[256,512]{1,0:T(8,128)(2,1)S(1)}, bf16[256,512]{1,0:T(8,128)(2,1)S(1)}, u32[]{:S(2)}, u32[]{:S(2)}) collective-permute-start(bf16[256,512]{1,0:T(8,128)(2,1)S(1)} %get-tuple-element.86), channel_id=1, source_target_pairs={{0,1},{1,0},{2,3},{3,2},{4,5},{5,4},{6,7},{7,6},{8,9},{9,8},{10,11... | collective-permute-start | bytes 786440 | tf_op jit(solution)/shard_map/ppermute | solution.py:67
  (106 shorter events, 28.6 us)
Async XLA Ops:
  4.5 7.7 %collective-permute-start.1 = (bf16[256,4608]{1,0:T(8,128)(2,1)}, bf16[256,4608]{1,0:T(8,128)(2,1)S(1)}, u32[]{:S(2)}, u32[]{:S(2)}) collective-permute-start(bf16[256,4608]{1,0:T(8,128)(2,1)} %get-tuple-element.48), channel_id=1, source_target_pairs={{0,1},{1,0},{2,3},{3,2},{4,5},{5,4},{6,7},{7,6},{8,9},{9,8},{10,11... | collective-permute-start | bytes 7077896 | tf_op jit(solution)/shard_map/ppermute | solution.py:67
  19.5 19.3 %collective-permute-start.2 = (bf16[8,64,512]{2,1,0:T(8,128)(2,1)S(1)}, bf16[8,64,512]{2,1,0:T(8,128)(2,1)S(1)}, u32[]{:S(2)}, u32[]{:S(2)}) collective-permute-start(bf16[8,64,512]{2,1,0:T(8,128)(2,1)S(1)} %get-tuple-element.51), channel_id=1, source_target_pairs={{0,2},{1,5},{2,0},{3,7},{4,6},{5,1},{6,4},{7,3},{8,10},{9,13},{10,... | collective-permute-start | bytes 1572872 | tf_op jit(solution)/shard_map/ppermute | solution.py:59
  19.6 19.2 %collective-permute-start.3 = (bf16[8,64,512]{2,1,0:T(8,128)(2,1)S(1)}, bf16[8,64,512]{2,1,0:T(8,128)(2,1)S(1)}, u32[]{:S(2)}, u32[]{:S(2)}) collective-permute-start(bf16[8,64,512]{2,1,0:T(8,128)(2,1)S(1)} %get-tuple-element.53), channel_id=1, source_target_pairs={{0,130},{1,13},{2,128},{3,15},{4,134},{5,9},{6,132},{7,11},{8,138}... | collective-permute-start | bytes 1572872 | tf_op jit(solution)/shard_map/ppermute | solution.py:59
  21.0 17.8 %collective-permute-start.4 = (bf16[8,64,512]{2,1,0:T(8,128)(2,1)S(1)}, bf16[8,64,512]{2,1,0:T(8,128)(2,1)S(1)}, u32[]{:S(2)}, u32[]{:S(2)}) collective-permute-start(bf16[8,64,512]{2,1,0:T(8,128)(2,1)S(1)} %get-tuple-element.55), channel_id=1, source_target_pairs={{0,4},{1,3},{2,6},{3,1},{4,0},{5,7},{6,2},{7,5},{8,12},{9,11},{10,... | collective-permute-start | bytes 1572872 | tf_op jit(solution)/shard_map/ppermute | solution.py:59
  22.2 16.6 %collective-permute-start.5 = (bf16[8,64,512]{2,1,0:T(8,128)(2,1)S(1)}, bf16[8,64,512]{2,1,0:T(8,128)(2,1)S(1)}, u32[]{:S(2)}, u32[]{:S(2)}) collective-permute-start(bf16[8,64,512]{2,1,0:T(8,128)(2,1)S(1)} %get-tuple-element.57), channel_id=1, source_target_pairs={{0,12},{1,131},{2,14},{3,129},{4,8},{5,135},{6,10},{7,133},{8,4},{... | collective-permute-start | bytes 1572872 | tf_op jit(solution)/shard_map/ppermute | solution.py:59
  24.1 14.7 %collective-permute-start = (f32[3,32,512]{2,1,0:T(8,128)S(1)}, f32[3,32,512]{2,1,0:T(8,128)S(1)}, u32[]{:S(2)}, u32[]{:S(2)}) collective-permute-start(f32[3,32,512]{2,1,0:T(8,128)S(1)} %get-tuple-element.47), channel_id=1, source_target_pairs={{0,112},{1,113},{2,114},{3,115},{4,116},{5,117},{6,118},{7,119},{8... | collective-permute-start | bytes 589832 | tf_op jit(solution)/shard_map/ppermute | solution.py:63
  39.3 21.9 %collective-permute-start.8 = (bf16[256,4096]{1,0:T(8,128)(2,1)S(1)}, bf16[256,4096]{1,0:T(8,128)(2,1)S(1)}, u32[]{:S(2)}, u32[]{:S(2)}) collective-permute-start(bf16[256,4096]{1,0:T(8,128)(2,1)S(1)} %get-tuple-element.63), channel_id=1, source_target_pairs={{0,1},{1,0},{2,3},{3,2},{4,5},{5,4},{6,7},{7,6},{8,9},{9,8},{10,11... | collective-permute-start | bytes 6291464 | tf_op jit(solution)/shard_map/ppermute | solution.py:67
  40.4 7.2 %collective-permute-start.10 = (bf16[4,64,512]{2,1,0:T(8,128)(2,1)S(1)}, bf16[4,64,512]{2,1,0:T(8,128)(2,1)S(1)}, u32[]{:S(2)}, u32[]{:S(2)}) collective-permute-start(bf16[4,64,512]{2,1,0:T(8,128)(2,1)S(1)} %get-tuple-element.67), channel_id=1, source_target_pairs={{0,12},{1,131},{2,14},{3,129},{4,8},{5,135},{6,10},{7,133},{8,4},{... | collective-permute-start | bytes 786440 | tf_op jit(solution)/shard_map/ppermute | solution.py:59
  41.2 8.0 %collective-permute-start.14 = (bf16[4,64,512]{2,1,0:T(8,128)(2,1)S(1)}, bf16[4,64,512]{2,1,0:T(8,128)(2,1)S(1)}, u32[]{:S(2)}, u32[]{:S(2)}) collective-permute-start(bf16[4,64,512]{2,1,0:T(8,128)(2,1)S(1)} %get-tuple-element.73), channel_id=1, source_target_pairs={{0,2},{1,5},{2,0},{3,7},{4,6},{5,1},{6,4},{7,3},{8,10},{9,13},{10,... | collective-permute-start | bytes 786440 | tf_op jit(solution)/shard_map/ppermute | solution.py:59
  41.6 8.8 %collective-permute-start.18 = (bf16[4,64,512]{2,1,0:T(8,128)(2,1)S(1)}, bf16[4,64,512]{2,1,0:T(8,128)(2,1)S(1)}, u32[]{:S(2)}, u32[]{:S(2)}) collective-permute-start(bf16[4,64,512]{2,1,0:T(8,128)(2,1)S(1)} %get-tuple-element.79), channel_id=1, source_target_pairs={{0,130},{1,13},{2,128},{3,15},{4,134},{5,9},{6,132},{7,11},{8,138}... | collective-permute-start | bytes 786440 | tf_op jit(solution)/shard_map/ppermute | solution.py:59
  42.2 9.9 %collective-permute-start.6 = (bf16[4,64,512]{2,1,0:T(8,128)(2,1)S(1)}, bf16[4,64,512]{2,1,0:T(8,128)(2,1)S(1)}, u32[]{:S(2)}, u32[]{:S(2)}) collective-permute-start(bf16[4,64,512]{2,1,0:T(8,128)(2,1)S(1)} %get-tuple-element.60), channel_id=1, source_target_pairs={{0,4},{1,3},{2,6},{3,1},{4,0},{5,7},{6,2},{7,5},{8,12},{9,11},{10,... | collective-permute-start | bytes 786440 | tf_op jit(solution)/shard_map/ppermute | solution.py:59
  49.2 5.1 %collective-permute-start.15 = (bf16[2,64,512]{2,1,0:T(8,128)(2,1)S(1)}, bf16[2,64,512]{2,1,0:T(8,128)(2,1)S(1)}, u32[]{:S(2)}, u32[]{:S(2)}) collective-permute-start(bf16[2,64,512]{2,1,0:T(8,128)(2,1)S(1)} %get-tuple-element.75), channel_id=1, source_target_pairs={{0,12},{1,131},{2,14},{3,129},{4,8},{5,135},{6,10},{7,133},{8,4},{... | collective-permute-start | bytes 393224 | tf_op jit(solution)/shard_map/ppermute | solution.py:59
  50.4 5.2 %collective-permute-start.19 = (bf16[2,64,512]{2,1,0:T(8,128)(2,1)S(1)}, bf16[2,64,512]{2,1,0:T(8,128)(2,1)S(1)}, u32[]{:S(2)}, u32[]{:S(2)}) collective-permute-start(bf16[2,64,512]{2,1,0:T(8,128)(2,1)S(1)} %get-tuple-element.81), channel_id=1, source_target_pairs={{0,4},{1,3},{2,6},{3,1},{4,0},{5,7},{6,2},{7,5},{8,12},{9,11},{10,... | collective-permute-start | bytes 393224 | tf_op jit(solution)/shard_map/ppermute | solution.py:59
  51.8 4.9 %collective-permute-start.12 = (bf16[64,512]{1,0:T(8,128)(2,1)S(1)}, bf16[64,512]{1,0:T(8,128)(2,1)S(1)}, u32[]{:S(2)}, u32[]{:S(2)}) collective-permute-start(bf16[64,512]{1,0:T(8,128)(2,1)S(1)} %bitcast.84), channel_id=1, source_target_pairs={{0,4},{1,3},{2,6},{3,1},{4,0},{5,7},{6,2},{7,5},{8,12},{9,11},{10,... | collective-permute-start | bytes 196616 | tf_op jit(solution)/shard_map/ppermute | solution.py:59
  52.2 9.0 %collective-permute-start.7 = (bf16[2,64,512]{2,1,0:T(8,128)(2,1)S(1)}, bf16[2,64,512]{2,1,0:T(8,128)(2,1)S(1)}, u32[]{:S(2)}, u32[]{:S(2)}) collective-permute-start(bf16[2,64,512]{2,1,0:T(8,128)(2,1)S(1)} %get-tuple-element.62), channel_id=1, source_target_pairs={{0,130},{1,13},{2,128},{3,15},{4,134},{5,9},{6,132},{7,11},{8,138}... | collective-permute-start | bytes 393224 | tf_op jit(solution)/shard_map/ppermute | solution.py:59
  54.4 5.0 %collective-permute-start.16 = (bf16[64,512]{1,0:T(8,128)(2,1)S(1)}, bf16[64,512]{1,0:T(8,128)(2,1)S(1)}, u32[]{:S(2)}, u32[]{:S(2)}) collective-permute-start(bf16[64,512]{1,0:T(8,128)(2,1)S(1)} %bitcast.85), channel_id=1, source_target_pairs={{0,130},{1,13},{2,128},{3,15},{4,134},{5,9},{6,132},{7,11},{8,138}... | collective-permute-start | bytes 196616 | tf_op jit(solution)/shard_map/ppermute | solution.py:59
  56.7 5.5 %collective-permute-start.13 = (bf16[64,512]{1,0:T(8,128)(2,1)S(1)}, bf16[64,512]{1,0:T(8,128)(2,1)S(1)}, u32[]{:S(2)}, u32[]{:S(2)}) collective-permute-start(bf16[64,512]{1,0:T(8,128)(2,1)S(1)} %fusion.17), channel_id=1, source_target_pairs={{0,16},{1,17},{2,18},{3,19},{4,20},{5,21},{6,22},{7,23},{8,24},{9,... | collective-permute-start | bytes 196616 | tf_op jit(solution)/shard_map/ppermute | solution.py:63
  59.5 5.4 %collective-permute-start.21 = (bf16[64,512]{1,0:T(8,128)(2,1)S(1)}, bf16[64,512]{1,0:T(8,128)(2,1)S(1)}, u32[]{:S(2)}, u32[]{:S(2)}) collective-permute-start(bf16[64,512]{1,0:T(8,128)(2,1)S(1)} %fusion.15), channel_id=1, source_target_pairs={{0,48},{1,49},{2,50},{3,51},{4,52},{5,53},{6,54},{7,55},{8,56},{9,... | collective-permute-start | bytes 196616 | tf_op jit(solution)/shard_map/ppermute | solution.py:63
  65.7 6.0 %collective-permute-start.22 = (bf16[64,512]{1,0:T(8,128)(2,1)S(1)}, bf16[64,512]{1,0:T(8,128)(2,1)S(1)}, u32[]{:S(2)}, u32[]{:S(2)}) collective-permute-start(bf16[64,512]{1,0:T(8,128)(2,1)S(1)} %fusion.21), channel_id=1, source_target_pairs={{0,112},{1,113},{2,114},{3,115},{4,116},{5,117},{6,118},{7,119},{8... | collective-permute-start | bytes 196616 | tf_op jit(solution)/shard_map/ppermute | solution.py:63
  72.0 5.0 %collective-permute-start.37 = (bf16[64,512]{1,0:T(8,128)(2,1)S(1)}, bf16[64,512]{1,0:T(8,128)(2,1)S(1)}, u32[]{:S(2)}, u32[]{:S(2)}) collective-permute-start(bf16[64,512]{1,0:T(8,128)(2,1)S(1)} %fusion.12), channel_id=1, source_target_pairs={{0,48},{1,49},{2,50},{3,51},{4,52},{5,53},{6,54},{7,55},{8,56},{9,... | collective-permute-start | bytes 196616 | tf_op jit(solution)/shard_map/ppermute | solution.py:63
  80.2 5.1 %collective-permute-start.24 = (bf16[2,64,512]{2,1,0:T(8,128)(2,1)S(1)}, bf16[2,64,512]{2,1,0:T(8,128)(2,1)S(1)}, u32[]{:S(2)}, u32[]{:S(2)}) collective-permute-start(bf16[2,64,512]{2,1,0:T(8,128)(2,1)S(1)} %join.12.here), channel_id=1, source_target_pairs={{0,130},{1,13},{2,128},{3,15},{4,134},{5,9},{6,132},{7,11},{8,138}... | collective-permute-start | bytes 393224 | tf_op jit(solution)/shard_map/ppermute | solution.py:59
  81.7 5.0 %collective-permute-start.39 = (bf16[2,64,512]{2,1,0:T(8,128)(2,1)S(1)}, bf16[2,64,512]{2,1,0:T(8,128)(2,1)S(1)}, u32[]{:S(2)}, u32[]{:S(2)}) collective-permute-start(bf16[2,64,512]{2,1,0:T(8,128)(2,1)S(1)} %join.21.here), channel_id=1, source_target_pairs={{0,4},{1,3},{2,6},{3,1},{4,0},{5,7},{6,2},{7,5},{8,12},{9,11},{10,... | collective-permute-start | bytes 393224 | tf_op jit(solution)/shard_map/ppermute | solution.py:59
  82.8 5.3 %collective-permute-start.34 = (bf16[2,64,512]{2,1,0:T(8,128)(2,1)S(1)}, bf16[2,64,512]{2,1,0:T(8,128)(2,1)S(1)}, u32[]{:S(2)}, u32[]{:S(2)}) collective-permute-start(bf16[2,64,512]{2,1,0:T(8,128)(2,1)S(1)} %join.18.here), channel_id=1, source_target_pairs={{0,12},{1,131},{2,14},{3,129},{4,8},{5,135},{6,10},{7,133},{8,4},{... | collective-permute-start | bytes 393224 | tf_op jit(solution)/shard_map/ppermute | solution.py:59
  85.4 6.0 %collective-permute-start.25 = (bf16[4,64,512]{2,1,0:T(8,128)(2,1)S(1)}, bf16[4,64,512]{2,1,0:T(8,128)(2,1)S(1)}, u32[]{:S(2)}, u32[]{:S(2)}) collective-permute-start(bf16[4,64,512]{2,1,0:T(8,128)(2,1)S(1)} %join.13.here), channel_id=1, source_target_pairs={{0,4},{1,3},{2,6},{3,1},{4,0},{5,7},{6,2},{7,5},{8,12},{9,11},{10,... | collective-permute-start | bytes 786440 | tf_op jit(solution)/shard_map/ppermute | solution.py:59
  86.8 6.5 %collective-permute-start.40 = (bf16[4,64,512]{2,1,0:T(8,128)(2,1)S(1)}, bf16[4,64,512]{2,1,0:T(8,128)(2,1)S(1)}, u32[]{:S(2)}, u32[]{:S(2)}) collective-permute-start(bf16[4,64,512]{2,1,0:T(8,128)(2,1)S(1)} %join.22.here), channel_id=1, source_target_pairs={{0,130},{1,13},{2,128},{3,15},{4,134},{5,9},{6,132},{7,11},{8,138}... | collective-permute-start | bytes 786440 | tf_op jit(solution)/shard_map/ppermute | solution.py:59
  88.2 6.5 %collective-permute-start.35 = (bf16[4,64,512]{2,1,0:T(8,128)(2,1)S(1)}, bf16[4,64,512]{2,1,0:T(8,128)(2,1)S(1)}, u32[]{:S(2)}, u32[]{:S(2)}) collective-permute-start(bf16[4,64,512]{2,1,0:T(8,128)(2,1)S(1)} %join.19.here), channel_id=1, source_target_pairs={{0,2},{1,5},{2,0},{3,7},{4,6},{5,1},{6,4},{7,3},{8,10},{9,13},{10,... | collective-permute-start | bytes 786440 | tf_op jit(solution)/shard_map/ppermute | solution.py:59
  88.5 7.8 %collective-permute-start.30 = (bf16[4,64,512]{2,1,0:T(8,128)(2,1)S(1)}, bf16[4,64,512]{2,1,0:T(8,128)(2,1)S(1)}, u32[]{:S(2)}, u32[]{:S(2)}) collective-permute-start(bf16[4,64,512]{2,1,0:T(8,128)(2,1)S(1)} %join.16.here), channel_id=1, source_target_pairs={{0,12},{1,131},{2,14},{3,129},{4,8},{5,135},{6,10},{7,133},{8,4},{... | collective-permute-start | bytes 786440 | tf_op jit(solution)/shard_map/ppermute | solution.py:59
  91.4 11.0 %collective-permute-start.26 = (bf16[8,64,512]{2,1,0:T(8,128)(2,1)S(1)}, bf16[8,64,512]{2,1,0:T(8,128)(2,1)S(1)}, u32[]{:S(2)}, u32[]{:S(2)}) collective-permute-start(bf16[8,64,512]{2,1,0:T(8,128)(2,1)S(1)} %join.14.refs_0_), channel_id=1, source_target_pairs={{0,2},{1,5},{2,0},{3,7},{4,6},{5,1},{6,4},{7,3},{8,10},{9,13},{10,... | collective-permute-start | bytes 1572872 | tf_op jit(solution)/shard_map/ppermute | solution.py:59
  93.4 9.3 %collective-permute-start.41 = (bf16[8,64,512]{2,1,0:T(8,128)(2,1)S(1)}, bf16[8,64,512]{2,1,0:T(8,128)(2,1)S(1)}, u32[]{:S(2)}, u32[]{:S(2)}) collective-permute-start(bf16[8,64,512]{2,1,0:T(8,128)(2,1)S(1)} %join.23.refs_6_), channel_id=1, source_target_pairs={{0,12},{1,131},{2,14},{3,129},{4,8},{5,135},{6,10},{7,133},{8,4},{... | collective-permute-start | bytes 1572872 | tf_op jit(solution)/shard_map/ppermute | solution.py:59
  94.7 10.2 %collective-permute-start.36 = (bf16[8,64,512]{2,1,0:T(8,128)(2,1)S(1)}, bf16[8,64,512]{2,1,0:T(8,128)(2,1)S(1)}, u32[]{:S(2)}, u32[]{:S(2)}) collective-permute-start(bf16[8,64,512]{2,1,0:T(8,128)(2,1)S(1)} %join.20.refs_4_), channel_id=1, source_target_pairs={{0,4},{1,3},{2,6},{3,1},{4,0},{5,7},{6,2},{7,5},{8,12},{9,11},{10,... | collective-permute-start | bytes 1572872 | tf_op jit(solution)/shard_map/ppermute | solution.py:59
  96.2 10.0 %collective-permute-start.31 = (bf16[8,64,512]{2,1,0:T(8,128)(2,1)S(1)}, bf16[8,64,512]{2,1,0:T(8,128)(2,1)S(1)}, u32[]{:S(2)}, u32[]{:S(2)}) collective-permute-start(bf16[8,64,512]{2,1,0:T(8,128)(2,1)S(1)} %join.17.refs_2_), channel_id=1, source_target_pairs={{0,130},{1,13},{2,128},{3,15},{4,134},{5,9},{6,132},{7,11},{8,138}... | collective-permute-start | bytes 1572872 | tf_op jit(solution)/shard_map/ppermute | solution.py:59
  109.9 14.7 %collective-permute-start.42 = (bf16[256,512]{1,0:T(8,128)(2,1)S(1)}, bf16[256,512]{1,0:T(8,128)(2,1)S(1)}, u32[]{:S(2)}, u32[]{:S(2)}) collective-permute-start(bf16[256,512]{1,0:T(8,128)(2,1)S(1)} %get-tuple-element.86), channel_id=1, source_target_pairs={{0,1},{1,0},{2,3},{3,2},{4,5},{5,4},{6,7},{7,6},{8,9},{9,8},{10,11... | collective-permute-start | bytes 786440 | tf_op jit(solution)/shard_map/ppermute | solution.py:67
  (19 other events, 103.5 us)

commit v7 on v6

--- a/solution.py
+++ b/solution.py
@@ -25,7 +25,8 @@
 PARTS = 4
 ROWS = 64
 
-ORDERS = ((0, 2, 1, 3), (1, 3, 0, 2), (2, 0, 3, 1), (3, 1, 2, 0))
+ORDERS = ((0, 2, 1, 3), (1, 3, 0, 2), (2, 0, 1, 3), (3, 1, 0, 2))
+COUPLES = ((0, 2, 1, 3), (1, 3, 0, 2))
 
 
 def moves(change):
@@ -59,6 +60,15 @@
     return lax.ppermute(array, AXES, PAIRINGS[pairing])
 
 
+def around(couple, first, second):
+    both = moves(lambda *here: pair(first, *pair(second, *here)))
+    return [
+        across(couple[1], second),
+        across(couple[2], first),
+        lax.ppermute(couple[3], AXES, both),
+    ]
+
+
 def z_swap(array, mask):
     return lax.ppermute(array, AXES, moves(lambda xh, z, y, xl, c: (xh, z ^ mask, y, xl, c)))
 
@@ -110,17 +120,15 @@
         copy.wait()
 
 
-def theirs_of(source, packed, sems, pieces=1):
+def theirs_of(source, packed, sems):
     where = place()
-    rows = TOK // pieces
     return [
         pltpu.make_async_copy(
-            source.at[pl.ds(i * rows, rows), columns_of(where, r, 1 - where[4])],
-            packed.at[pl.ds(i * rows, rows), pl.ds(r * BLOCK, BLOCK)],
-            sems.at[r * pieces + i],
+            source.at[:, columns_of(where, r, 1 - where[4])],
+            packed.at[:, pl.ds(r * BLOCK, BLOCK)],
+            sems.at[r],
         )
         for r in range(BLOCKS)
-        for i in range(pieces)
     ]
 
 
@@ -128,16 +136,13 @@
 
 
 DONE = jax.ShapeDtypeStruct((8, 128), jnp.float32)
-
-
-PIECES = 4
 
 
 def pack_acts_kernel(acts, grads, packed, done, sems):
     done[...] = jnp.zeros_like(done)
     run_all(
-        theirs_of(acts, packed, sems, PIECES)
-        + [pltpu.make_async_copy(grads, packed.at[:, pl.ds(HALF, COLS)], sems.at[BLOCKS * PIECES])]
+        theirs_of(acts, packed, sems)
+        + [pltpu.make_async_copy(grads, packed.at[:, pl.ds(HALF, COLS)], sems.at[BLOCKS])]
     )
 
 
@@ -147,7 +152,7 @@
         out_shape=(jax.ShapeDtypeStruct((TOK, HALF + COLS), jnp.bfloat16), DONE),
         in_specs=[ANY, ANY],
         out_specs=(VMEM, VMEM),
-        scratch_shapes=[pltpu.SemaphoreType.DMA((BLOCKS * PIECES + 1,))],
+        scratch_shapes=[pltpu.SemaphoreType.DMA((BLOCKS + 1,))],
         compiler_params=WHOLE,
         cost_estimate=cost(0, 4 << 20),
         name="pack_acts",
@@ -269,6 +274,49 @@
         cost_estimate=cost(n * blocks << 15, n * blocks * 3 << 16),
         name="add_halves",
     )(*pairs, *after, *through)
+
+
+def couple_kernel(*refs):
+    outs = refs[-4 * len(COUPLES) :]
+    for c, parts in enumerate(COUPLES):
+        for j, m in enumerate(parts[:2]):
+            keep, got = refs[2 * m : 2 * m + 2]
+            for i in range(4):
+                outs[4 * c + i][j] = (
+                    keep[i].astype(jnp.float32) + got[i].astype(jnp.float32)
+                ).astype(jnp.bfloat16)
+
+
+def add_couples(pairs, after):
+    block = jax.ShapeDtypeStruct((2, ROWS, COLS), jnp.bfloat16)
+    return pl.pallas_call(
+        couple_kernel,
+        out_shape=(block,) * (4 * len(COUPLES)),
+        in_specs=[VMEM] * len(pairs) + [ANY],
+        out_specs=(VMEM,) * (4 * len(COUPLES)),
+        compiler_params=PARAMS,
+        cost_estimate=cost(1 << 19, 3 << 20),
+        name="add_couples",
+    )(*pairs, after)
+
+
+def spread_kernel(*refs):
+    for i in range(4):
+        for j in range(2):
+            refs[4 + j][i] = refs[i][j]
+
+
+def spread(couple):
+    part = jax.ShapeDtypeStruct((4, ROWS, COLS), jnp.bfloat16)
+    return pl.pallas_call(
+        spread_kernel,
+        out_shape=(part,) * 2,
+        in_specs=[VMEM] * 4,
+        out_specs=(VMEM,) * 2,
+        compiler_params=PARAMS,
+        cost_estimate=cost(0, 1 << 20),
+        name="spread",
+    )(*couple)
 
 
 def join_kernel(dim, here, got, both):
@@ -415,14 +463,18 @@
         dims.append(w - (v < w))
     *sums, packed_tokens = add_halves(pairs, dims, (state,), (packed_tokens,))
     tokens = core_swap(packed_tokens)
-    parts = []
-    for m, (_, w, p, q) in enumerate(ORDERS):
-        keep, send = sums[2 * m : 2 * m + 2]
-        keep, send = add_halves([keep, across(send, w)], [int(p > q)])
-        keep, send = add_halves([keep, across(send, p)], [0], () if m else (tokens,))
-        total = wide(keep[0]) + wide(across(send[0], q))
-        parts.append(total.astype(jnp.bfloat16) if m else total)
-    return parts, tokens
+    pairs = []
+    for m, (_, w, _, _) in enumerate(ORDERS):
+        pairs += [sums[2 * m], across(sums[2 * m + 1], w)]
+    blocks = add_couples(pairs, tokens)
+    parts = [None] * PARTS
+    for c, (a, b, first, second) in enumerate(COUPLES):
+        couple = blocks[4 * c : 4 * c + 4]
+        total = wide(couple[0])
+        for got in around(couple, first, second):
+            total = total + wide(got)
+        parts[a], parts[b] = total[0], total[1]
+    return [parts[0]] + [part.astype(jnp.bfloat16) for part in parts[1:]], tokens
 
 
 def reduce_z(parts):
@@ -434,12 +486,14 @@
 
 
 def gather_parts(rows):
-    halves = []
-    for m, (v, w, p, q) in enumerate(ORDERS):
-        part = (z_swap(rows, m) if m else rows)[None]
-        for bit, dim in ((q, 0), (p, sorted((p, q)).index(p)), (w, w - (v < w))):
-            part = join(part, across(part, bit), dim)
-        halves += [part, across(part, v)]
+    halves = [None] * (2 * PARTS)
+    for a, b, first, second in COUPLES:
+        couple = jnp.stack([z_swap(rows, m) if m else rows for m in (a, b)])
+        parts = spread([couple] + around([couple] * 4, first, second))
+        for m, part in zip((a, b), parts):
+            v, w = ORDERS[m][:2]
+            part = join(part, across(part, w), w - (v < w))
+            halves[2 * m : 2 * m + 2] = [part, across(part, v)]
     return halves
 
 

time: 126 us -> 132 us (1.048)
  waiting for transfers between devices: 41.7 us -> 53.2 us
  starting transfers between devices: 60.7 us -> 55.7 us
    ppermute x32 -> x24, starting transfers between devices: 27.6 us -> 17.6 us  [across(): return lax.ppermute(array, AXES, PAIRINGS[pairing])]
    ppermute x0 -> x4, starting transfers between devices: none -> 9.89 us  [around(): lax.ppermute(couple[3], AXES, both)]
    ppermute x0 -> x4, waiting for transfers between devices: none -> 7.26 us  [around(): lax.ppermute(couple[3], AXES, both)]
    ppermute x3, starting transfers between devices: 17.8 us -> 13.9 us  [core_swap(): lax.ppermute(array, AXES, moves(lambda xh, z, y, xl, c: (xh, z, y, xl, 1...]
    ppermute x8, waiting for transfers between devices: 15.8 us -> 18.4 us  [z_swap(): lax.ppermute(array, AXES, moves(lambda xh, z, y, xl, c: (xh, z ^ mask, y,...]
    ppermute x32 -> x24, waiting for transfers between devices: 25.3 us -> 26.9 us  [across(): return lax.ppermute(array, AXES, PAIRINGS[pairing])]
  transfers between devices with their start and end apart: 43 -> 39, of which waited for: 25 -> 19; matrix products, arithmetic and copies ran while one was open for 1% -> 1% of each run, Pallas kernels for 1% -> 1%
where the time goes in v7:
time: 132 us; the launch traced here: 131 us
  starting transfers between devices  55.7 us (42%)
  waiting for transfers between devices  53.2 us (40%)
  Pallas kernels  15.4 us (12%)
  local copies, waits for them, and re-layouts  3.62 us (3%)
  other arithmetic  2.55 us (2%)
    ppermute x24, waiting for transfers between devices, across(): return lax.ppermute(array, AXES, PAIRINGS[pairing])  26.9 us
    ppermute x8, waiting for transfers between devices, z_swap(): lax.ppermute(array, AXES, moves(lambda xh, z, y, xl, c: (xh, z ^ mask, y,...  18.4 us
    ppermute x24, starting transfers between devices, across(): return lax.ppermute(array, AXES, PAIRINGS[pairing])  17.6 us
    ppermute x8, starting transfers between devices, z_swap(): lax.ppermute(array, AXES, moves(lambda xh, z, y, xl, c: (xh, z ^ mask, y,...  14.3 us
    ppermute x3, starting transfers between devices, core_swap(): lax.ppermute(array, AXES, moves(lambda xh, z, y, xl, c: (xh, z, y, xl, 1...  13.9 us
    ppermute x4, starting transfers between devices, around(): lax.ppermute(couple[3], AXES, both)  9.89 us
    ppermute x4, waiting for transfers between devices, around(): lax.ppermute(couple[3], AXES, both)  7.26 us
    pallas_call x1, Pallas kernels, gradient_term(): pl.pallas_call(term_kernel, out_shape=(half,) * (2 * PARTS), in_specs=[AN...  6.59 us
  transfers between devices with their start and end apart: 39, of which 19 were waited for; matrix products, arithmetic and copies ran while one was open for 1% of the time, Pallas kernels for 1%

profile of v7, /device:TPU:1, one launch (start us, length us, event | category | flops | bytes accessed | tf_op | source)
XLA Modules:
  0.0 131.4 jit_solution(13159628304219950719)
XLA Ops:
  0.7 3.4 %pack_acts.1 = (bf16[256,4608]{1,0:T(8,128)(2,1)}, f32[8,128]{1,0:T(8,128)}) custom-call(bf16[256,8192]{1,0:T(8,128)(2,1)} %acts.3, bf16[256,512]{1,0:T(8,128)(2,1)} %grads.3), custom_call_target="tpu_custom_call" | custom-call | bytes 4194304 | tf_op jit(solution)/shard_map/pack_acts/pallas_call | solution.py:150
  4.1 3.3 %collective-permute-start.1 = (bf16[256,4608]{1,0:T(8,128)(2,1)}, bf16[256,4608]{1,0:T(8,128)(2,1)S(1)}, u32[]{:S(2)}, u32[]{:S(2)}) collective-permute-start(bf16[256,4608]{1,0:T(8,128)(2,1)} %get-tuple-element.44), channel_id=1, source_target_pairs={{0,1},{1,0},{2,3},{3,2},{4,5},{5,4},{6,7},{7,6},{8,9},{9,8},{10,11... | collective-permute-start | bytes 7077896 | tf_op jit(solution)/shard_map/ppermute | solution.py:77
  7.4 2.2 %copy-done = bf16[256,8192]{1,0:T(8,128)(2,1)S(1)} copy-done((bf16[256,8192]{1,0:T(8,128)(2,1)S(1)}, bf16[256,8192]{1,0:T(8,128)(2,1)}, u32[]{:S(2)}) %copy-start) | copy-done | bytes 4194328
  12.5 6.6 %gradient_term.1 = (bf16[8,64,512]{2,1,0:T(8,128)(2,1)S(1)}, bf16[8,64,512]{2,1,0:T(8,128)(2,1)S(1)}, bf16[8,64,512]{2,1,0:T(8,128)(2,1)S(1)}, bf16[8,64,512]{2,...) custom-call(bf16[256,8192]{1,0:T(8,128)(2,1)S(1)} %copy-done.2, ...), custom_call_target="tpu_custom_call" | custom-call | flops 2147483648 | bytes 9437184 | tf_op jit(solution)/shard_map/gradient_term/pallas_call | solution.py:234
  19.2 1.4 %collective-permute-start.3 = (bf16[8,64,512]{2,1,0:T(8,128)(2,1)S(1)}, bf16[8,64,512]{2,1,0:T(8,128)(2,1)S(1)}, u32[]{:S(2)}, u32[]{:S(2)}) collective-permute-start(bf16[8,64,512]{2,1,0:T(8,128)(2,1)S(1)} %get-tuple-element.49), channel_id=1, source_target_pairs={{0,130},{1,13},{2,128},{3,15},{4,134},{5,9},{6,132},{7,11},{8,138}... | collective-permute-start | bytes 1572872 | tf_op jit(solution)/shard_map/ppermute | solution.py:60
  21.8 1.8 %collective-permute-start.5 = (bf16[8,64,512]{2,1,0:T(8,128)(2,1)S(1)}, bf16[8,64,512]{2,1,0:T(8,128)(2,1)S(1)}, u32[]{:S(2)}, u32[]{:S(2)}) collective-permute-start(bf16[8,64,512]{2,1,0:T(8,128)(2,1)S(1)} %get-tuple-element.53), channel_id=1, source_target_pairs={{0,12},{1,131},{2,14},{3,129},{4,8},{5,135},{6,10},{7,133},{8,4},{... | collective-permute-start | bytes 1572872 | tf_op jit(solution)/shard_map/ppermute | solution.py:60
  23.6 5.6 %collective-permute-start = (f32[3,32,512]{2,1,0:T(8,128)S(1)}, f32[3,32,512]{2,1,0:T(8,128)S(1)}, u32[]{:S(2)}, u32[]{:S(2)}) collective-permute-start(f32[3,32,512]{2,1,0:T(8,128)S(1)} %get-tuple-element.43), channel_id=1, source_target_pairs={{0,112},{1,113},{2,114},{3,115},{4,116},{5,117},{6,118},{7,119},{8... | collective-permute-start | bytes 589832 | tf_op jit(solution)/shard_map/ppermute | solution.py:73
  29.2 9.1 %collective-permute-done.refs_8_ = f32[3,32,512]{2,1,0:T(8,128)S(1)} collective-permute-done((f32[3,32,512]{2,1,0:T(8,128)S(1)}, f32[3,32,512]{2,1,0:T(8,128)S(1)}, u32[]{:S(2)}, u32[]{:S(2)}) %collective-permute-start) | collective-permute-done | bytes 196640 | tf_op jit(solution)/shard_map/ppermute | solution.py:73
  41.8 4.2 %collective-permute-done.6.refs_1_ = bf16[4,64,512]{2,1,0:T(8,128)(2,1)S(1)} collective-permute-done((bf16[4,64,512]{2,1,0:T(8,128)(2,1)S(1)}, bf16[4,64,512]{2,1,0:T(8,128)(2,1)S(1)}, u32[]{:S(2)}, u32[]{:S(2)}) %collective-permute-start.6) | collective-permute-done | bytes 262176 | tf_op jit(solution)/shard_map/ppermute | solution.py:60
  47.2 1.5 %collective-permute-done.8.refs_5_ = bf16[4,64,512]{2,1,0:T(8,128)(2,1)S(1)} collective-permute-done((bf16[4,64,512]{2,1,0:T(8,128)(2,1)S(1)}, bf16[4,64,512]{2,1,0:T(8,128)(2,1)S(1)}, u32[]{:S(2)}, u32[]{:S(2)}) %collective-permute-start.8) | collective-permute-done | bytes 262176 | tf_op jit(solution)/shard_map/ppermute | solution.py:60
  48.7 1.8 %collective-permute-done.9.refs_7_ = bf16[4,64,512]{2,1,0:T(8,128)(2,1)S(1)} collective-permute-done((bf16[4,64,512]{2,1,0:T(8,128)(2,1)S(1)}, bf16[4,64,512]{2,1,0:T(8,128)(2,1)S(1)}, u32[]{:S(2)}, u32[]{:S(2)}) %collective-permute-start.9) | collective-permute-done | bytes 262176 | tf_op jit(solution)/shard_map/ppermute | solution.py:60
  51.2 2.5 %collective-permute-start.16 = (bf16[2,64,512]{2,1,0:T(8,128)(2,1)S(1)}, bf16[2,64,512]{2,1,0:T(8,128)(2,1)S(1)}, u32[]{:S(2)}, u32[]{:S(2)}) collective-permute-start(bf16[2,64,512]{2,1,0:T(8,128)(2,1)S(1)} %get-tuple-element.71), channel_id=1, source_target_pairs={{0,6},{1,7},{2,4},{3,5},{4,2},{5,3},{6,0},{7,1},{8,14},{9,15},{10,... | collective-permute-start | bytes 393224 | tf_op jit(solution)/shard_map/ppermute | solution.py:68
  55.5 3.2 %collective-permute-start.13 = (bf16[2,64,512]{2,1,0:T(8,128)(2,1)S(1)}, bf16[2,64,512]{2,1,0:T(8,128)(2,1)S(1)}, u32[]{:S(2)}, u32[]{:S(2)}) collective-permute-start(bf16[2,64,512]{2,1,0:T(8,128)(2,1)S(1)} %get-tuple-element.67), channel_id=1, source_target_pairs={{0,142},{1,143},{2,140},{3,141},{4,138},{5,139},{6,136},{7,137},{8... | collective-permute-start | bytes 393224 | tf_op jit(solution)/shard_map/ppermute | solution.py:68
  59.0 1.7 %collective-permute-start.19 = (bf16[64,512]{1,0:T(8,128)(2,1)S(1)}, bf16[64,512]{1,0:T(8,128)(2,1)S(1)}, u32[]{:S(2)}, u32[]{:S(2)}) collective-permute-start(bf16[64,512]{1,0:T(8,128)(2,1)S(1)} %get-tuple-element.88), channel_id=1, source_target_pairs={{0,48},{1,49},{2,50},{3,51},{4,52},{5,53},{6,54},{7,55},{8,56},{9,... | collective-permute-start | bytes 196616 | tf_op jit(solution)/shard_map/ppermute | solution.py:73
  60.7 3.1 %collective-permute-done.13 = bf16[2,64,512]{2,1,0:T(8,128)(2,1)S(1)} collective-permute-done((bf16[2,64,512]{2,1,0:T(8,128)(2,1)S(1)}, bf16[2,64,512]{2,1,0:T(8,128)(2,1)S(1)}, u32[]{:S(2)}, u32[]{:S(2)}) %collective-permute-start.13) | collective-permute-done | bytes 131104 | tf_op jit(solution)/shard_map/ppermute | solution.py:68
  64.1 4.9 %collective-permute-done.18 = bf16[64,512]{1,0:T(8,128)(2,1)S(1)} collective-permute-done((bf16[64,512]{1,0:T(8,128)(2,1)S(1)}, bf16[64,512]{1,0:T(8,128)(2,1)S(1)}, u32[]{:S(2)}, u32[]{:S(2)}) %collective-permute-start.18) | collective-permute-done | bytes 65568 | tf_op jit(solution)/shard_map/ppermute | solution.py:73
  69.0 4.0 %collective-permute-start.20 = (bf16[64,512]{1,0:T(8,128)(2,1)S(1)}, bf16[64,512]{1,0:T(8,128)(2,1)S(1)}, u32[]{:S(2)}, u32[]{:S(2)}) collective-permute-start(bf16[64,512]{1,0:T(8,128)(2,1)S(1)} %fusion.15), channel_id=1, source_target_pairs={{0,112},{1,113},{2,114},{3,115},{4,116},{5,117},{6,118},{7,119},{8... | collective-permute-start | bytes 196616 | tf_op jit(solution)/shard_map/ppermute | solution.py:73
  73.0 1.6 %collective-permute-done.20 = bf16[64,512]{1,0:T(8,128)(2,1)S(1)} collective-permute-done((bf16[64,512]{1,0:T(8,128)(2,1)S(1)}, bf16[64,512]{1,0:T(8,128)(2,1)S(1)}, u32[]{:S(2)}, u32[]{:S(2)}) %collective-permute-start.20) | collective-permute-done | bytes 65568 | tf_op jit(solution)/shard_map/ppermute | solution.py:73
  75.2 1.5 %collective-permute-start.28 = (bf16[64,512]{1,0:T(8,128)(2,1)S(1)}, bf16[64,512]{1,0:T(8,128)(2,1)S(1)}, u32[]{:S(2)}, u32[]{:S(2)}) collective-permute-start(bf16[64,512]{1,0:T(8,128)(2,1)S(1)} %fusion.16), channel_id=1, source_target_pairs={{0,48},{1,49},{2,50},{3,51},{4,52},{5,53},{6,54},{7,55},{8,56},{9,... | collective-permute-start | bytes 196616 | tf_op jit(solution)/shard_map/ppermute | solution.py:73
  78.4 2.0 %collective-permute-done.28 = bf16[64,512]{1,0:T(8,128)(2,1)S(1)} collective-permute-done((bf16[64,512]{1,0:T(8,128)(2,1)S(1)}, bf16[64,512]{1,0:T(8,128)(2,1)S(1)}, u32[]{:S(2)}, u32[]{:S(2)}) %collective-permute-start.28) | collective-permute-done | bytes 65568 | tf_op jit(solution)/shard_map/ppermute | solution.py:73
  80.6 2.5 %collective-permute-start.31 = (bf16[2,64,512]{2,1,0:T(8,128)(2,1)S(1)}, bf16[2,64,512]{2,1,0:T(8,128)(2,1)S(1)}, u32[]{:S(2)}, u32[]{:S(2)}) collective-permute-start(bf16[2,64,512]{2,1,0:T(8,128)(2,1)S(1)} %pad_maximum_fusion.2.refs_0_), channel_id=1, source_target_pairs={{0,6},{1,7},{2,4},{3,5},{4,2},{5,3},{6,0},{7,1},{8,14},{9,15},{10,... | collective-permute-start | bytes 393224 | tf_op jit(solution)/shard_map/ppermute | solution.py:68
  83.2 1.5 %collective-permute-start.22 = (bf16[2,64,512]{2,1,0:T(8,128)(2,1)S(1)}, bf16[2,64,512]{2,1,0:T(8,128)(2,1)S(1)}, u32[]{:S(2)}, u32[]{:S(2)}) collective-permute-start(bf16[2,64,512]{2,1,0:T(8,128)(2,1)S(1)} %pad_maximum_fusion.1.refs_0_), channel_id=1, source_target_pairs={{0,12},{1,131},{2,14},{3,129},{4,8},{5,135},{6,10},{7,133},{8,4},{... | collective-permute-start | bytes 393224 | tf_op jit(solution)/shard_map/ppermute | solution.py:60
  84.6 2.1 %collective-permute-start.23 = (bf16[2,64,512]{2,1,0:T(8,128)(2,1)S(1)}, bf16[2,64,512]{2,1,0:T(8,128)(2,1)S(1)}, u32[]{:S(2)}, u32[]{:S(2)}) collective-permute-start(bf16[2,64,512]{2,1,0:T(8,128)(2,1)S(1)} %pad_maximum_fusion.1.refs_0_), channel_id=1, source_target_pairs={{0,130},{1,13},{2,128},{3,15},{4,134},{5,9},{6,132},{7,11},{8,138}... | collective-permute-start | bytes 393224 | tf_op jit(solution)/shard_map/ppermute | solution.py:60
  86.7 1.6 %collective-permute-start.24 = (bf16[2,64,512]{2,1,0:T(8,128)(2,1)S(1)}, bf16[2,64,512]{2,1,0:T(8,128)(2,1)S(1)}, u32[]{:S(2)}, u32[]{:S(2)}) collective-permute-start(bf16[2,64,512]{2,1,0:T(8,128)(2,1)S(1)} %pad_maximum_fusion.1.refs_0_), channel_id=1, source_target_pairs={{0,142},{1,143},{2,140},{3,141},{4,138},{5,139},{6,136},{7,137},{8... | collective-permute-start | bytes 393224 | tf_op jit(solution)/shard_map/ppermute | solution.py:68
  89.8 4.2 %collective-permute-done.24.refs_3_ = bf16[2,64,512]{2,1,0:T(8,128)(2,1)S(1)} collective-permute-done((bf16[2,64,512]{2,1,0:T(8,128)(2,1)S(1)}, bf16[2,64,512]{2,1,0:T(8,128)(2,1)S(1)}, u32[]{:S(2)}, u32[]{:S(2)}) %collective-permute-start.24) | collective-permute-done | bytes 131104 | tf_op jit(solution)/shard_map/ppermute | solution.py:68
  94.7 3.3 %collective-permute-done.36.got = bf16[4,64,512]{2,1,0:T(8,128)(2,1)S(1)} collective-permute-done((bf16[4,64,512]{2,1,0:T(8,128)(2,1)S(1)}, bf16[4,64,512]{2,1,0:T(8,128)(2,1)S(1)}, u32[]{:S(2)}, u32[]{:S(2)}) %collective-permute-start.36) | collective-permute-done | bytes 262176 | tf_op jit(solution)/shard_map/ppermute | solution.py:60
  99.5 3.4 %collective-permute-done.32.got = bf16[4,64,512]{2,1,0:T(8,128)(2,1)S(1)} collective-permute-done((bf16[4,64,512]{2,1,0:T(8,128)(2,1)S(1)}, bf16[4,64,512]{2,1,0:T(8,128)(2,1)S(1)}, u32[]{:S(2)}, u32[]{:S(2)}) %collective-permute-start.32) | collective-permute-done | bytes 262176 | tf_op jit(solution)/shard_map/ppermute | solution.py:60
  103.0 2.3 %collective-permute-start.26 = (bf16[8,64,512]{2,1,0:T(8,128)(2,1)S(1)}, bf16[8,64,512]{2,1,0:T(8,128)(2,1)S(1)}, u32[]{:S(2)}, u32[]{:S(2)}) collective-permute-start(bf16[8,64,512]{2,1,0:T(8,128)(2,1)S(1)} %join.4.refs_0_), channel_id=1, source_target_pairs={{0,2},{1,5},{2,0},{3,7},{4,6},{5,1},{6,4},{7,3},{8,10},{9,13},{10,... | collective-permute-start | bytes 1572872 | tf_op jit(solution)/shard_map/ppermute | solution.py:60
  105.3 5.4 %collective-permute-done.37.refs_7_ = bf16[8,64,512]{2,1,0:T(8,128)(2,1)S(1)} collective-permute-done((bf16[8,64,512]{2,1,0:T(8,128)(2,1)S(1)}, bf16[8,64,512]{2,1,0:T(8,128)(2,1)S(1)}, u32[]{:S(2)}, u32[]{:S(2)}) %collective-permute-start.37) | collective-permute-done | bytes 524320 | tf_op jit(solution)/shard_map/ppermute | solution.py:60
  110.8 5.2 %collective-permute-done.33.refs_3_ = bf16[8,64,512]{2,1,0:T(8,128)(2,1)S(1)} collective-permute-done((bf16[8,64,512]{2,1,0:T(8,128)(2,1)S(1)}, bf16[8,64,512]{2,1,0:T(8,128)(2,1)S(1)}, u32[]{:S(2)}, u32[]{:S(2)}) %collective-permute-start.33) | collective-permute-done | bytes 524320 | tf_op jit(solution)/shard_map/ppermute | solution.py:60
  116.1 3.7 %project.1 = (bf16[512,512]{1,0:T(8,128)(2,1)}, f32[256,512]{1,0:T(8,128)S(1)}, bf16[256,512]{1,0:T(8,128)(2,1)S(1)}) custom-call(bf16[256,8192]{1,0:T(8,128)(2,1)S(1)} %copy-done.1, bf16[256,4096]{1,0:T(8,128)(2,1)S(1)} %collective-permute-done.10.refs_8_.got, bf16[8,64,512]{2,1,0:T(8,128)(2,1)S(1)} %join.4.refs_0_, ...), custom_call_target="tpu_custom_call" | custom-call | flops 2147483648 | bytes 9437184 | tf_op jit(solution)/shard_map/project/pallas_call | solution.py:414
  119.8 9.5 %collective-permute-start.38 = (bf16[256,512]{1,0:T(8,128)(2,1)S(1)}, bf16[256,512]{1,0:T(8,128)(2,1)S(1)}, u32[]{:S(2)}, u32[]{:S(2)}) collective-permute-start(bf16[256,512]{1,0:T(8,128)(2,1)S(1)} %get-tuple-element.78), channel_id=1, source_target_pairs={{0,1},{1,0},{2,3},{3,2},{4,5},{5,4},{6,7},{7,6},{8,9},{9,8},{10,11... | collective-permute-start | bytes 786440 | tf_op jit(solution)/shard_map/ppermute | solution.py:77
  (88 shorter events, 20.4 us)
Async XLA Ops:
  4.1 7.7 %collective-permute-start.1 = (bf16[256,4608]{1,0:T(8,128)(2,1)}, bf16[256,4608]{1,0:T(8,128)(2,1)S(1)}, u32[]{:S(2)}, u32[]{:S(2)}) collective-permute-start(bf16[256,4608]{1,0:T(8,128)(2,1)} %get-tuple-element.44), channel_id=1, source_target_pairs={{0,1},{1,0},{2,3},{3,2},{4,5},{5,4},{6,7},{7,6},{8,9},{9,8},{10,11... | collective-permute-start | bytes 7077896 | tf_op jit(solution)/shard_map/ppermute | solution.py:77
  19.1 19.2 %collective-permute-start.2 = (bf16[8,64,512]{2,1,0:T(8,128)(2,1)S(1)}, bf16[8,64,512]{2,1,0:T(8,128)(2,1)S(1)}, u32[]{:S(2)}, u32[]{:S(2)}) collective-permute-start(bf16[8,64,512]{2,1,0:T(8,128)(2,1)S(1)} %get-tuple-element.47), channel_id=1, source_target_pairs={{0,2},{1,5},{2,0},{3,7},{4,6},{5,1},{6,4},{7,3},{8,10},{9,13},{10,... | collective-permute-start | bytes 1572872 | tf_op jit(solution)/shard_map/ppermute | solution.py:60
  19.2 19.1 %collective-permute-start.3 = (bf16[8,64,512]{2,1,0:T(8,128)(2,1)S(1)}, bf16[8,64,512]{2,1,0:T(8,128)(2,1)S(1)}, u32[]{:S(2)}, u32[]{:S(2)}) collective-permute-start(bf16[8,64,512]{2,1,0:T(8,128)(2,1)S(1)} %get-tuple-element.49), channel_id=1, source_target_pairs={{0,130},{1,13},{2,128},{3,15},{4,134},{5,9},{6,132},{7,11},{8,138}... | collective-permute-start | bytes 1572872 | tf_op jit(solution)/shard_map/ppermute | solution.py:60
  20.6 17.7 %collective-permute-start.4 = (bf16[8,64,512]{2,1,0:T(8,128)(2,1)S(1)}, bf16[8,64,512]{2,1,0:T(8,128)(2,1)S(1)}, u32[]{:S(2)}, u32[]{:S(2)}) collective-permute-start(bf16[8,64,512]{2,1,0:T(8,128)(2,1)S(1)} %get-tuple-element.51), channel_id=1, source_target_pairs={{0,4},{1,3},{2,6},{3,1},{4,0},{5,7},{6,2},{7,5},{8,12},{9,11},{10,... | collective-permute-start | bytes 1572872 | tf_op jit(solution)/shard_map/ppermute | solution.py:60
  21.8 16.5 %collective-permute-start.5 = (bf16[8,64,512]{2,1,0:T(8,128)(2,1)S(1)}, bf16[8,64,512]{2,1,0:T(8,128)(2,1)S(1)}, u32[]{:S(2)}, u32[]{:S(2)}) collective-permute-start(bf16[8,64,512]{2,1,0:T(8,128)(2,1)S(1)} %get-tuple-element.53), channel_id=1, source_target_pairs={{0,12},{1,131},{2,14},{3,129},{4,8},{5,135},{6,10},{7,133},{8,4},{... | collective-permute-start | bytes 1572872 | tf_op jit(solution)/shard_map/ppermute | solution.py:60
  23.6 14.7 %collective-permute-start = (f32[3,32,512]{2,1,0:T(8,128)S(1)}, f32[3,32,512]{2,1,0:T(8,128)S(1)}, u32[]{:S(2)}, u32[]{:S(2)}) collective-permute-start(f32[3,32,512]{2,1,0:T(8,128)S(1)} %get-tuple-element.43), channel_id=1, source_target_pairs={{0,112},{1,113},{2,114},{3,115},{4,116},{5,117},{6,118},{7,119},{8... | collective-permute-start | bytes 589832 | tf_op jit(solution)/shard_map/ppermute | solution.py:73
  38.8 11.8 %collective-permute-start.10 = (bf16[256,4096]{1,0:T(8,128)(2,1)S(1)}, bf16[256,4096]{1,0:T(8,128)(2,1)S(1)}, u32[]{:S(2)}, u32[]{:S(2)}) collective-permute-start(bf16[256,4096]{1,0:T(8,128)(2,1)S(1)} %get-tuple-element.63), channel_id=1, source_target_pairs={{0,1},{1,0},{2,3},{3,2},{4,5},{5,4},{6,7},{7,6},{8,9},{9,8},{10,11... | collective-permute-start | bytes 6291464 | tf_op jit(solution)/shard_map/ppermute | solution.py:77
  39.8 6.1 %collective-permute-start.6 = (bf16[4,64,512]{2,1,0:T(8,128)(2,1)S(1)}, bf16[4,64,512]{2,1,0:T(8,128)(2,1)S(1)}, u32[]{:S(2)}, u32[]{:S(2)}) collective-permute-start(bf16[4,64,512]{2,1,0:T(8,128)(2,1)S(1)} %get-tuple-element.56), channel_id=1, source_target_pairs={{0,4},{1,3},{2,6},{3,1},{4,0},{5,7},{6,2},{7,5},{8,12},{9,11},{10,... | collective-permute-start | bytes 786440 | tf_op jit(solution)/shard_map/ppermute | solution.py:60
  40.1 7.1 %collective-permute-start.7 = (bf16[4,64,512]{2,1,0:T(8,128)(2,1)S(1)}, bf16[4,64,512]{2,1,0:T(8,128)(2,1)S(1)}, u32[]{:S(2)}, u32[]{:S(2)}) collective-permute-start(bf16[4,64,512]{2,1,0:T(8,128)(2,1)S(1)} %get-tuple-element.58), channel_id=1, source_target_pairs={{0,12},{1,131},{2,14},{3,129},{4,8},{5,135},{6,10},{7,133},{8,4},{... | collective-permute-start | bytes 786440 | tf_op jit(solution)/shard_map/ppermute | solution.py:60
  40.8 8.0 %collective-permute-start.8 = (bf16[4,64,512]{2,1,0:T(8,128)(2,1)S(1)}, bf16[4,64,512]{2,1,0:T(8,128)(2,1)S(1)}, u32[]{:S(2)}, u32[]{:S(2)}) collective-permute-start(bf16[4,64,512]{2,1,0:T(8,128)(2,1)S(1)} %get-tuple-element.60), channel_id=1, source_target_pairs={{0,2},{1,5},{2,0},{3,7},{4,6},{5,1},{6,4},{7,3},{8,10},{9,13},{10,... | collective-permute-start | bytes 786440 | tf_op jit(solution)/shard_map/ppermute | solution.py:60
  41.2 9.4 %collective-permute-start.9 = (bf16[4,64,512]{2,1,0:T(8,128)(2,1)S(1)}, bf16[4,64,512]{2,1,0:T(8,128)(2,1)S(1)}, u32[]{:S(2)}, u32[]{:S(2)}) collective-permute-start(bf16[4,64,512]{2,1,0:T(8,128)(2,1)S(1)} %get-tuple-element.62), channel_id=1, source_target_pairs={{0,130},{1,13},{2,128},{3,15},{4,134},{5,9},{6,132},{7,11},{8,138}... | collective-permute-start | bytes 786440 | tf_op jit(solution)/shard_map/ppermute | solution.py:60
  51.1 7.6 %collective-permute-start.15 = (bf16[2,64,512]{2,1,0:T(8,128)(2,1)S(1)}, bf16[2,64,512]{2,1,0:T(8,128)(2,1)S(1)}, u32[]{:S(2)}, u32[]{:S(2)}) collective-permute-start(bf16[2,64,512]{2,1,0:T(8,128)(2,1)S(1)} %get-tuple-element.70), channel_id=1, source_target_pairs={{0,2},{1,5},{2,0},{3,7},{4,6},{5,1},{6,4},{7,3},{8,10},{9,13},{10,... | collective-permute-start | bytes 393224 | tf_op jit(solution)/shard_map/ppermute | solution.py:60
  51.2 7.6 %collective-permute-start.16 = (bf16[2,64,512]{2,1,0:T(8,128)(2,1)S(1)}, bf16[2,64,512]{2,1,0:T(8,128)(2,1)S(1)}, u32[]{:S(2)}, u32[]{:S(2)}) collective-permute-start(bf16[2,64,512]{2,1,0:T(8,128)(2,1)S(1)} %get-tuple-element.71), channel_id=1, source_target_pairs={{0,6},{1,7},{2,4},{3,5},{4,2},{5,3},{6,0},{7,1},{8,14},{9,15},{10,... | collective-permute-start | bytes 393224 | tf_op jit(solution)/shard_map/ppermute | solution.py:68
  53.7 7.0 %collective-permute-start.11 = (bf16[2,64,512]{2,1,0:T(8,128)(2,1)S(1)}, bf16[2,64,512]{2,1,0:T(8,128)(2,1)S(1)}, u32[]{:S(2)}, u32[]{:S(2)}) collective-permute-start(bf16[2,64,512]{2,1,0:T(8,128)(2,1)S(1)} %get-tuple-element.65), channel_id=1, source_target_pairs={{0,12},{1,131},{2,14},{3,129},{4,8},{5,135},{6,10},{7,133},{8,4},{... | collective-permute-start | bytes 393224 | tf_op jit(solution)/shard_map/ppermute | solution.py:60
  54.4 6.3 %collective-permute-start.12 = (bf16[2,64,512]{2,1,0:T(8,128)(2,1)S(1)}, bf16[2,64,512]{2,1,0:T(8,128)(2,1)S(1)}, u32[]{:S(2)}, u32[]{:S(2)}) collective-permute-start(bf16[2,64,512]{2,1,0:T(8,128)(2,1)S(1)} %get-tuple-element.66), channel_id=1, source_target_pairs={{0,130},{1,13},{2,128},{3,15},{4,134},{5,9},{6,132},{7,11},{8,138}... | collective-permute-start | bytes 393224 | tf_op jit(solution)/shard_map/ppermute | solution.py:60
  55.5 8.2 %collective-permute-start.13 = (bf16[2,64,512]{2,1,0:T(8,128)(2,1)S(1)}, bf16[2,64,512]{2,1,0:T(8,128)(2,1)S(1)}, u32[]{:S(2)}, u32[]{:S(2)}) collective-permute-start(bf16[2,64,512]{2,1,0:T(8,128)(2,1)S(1)} %get-tuple-element.67), channel_id=1, source_target_pairs={{0,142},{1,143},{2,140},{3,141},{4,138},{5,139},{6,136},{7,137},{8... | collective-permute-start | bytes 393224 | tf_op jit(solution)/shard_map/ppermute | solution.py:68
  69.0 5.6 %collective-permute-start.20 = (bf16[64,512]{1,0:T(8,128)(2,1)S(1)}, bf16[64,512]{1,0:T(8,128)(2,1)S(1)}, u32[]{:S(2)}, u32[]{:S(2)}) collective-permute-start(bf16[64,512]{1,0:T(8,128)(2,1)S(1)} %fusion.15), channel_id=1, source_target_pairs={{0,112},{1,113},{2,114},{3,115},{4,116},{5,117},{6,118},{7,119},{8... | collective-permute-start | bytes 196616 | tf_op jit(solution)/shard_map/ppermute | solution.py:73
  76.7 6.4 %collective-permute-start.21 = (bf16[64,512]{1,0:T(8,128)(2,1)S(1)}, bf16[64,512]{1,0:T(8,128)(2,1)S(1)}, u32[]{:S(2)}, u32[]{:S(2)}) collective-permute-start(bf16[64,512]{1,0:T(8,128)(2,1)S(1)} %fusion.16), channel_id=1, source_target_pairs={{0,32},{1,33},{2,34},{3,35},{4,36},{5,37},{6,38},{7,39},{8,40},{9,... | collective-permute-start | bytes 196616 | tf_op jit(solution)/shard_map/ppermute | solution.py:73
  80.4 6.3 %collective-permute-start.29 = (bf16[2,64,512]{2,1,0:T(8,128)(2,1)S(1)}, bf16[2,64,512]{2,1,0:T(8,128)(2,1)S(1)}, u32[]{:S(2)}, u32[]{:S(2)}) collective-permute-start(bf16[2,64,512]{2,1,0:T(8,128)(2,1)S(1)} %pad_maximum_fusion.2.refs_0_), channel_id=1, source_target_pairs={{0,4},{1,3},{2,6},{3,1},{4,0},{5,7},{6,2},{7,5},{8,12},{9,11},{10,... | collective-permute-start | bytes 393224 | tf_op jit(solution)/shard_map/ppermute | solution.py:60
  80.5 7.8 %collective-permute-start.30 = (bf16[2,64,512]{2,1,0:T(8,128)(2,1)S(1)}, bf16[2,64,512]{2,1,0:T(8,128)(2,1)S(1)}, u32[]{:S(2)}, u32[]{:S(2)}) collective-permute-start(bf16[2,64,512]{2,1,0:T(8,128)(2,1)S(1)} %pad_maximum_fusion.2.refs_0_), channel_id=1, source_target_pairs={{0,2},{1,5},{2,0},{3,7},{4,6},{5,1},{6,4},{7,3},{8,10},{9,13},{10,... | collective-permute-start | bytes 393224 | tf_op jit(solution)/shard_map/ppermute | solution.py:60
  80.6 7.7 %collective-permute-start.31 = (bf16[2,64,512]{2,1,0:T(8,128)(2,1)S(1)}, bf16[2,64,512]{2,1,0:T(8,128)(2,1)S(1)}, u32[]{:S(2)}, u32[]{:S(2)}) collective-permute-start(bf16[2,64,512]{2,1,0:T(8,128)(2,1)S(1)} %pad_maximum_fusion.2.refs_0_), channel_id=1, source_target_pairs={{0,6},{1,7},{2,4},{3,5},{4,2},{5,3},{6,0},{7,1},{8,14},{9,15},{10,... | collective-permute-start | bytes 393224 | tf_op jit(solution)/shard_map/ppermute | solution.py:68
  83.2 6.6 %collective-permute-start.22 = (bf16[2,64,512]{2,1,0:T(8,128)(2,1)S(1)}, bf16[2,64,512]{2,1,0:T(8,128)(2,1)S(1)}, u32[]{:S(2)}, u32[]{:S(2)}) collective-permute-start(bf16[2,64,512]{2,1,0:T(8,128)(2,1)S(1)} %pad_maximum_fusion.1.refs_0_), channel_id=1, source_target_pairs={{0,12},{1,131},{2,14},{3,129},{4,8},{5,135},{6,10},{7,133},{8,4},{... | collective-permute-start | bytes 393224 | tf_op jit(solution)/shard_map/ppermute | solution.py:60
  86.7 7.2 %collective-permute-start.24 = (bf16[2,64,512]{2,1,0:T(8,128)(2,1)S(1)}, bf16[2,64,512]{2,1,0:T(8,128)(2,1)S(1)}, u32[]{:S(2)}, u32[]{:S(2)}) collective-permute-start(bf16[2,64,512]{2,1,0:T(8,128)(2,1)S(1)} %pad_maximum_fusion.1.refs_0_), channel_id=1, source_target_pairs={{0,142},{1,143},{2,140},{3,141},{4,138},{5,139},{6,136},{7,137},{8... | collective-permute-start | bytes 393224 | tf_op jit(solution)/shard_map/ppermute | solution.py:68
  88.4 9.6 %collective-permute-start.36 = (bf16[4,64,512]{2,1,0:T(8,128)(2,1)S(1)}, bf16[4,64,512]{2,1,0:T(8,128)(2,1)S(1)}, u32[]{:S(2)}, u32[]{:S(2)}) collective-permute-start(bf16[4,64,512]{2,1,0:T(8,128)(2,1)S(1)} %get-tuple-element.75.here), channel_id=1, source_target_pairs={{0,130},{1,13},{2,128},{3,15},{4,134},{5,9},{6,132},{7,11},{8,138}... | collective-permute-start | bytes 786440 | tf_op jit(solution)/shard_map/ppermute | solution.py:60
  94.0 5.3 %collective-permute-start.34 = (bf16[4,64,512]{2,1,0:T(8,128)(2,1)S(1)}, bf16[4,64,512]{2,1,0:T(8,128)(2,1)S(1)}, u32[]{:S(2)}, u32[]{:S(2)}) collective-permute-start(bf16[4,64,512]{2,1,0:T(8,128)(2,1)S(1)} %get-tuple-element.74.here), channel_id=1, source_target_pairs={{0,2},{1,5},{2,0},{3,7},{4,6},{5,1},{6,4},{7,3},{8,10},{9,13},{10,... | collective-permute-start | bytes 786440 | tf_op jit(solution)/shard_map/ppermute | solution.py:60
  94.1 8.7 %collective-permute-start.32 = (bf16[4,64,512]{2,1,0:T(8,128)(2,1)S(1)}, bf16[4,64,512]{2,1,0:T(8,128)(2,1)S(1)}, u32[]{:S(2)}, u32[]{:S(2)}) collective-permute-start(bf16[4,64,512]{2,1,0:T(8,128)(2,1)S(1)} %get-tuple-element.73.here), channel_id=1, source_target_pairs={{0,12},{1,131},{2,14},{3,129},{4,8},{5,135},{6,10},{7,133},{8,4},{... | collective-permute-start | bytes 786440 | tf_op jit(solution)/shard_map/ppermute | solution.py:60
  94.7 8.3 %collective-permute-start.25 = (bf16[4,64,512]{2,1,0:T(8,128)(2,1)S(1)}, bf16[4,64,512]{2,1,0:T(8,128)(2,1)S(1)}, u32[]{:S(2)}, u32[]{:S(2)}) collective-permute-start(bf16[4,64,512]{2,1,0:T(8,128)(2,1)S(1)} %get-tuple-element.72.here), channel_id=1, source_target_pairs={{0,4},{1,3},{2,6},{3,1},{4,0},{5,7},{6,2},{7,5},{8,12},{9,11},{10,... | collective-permute-start | bytes 786440 | tf_op jit(solution)/shard_map/ppermute | solution.py:60
  98.1 12.7 %collective-permute-start.37 = (bf16[8,64,512]{2,1,0:T(8,128)(2,1)S(1)}, bf16[8,64,512]{2,1,0:T(8,128)(2,1)S(1)}, u32[]{:S(2)}, u32[]{:S(2)}) collective-permute-start(bf16[8,64,512]{2,1,0:T(8,128)(2,1)S(1)} %join.7.refs_6_), channel_id=1, source_target_pairs={{0,12},{1,131},{2,14},{3,129},{4,8},{5,135},{6,10},{7,133},{8,4},{... | collective-permute-start | bytes 1572872 | tf_op jit(solution)/shard_map/ppermute | solution.py:60
  99.4 11.4 %collective-permute-start.35 = (bf16[8,64,512]{2,1,0:T(8,128)(2,1)S(1)}, bf16[8,64,512]{2,1,0:T(8,128)(2,1)S(1)}, u32[]{:S(2)}, u32[]{:S(2)}) collective-permute-start(bf16[8,64,512]{2,1,0:T(8,128)(2,1)S(1)} %join.6.refs_4_), channel_id=1, source_target_pairs={{0,4},{1,3},{2,6},{3,1},{4,0},{5,7},{6,2},{7,5},{8,12},{9,11},{10,... | collective-permute-start | bytes 1572872 | tf_op jit(solution)/shard_map/ppermute | solution.py:60
  102.9 13.1 %collective-permute-start.33 = (bf16[8,64,512]{2,1,0:T(8,128)(2,1)S(1)}, bf16[8,64,512]{2,1,0:T(8,128)(2,1)S(1)}, u32[]{:S(2)}, u32[]{:S(2)}) collective-permute-start(bf16[8,64,512]{2,1,0:T(8,128)(2,1)S(1)} %join.5.refs_2_), channel_id=1, source_target_pairs={{0,130},{1,13},{2,128},{3,15},{4,134},{5,9},{6,132},{7,11},{8,138}... | collective-permute-start | bytes 1572872 | tf_op jit(solution)/shard_map/ppermute | solution.py:60
  103.0 13.0 %collective-permute-start.26 = (bf16[8,64,512]{2,1,0:T(8,128)(2,1)S(1)}, bf16[8,64,512]{2,1,0:T(8,128)(2,1)S(1)}, u32[]{:S(2)}, u32[]{:S(2)}) collective-permute-start(bf16[8,64,512]{2,1,0:T(8,128)(2,1)S(1)} %join.4.refs_0_), channel_id=1, source_target_pairs={{0,2},{1,5},{2,0},{3,7},{4,6},{5,1},{6,4},{7,3},{8,10},{9,13},{10,... | collective-permute-start | bytes 1572872 | tf_op jit(solution)/shard_map/ppermute | solution.py:60
  119.8 10.8 %collective-permute-start.38 = (bf16[256,512]{1,0:T(8,128)(2,1)S(1)}, bf16[256,512]{1,0:T(8,128)(2,1)S(1)}, u32[]{:S(2)}, u32[]{:S(2)}) collective-permute-start(bf16[256,512]{1,0:T(8,128)(2,1)S(1)} %get-tuple-element.78), channel_id=1, source_target_pairs={{0,1},{1,0},{2,3},{3,2},{4,5},{5,4},{6,7},{7,6},{8,9},{9,8},{10,11... | collective-permute-start | bytes 786440 | tf_op jit(solution)/shard_map/ppermute | solution.py:77
  (15 other events, 98.3 us)

commit v8 on v7

--- a/solution.py
+++ b/solution.py
@@ -298,25 +298,6 @@
         cost_estimate=cost(1 << 19, 3 << 20),
         name="add_couples",
     )(*pairs, after)
-
-
-def spread_kernel(*refs):
-    for i in range(4):
-        for j in range(2):
-            refs[4 + j][i] = refs[i][j]
-
-
-def spread(couple):
-    part = jax.ShapeDtypeStruct((4, ROWS, COLS), jnp.bfloat16)
-    return pl.pallas_call(
-        spread_kernel,
-        out_shape=(part,) * 2,
-        in_specs=[VMEM] * 4,
-        out_specs=(VMEM,) * 2,
-        compiler_params=PARAMS,
-        cost_estimate=cost(0, 1 << 20),
-        name="spread",
-    )(*couple)
 
 
 def join_kernel(dim, here, got, both):
@@ -486,14 +467,13 @@
 
 
 def gather_parts(rows):
-    halves = [None] * (2 * PARTS)
-    for a, b, first, second in COUPLES:
-        couple = jnp.stack([z_swap(rows, m) if m else rows for m in (a, b)])
-        parts = spread([couple] + around([couple] * 4, first, second))
-        for m, part in zip((a, b), parts):
-            v, w = ORDERS[m][:2]
-            part = join(part, across(part, w), w - (v < w))
-            halves[2 * m : 2 * m + 2] = [part, across(part, v)]
+    halves = []
+    for m, (v, w, p, q) in enumerate(ORDERS):
+        p, q = (q, p) if m in (2, 3) else (p, q)
+        part = (z_swap(rows, m) if m else rows)[None]
+        for bit, dim in ((q, 0), (p, int(p > q)), (w, w - (v < w))):
+            part = join(part, across(part, bit), dim)
+        halves += [part, across(part, v)]
     return halves
 
 

time: 132 us -> 128 us (0.970)
  waiting for transfers between devices: 53.2 us -> 42.1 us
  starting transfers between devices: 55.7 us -> 63.1 us
    ppermute x24 -> x28, starting transfers between devices: 17.6 us -> 27 us  [across(): return lax.ppermute(array, AXES, PAIRINGS[pairing])]
    ppermute x24 -> x28, waiting for transfers between devices: 26.9 us -> 20.5 us  [across(): return lax.ppermute(array, AXES, PAIRINGS[pairing])]
    ppermute x4 -> x2, waiting for transfers between devices: 7.26 us -> 3.09 us  [around(): lax.ppermute(couple[3], AXES, both)]
    ppermute x4 -> x2, starting transfers between devices: 9.89 us -> 5.75 us  [around(): lax.ppermute(couple[3], AXES, both)]
  transfers between devices with their start and end apart: 39 -> 41, of which waited for: 19 -> 21; matrix products, arithmetic and copies ran while one was open for 1% -> 1% of each run, Pallas kernels for 1% -> 1%
where the time goes in v8:
time: 128 us
  starting transfers between devices  63.1 us (49%)
  waiting for transfers between devices  42.1 us (33%)
  Pallas kernels  15.5 us (12%)
  local copies, waits for them, and re-layouts  3.62 us (3%)
  other arithmetic  2.53 us (2%)
    ppermute x28, starting transfers between devices, across(): return lax.ppermute(array, AXES, PAIRINGS[pairing])  27 us
    ppermute x28, waiting for transfers between devices, across(): return lax.ppermute(array, AXES, PAIRINGS[pairing])  20.5 us
    ppermute x8, waiting for transfers between devices, z_swap(): lax.ppermute(array, AXES, moves(lambda xh, z, y, xl, c: (xh, z ^ mask, y,...  17.9 us
    ppermute x8, starting transfers between devices, z_swap(): lax.ppermute(array, AXES, moves(lambda xh, z, y, xl, c: (xh, z ^ mask, y,...  15.2 us
    ppermute x3, starting transfers between devices, core_swap(): lax.ppermute(array, AXES, moves(lambda xh, z, y, xl, c: (xh, z, y, xl, 1...  15.1 us
    pallas_call x1, Pallas kernels, gradient_term(): pl.pallas_call(term_kernel, out_shape=(half,) * (2 * PARTS), in_specs=[AN...  6.59 us
    ppermute x2, starting transfers between devices, around(): lax.ppermute(couple[3], AXES, both)  5.75 us
    pallas_call x1, Pallas kernels, project(): pl.pallas_call(project_kernel, out_shape=(jax.ShapeDtypeStruct((2 * BLOCK...  3.67 us
  transfers between devices with their start and end apart: 41, of which 21 were waited for; matrix products, arithmetic and copies ran while one was open for 1% of the time, Pallas kernels for 1%

profile of v8, /device:TPU:1, one launch (start us, length us, event | category | flops | bytes accessed | tf_op | source)
XLA Modules:
  0.0 127.7 jit_solution(7859059427906547270)
XLA Ops:
  0.7 3.4 %pack_acts.1 = (bf16[256,4608]{1,0:T(8,128)(2,1)}, f32[8,128]{1,0:T(8,128)}) custom-call(bf16[256,8192]{1,0:T(8,128)(2,1)} %acts.3, bf16[256,512]{1,0:T(8,128)(2,1)} %grads.3), custom_call_target="tpu_custom_call" | custom-call | bytes 4194304 | tf_op jit(solution)/shard_map/pack_acts/pallas_call | solution.py:150
  4.1 3.3 %collective-permute-start.1 = (bf16[256,4608]{1,0:T(8,128)(2,1)}, bf16[256,4608]{1,0:T(8,128)(2,1)S(1)}, u32[]{:S(2)}, u32[]{:S(2)}) collective-permute-start(bf16[256,4608]{1,0:T(8,128)(2,1)} %get-tuple-element.40), channel_id=1, source_target_pairs={{0,1},{1,0},{2,3},{3,2},{4,5},{5,4},{6,7},{7,6},{8,9},{9,8},{10,11... | collective-permute-start | bytes 7077896 | tf_op jit(solution)/shard_map/ppermute | solution.py:77
  7.4 2.2 %copy-done = bf16[256,8192]{1,0:T(8,128)(2,1)S(1)} copy-done((bf16[256,8192]{1,0:T(8,128)(2,1)S(1)}, bf16[256,8192]{1,0:T(8,128)(2,1)}, u32[]{:S(2)}) %copy-start) | copy-done | bytes 4194328
  12.5 6.6 %gradient_term.1 = (bf16[8,64,512]{2,1,0:T(8,128)(2,1)S(1)}, bf16[8,64,512]{2,1,0:T(8,128)(2,1)S(1)}, bf16[8,64,512]{2,1,0:T(8,128)(2,1)S(1)}, bf16[8,64,512]{2,...) custom-call(bf16[256,8192]{1,0:T(8,128)(2,1)S(1)} %copy-done.2, ...), custom_call_target="tpu_custom_call" | custom-call | flops 2147483648 | bytes 9437184 | tf_op jit(solution)/shard_map/gradient_term/pallas_call | solution.py:234
  19.2 1.4 %collective-permute-start.3 = (bf16[8,64,512]{2,1,0:T(8,128)(2,1)S(1)}, bf16[8,64,512]{2,1,0:T(8,128)(2,1)S(1)}, u32[]{:S(2)}, u32[]{:S(2)}) collective-permute-start(bf16[8,64,512]{2,1,0:T(8,128)(2,1)S(1)} %get-tuple-element.45), channel_id=1, source_target_pairs={{0,130},{1,13},{2,128},{3,15},{4,134},{5,9},{6,132},{7,11},{8,138}... | collective-permute-start | bytes 1572872 | tf_op jit(solution)/shard_map/ppermute | solution.py:60
  21.8 1.8 %collective-permute-start.5 = (bf16[8,64,512]{2,1,0:T(8,128)(2,1)S(1)}, bf16[8,64,512]{2,1,0:T(8,128)(2,1)S(1)}, u32[]{:S(2)}, u32[]{:S(2)}) collective-permute-start(bf16[8,64,512]{2,1,0:T(8,128)(2,1)S(1)} %get-tuple-element.49), channel_id=1, source_target_pairs={{0,12},{1,131},{2,14},{3,129},{4,8},{5,135},{6,10},{7,133},{8,4},{... | collective-permute-start | bytes 1572872 | tf_op jit(solution)/shard_map/ppermute | solution.py:60
  23.6 5.6 %collective-permute-start = (f32[3,32,512]{2,1,0:T(8,128)S(1)}, f32[3,32,512]{2,1,0:T(8,128)S(1)}, u32[]{:S(2)}, u32[]{:S(2)}) collective-permute-start(f32[3,32,512]{2,1,0:T(8,128)S(1)} %get-tuple-element.39), channel_id=1, source_target_pairs={{0,112},{1,113},{2,114},{3,115},{4,116},{5,117},{6,118},{7,119},{8... | collective-permute-start | bytes 589832 | tf_op jit(solution)/shard_map/ppermute | solution.py:73
  29.2 9.1 %collective-permute-done.refs_8_ = f32[3,32,512]{2,1,0:T(8,128)S(1)} collective-permute-done((f32[3,32,512]{2,1,0:T(8,128)S(1)}, f32[3,32,512]{2,1,0:T(8,128)S(1)}, u32[]{:S(2)}, u32[]{:S(2)}) %collective-permute-start) | collective-permute-done | bytes 196640 | tf_op jit(solution)/shard_map/ppermute | solution.py:73
  41.8 4.2 %collective-permute-done.6.refs_1_ = bf16[4,64,512]{2,1,0:T(8,128)(2,1)S(1)} collective-permute-done((bf16[4,64,512]{2,1,0:T(8,128)(2,1)S(1)}, bf16[4,64,512]{2,1,0:T(8,128)(2,1)S(1)}, u32[]{:S(2)}, u32[]{:S(2)}) %collective-permute-start.6) | collective-permute-done | bytes 262176 | tf_op jit(solution)/shard_map/ppermute | solution.py:60
  47.2 1.5 %collective-permute-done.8.refs_5_ = bf16[4,64,512]{2,1,0:T(8,128)(2,1)S(1)} collective-permute-done((bf16[4,64,512]{2,1,0:T(8,128)(2,1)S(1)}, bf16[4,64,512]{2,1,0:T(8,128)(2,1)S(1)}, u32[]{:S(2)}, u32[]{:S(2)}) %collective-permute-start.8) | collective-permute-done | bytes 262176 | tf_op jit(solution)/shard_map/ppermute | solution.py:60
  48.7 1.8 %collective-permute-done.9.refs_7_ = bf16[4,64,512]{2,1,0:T(8,128)(2,1)S(1)} collective-permute-done((bf16[4,64,512]{2,1,0:T(8,128)(2,1)S(1)}, bf16[4,64,512]{2,1,0:T(8,128)(2,1)S(1)}, u32[]{:S(2)}, u32[]{:S(2)}) %collective-permute-start.9) | collective-permute-done | bytes 262176 | tf_op jit(solution)/shard_map/ppermute | solution.py:60
  51.2 2.5 %collective-permute-start.16 = (bf16[2,64,512]{2,1,0:T(8,128)(2,1)S(1)}, bf16[2,64,512]{2,1,0:T(8,128)(2,1)S(1)}, u32[]{:S(2)}, u32[]{:S(2)}) collective-permute-start(bf16[2,64,512]{2,1,0:T(8,128)(2,1)S(1)} %get-tuple-element.67), channel_id=1, source_target_pairs={{0,6},{1,7},{2,4},{3,5},{4,2},{5,3},{6,0},{7,1},{8,14},{9,15},{10,... | collective-permute-start | bytes 393224 | tf_op jit(solution)/shard_map/ppermute | solution.py:68
  55.5 3.2 %collective-permute-start.13 = (bf16[2,64,512]{2,1,0:T(8,128)(2,1)S(1)}, bf16[2,64,512]{2,1,0:T(8,128)(2,1)S(1)}, u32[]{:S(2)}, u32[]{:S(2)}) collective-permute-start(bf16[2,64,512]{2,1,0:T(8,128)(2,1)S(1)} %get-tuple-element.63), channel_id=1, source_target_pairs={{0,142},{1,143},{2,140},{3,141},{4,138},{5,139},{6,136},{7,137},{8... | collective-permute-start | bytes 393224 | tf_op jit(solution)/shard_map/ppermute | solution.py:68
  59.0 1.7 %collective-permute-start.19 = (bf16[64,512]{1,0:T(8,128)(2,1)S(1)}, bf16[64,512]{1,0:T(8,128)(2,1)S(1)}, u32[]{:S(2)}, u32[]{:S(2)}) collective-permute-start(bf16[64,512]{1,0:T(8,128)(2,1)S(1)} %get-tuple-element.80), channel_id=1, source_target_pairs={{0,48},{1,49},{2,50},{3,51},{4,52},{5,53},{6,54},{7,55},{8,56},{9,... | collective-permute-start | bytes 196616 | tf_op jit(solution)/shard_map/ppermute | solution.py:73
  60.7 3.1 %collective-permute-done.13 = bf16[2,64,512]{2,1,0:T(8,128)(2,1)S(1)} collective-permute-done((bf16[2,64,512]{2,1,0:T(8,128)(2,1)S(1)}, bf16[2,64,512]{2,1,0:T(8,128)(2,1)S(1)}, u32[]{:S(2)}, u32[]{:S(2)}) %collective-permute-start.13) | collective-permute-done | bytes 131104 | tf_op jit(solution)/shard_map/ppermute | solution.py:68
  64.1 4.9 %collective-permute-done.18 = bf16[64,512]{1,0:T(8,128)(2,1)S(1)} collective-permute-done((bf16[64,512]{1,0:T(8,128)(2,1)S(1)}, bf16[64,512]{1,0:T(8,128)(2,1)S(1)}, u32[]{:S(2)}, u32[]{:S(2)}) %collective-permute-start.18) | collective-permute-done | bytes 65568 | tf_op jit(solution)/shard_map/ppermute | solution.py:73
  69.0 4.0 %collective-permute-start.20 = (bf16[64,512]{1,0:T(8,128)(2,1)S(1)}, bf16[64,512]{1,0:T(8,128)(2,1)S(1)}, u32[]{:S(2)}, u32[]{:S(2)}) collective-permute-start(bf16[64,512]{1,0:T(8,128)(2,1)S(1)} %fusion.15), channel_id=1, source_target_pairs={{0,112},{1,113},{2,114},{3,115},{4,116},{5,117},{6,118},{7,119},{8... | collective-permute-start | bytes 196616 | tf_op jit(solution)/shard_map/ppermute | solution.py:73
  73.0 1.6 %collective-permute-done.20 = bf16[64,512]{1,0:T(8,128)(2,1)S(1)} collective-permute-done((bf16[64,512]{1,0:T(8,128)(2,1)S(1)}, bf16[64,512]{1,0:T(8,128)(2,1)S(1)}, u32[]{:S(2)}, u32[]{:S(2)}) %collective-permute-start.20) | collective-permute-done | bytes 65568 | tf_op jit(solution)/shard_map/ppermute | solution.py:73
  74.9 1.7 %collective-permute-start.35 = (bf16[64,512]{1,0:T(8,128)(2,1)S(1)}, bf16[64,512]{1,0:T(8,128)(2,1)S(1)}, u32[]{:S(2)}, u32[]{:S(2)}) collective-permute-start(bf16[64,512]{1,0:T(8,128)(2,1)S(1)} %fusion.16), channel_id=1, source_target_pairs={{0,48},{1,49},{2,50},{3,51},{4,52},{5,53},{6,54},{7,55},{8,56},{9,... | collective-permute-start | bytes 196616 | tf_op jit(solution)/shard_map/ppermute | solution.py:73
  76.6 1.9 %collective-permute-start.25 = (bf16[64,512]{1,0:T(8,128)(2,1)S(1)}, bf16[64,512]{1,0:T(8,128)(2,1)S(1)}, u32[]{:S(2)}, u32[]{:S(2)}) collective-permute-start(bf16[64,512]{1,0:T(8,128)(2,1)S(1)} %fusion.16), channel_id=1, source_target_pairs={{0,16},{1,17},{2,18},{3,19},{4,20},{5,21},{6,22},{7,23},{8,24},{9,... | collective-permute-start | bytes 196616 | tf_op jit(solution)/shard_map/ppermute | solution.py:73
  82.9 1.7 %collective-permute-start.22 = (bf16[2,64,512]{2,1,0:T(8,128)(2,1)S(1)}, bf16[2,64,512]{2,1,0:T(8,128)(2,1)S(1)}, u32[]{:S(2)}, u32[]{:S(2)}) collective-permute-start(bf16[2,64,512]{2,1,0:T(8,128)(2,1)S(1)} %join.12.here), channel_id=1, source_target_pairs={{0,130},{1,13},{2,128},{3,15},{4,134},{5,9},{6,132},{7,11},{8,138}... | collective-permute-start | bytes 393224 | tf_op jit(solution)/shard_map/ppermute | solution.py:60
  84.6 1.5 %collective-permute-start.37 = (bf16[2,64,512]{2,1,0:T(8,128)(2,1)S(1)}, bf16[2,64,512]{2,1,0:T(8,128)(2,1)S(1)}, u32[]{:S(2)}, u32[]{:S(2)}) collective-permute-start(bf16[2,64,512]{2,1,0:T(8,128)(2,1)S(1)} %join.21.here), channel_id=1, source_target_pairs={{0,4},{1,3},{2,6},{3,1},{4,0},{5,7},{6,2},{7,5},{8,12},{9,11},{10,... | collective-permute-start | bytes 393224 | tf_op jit(solution)/shard_map/ppermute | solution.py:60
  89.5 2.0 %collective-permute-start.38 = (bf16[4,64,512]{2,1,0:T(8,128)(2,1)S(1)}, bf16[4,64,512]{2,1,0:T(8,128)(2,1)S(1)}, u32[]{:S(2)}, u32[]{:S(2)}) collective-permute-start(bf16[4,64,512]{2,1,0:T(8,128)(2,1)S(1)} %join.22.here), channel_id=1, source_target_pairs={{0,130},{1,13},{2,128},{3,15},{4,134},{5,9},{6,132},{7,11},{8,138}... | collective-permute-start | bytes 786440 | tf_op jit(solution)/shard_map/ppermute | solution.py:60
  91.7 1.6 %collective-permute-start.28 = (bf16[4,64,512]{2,1,0:T(8,128)(2,1)S(1)}, bf16[4,64,512]{2,1,0:T(8,128)(2,1)S(1)}, u32[]{:S(2)}, u32[]{:S(2)}) collective-permute-start(bf16[4,64,512]{2,1,0:T(8,128)(2,1)S(1)} %join.16.here), channel_id=1, source_target_pairs={{0,12},{1,131},{2,14},{3,129},{4,8},{5,135},{6,10},{7,133},{8,4},{... | collective-permute-start | bytes 786440 | tf_op jit(solution)/shard_map/ppermute | solution.py:60
  93.4 2.3 %collective-permute-start.24 = (bf16[8,64,512]{2,1,0:T(8,128)(2,1)S(1)}, bf16[8,64,512]{2,1,0:T(8,128)(2,1)S(1)}, u32[]{:S(2)}, u32[]{:S(2)}) collective-permute-start(bf16[8,64,512]{2,1,0:T(8,128)(2,1)S(1)} %join.14.refs_0_), channel_id=1, source_target_pairs={{0,2},{1,5},{2,0},{3,7},{4,6},{5,1},{6,4},{7,3},{8,10},{9,13},{10,... | collective-permute-start | bytes 1572872 | tf_op jit(solution)/shard_map/ppermute | solution.py:60
  96.3 1.9 %collective-permute-start.39 = (bf16[8,64,512]{2,1,0:T(8,128)(2,1)S(1)}, bf16[8,64,512]{2,1,0:T(8,128)(2,1)S(1)}, u32[]{:S(2)}, u32[]{:S(2)}) collective-permute-start(bf16[8,64,512]{2,1,0:T(8,128)(2,1)S(1)} %join.23.refs_6_), channel_id=1, source_target_pairs={{0,12},{1,131},{2,14},{3,129},{4,8},{5,135},{6,10},{7,133},{8,4},{... | collective-permute-start | bytes 1572872 | tf_op jit(solution)/shard_map/ppermute | solution.py:60
  99.1 2.1 %collective-permute-start.29 = (bf16[8,64,512]{2,1,0:T(8,128)(2,1)S(1)}, bf16[8,64,512]{2,1,0:T(8,128)(2,1)S(1)}, u32[]{:S(2)}, u32[]{:S(2)}) collective-permute-start(bf16[8,64,512]{2,1,0:T(8,128)(2,1)S(1)} %join.17.refs_2_), channel_id=1, source_target_pairs={{0,130},{1,13},{2,128},{3,15},{4,134},{5,9},{6,132},{7,11},{8,138}... | collective-permute-start | bytes 1572872 | tf_op jit(solution)/shard_map/ppermute | solution.py:60
  101.2 5.8 %collective-permute-done.24.refs_1_ = bf16[8,64,512]{2,1,0:T(8,128)(2,1)S(1)} collective-permute-done((bf16[8,64,512]{2,1,0:T(8,128)(2,1)S(1)}, bf16[8,64,512]{2,1,0:T(8,128)(2,1)S(1)}, u32[]{:S(2)}, u32[]{:S(2)}) %collective-permute-start.24) | collective-permute-done | bytes 524320 | tf_op jit(solution)/shard_map/ppermute | solution.py:60
  107.0 1.7 %collective-permute-done.39.refs_7_ = bf16[8,64,512]{2,1,0:T(8,128)(2,1)S(1)} collective-permute-done((bf16[8,64,512]{2,1,0:T(8,128)(2,1)S(1)}, bf16[8,64,512]{2,1,0:T(8,128)(2,1)S(1)}, u32[]{:S(2)}, u32[]{:S(2)}) %collective-permute-start.39) | collective-permute-done | bytes 524320 | tf_op jit(solution)/shard_map/ppermute | solution.py:60
  108.7 1.9 %collective-permute-done.34.refs_5_ = bf16[8,64,512]{2,1,0:T(8,128)(2,1)S(1)} collective-permute-done((bf16[8,64,512]{2,1,0:T(8,128)(2,1)S(1)}, bf16[8,64,512]{2,1,0:T(8,128)(2,1)S(1)}, u32[]{:S(2)}, u32[]{:S(2)}) %collective-permute-start.34) | collective-permute-done | bytes 524320 | tf_op jit(solution)/shard_map/ppermute | solution.py:60
  111.2 3.7 %project.1 = (bf16[512,512]{1,0:T(8,128)(2,1)}, f32[256,512]{1,0:T(8,128)S(1)}, bf16[256,512]{1,0:T(8,128)(2,1)S(1)}) custom-call(bf16[256,8192]{1,0:T(8,128)(2,1)S(1)} %copy-done.1, bf16[256,4096]{1,0:T(8,128)(2,1)S(1)} %collective-permute-done.10.refs_8_.got, bf16[8,64,512]{2,1,0:T(8,128)(2,1)S(1)} %join.14.refs_0_, ...), custom_call_target="tpu_custom_call" | custom-call | flops 2147483648 | bytes 9437184 | tf_op jit(solution)/shard_map/project/pallas_call | solution.py:395
  114.9 10.7 %collective-permute-start.40 = (bf16[256,512]{1,0:T(8,128)(2,1)S(1)}, bf16[256,512]{1,0:T(8,128)(2,1)S(1)}, u32[]{:S(2)}, u32[]{:S(2)}) collective-permute-start(bf16[256,512]{1,0:T(8,128)(2,1)S(1)} %get-tuple-element.70), channel_id=1, source_target_pairs={{0,1},{1,0},{2,3},{3,2},{4,5},{5,4},{6,7},{7,6},{8,9},{9,8},{10,11... | collective-permute-start | bytes 786440 | tf_op jit(solution)/shard_map/ppermute | solution.py:77
  (96 shorter events, 24.2 us)
Async XLA Ops:
  4.1 7.7 %collective-permute-start.1 = (bf16[256,4608]{1,0:T(8,128)(2,1)}, bf16[256,4608]{1,0:T(8,128)(2,1)S(1)}, u32[]{:S(2)}, u32[]{:S(2)}) collective-permute-start(bf16[256,4608]{1,0:T(8,128)(2,1)} %get-tuple-element.40), channel_id=1, source_target_pairs={{0,1},{1,0},{2,3},{3,2},{4,5},{5,4},{6,7},{7,6},{8,9},{9,8},{10,11... | collective-permute-start | bytes 7077896 | tf_op jit(solution)/shard_map/ppermute | solution.py:77
  19.1 19.2 %collective-permute-start.2 = (bf16[8,64,512]{2,1,0:T(8,128)(2,1)S(1)}, bf16[8,64,512]{2,1,0:T(8,128)(2,1)S(1)}, u32[]{:S(2)}, u32[]{:S(2)}) collective-permute-start(bf16[8,64,512]{2,1,0:T(8,128)(2,1)S(1)} %get-tuple-element.43), channel_id=1, source_target_pairs={{0,2},{1,5},{2,0},{3,7},{4,6},{5,1},{6,4},{7,3},{8,10},{9,13},{10,... | collective-permute-start | bytes 1572872 | tf_op jit(solution)/shard_map/ppermute | solution.py:60
  19.2 19.1 %collective-permute-start.3 = (bf16[8,64,512]{2,1,0:T(8,128)(2,1)S(1)}, bf16[8,64,512]{2,1,0:T(8,128)(2,1)S(1)}, u32[]{:S(2)}, u32[]{:S(2)}) collective-permute-start(bf16[8,64,512]{2,1,0:T(8,128)(2,1)S(1)} %get-tuple-element.45), channel_id=1, source_target_pairs={{0,130},{1,13},{2,128},{3,15},{4,134},{5,9},{6,132},{7,11},{8,138}... | collective-permute-start | bytes 1572872 | tf_op jit(solution)/shard_map/ppermute | solution.py:60
  20.6 17.7 %collective-permute-start.4 = (bf16[8,64,512]{2,1,0:T(8,128)(2,1)S(1)}, bf16[8,64,512]{2,1,0:T(8,128)(2,1)S(1)}, u32[]{:S(2)}, u32[]{:S(2)}) collective-permute-start(bf16[8,64,512]{2,1,0:T(8,128)(2,1)S(1)} %get-tuple-element.47), channel_id=1, source_target_pairs={{0,4},{1,3},{2,6},{3,1},{4,0},{5,7},{6,2},{7,5},{8,12},{9,11},{10,... | collective-permute-start | bytes 1572872 | tf_op jit(solution)/shard_map/ppermute | solution.py:60
  21.8 16.5 %collective-permute-start.5 = (bf16[8,64,512]{2,1,0:T(8,128)(2,1)S(1)}, bf16[8,64,512]{2,1,0:T(8,128)(2,1)S(1)}, u32[]{:S(2)}, u32[]{:S(2)}) collective-permute-start(bf16[8,64,512]{2,1,0:T(8,128)(2,1)S(1)} %get-tuple-element.49), channel_id=1, source_target_pairs={{0,12},{1,131},{2,14},{3,129},{4,8},{5,135},{6,10},{7,133},{8,4},{... | collective-permute-start | bytes 1572872 | tf_op jit(solution)/shard_map/ppermute | solution.py:60
  23.6 14.7 %collective-permute-start = (f32[3,32,512]{2,1,0:T(8,128)S(1)}, f32[3,32,512]{2,1,0:T(8,128)S(1)}, u32[]{:S(2)}, u32[]{:S(2)}) collective-permute-start(f32[3,32,512]{2,1,0:T(8,128)S(1)} %get-tuple-element.39), channel_id=1, source_target_pairs={{0,112},{1,113},{2,114},{3,115},{4,116},{5,117},{6,118},{7,119},{8... | collective-permute-start | bytes 589832 | tf_op jit(solution)/shard_map/ppermute | solution.py:73
  38.8 11.8 %collective-permute-start.10 = (bf16[256,4096]{1,0:T(8,128)(2,1)S(1)}, bf16[256,4096]{1,0:T(8,128)(2,1)S(1)}, u32[]{:S(2)}, u32[]{:S(2)}) collective-permute-start(bf16[256,4096]{1,0:T(8,128)(2,1)S(1)} %get-tuple-element.59), channel_id=1, source_target_pairs={{0,1},{1,0},{2,3},{3,2},{4,5},{5,4},{6,7},{7,6},{8,9},{9,8},{10,11... | collective-permute-start | bytes 6291464 | tf_op jit(solution)/shard_map/ppermute | solution.py:77
  39.8 6.1 %collective-permute-start.6 = (bf16[4,64,512]{2,1,0:T(8,128)(2,1)S(1)}, bf16[4,64,512]{2,1,0:T(8,128)(2,1)S(1)}, u32[]{:S(2)}, u32[]{:S(2)}) collective-permute-start(bf16[4,64,512]{2,1,0:T(8,128)(2,1)S(1)} %get-tuple-element.52), channel_id=1, source_target_pairs={{0,4},{1,3},{2,6},{3,1},{4,0},{5,7},{6,2},{7,5},{8,12},{9,11},{10,... | collective-permute-start | bytes 786440 | tf_op jit(solution)/shard_map/ppermute | solution.py:60
  40.1 7.1 %collective-permute-start.7 = (bf16[4,64,512]{2,1,0:T(8,128)(2,1)S(1)}, bf16[4,64,512]{2,1,0:T(8,128)(2,1)S(1)}, u32[]{:S(2)}, u32[]{:S(2)}) collective-permute-start(bf16[4,64,512]{2,1,0:T(8,128)(2,1)S(1)} %get-tuple-element.54), channel_id=1, source_target_pairs={{0,12},{1,131},{2,14},{3,129},{4,8},{5,135},{6,10},{7,133},{8,4},{... | collective-permute-start | bytes 786440 | tf_op jit(solution)/shard_map/ppermute | solution.py:60
  40.8 8.0 %collective-permute-start.8 = (bf16[4,64,512]{2,1,0:T(8,128)(2,1)S(1)}, bf16[4,64,512]{2,1,0:T(8,128)(2,1)S(1)}, u32[]{:S(2)}, u32[]{:S(2)}) collective-permute-start(bf16[4,64,512]{2,1,0:T(8,128)(2,1)S(1)} %get-tuple-element.56), channel_id=1, source_target_pairs={{0,2},{1,5},{2,0},{3,7},{4,6},{5,1},{6,4},{7,3},{8,10},{9,13},{10,... | collective-permute-start | bytes 786440 | tf_op jit(solution)/shard_map/ppermute | solution.py:60
  41.2 9.4 %collective-permute-start.9 = (bf16[4,64,512]{2,1,0:T(8,128)(2,1)S(1)}, bf16[4,64,512]{2,1,0:T(8,128)(2,1)S(1)}, u32[]{:S(2)}, u32[]{:S(2)}) collective-permute-start(bf16[4,64,512]{2,1,0:T(8,128)(2,1)S(1)} %get-tuple-element.58), channel_id=1, source_target_pairs={{0,130},{1,13},{2,128},{3,15},{4,134},{5,9},{6,132},{7,11},{8,138}... | collective-permute-start | bytes 786440 | tf_op jit(solution)/shard_map/ppermute | solution.py:60
  51.1 7.6 %collective-permute-start.15 = (bf16[2,64,512]{2,1,0:T(8,128)(2,1)S(1)}, bf16[2,64,512]{2,1,0:T(8,128)(2,1)S(1)}, u32[]{:S(2)}, u32[]{:S(2)}) collective-permute-start(bf16[2,64,512]{2,1,0:T(8,128)(2,1)S(1)} %get-tuple-element.66), channel_id=1, source_target_pairs={{0,2},{1,5},{2,0},{3,7},{4,6},{5,1},{6,4},{7,3},{8,10},{9,13},{10,... | collective-permute-start | bytes 393224 | tf_op jit(solution)/shard_map/ppermute | solution.py:60
  51.2 7.6 %collective-permute-start.16 = (bf16[2,64,512]{2,1,0:T(8,128)(2,1)S(1)}, bf16[2,64,512]{2,1,0:T(8,128)(2,1)S(1)}, u32[]{:S(2)}, u32[]{:S(2)}) collective-permute-start(bf16[2,64,512]{2,1,0:T(8,128)(2,1)S(1)} %get-tuple-element.67), channel_id=1, source_target_pairs={{0,6},{1,7},{2,4},{3,5},{4,2},{5,3},{6,0},{7,1},{8,14},{9,15},{10,... | collective-permute-start | bytes 393224 | tf_op jit(solution)/shard_map/ppermute | solution.py:68
  53.7 7.0 %collective-permute-start.11 = (bf16[2,64,512]{2,1,0:T(8,128)(2,1)S(1)}, bf16[2,64,512]{2,1,0:T(8,128)(2,1)S(1)}, u32[]{:S(2)}, u32[]{:S(2)}) collective-permute-start(bf16[2,64,512]{2,1,0:T(8,128)(2,1)S(1)} %get-tuple-element.61), channel_id=1, source_target_pairs={{0,12},{1,131},{2,14},{3,129},{4,8},{5,135},{6,10},{7,133},{8,4},{... | collective-permute-start | bytes 393224 | tf_op jit(solution)/shard_map/ppermute | solution.py:60
  54.4 6.3 %collective-permute-start.12 = (bf16[2,64,512]{2,1,0:T(8,128)(2,1)S(1)}, bf16[2,64,512]{2,1,0:T(8,128)(2,1)S(1)}, u32[]{:S(2)}, u32[]{:S(2)}) collective-permute-start(bf16[2,64,512]{2,1,0:T(8,128)(2,1)S(1)} %get-tuple-element.62), channel_id=1, source_target_pairs={{0,130},{1,13},{2,128},{3,15},{4,134},{5,9},{6,132},{7,11},{8,138}... | collective-permute-start | bytes 393224 | tf_op jit(solution)/shard_map/ppermute | solution.py:60
  55.5 8.2 %collective-permute-start.13 = (bf16[2,64,512]{2,1,0:T(8,128)(2,1)S(1)}, bf16[2,64,512]{2,1,0:T(8,128)(2,1)S(1)}, u32[]{:S(2)}, u32[]{:S(2)}) collective-permute-start(bf16[2,64,512]{2,1,0:T(8,128)(2,1)S(1)} %get-tuple-element.63), channel_id=1, source_target_pairs={{0,142},{1,143},{2,140},{3,141},{4,138},{5,139},{6,136},{7,137},{8... | collective-permute-start | bytes 393224 | tf_op jit(solution)/shard_map/ppermute | solution.py:68
  58.9 5.2 %collective-permute-start.17 = (bf16[64,512]{1,0:T(8,128)(2,1)S(1)}, bf16[64,512]{1,0:T(8,128)(2,1)S(1)}, u32[]{:S(2)}, u32[]{:S(2)}) collective-permute-start(bf16[64,512]{1,0:T(8,128)(2,1)S(1)} %get-tuple-element.79), channel_id=1, source_target_pairs={{0,16},{1,17},{2,18},{3,19},{4,20},{5,21},{6,22},{7,23},{8,24},{9,... | collective-permute-start | bytes 196616 | tf_op jit(solution)/shard_map/ppermute | solution.py:73
  63.8 5.1 %collective-permute-start.18 = (bf16[64,512]{1,0:T(8,128)(2,1)S(1)}, bf16[64,512]{1,0:T(8,128)(2,1)S(1)}, u32[]{:S(2)}, u32[]{:S(2)}) collective-permute-start(bf16[64,512]{1,0:T(8,128)(2,1)S(1)} %fusion.20), channel_id=1, source_target_pairs={{0,32},{1,33},{2,34},{3,35},{4,36},{5,37},{6,38},{7,39},{8,40},{9,... | collective-permute-start | bytes 196616 | tf_op jit(solution)/shard_map/ppermute | solution.py:73
  69.0 5.6 %collective-permute-start.20 = (bf16[64,512]{1,0:T(8,128)(2,1)S(1)}, bf16[64,512]{1,0:T(8,128)(2,1)S(1)}, u32[]{:S(2)}, u32[]{:S(2)}) collective-permute-start(bf16[64,512]{1,0:T(8,128)(2,1)S(1)} %fusion.15), channel_id=1, source_target_pairs={{0,112},{1,113},{2,114},{3,115},{4,116},{5,117},{6,118},{7,119},{8... | collective-permute-start | bytes 196616 | tf_op jit(solution)/shard_map/ppermute | solution.py:73
  74.9 5.6 %collective-permute-start.35 = (bf16[64,512]{1,0:T(8,128)(2,1)S(1)}, bf16[64,512]{1,0:T(8,128)(2,1)S(1)}, u32[]{:S(2)}, u32[]{:S(2)}) collective-permute-start(bf16[64,512]{1,0:T(8,128)(2,1)S(1)} %fusion.16), channel_id=1, source_target_pairs={{0,48},{1,49},{2,50},{3,51},{4,52},{5,53},{6,54},{7,55},{8,56},{9,... | collective-permute-start | bytes 196616 | tf_op jit(solution)/shard_map/ppermute | solution.py:73
  76.6 5.1 %collective-permute-start.30 = (bf16[64,512]{1,0:T(8,128)(2,1)S(1)}, bf16[64,512]{1,0:T(8,128)(2,1)S(1)}, u32[]{:S(2)}, u32[]{:S(2)}) collective-permute-start(bf16[64,512]{1,0:T(8,128)(2,1)S(1)} %fusion.16), channel_id=1, source_target_pairs={{0,32},{1,33},{2,34},{3,35},{4,36},{5,37},{6,38},{7,39},{8,40},{9,... | collective-permute-start | bytes 196616 | tf_op jit(solution)/shard_map/ppermute | solution.py:73
  76.6 6.1 %collective-permute-start.25 = (bf16[64,512]{1,0:T(8,128)(2,1)S(1)}, bf16[64,512]{1,0:T(8,128)(2,1)S(1)}, u32[]{:S(2)}, u32[]{:S(2)}) collective-permute-start(bf16[64,512]{1,0:T(8,128)(2,1)S(1)} %fusion.16), channel_id=1, source_target_pairs={{0,16},{1,17},{2,18},{3,19},{4,20},{5,21},{6,22},{7,23},{8,24},{9,... | collective-permute-start | bytes 196616 | tf_op jit(solution)/shard_map/ppermute | solution.py:73
  86.2 5.2 %collective-permute-start.32 = (bf16[2,64,512]{2,1,0:T(8,128)(2,1)S(1)}, bf16[2,64,512]{2,1,0:T(8,128)(2,1)S(1)}, u32[]{:S(2)}, u32[]{:S(2)}) collective-permute-start(bf16[2,64,512]{2,1,0:T(8,128)(2,1)S(1)} %join.18.here), channel_id=1, source_target_pairs={{0,12},{1,131},{2,14},{3,129},{4,8},{5,135},{6,10},{7,133},{8,4},{... | collective-permute-start | bytes 393224 | tf_op jit(solution)/shard_map/ppermute | solution.py:60
  88.0 5.3 %collective-permute-start.23 = (bf16[4,64,512]{2,1,0:T(8,128)(2,1)S(1)}, bf16[4,64,512]{2,1,0:T(8,128)(2,1)S(1)}, u32[]{:S(2)}, u32[]{:S(2)}) collective-permute-start(bf16[4,64,512]{2,1,0:T(8,128)(2,1)S(1)} %join.13.here), channel_id=1, source_target_pairs={{0,4},{1,3},{2,6},{3,1},{4,0},{5,7},{6,2},{7,5},{8,12},{9,11},{10,... | collective-permute-start | bytes 786440 | tf_op jit(solution)/shard_map/ppermute | solution.py:60
  89.5 6.7 %collective-permute-start.38 = (bf16[4,64,512]{2,1,0:T(8,128)(2,1)S(1)}, bf16[4,64,512]{2,1,0:T(8,128)(2,1)S(1)}, u32[]{:S(2)}, u32[]{:S(2)}) collective-permute-start(bf16[4,64,512]{2,1,0:T(8,128)(2,1)S(1)} %join.22.here), channel_id=1, source_target_pairs={{0,130},{1,13},{2,128},{3,15},{4,134},{5,9},{6,132},{7,11},{8,138}... | collective-permute-start | bytes 786440 | tf_op jit(solution)/shard_map/ppermute | solution.py:60
  91.5 7.0 %collective-permute-start.33 = (bf16[4,64,512]{2,1,0:T(8,128)(2,1)S(1)}, bf16[4,64,512]{2,1,0:T(8,128)(2,1)S(1)}, u32[]{:S(2)}, u32[]{:S(2)}) collective-permute-start(bf16[4,64,512]{2,1,0:T(8,128)(2,1)S(1)} %join.19.here), channel_id=1, source_target_pairs={{0,2},{1,5},{2,0},{3,7},{4,6},{5,1},{6,4},{7,3},{8,10},{9,13},{10,... | collective-permute-start | bytes 786440 | tf_op jit(solution)/shard_map/ppermute | solution.py:60
  91.7 7.4 %collective-permute-start.28 = (bf16[4,64,512]{2,1,0:T(8,128)(2,1)S(1)}, bf16[4,64,512]{2,1,0:T(8,128)(2,1)S(1)}, u32[]{:S(2)}, u32[]{:S(2)}) collective-permute-start(bf16[4,64,512]{2,1,0:T(8,128)(2,1)S(1)} %join.16.here), channel_id=1, source_target_pairs={{0,12},{1,131},{2,14},{3,129},{4,8},{5,135},{6,10},{7,133},{8,4},{... | collective-permute-start | bytes 786440 | tf_op jit(solution)/shard_map/ppermute | solution.py:60
  93.4 13.6 %collective-permute-start.24 = (bf16[8,64,512]{2,1,0:T(8,128)(2,1)S(1)}, bf16[8,64,512]{2,1,0:T(8,128)(2,1)S(1)}, u32[]{:S(2)}, u32[]{:S(2)}) collective-permute-start(bf16[8,64,512]{2,1,0:T(8,128)(2,1)S(1)} %join.14.refs_0_), channel_id=1, source_target_pairs={{0,2},{1,5},{2,0},{3,7},{4,6},{5,1},{6,4},{7,3},{8,10},{9,13},{10,... | collective-permute-start | bytes 1572872 | tf_op jit(solution)/shard_map/ppermute | solution.py:60
  96.3 12.4 %collective-permute-start.39 = (bf16[8,64,512]{2,1,0:T(8,128)(2,1)S(1)}, bf16[8,64,512]{2,1,0:T(8,128)(2,1)S(1)}, u32[]{:S(2)}, u32[]{:S(2)}) collective-permute-start(bf16[8,64,512]{2,1,0:T(8,128)(2,1)S(1)} %join.23.refs_6_), channel_id=1, source_target_pairs={{0,12},{1,131},{2,14},{3,129},{4,8},{5,135},{6,10},{7,133},{8,4},{... | collective-permute-start | bytes 1572872 | tf_op jit(solution)/shard_map/ppermute | solution.py:60
  98.6 12.1 %collective-permute-start.34 = (bf16[8,64,512]{2,1,0:T(8,128)(2,1)S(1)}, bf16[8,64,512]{2,1,0:T(8,128)(2,1)S(1)}, u32[]{:S(2)}, u32[]{:S(2)}) collective-permute-start(bf16[8,64,512]{2,1,0:T(8,128)(2,1)S(1)} %join.20.refs_4_), channel_id=1, source_target_pairs={{0,4},{1,3},{2,6},{3,1},{4,0},{5,7},{6,2},{7,5},{8,12},{9,11},{10,... | collective-permute-start | bytes 1572872 | tf_op jit(solution)/shard_map/ppermute | solution.py:60
  99.1 12.1 %collective-permute-start.29 = (bf16[8,64,512]{2,1,0:T(8,128)(2,1)S(1)}, bf16[8,64,512]{2,1,0:T(8,128)(2,1)S(1)}, u32[]{:S(2)}, u32[]{:S(2)}) collective-permute-start(bf16[8,64,512]{2,1,0:T(8,128)(2,1)S(1)} %join.17.refs_2_), channel_id=1, source_target_pairs={{0,130},{1,13},{2,128},{3,15},{4,134},{5,9},{6,132},{7,11},{8,138}... | collective-permute-start | bytes 1572872 | tf_op jit(solution)/shard_map/ppermute | solution.py:60
  114.9 12.0 %collective-permute-start.40 = (bf16[256,512]{1,0:T(8,128)(2,1)S(1)}, bf16[256,512]{1,0:T(8,128)(2,1)S(1)}, u32[]{:S(2)}, u32[]{:S(2)}) collective-permute-start(bf16[256,512]{1,0:T(8,128)(2,1)S(1)} %get-tuple-element.70), channel_id=1, source_target_pairs={{0,1},{1,0},{2,3},{3,2},{4,5},{5,4},{6,7},{7,6},{8,9},{9,8},{10,11... | collective-permute-start | bytes 786440 | tf_op jit(solution)/shard_map/ppermute | solution.py:77
  (17 other events, 97.8 us)

commit v9 on v6

--- a/solution.py
+++ b/solution.py
@@ -130,7 +130,7 @@
 DONE = jax.ShapeDtypeStruct((8, 128), jnp.float32)
 
 
-PIECES = 4
+PIECES = 1
 
 
 def pack_acts_kernel(acts, grads, packed, done, sems):
@@ -295,31 +295,40 @@
 STRIPE = 1024
 
 
-def project_kernel(tokens, got, *refs):
+def stage_kernel(tokens, got, *refs):
+    both, sems = refs[-2:]
+    where = place()
+    run_all(
+        [
+            pltpu.make_async_copy(
+                tokens.at[:, columns_of(where, r, where[4])],
+                both.at[pl.ds(0, TOK), pl.ds(r * BLOCK, BLOCK)],
+                sems.at[r],
+            )
+            for r in range(BLOCKS)
+        ]
+        + [pltpu.make_async_copy(got, both.at[pl.ds(TOK, TOK)], sems.at[BLOCKS])]
+    )
+
+
+def stage(tokens, got, after):
+    return pl.pallas_call(
+        stage_kernel,
+        out_shape=jax.ShapeDtypeStruct((2 * TOK, HALF), jnp.bfloat16),
+        in_specs=[ANY, ANY] + [VMEM] * len(after),
+        out_specs=VMEM,
+        scratch_shapes=[pltpu.SemaphoreType.DMA((BLOCKS + 1,))],
+        compiler_params=PARAMS,
+        cost_estimate=cost(0, 8 << 20),
+        name="stage",
+    )(tokens, got, *after)
+
+
+def project_kernel(both, *refs):
     halves = refs[: 2 * PARTS]
-    kept, mine, theirs, both, weights, total, sems = refs[2 * PARTS :]
+    kept, mine, theirs, weights, total = refs[2 * PARTS :]
     where = place()
-    token_copies = [
-        pltpu.make_async_copy(
-            tokens.at[:, columns_of(where, r, where[4])],
-            both.at[:TOK, pl.ds(r * BLOCK, BLOCK)],
-            sems.at[r],
-        )
-        for r in range(BLOCKS)
-    ]
-    got_copies = [
-        pltpu.make_async_copy(
-            got.at[:, pl.ds(s * STRIPE, STRIPE)],
-            both.at[TOK:, pl.ds(s * STRIPE, STRIPE)],
-            sems.at[BLOCKS + s],
-        )
-        for s in range(HALF // STRIPE)
-    ]
     per = STRIPE // BLOCK
-    for s in range(HALF // STRIPE):
-        for k in range(per):
-            token_copies[s * per + k].start()
-        got_copies[s].start()
     starts = [pair_starts(where, m) for m in range(PARTS)]
 
     def keep_block(x_hi, block):
@@ -332,8 +341,6 @@
                 for j in range(2):
                     at = pl.ds(pl.multiple_of(k * BLOCK + starts[m][j], 32), 32)
                     weights[s % 2, at] = halves[2 * m + side][slot, j * 32 : j * 32 + 32]
-            token_copies[s * per + k].wait()
-        got_copies[s].wait()
         if s == 0:
             keep_block(where[0], weights[0, :BLOCK])
 
@@ -362,7 +369,7 @@
             theirs[...] = product[TOK:].astype(jnp.bfloat16)
 
 
-def project(tokens, got, halves):
+def project(both, halves):
     return pl.pallas_call(
         project_kernel,
         out_shape=(
@@ -370,18 +377,16 @@
             jax.ShapeDtypeStruct((TOK, COLS), jnp.float32),
             jax.ShapeDtypeStruct((TOK, COLS), jnp.bfloat16),
         ),
-        in_specs=[ANY, ANY] + [VMEM] * (2 * PARTS),
+        in_specs=[VMEM] * (1 + 2 * PARTS),
         out_specs=(VMEM,) * 3,
         scratch_shapes=[
-            pltpu.VMEM((2 * TOK, HALF), jnp.bfloat16),
             pltpu.VMEM((2, STRIPE, COLS), jnp.bfloat16),
             pltpu.VMEM((2 * TOK, COLS), jnp.float32),
-            pltpu.SemaphoreType.DMA((BLOCKS + HALF // STRIPE,)),
         ],
         compiler_params=PARAMS,
         cost_estimate=cost(2 * 2 * TOK * HALF * COLS, 9 << 20),
         name="project",
-    )(tokens, got, *halves)
+    )(both, *halves)
 
 
 def adamw_update(gradient, master_weights, first_moment, second_moment):
@@ -459,7 +464,9 @@
     new_master, new_first, new_second = (jnp.where(low, u[0], u[1]) for u in updated)
     rows = updated[0].astype(jnp.bfloat16).reshape(64, COLS)
 
-    kept_weights, mine, theirs = project(next_tokens, got_tokens, gather_parts(rows))
+    gathered = gather_parts(rows)
+    both = stage(next_tokens, got_tokens, gathered[::2])
+    kept_weights, mine, theirs = project(both, gathered)
     projection = (mine + wide(core_swap(theirs))).astype(jnp.bfloat16)
     return (new_master, new_first, new_second, kept_weights, projection)
 

time: 126 us -> 125 us (level)
  waiting for transfers between devices: 41.7 us -> 44 us
  starting transfers between devices: 60.7 us -> 58.6 us
    ppermute x8, waiting for transfers between devices: 15.8 us -> 17.5 us  [z_swap(): lax.ppermute(array, AXES, moves(lambda xh, z, y, xl, c: (xh, z ^ mask, y,...]
    ppermute x3, starting transfers between devices: 17.8 us -> 16.2 us  [core_swap(): lax.ppermute(array, AXES, moves(lambda xh, z, y, xl, c: (xh, z, y, xl, 1...]
  transfers between devices with their start and end apart: 43 -> 43, of which waited for: 25 -> 22; matrix products, arithmetic and copies ran while one was open for 1% -> 1% of each run, Pallas kernels for 1% -> 2%
where the time goes in v9:
time: 125 us
  starting transfers between devices  58.6 us (47%)
  waiting for transfers between devices  44 us (35%)
  Pallas kernels  15.3 us (12%)
  local copies, waits for them, and re-layouts  3.59 us (3%)
  other arithmetic  2.46 us (2%)
    ppermute x32, starting transfers between devices, across(): return lax.ppermute(array, AXES, PAIRINGS[pairing])  27.2 us
    ppermute x32, waiting for transfers between devices, across(): return lax.ppermute(array, AXES, PAIRINGS[pairing])  25.9 us
    ppermute x8, waiting for transfers between devices, z_swap(): lax.ppermute(array, AXES, moves(lambda xh, z, y, xl, c: (xh, z ^ mask, y,...  17.5 us
    ppermute x3, starting transfers between devices, core_swap(): lax.ppermute(array, AXES, moves(lambda xh, z, y, xl, c: (xh, z, y, xl, 1...  16.2 us
    ppermute x8, starting transfers between devices, z_swap(): lax.ppermute(array, AXES, moves(lambda xh, z, y, xl, c: (xh, z ^ mask, y,...  15.2 us
    pallas_call x1, Pallas kernels, gradient_term(): pl.pallas_call(term_kernel, out_shape=(half,) * (2 * PARTS), in_specs=[AN...  6.59 us
    unnamed x16, local copies, waits for them, and re-layouts  3.59 us
    pallas_call x1, Pallas kernels, pack_acts(): pl.pallas_call(pack_acts_kernel, out_shape=(jax.ShapeDtypeStruct((TOK, HA...  3.4 us
  transfers between devices with their start and end apart: 43, of which 22 were waited for; matrix products, arithmetic and copies ran while one was open for 1% of the time, Pallas kernels for 2%

profile of v9, /device:TPU:1, one launch (start us, length us, event | category | flops | bytes accessed | tf_op | source)
XLA Modules:
  0.0 124.9 jit_solution(16835531352366224121)
XLA Ops:
  0.7 3.4 %pack_acts.1 = (bf16[256,4608]{1,0:T(8,128)(2,1)}, f32[8,128]{1,0:T(8,128)}) custom-call(bf16[256,8192]{1,0:T(8,128)(2,1)} %acts.3, bf16[256,512]{1,0:T(8,128)(2,1)} %grads.3), custom_call_target="tpu_custom_call" | custom-call | bytes 4194304 | tf_op jit(solution)/shard_map/pack_acts/pallas_call | solution.py:145
  4.1 3.3 %collective-permute-start.1 = (bf16[256,4608]{1,0:T(8,128)(2,1)}, bf16[256,4608]{1,0:T(8,128)(2,1)S(1)}, u32[]{:S(2)}, u32[]{:S(2)}) collective-permute-start(bf16[256,4608]{1,0:T(8,128)(2,1)} %get-tuple-element.48), channel_id=1, source_target_pairs={{0,1},{1,0},{2,3},{3,2},{4,5},{5,4},{6,7},{7,6},{8,9},{9,8},{10,11... | collective-permute-start | bytes 7077896 | tf_op jit(solution)/shard_map/ppermute | solution.py:67
  7.4 2.2 %copy-done = bf16[256,8192]{1,0:T(8,128)(2,1)S(1)} copy-done((bf16[256,8192]{1,0:T(8,128)(2,1)S(1)}, bf16[256,8192]{1,0:T(8,128)(2,1)}, u32[]{:S(2)}) %copy-start) | copy-done | bytes 4194328
  12.5 6.6 %gradient_term.1 = (bf16[8,64,512]{2,1,0:T(8,128)(2,1)S(1)}, bf16[8,64,512]{2,1,0:T(8,128)(2,1)S(1)}, bf16[8,64,512]{2,1,0:T(8,128)(2,1)S(1)}, bf16[8,64,512]{2,...) custom-call(bf16[256,8192]{1,0:T(8,128)(2,1)S(1)} %copy-done.2, ...), custom_call_target="tpu_custom_call" | custom-call | flops 2147483648 | bytes 9437184 | tf_op jit(solution)/shard_map/gradient_term/pallas_call | solution.py:229
  19.2 1.4 %collective-permute-start.3 = (bf16[8,64,512]{2,1,0:T(8,128)(2,1)S(1)}, bf16[8,64,512]{2,1,0:T(8,128)(2,1)S(1)}, u32[]{:S(2)}, u32[]{:S(2)}) collective-permute-start(bf16[8,64,512]{2,1,0:T(8,128)(2,1)S(1)} %get-tuple-element.53), channel_id=1, source_target_pairs={{0,130},{1,13},{2,128},{3,15},{4,134},{5,9},{6,132},{7,11},{8,138}... | collective-permute-start | bytes 1572872 | tf_op jit(solution)/shard_map/ppermute | solution.py:59
  21.8 1.8 %collective-permute-start.5 = (bf16[8,64,512]{2,1,0:T(8,128)(2,1)S(1)}, bf16[8,64,512]{2,1,0:T(8,128)(2,1)S(1)}, u32[]{:S(2)}, u32[]{:S(2)}) collective-permute-start(bf16[8,64,512]{2,1,0:T(8,128)(2,1)S(1)} %get-tuple-element.57), channel_id=1, source_target_pairs={{0,12},{1,131},{2,14},{3,129},{4,8},{5,135},{6,10},{7,133},{8,4},{... | collective-permute-start | bytes 1572872 | tf_op jit(solution)/shard_map/ppermute | solution.py:59
  23.6 5.6 %collective-permute-start = (f32[3,32,512]{2,1,0:T(8,128)S(1)}, f32[3,32,512]{2,1,0:T(8,128)S(1)}, u32[]{:S(2)}, u32[]{:S(2)}) collective-permute-start(f32[3,32,512]{2,1,0:T(8,128)S(1)} %get-tuple-element.47), channel_id=1, source_target_pairs={{0,112},{1,113},{2,114},{3,115},{4,116},{5,117},{6,118},{7,119},{8... | collective-permute-start | bytes 589832 | tf_op jit(solution)/shard_map/ppermute | solution.py:63
  29.2 9.1 %collective-permute-done.refs_8_ = f32[3,32,512]{2,1,0:T(8,128)S(1)} collective-permute-done((f32[3,32,512]{2,1,0:T(8,128)S(1)}, f32[3,32,512]{2,1,0:T(8,128)S(1)}, u32[]{:S(2)}, u32[]{:S(2)}) %collective-permute-start) | collective-permute-done | bytes 196640 | tf_op jit(solution)/shard_map/ppermute | solution.py:63
  41.8 5.3 %collective-permute-done.10.refs_1_ = bf16[4,64,512]{2,1,0:T(8,128)(2,1)S(1)} collective-permute-done((bf16[4,64,512]{2,1,0:T(8,128)(2,1)S(1)}, bf16[4,64,512]{2,1,0:T(8,128)(2,1)S(1)}, u32[]{:S(2)}, u32[]{:S(2)}) %collective-permute-start.10) | collective-permute-done | bytes 262176 | tf_op jit(solution)/shard_map/ppermute | solution.py:59
  47.2 1.3 %collective-permute-start.11 = (bf16[2,64,512]{2,1,0:T(8,128)(2,1)S(1)}, bf16[2,64,512]{2,1,0:T(8,128)(2,1)S(1)}, u32[]{:S(2)}, u32[]{:S(2)}) collective-permute-start(bf16[2,64,512]{2,1,0:T(8,128)(2,1)S(1)} %get-tuple-element.69), channel_id=1, source_target_pairs={{0,2},{1,5},{2,0},{3,7},{4,6},{5,1},{6,4},{7,3},{8,10},{9,13},{10,... | collective-permute-start | bytes 393224 | tf_op jit(solution)/shard_map/ppermute | solution.py:59
  48.5 1.5 %collective-permute-start.15 = (bf16[2,64,512]{2,1,0:T(8,128)(2,1)S(1)}, bf16[2,64,512]{2,1,0:T(8,128)(2,1)S(1)}, u32[]{:S(2)}, u32[]{:S(2)}) collective-permute-start(bf16[2,64,512]{2,1,0:T(8,128)(2,1)S(1)} %get-tuple-element.75), channel_id=1, source_target_pairs={{0,12},{1,131},{2,14},{3,129},{4,8},{5,135},{6,10},{7,133},{8,4},{... | collective-permute-start | bytes 393224 | tf_op jit(solution)/shard_map/ppermute | solution.py:59
  56.5 2.3 %collective-permute-done.16 = bf16[64,512]{1,0:T(8,128)(2,1)S(1)} collective-permute-done((bf16[64,512]{1,0:T(8,128)(2,1)S(1)}, bf16[64,512]{1,0:T(8,128)(2,1)S(1)}, u32[]{:S(2)}, u32[]{:S(2)}) %collective-permute-start.16) | collective-permute-done | bytes 65568 | tf_op jit(solution)/shard_map/ppermute | solution.py:59
  59.2 1.4 %collective-permute-start.21 = (bf16[64,512]{1,0:T(8,128)(2,1)S(1)}, bf16[64,512]{1,0:T(8,128)(2,1)S(1)}, u32[]{:S(2)}, u32[]{:S(2)}) collective-permute-start(bf16[64,512]{1,0:T(8,128)(2,1)S(1)} %fusion.15), channel_id=1, source_target_pairs={{0,48},{1,49},{2,50},{3,51},{4,52},{5,53},{6,54},{7,55},{8,56},{9,... | collective-permute-start | bytes 196616 | tf_op jit(solution)/shard_map/ppermute | solution.py:63
  61.9 1.3 %collective-permute-done.17 = bf16[64,512]{1,0:T(8,128)(2,1)S(1)} collective-permute-done((bf16[64,512]{1,0:T(8,128)(2,1)S(1)}, bf16[64,512]{1,0:T(8,128)(2,1)S(1)}, u32[]{:S(2)}, u32[]{:S(2)}) %collective-permute-start.17) | collective-permute-done | bytes 65568 | tf_op jit(solution)/shard_map/ppermute | solution.py:63
  63.3 1.5 %collective-permute-done.21 = bf16[64,512]{1,0:T(8,128)(2,1)S(1)} collective-permute-done((bf16[64,512]{1,0:T(8,128)(2,1)S(1)}, bf16[64,512]{1,0:T(8,128)(2,1)S(1)}, u32[]{:S(2)}, u32[]{:S(2)}) %collective-permute-start.21) | collective-permute-done | bytes 65568 | tf_op jit(solution)/shard_map/ppermute | solution.py:63
  65.1 4.1 %collective-permute-start.22 = (bf16[64,512]{1,0:T(8,128)(2,1)S(1)}, bf16[64,512]{1,0:T(8,128)(2,1)S(1)}, u32[]{:S(2)}, u32[]{:S(2)}) collective-permute-start(bf16[64,512]{1,0:T(8,128)(2,1)S(1)} %fusion.21), channel_id=1, source_target_pairs={{0,112},{1,113},{2,114},{3,115},{4,116},{5,117},{6,118},{7,119},{8... | collective-permute-start | bytes 196616 | tf_op jit(solution)/shard_map/ppermute | solution.py:63
  69.3 2.2 %collective-permute-done.22 = bf16[64,512]{1,0:T(8,128)(2,1)S(1)} collective-permute-done((bf16[64,512]{1,0:T(8,128)(2,1)S(1)}, bf16[64,512]{1,0:T(8,128)(2,1)S(1)}, u32[]{:S(2)}, u32[]{:S(2)}) %collective-permute-start.22) | collective-permute-done | bytes 65568 | tf_op jit(solution)/shard_map/ppermute | solution.py:63
  71.7 1.8 %collective-permute-start.34 = (bf16[64,512]{1,0:T(8,128)(2,1)S(1)}, bf16[64,512]{1,0:T(8,128)(2,1)S(1)}, u32[]{:S(2)}, u32[]{:S(2)}) collective-permute-start(bf16[64,512]{1,0:T(8,128)(2,1)S(1)} %fusion.12), channel_id=1, source_target_pairs={{0,48},{1,49},{2,50},{3,51},{4,52},{5,53},{6,54},{7,55},{8,56},{9,... | collective-permute-start | bytes 196616 | tf_op jit(solution)/shard_map/ppermute | solution.py:63
  73.5 1.9 %collective-permute-start.30 = (bf16[64,512]{1,0:T(8,128)(2,1)S(1)}, bf16[64,512]{1,0:T(8,128)(2,1)S(1)}, u32[]{:S(2)}, u32[]{:S(2)}) collective-permute-start(bf16[64,512]{1,0:T(8,128)(2,1)S(1)} %fusion.12), channel_id=1, source_target_pairs={{0,32},{1,33},{2,34},{3,35},{4,36},{5,37},{6,38},{7,39},{8,40},{9,... | collective-permute-start | bytes 196616 | tf_op jit(solution)/shard_map/ppermute | solution.py:63
  76.8 2.2 %collective-permute-done.30 = bf16[64,512]{1,0:T(8,128)(2,1)S(1)} collective-permute-done((bf16[64,512]{1,0:T(8,128)(2,1)S(1)}, bf16[64,512]{1,0:T(8,128)(2,1)S(1)}, u32[]{:S(2)}, u32[]{:S(2)}) %collective-permute-start.30) | collective-permute-done | bytes 65568 | tf_op jit(solution)/shard_map/ppermute | solution.py:63
  79.8 1.9 %collective-permute-start.24 = (bf16[2,64,512]{2,1,0:T(8,128)(2,1)S(1)}, bf16[2,64,512]{2,1,0:T(8,128)(2,1)S(1)}, u32[]{:S(2)}, u32[]{:S(2)}) collective-permute-start(bf16[2,64,512]{2,1,0:T(8,128)(2,1)S(1)} %join.12.here), channel_id=1, source_target_pairs={{0,130},{1,13},{2,128},{3,15},{4,134},{5,9},{6,132},{7,11},{8,138}... | collective-permute-start | bytes 393224 | tf_op jit(solution)/shard_map/ppermute | solution.py:59
  81.7 1.5 %collective-permute-start.36 = (bf16[2,64,512]{2,1,0:T(8,128)(2,1)S(1)}, bf16[2,64,512]{2,1,0:T(8,128)(2,1)S(1)}, u32[]{:S(2)}, u32[]{:S(2)}) collective-permute-start(bf16[2,64,512]{2,1,0:T(8,128)(2,1)S(1)} %join.21.here), channel_id=1, source_target_pairs={{0,4},{1,3},{2,6},{3,1},{4,0},{5,7},{6,2},{7,5},{8,12},{9,11},{10,... | collective-permute-start | bytes 393224 | tf_op jit(solution)/shard_map/ppermute | solution.py:59
  85.1 1.4 %collective-permute-start.25 = (bf16[4,64,512]{2,1,0:T(8,128)(2,1)S(1)}, bf16[4,64,512]{2,1,0:T(8,128)(2,1)S(1)}, u32[]{:S(2)}, u32[]{:S(2)}) collective-permute-start(bf16[4,64,512]{2,1,0:T(8,128)(2,1)S(1)} %join.13.here), channel_id=1, source_target_pairs={{0,4},{1,3},{2,6},{3,1},{4,0},{5,7},{6,2},{7,5},{8,12},{9,11},{10,... | collective-permute-start | bytes 786440 | tf_op jit(solution)/shard_map/ppermute | solution.py:59
  86.5 2.3 %collective-permute-start.37 = (bf16[4,64,512]{2,1,0:T(8,128)(2,1)S(1)}, bf16[4,64,512]{2,1,0:T(8,128)(2,1)S(1)}, u32[]{:S(2)}, u32[]{:S(2)}) collective-permute-start(bf16[4,64,512]{2,1,0:T(8,128)(2,1)S(1)} %join.22.here), channel_id=1, source_target_pairs={{0,130},{1,13},{2,128},{3,15},{4,134},{5,9},{6,132},{7,11},{8,138}... | collective-permute-start | bytes 786440 | tf_op jit(solution)/shard_map/ppermute | solution.py:59
  88.9 1.9 %collective-permute-start.29 = (bf16[4,64,512]{2,1,0:T(8,128)(2,1)S(1)}, bf16[4,64,512]{2,1,0:T(8,128)(2,1)S(1)}, u32[]{:S(2)}, u32[]{:S(2)}) collective-permute-start(bf16[4,64,512]{2,1,0:T(8,128)(2,1)S(1)} %join.16.here), channel_id=1, source_target_pairs={{0,12},{1,131},{2,14},{3,129},{4,8},{5,135},{6,10},{7,133},{8,4},{... | collective-permute-start | bytes 786440 | tf_op jit(solution)/shard_map/ppermute | solution.py:59
  94.3 1.3 %collective-permute-done.33.got = bf16[4,64,512]{2,1,0:T(8,128)(2,1)S(1)} collective-permute-done((bf16[4,64,512]{2,1,0:T(8,128)(2,1)S(1)}, bf16[4,64,512]{2,1,0:T(8,128)(2,1)S(1)}, u32[]{:S(2)}, u32[]{:S(2)}) %collective-permute-start.33) | collective-permute-done | bytes 262176 | tf_op jit(solution)/shard_map/ppermute | solution.py:59
  96.9 1.3 %collective-permute-start.39 = (bf16[8,64,512]{2,1,0:T(8,128)(2,1)S(1)}, bf16[8,64,512]{2,1,0:T(8,128)(2,1)S(1)}, u32[]{:S(2)}, u32[]{:S(2)}) collective-permute-start(bf16[8,64,512]{2,1,0:T(8,128)(2,1)S(1)} %join.17.refs_1_.refs_2_), channel_id=1, source_target_pairs={{0,130},{1,13},{2,128},{3,15},{4,134},{5,9},{6,132},{7,11},{8,138}... | collective-permute-start | bytes 1572872 | tf_op jit(solution)/shard_map/ppermute | solution.py:59
  98.9 4.4 %collective-permute-done.38.refs_1_ = bf16[8,64,512]{2,1,0:T(8,128)(2,1)S(1)} collective-permute-done((bf16[8,64,512]{2,1,0:T(8,128)(2,1)S(1)}, bf16[8,64,512]{2,1,0:T(8,128)(2,1)S(1)}, u32[]{:S(2)}, u32[]{:S(2)}) %collective-permute-start.38) | collective-permute-done | bytes 524320 | tf_op jit(solution)/shard_map/ppermute | solution.py:59
  103.3 2.2 %collective-permute-done.40.refs_5_ = bf16[8,64,512]{2,1,0:T(8,128)(2,1)S(1)} collective-permute-done((bf16[8,64,512]{2,1,0:T(8,128)(2,1)S(1)}, bf16[8,64,512]{2,1,0:T(8,128)(2,1)S(1)}, u32[]{:S(2)}, u32[]{:S(2)}) %collective-permute-start.40) | collective-permute-done | bytes 524320 | tf_op jit(solution)/shard_map/ppermute | solution.py:59
  105.5 2.9 %collective-permute-done.39.refs_3_ = bf16[8,64,512]{2,1,0:T(8,128)(2,1)S(1)} collective-permute-done((bf16[8,64,512]{2,1,0:T(8,128)(2,1)S(1)}, bf16[8,64,512]{2,1,0:T(8,128)(2,1)S(1)}, u32[]{:S(2)}, u32[]{:S(2)}) %collective-permute-start.39) | collective-permute-done | bytes 524320 | tf_op jit(solution)/shard_map/ppermute | solution.py:59
  108.4 2.6 %project.1 = (bf16[512,512]{1,0:T(8,128)(2,1)}, f32[256,512]{1,0:T(8,128)S(1)}, bf16[256,512]{1,0:T(8,128)(2,1)S(1)}) custom-call(bf16[512,4096]{1,0:T(8,128)(2,1)S(1)} %stage.1.both, bf16[8,64,512]{2,1,0:T(8,128)(2,1)S(1)} %join.14.refs_0_, bf16[8,64,512]{2,1,0:T(8,128)(2,1)S(1)} %collective-permute-done.38.refs_1_, ...), custom_call_target="tpu_custom_call" | custom-call | flops 2147483648 | bytes 9437184 | tf_op jit(solution)/shard_map/project/pallas_call | solution.py:373
  111.0 11.8 %collective-permute-start.42 = (bf16[256,512]{1,0:T(8,128)(2,1)S(1)}, bf16[256,512]{1,0:T(8,128)(2,1)S(1)}, u32[]{:S(2)}, u32[]{:S(2)}) collective-permute-start(bf16[256,512]{1,0:T(8,128)(2,1)S(1)} %get-tuple-element.86), channel_id=1, source_target_pairs={{0,1},{1,0},{2,3},{3,2},{4,5},{5,4},{6,7},{7,6},{8,9},{9,8},{10,11... | collective-permute-start | bytes 786440 | tf_op jit(solution)/shard_map/ppermute | solution.py:67
  (107 shorter events, 28.0 us)
Async XLA Ops:
  4.1 7.7 %collective-permute-start.1 = (bf16[256,4608]{1,0:T(8,128)(2,1)}, bf16[256,4608]{1,0:T(8,128)(2,1)S(1)}, u32[]{:S(2)}, u32[]{:S(2)}) collective-permute-start(bf16[256,4608]{1,0:T(8,128)(2,1)} %get-tuple-element.48), channel_id=1, source_target_pairs={{0,1},{1,0},{2,3},{3,2},{4,5},{5,4},{6,7},{7,6},{8,9},{9,8},{10,11... | collective-permute-start | bytes 7077896 | tf_op jit(solution)/shard_map/ppermute | solution.py:67
  19.1 19.2 %collective-permute-start.2 = (bf16[8,64,512]{2,1,0:T(8,128)(2,1)S(1)}, bf16[8,64,512]{2,1,0:T(8,128)(2,1)S(1)}, u32[]{:S(2)}, u32[]{:S(2)}) collective-permute-start(bf16[8,64,512]{2,1,0:T(8,128)(2,1)S(1)} %get-tuple-element.51), channel_id=1, source_target_pairs={{0,2},{1,5},{2,0},{3,7},{4,6},{5,1},{6,4},{7,3},{8,10},{9,13},{10,... | collective-permute-start | bytes 1572872 | tf_op jit(solution)/shard_map/ppermute | solution.py:59
  19.2 19.1 %collective-permute-start.3 = (bf16[8,64,512]{2,1,0:T(8,128)(2,1)S(1)}, bf16[8,64,512]{2,1,0:T(8,128)(2,1)S(1)}, u32[]{:S(2)}, u32[]{:S(2)}) collective-permute-start(bf16[8,64,512]{2,1,0:T(8,128)(2,1)S(1)} %get-tuple-element.53), channel_id=1, source_target_pairs={{0,130},{1,13},{2,128},{3,15},{4,134},{5,9},{6,132},{7,11},{8,138}... | collective-permute-start | bytes 1572872 | tf_op jit(solution)/shard_map/ppermute | solution.py:59
  20.6 17.7 %collective-permute-start.4 = (bf16[8,64,512]{2,1,0:T(8,128)(2,1)S(1)}, bf16[8,64,512]{2,1,0:T(8,128)(2,1)S(1)}, u32[]{:S(2)}, u32[]{:S(2)}) collective-permute-start(bf16[8,64,512]{2,1,0:T(8,128)(2,1)S(1)} %get-tuple-element.55), channel_id=1, source_target_pairs={{0,4},{1,3},{2,6},{3,1},{4,0},{5,7},{6,2},{7,5},{8,12},{9,11},{10,... | collective-permute-start | bytes 1572872 | tf_op jit(solution)/shard_map/ppermute | solution.py:59
  21.8 16.5 %collective-permute-start.5 = (bf16[8,64,512]{2,1,0:T(8,128)(2,1)S(1)}, bf16[8,64,512]{2,1,0:T(8,128)(2,1)S(1)}, u32[]{:S(2)}, u32[]{:S(2)}) collective-permute-start(bf16[8,64,512]{2,1,0:T(8,128)(2,1)S(1)} %get-tuple-element.57), channel_id=1, source_target_pairs={{0,12},{1,131},{2,14},{3,129},{4,8},{5,135},{6,10},{7,133},{8,4},{... | collective-permute-start | bytes 1572872 | tf_op jit(solution)/shard_map/ppermute | solution.py:59
  23.6 14.7 %collective-permute-start = (f32[3,32,512]{2,1,0:T(8,128)S(1)}, f32[3,32,512]{2,1,0:T(8,128)S(1)}, u32[]{:S(2)}, u32[]{:S(2)}) collective-permute-start(f32[3,32,512]{2,1,0:T(8,128)S(1)} %get-tuple-element.47), channel_id=1, source_target_pairs={{0,112},{1,113},{2,114},{3,115},{4,116},{5,117},{6,118},{7,119},{8... | collective-permute-start | bytes 589832 | tf_op jit(solution)/shard_map/ppermute | solution.py:63
  38.8 21.8 %collective-permute-start.8 = (bf16[256,4096]{1,0:T(8,128)(2,1)S(1)}, bf16[256,4096]{1,0:T(8,128)(2,1)S(1)}, u32[]{:S(2)}, u32[]{:S(2)}) collective-permute-start(bf16[256,4096]{1,0:T(8,128)(2,1)S(1)} %get-tuple-element.63), channel_id=1, source_target_pairs={{0,1},{1,0},{2,3},{3,2},{4,5},{5,4},{6,7},{7,6},{8,9},{9,8},{10,11... | collective-permute-start | bytes 6291464 | tf_op jit(solution)/shard_map/ppermute | solution.py:67
  39.9 7.2 %collective-permute-start.10 = (bf16[4,64,512]{2,1,0:T(8,128)(2,1)S(1)}, bf16[4,64,512]{2,1,0:T(8,128)(2,1)S(1)}, u32[]{:S(2)}, u32[]{:S(2)}) collective-permute-start(bf16[4,64,512]{2,1,0:T(8,128)(2,1)S(1)} %get-tuple-element.67), channel_id=1, source_target_pairs={{0,12},{1,131},{2,14},{3,129},{4,8},{5,135},{6,10},{7,133},{8,4},{... | collective-permute-start | bytes 786440 | tf_op jit(solution)/shard_map/ppermute | solution.py:59
  40.8 7.7 %collective-permute-start.14 = (bf16[4,64,512]{2,1,0:T(8,128)(2,1)S(1)}, bf16[4,64,512]{2,1,0:T(8,128)(2,1)S(1)}, u32[]{:S(2)}, u32[]{:S(2)}) collective-permute-start(bf16[4,64,512]{2,1,0:T(8,128)(2,1)S(1)} %get-tuple-element.73), channel_id=1, source_target_pairs={{0,2},{1,5},{2,0},{3,7},{4,6},{5,1},{6,4},{7,3},{8,10},{9,13},{10,... | collective-permute-start | bytes 786440 | tf_op jit(solution)/shard_map/ppermute | solution.py:59
  41.2 8.9 %collective-permute-start.18 = (bf16[4,64,512]{2,1,0:T(8,128)(2,1)S(1)}, bf16[4,64,512]{2,1,0:T(8,128)(2,1)S(1)}, u32[]{:S(2)}, u32[]{:S(2)}) collective-permute-start(bf16[4,64,512]{2,1,0:T(8,128)(2,1)S(1)} %get-tuple-element.79), channel_id=1, source_target_pairs={{0,130},{1,13},{2,128},{3,15},{4,134},{5,9},{6,132},{7,11},{8,138}... | collective-permute-start | bytes 786440 | tf_op jit(solution)/shard_map/ppermute | solution.py:59
  41.8 10.0 %collective-permute-start.6 = (bf16[4,64,512]{2,1,0:T(8,128)(2,1)S(1)}, bf16[4,64,512]{2,1,0:T(8,128)(2,1)S(1)}, u32[]{:S(2)}, u32[]{:S(2)}) collective-permute-start(bf16[4,64,512]{2,1,0:T(8,128)(2,1)S(1)} %get-tuple-element.60), channel_id=1, source_target_pairs={{0,4},{1,3},{2,6},{3,1},{4,0},{5,7},{6,2},{7,5},{8,12},{9,11},{10,... | collective-permute-start | bytes 786440 | tf_op jit(solution)/shard_map/ppermute | solution.py:59
  48.5 5.3 %collective-permute-start.15 = (bf16[2,64,512]{2,1,0:T(8,128)(2,1)S(1)}, bf16[2,64,512]{2,1,0:T(8,128)(2,1)S(1)}, u32[]{:S(2)}, u32[]{:S(2)}) collective-permute-start(bf16[2,64,512]{2,1,0:T(8,128)(2,1)S(1)} %get-tuple-element.75), channel_id=1, source_target_pairs={{0,12},{1,131},{2,14},{3,129},{4,8},{5,135},{6,10},{7,133},{8,4},{... | collective-permute-start | bytes 393224 | tf_op jit(solution)/shard_map/ppermute | solution.py:59
  50.1 5.5 %collective-permute-start.19 = (bf16[2,64,512]{2,1,0:T(8,128)(2,1)S(1)}, bf16[2,64,512]{2,1,0:T(8,128)(2,1)S(1)}, u32[]{:S(2)}, u32[]{:S(2)}) collective-permute-start(bf16[2,64,512]{2,1,0:T(8,128)(2,1)S(1)} %get-tuple-element.81), channel_id=1, source_target_pairs={{0,4},{1,3},{2,6},{3,1},{4,0},{5,7},{6,2},{7,5},{8,12},{9,11},{10,... | collective-permute-start | bytes 393224 | tf_op jit(solution)/shard_map/ppermute | solution.py:59
  51.1 5.3 %collective-permute-start.12 = (bf16[64,512]{1,0:T(8,128)(2,1)S(1)}, bf16[64,512]{1,0:T(8,128)(2,1)S(1)}, u32[]{:S(2)}, u32[]{:S(2)}) collective-permute-start(bf16[64,512]{1,0:T(8,128)(2,1)S(1)} %bitcast.84), channel_id=1, source_target_pairs={{0,4},{1,3},{2,6},{3,1},{4,0},{5,7},{6,2},{7,5},{8,12},{9,11},{10,... | collective-permute-start | bytes 196616 | tf_op jit(solution)/shard_map/ppermute | solution.py:59
  51.8 8.8 %collective-permute-start.7 = (bf16[2,64,512]{2,1,0:T(8,128)(2,1)S(1)}, bf16[2,64,512]{2,1,0:T(8,128)(2,1)S(1)}, u32[]{:S(2)}, u32[]{:S(2)}) collective-permute-start(bf16[2,64,512]{2,1,0:T(8,128)(2,1)S(1)} %get-tuple-element.62), channel_id=1, source_target_pairs={{0,130},{1,13},{2,128},{3,15},{4,134},{5,9},{6,132},{7,11},{8,138}... | collective-permute-start | bytes 393224 | tf_op jit(solution)/shard_map/ppermute | solution.py:59
  56.4 5.5 %collective-permute-start.13 = (bf16[64,512]{1,0:T(8,128)(2,1)S(1)}, bf16[64,512]{1,0:T(8,128)(2,1)S(1)}, u32[]{:S(2)}, u32[]{:S(2)}) collective-permute-start(bf16[64,512]{1,0:T(8,128)(2,1)S(1)} %fusion.17), channel_id=1, source_target_pairs={{0,16},{1,17},{2,18},{3,19},{4,20},{5,21},{6,22},{7,23},{8,24},{9,... | collective-permute-start | bytes 196616 | tf_op jit(solution)/shard_map/ppermute | solution.py:63
  59.2 5.6 %collective-permute-start.21 = (bf16[64,512]{1,0:T(8,128)(2,1)S(1)}, bf16[64,512]{1,0:T(8,128)(2,1)S(1)}, u32[]{:S(2)}, u32[]{:S(2)}) collective-permute-start(bf16[64,512]{1,0:T(8,128)(2,1)S(1)} %fusion.15), channel_id=1, source_target_pairs={{0,48},{1,49},{2,50},{3,51},{4,52},{5,53},{6,54},{7,55},{8,56},{9,... | collective-permute-start | bytes 196616 | tf_op jit(solution)/shard_map/ppermute | solution.py:63
  65.1 6.3 %collective-permute-start.22 = (bf16[64,512]{1,0:T(8,128)(2,1)S(1)}, bf16[64,512]{1,0:T(8,128)(2,1)S(1)}, u32[]{:S(2)}, u32[]{:S(2)}) collective-permute-start(bf16[64,512]{1,0:T(8,128)(2,1)S(1)} %fusion.21), channel_id=1, source_target_pairs={{0,112},{1,113},{2,114},{3,115},{4,116},{5,117},{6,118},{7,119},{8... | collective-permute-start | bytes 196616 | tf_op jit(solution)/shard_map/ppermute | solution.py:63
  71.7 5.0 %collective-permute-start.34 = (bf16[64,512]{1,0:T(8,128)(2,1)S(1)}, bf16[64,512]{1,0:T(8,128)(2,1)S(1)}, u32[]{:S(2)}, u32[]{:S(2)}) collective-permute-start(bf16[64,512]{1,0:T(8,128)(2,1)S(1)} %fusion.12), channel_id=1, source_target_pairs={{0,48},{1,49},{2,50},{3,51},{4,52},{5,53},{6,54},{7,55},{8,56},{9,... | collective-permute-start | bytes 196616 | tf_op jit(solution)/shard_map/ppermute | solution.py:63
  73.5 5.4 %collective-permute-start.30 = (bf16[64,512]{1,0:T(8,128)(2,1)S(1)}, bf16[64,512]{1,0:T(8,128)(2,1)S(1)}, u32[]{:S(2)}, u32[]{:S(2)}) collective-permute-start(bf16[64,512]{1,0:T(8,128)(2,1)S(1)} %fusion.12), channel_id=1, source_target_pairs={{0,32},{1,33},{2,34},{3,35},{4,36},{5,37},{6,38},{7,39},{8,40},{9,... | collective-permute-start | bytes 196616 | tf_op jit(solution)/shard_map/ppermute | solution.py:63
  79.8 5.3 %collective-permute-start.24 = (bf16[2,64,512]{2,1,0:T(8,128)(2,1)S(1)}, bf16[2,64,512]{2,1,0:T(8,128)(2,1)S(1)}, u32[]{:S(2)}, u32[]{:S(2)}) collective-permute-start(bf16[2,64,512]{2,1,0:T(8,128)(2,1)S(1)} %join.12.here), channel_id=1, source_target_pairs={{0,130},{1,13},{2,128},{3,15},{4,134},{5,9},{6,132},{7,11},{8,138}... | collective-permute-start | bytes 393224 | tf_op jit(solution)/shard_map/ppermute | solution.py:59
  83.6 5.2 %collective-permute-start.32 = (bf16[2,64,512]{2,1,0:T(8,128)(2,1)S(1)}, bf16[2,64,512]{2,1,0:T(8,128)(2,1)S(1)}, u32[]{:S(2)}, u32[]{:S(2)}) collective-permute-start(bf16[2,64,512]{2,1,0:T(8,128)(2,1)S(1)} %join.18.here), channel_id=1, source_target_pairs={{0,12},{1,131},{2,14},{3,129},{4,8},{5,135},{6,10},{7,133},{8,4},{... | collective-permute-start | bytes 393224 | tf_op jit(solution)/shard_map/ppermute | solution.py:59
  83.7 5.2 %collective-permute-start.28 = (bf16[2,64,512]{2,1,0:T(8,128)(2,1)S(1)}, bf16[2,64,512]{2,1,0:T(8,128)(2,1)S(1)}, u32[]{:S(2)}, u32[]{:S(2)}) collective-permute-start(bf16[2,64,512]{2,1,0:T(8,128)(2,1)S(1)} %join.15.here), channel_id=1, source_target_pairs={{0,2},{1,5},{2,0},{3,7},{4,6},{5,1},{6,4},{7,3},{8,10},{9,13},{10,... | collective-permute-start | bytes 393224 | tf_op jit(solution)/shard_map/ppermute | solution.py:59
  85.1 5.8 %collective-permute-start.25 = (bf16[4,64,512]{2,1,0:T(8,128)(2,1)S(1)}, bf16[4,64,512]{2,1,0:T(8,128)(2,1)S(1)}, u32[]{:S(2)}, u32[]{:S(2)}) collective-permute-start(bf16[4,64,512]{2,1,0:T(8,128)(2,1)S(1)} %join.13.here), channel_id=1, source_target_pairs={{0,4},{1,3},{2,6},{3,1},{4,0},{5,7},{6,2},{7,5},{8,12},{9,11},{10,... | collective-permute-start | bytes 786440 | tf_op jit(solution)/shard_map/ppermute | solution.py:59
  86.5 6.5 %collective-permute-start.37 = (bf16[4,64,512]{2,1,0:T(8,128)(2,1)S(1)}, bf16[4,64,512]{2,1,0:T(8,128)(2,1)S(1)}, u32[]{:S(2)}, u32[]{:S(2)}) collective-permute-start(bf16[4,64,512]{2,1,0:T(8,128)(2,1)S(1)} %join.22.here), channel_id=1, source_target_pairs={{0,130},{1,13},{2,128},{3,15},{4,134},{5,9},{6,132},{7,11},{8,138}... | collective-permute-start | bytes 786440 | tf_op jit(solution)/shard_map/ppermute | solution.py:59
  88.8 6.8 %collective-permute-start.33 = (bf16[4,64,512]{2,1,0:T(8,128)(2,1)S(1)}, bf16[4,64,512]{2,1,0:T(8,128)(2,1)S(1)}, u32[]{:S(2)}, u32[]{:S(2)}) collective-permute-start(bf16[4,64,512]{2,1,0:T(8,128)(2,1)S(1)} %join.19.here), channel_id=1, source_target_pairs={{0,2},{1,5},{2,0},{3,7},{4,6},{5,1},{6,4},{7,3},{8,10},{9,13},{10,... | collective-permute-start | bytes 786440 | tf_op jit(solution)/shard_map/ppermute | solution.py:59
  88.9 7.9 %collective-permute-start.29 = (bf16[4,64,512]{2,1,0:T(8,128)(2,1)S(1)}, bf16[4,64,512]{2,1,0:T(8,128)(2,1)S(1)}, u32[]{:S(2)}, u32[]{:S(2)}) collective-permute-start(bf16[4,64,512]{2,1,0:T(8,128)(2,1)S(1)} %join.16.here), channel_id=1, source_target_pairs={{0,12},{1,131},{2,14},{3,129},{4,8},{5,135},{6,10},{7,133},{8,4},{... | collective-permute-start | bytes 786440 | tf_op jit(solution)/shard_map/ppermute | solution.py:59
  90.9 12.4 %collective-permute-start.38 = (bf16[8,64,512]{2,1,0:T(8,128)(2,1)S(1)}, bf16[8,64,512]{2,1,0:T(8,128)(2,1)S(1)}, u32[]{:S(2)}, u32[]{:S(2)}) collective-permute-start(bf16[8,64,512]{2,1,0:T(8,128)(2,1)S(1)} %join.14.refs_0_), channel_id=1, source_target_pairs={{0,2},{1,5},{2,0},{3,7},{4,6},{5,1},{6,4},{7,3},{8,10},{9,13},{10,... | collective-permute-start | bytes 1572872 | tf_op jit(solution)/shard_map/ppermute | solution.py:59
  93.0 10.3 %collective-permute-start.41 = (bf16[8,64,512]{2,1,0:T(8,128)(2,1)S(1)}, bf16[8,64,512]{2,1,0:T(8,128)(2,1)S(1)}, u32[]{:S(2)}, u32[]{:S(2)}) collective-permute-start(bf16[8,64,512]{2,1,0:T(8,128)(2,1)S(1)} %join.23.refs_3_.refs_6_), channel_id=1, source_target_pairs={{0,12},{1,131},{2,14},{3,129},{4,8},{5,135},{6,10},{7,133},{8,4},{... | collective-permute-start | bytes 1572872 | tf_op jit(solution)/shard_map/ppermute | solution.py:59
  95.7 9.8 %collective-permute-start.40 = (bf16[8,64,512]{2,1,0:T(8,128)(2,1)S(1)}, bf16[8,64,512]{2,1,0:T(8,128)(2,1)S(1)}, u32[]{:S(2)}, u32[]{:S(2)}) collective-permute-start(bf16[8,64,512]{2,1,0:T(8,128)(2,1)S(1)} %join.20.refs_2_.refs_4_), channel_id=1, source_target_pairs={{0,4},{1,3},{2,6},{3,1},{4,0},{5,7},{6,2},{7,5},{8,12},{9,11},{10,... | collective-permute-start | bytes 1572872 | tf_op jit(solution)/shard_map/ppermute | solution.py:59
  96.9 11.5 %collective-permute-start.39 = (bf16[8,64,512]{2,1,0:T(8,128)(2,1)S(1)}, bf16[8,64,512]{2,1,0:T(8,128)(2,1)S(1)}, u32[]{:S(2)}, u32[]{:S(2)}) collective-permute-start(bf16[8,64,512]{2,1,0:T(8,128)(2,1)S(1)} %join.17.refs_1_.refs_2_), channel_id=1, source_target_pairs={{0,130},{1,13},{2,128},{3,15},{4,134},{5,9},{6,132},{7,11},{8,138}... | collective-permute-start | bytes 1572872 | tf_op jit(solution)/shard_map/ppermute | solution.py:59
  111.0 13.2 %collective-permute-start.42 = (bf16[256,512]{1,0:T(8,128)(2,1)S(1)}, bf16[256,512]{1,0:T(8,128)(2,1)S(1)}, u32[]{:S(2)}, u32[]{:S(2)}) collective-permute-start(bf16[256,512]{1,0:T(8,128)(2,1)S(1)} %get-tuple-element.86), channel_id=1, source_target_pairs={{0,1},{1,0},{2,3},{3,2},{4,5},{5,4},{6,7},{7,6},{8,9},{9,8},{10,11... | collective-permute-start | bytes 786440 | tf_op jit(solution)/shard_map/ppermute | solution.py:67
  (19 other events, 94.1 us)

commit v10 on v9

--- a/solution.py
+++ b/solution.py
@@ -96,7 +96,6 @@
 ANY = pl.BlockSpec(memory_space=pl.ANY)
 VMEM = pl.BlockSpec(memory_space=pltpu.VMEM)
 PARAMS = pltpu.CompilerParams(vmem_limit_bytes=40 * 1024 * 1024)
-WHOLE = pltpu.CompilerParams(vmem_limit_bytes=60 * 1024 * 1024)
 
 
 def cost(flops, size):
@@ -148,7 +147,7 @@
         in_specs=[ANY, ANY],
         out_specs=(VMEM, VMEM),
         scratch_shapes=[pltpu.SemaphoreType.DMA((BLOCKS * PIECES + 1,))],
-        compiler_params=WHOLE,
+        compiler_params=PARAMS,
         cost_estimate=cost(0, 4 << 20),
         name="pack_acts",
     )(acts, grads)

time: 125 us -> 125 us (level)
  Pallas kernels: 15.3 us -> 12.4 us
  local copies, waits for them, and re-layouts: 3.59 us -> 5.99 us
    pallas_call x1, Pallas kernels: 3.4 us -> 0.55 us  [pack_acts(): pl.pallas_call(pack_acts_kernel, out_shape=(jax.ShapeDtypeStruct((TOK, HA...]
    unnamed x16 -> x18, local copies, waits for them, and re-layouts: 3.59 us -> 5.99 us
    ppermute x8, waiting for transfers between devices: 17.5 us -> 15.2 us  [z_swap(): lax.ppermute(array, AXES, moves(lambda xh, z, y, xl, c: (xh, z ^ mask, y,...]
    ppermute x32, waiting for transfers between devices: 25.9 us -> 27.9 us  [across(): return lax.ppermute(array, AXES, PAIRINGS[pairing])]
  transfers between devices with their start and end apart: 43 -> 43, of which waited for: 22 -> 23; matrix products, arithmetic and copies ran while one was open for 1% -> 1% of each run, Pallas kernels for 2% -> 2%
where the time goes in v10:
time: 125 us
  starting transfers between devices  59.6 us (48%)
  waiting for transfers between devices  43.9 us (35%)
  Pallas kernels  12.4 us (10%)
  local copies, waits for them, and re-layouts  5.99 us (5%)
  other arithmetic  2.47 us (2%)
    ppermute x32, starting transfers between devices, across(): return lax.ppermute(array, AXES, PAIRINGS[pairing])  28.1 us
    ppermute x32, waiting for transfers between devices, across(): return lax.ppermute(array, AXES, PAIRINGS[pairing])  27.9 us
    ppermute x3, starting transfers between devices, core_swap(): lax.ppermute(array, AXES, moves(lambda xh, z, y, xl, c: (xh, z, y, xl, 1...  15.8 us
    ppermute x8, starting transfers between devices, z_swap(): lax.ppermute(array, AXES, moves(lambda xh, z, y, xl, c: (xh, z ^ mask, y,...  15.7 us
    ppermute x8, waiting for transfers between devices, z_swap(): lax.ppermute(array, AXES, moves(lambda xh, z, y, xl, c: (xh, z ^ mask, y,...  15.2 us
    pallas_call x1, Pallas kernels, gradient_term(): pl.pallas_call(term_kernel, out_shape=(half,) * (2 * PARTS), in_specs=[AN...  6.55 us
    unnamed x18, local copies, waits for them, and re-layouts  5.99 us
    pallas_call x1, Pallas kernels, project(): pl.pallas_call(project_kernel, out_shape=(jax.ShapeDtypeStruct((2 * BLOCK...  2.6 us
  transfers between devices with their start and end apart: 43, of which 23 were waited for; matrix products, arithmetic and copies ran while one was open for 1% of the time, Pallas kernels for 2%

profile of v10, /device:TPU:1, one launch (start us, length us, event | category | flops | bytes accessed | tf_op | source)
XLA Modules:
  0.0 125.2 jit_solution(14581887419414921165)
XLA Ops:
  0.7 2.3 %copy-done.2 = bf16[256,8192]{1,0:T(8,128)(2,1)S(1)} copy-done((bf16[256,8192]{1,0:T(8,128)(2,1)S(1)}, bf16[256,8192]{1,0:T(8,128)(2,1)}, u32[]{:S(2)}) %copy-start.2) | copy-done | bytes 4194328
  4.7 3.3 %collective-permute-start.1 = (bf16[256,4608]{1,0:T(8,128)(2,1)S(1)}, bf16[256,4608]{1,0:T(8,128)(2,1)S(1)}, u32[]{:S(2)}, u32[]{:S(2)}) collective-permute-start(bf16[256,4608]{1,0:T(8,128)(2,1)S(1)} %get-tuple-element.48), channel_id=1, source_target_pairs={{0,1},{1,0},{2,3},{3,2},{4,5},{5,4},{6,7},{7,6},{8,9},{9,8},{10,11... | collective-permute-start | bytes 7077896 | tf_op jit(solution)/shard_map/ppermute | solution.py:67
  12.2 6.5 %gradient_term.1 = (bf16[8,64,512]{2,1,0:T(8,128)(2,1)S(1)}, bf16[8,64,512]{2,1,0:T(8,128)(2,1)S(1)}, bf16[8,64,512]{2,1,0:T(8,128)(2,1)S(1)}, bf16[8,64,512]{2,...) custom-call(bf16[256,8192]{1,0:T(8,128)(2,1)S(1)} %copy-done.3, ...), custom_call_target="tpu_custom_call" | custom-call | flops 2147483648 | bytes 9437184 | tf_op jit(solution)/shard_map/gradient_term/pallas_call | solution.py:228
  18.8 1.4 %collective-permute-start.3 = (bf16[8,64,512]{2,1,0:T(8,128)(2,1)S(1)}, bf16[8,64,512]{2,1,0:T(8,128)(2,1)S(1)}, u32[]{:S(2)}, u32[]{:S(2)}) collective-permute-start(bf16[8,64,512]{2,1,0:T(8,128)(2,1)S(1)} %get-tuple-element.53), channel_id=1, source_target_pairs={{0,130},{1,13},{2,128},{3,15},{4,134},{5,9},{6,132},{7,11},{8,138}... | collective-permute-start | bytes 1572872 | tf_op jit(solution)/shard_map/ppermute | solution.py:59
  20.3 1.2 collective-permute-start.4
  21.5 1.9 %collective-permute-start.5 = (bf16[8,64,512]{2,1,0:T(8,128)(2,1)S(1)}, bf16[8,64,512]{2,1,0:T(8,128)(2,1)S(1)}, u32[]{:S(2)}, u32[]{:S(2)}) collective-permute-start(bf16[8,64,512]{2,1,0:T(8,128)(2,1)S(1)} %get-tuple-element.57), channel_id=1, source_target_pairs={{0,12},{1,131},{2,14},{3,129},{4,8},{5,135},{6,10},{7,133},{8,4},{... | collective-permute-start | bytes 1572872 | tf_op jit(solution)/shard_map/ppermute | solution.py:59
  23.3 5.6 %collective-permute-start = (f32[3,32,512]{2,1,0:T(8,128)S(1)}, f32[3,32,512]{2,1,0:T(8,128)S(1)}, u32[]{:S(2)}, u32[]{:S(2)}) collective-permute-start(f32[3,32,512]{2,1,0:T(8,128)S(1)} %get-tuple-element.47), channel_id=1, source_target_pairs={{0,112},{1,113},{2,114},{3,115},{4,116},{5,117},{6,118},{7,119},{8... | collective-permute-start | bytes 589832 | tf_op jit(solution)/shard_map/ppermute | solution.py:63
  28.9 9.1 %collective-permute-done.refs_8_ = f32[3,32,512]{2,1,0:T(8,128)S(1)} collective-permute-done((f32[3,32,512]{2,1,0:T(8,128)S(1)}, f32[3,32,512]{2,1,0:T(8,128)S(1)}, u32[]{:S(2)}, u32[]{:S(2)}) %collective-permute-start) | collective-permute-done | bytes 196640 | tf_op jit(solution)/shard_map/ppermute | solution.py:63
  41.4 5.4 %collective-permute-done.10.refs_1_ = bf16[4,64,512]{2,1,0:T(8,128)(2,1)S(1)} collective-permute-done((bf16[4,64,512]{2,1,0:T(8,128)(2,1)S(1)}, bf16[4,64,512]{2,1,0:T(8,128)(2,1)S(1)}, u32[]{:S(2)}, u32[]{:S(2)}) %collective-permute-start.10) | collective-permute-done | bytes 262176 | tf_op jit(solution)/shard_map/ppermute | solution.py:59
  46.9 1.5 %collective-permute-start.11 = (bf16[2,64,512]{2,1,0:T(8,128)(2,1)S(1)}, bf16[2,64,512]{2,1,0:T(8,128)(2,1)S(1)}, u32[]{:S(2)}, u32[]{:S(2)}) collective-permute-start(bf16[2,64,512]{2,1,0:T(8,128)(2,1)S(1)} %get-tuple-element.69), channel_id=1, source_target_pairs={{0,2},{1,5},{2,0},{3,7},{4,6},{5,1},{6,4},{7,3},{8,10},{9,13},{10,... | collective-permute-start | bytes 393224 | tf_op jit(solution)/shard_map/ppermute | solution.py:59
  52.4 1.2 collective-permute-done.15.refs_1_
  56.1 2.5 %collective-permute-done.16 = bf16[64,512]{1,0:T(8,128)(2,1)S(1)} collective-permute-done((bf16[64,512]{1,0:T(8,128)(2,1)S(1)}, bf16[64,512]{1,0:T(8,128)(2,1)S(1)}, u32[]{:S(2)}, u32[]{:S(2)}) %collective-permute-start.16) | collective-permute-done | bytes 65568 | tf_op jit(solution)/shard_map/ppermute | solution.py:59
  60.6 2.3 %collective-permute-start.9 = (bf16[64,512]{1,0:T(8,128)(2,1)S(1)}, bf16[64,512]{1,0:T(8,128)(2,1)S(1)}, u32[]{:S(2)}, u32[]{:S(2)}) collective-permute-start(bf16[64,512]{1,0:T(8,128)(2,1)S(1)} %bitcast.83), channel_id=1, source_target_pairs={{0,12},{1,131},{2,14},{3,129},{4,8},{5,135},{6,10},{7,133},{8,4},{... | collective-permute-start | bytes 196616 | tf_op jit(solution)/shard_map/ppermute | solution.py:59
  62.9 1.9 %collective-permute-done.21 = bf16[64,512]{1,0:T(8,128)(2,1)S(1)} collective-permute-done((bf16[64,512]{1,0:T(8,128)(2,1)S(1)}, bf16[64,512]{1,0:T(8,128)(2,1)S(1)}, u32[]{:S(2)}, u32[]{:S(2)}) %collective-permute-start.21) | collective-permute-done | bytes 65568 | tf_op jit(solution)/shard_map/ppermute | solution.py:63
  65.1 4.5 %collective-permute-start.22 = (bf16[64,512]{1,0:T(8,128)(2,1)S(1)}, bf16[64,512]{1,0:T(8,128)(2,1)S(1)}, u32[]{:S(2)}, u32[]{:S(2)}) collective-permute-start(bf16[64,512]{1,0:T(8,128)(2,1)S(1)} %fusion.21), channel_id=1, source_target_pairs={{0,112},{1,113},{2,114},{3,115},{4,116},{5,117},{6,118},{7,119},{8... | collective-permute-start | bytes 196616 | tf_op jit(solution)/shard_map/ppermute | solution.py:63
  69.6 2.3 %collective-permute-done.22 = bf16[64,512]{1,0:T(8,128)(2,1)S(1)} collective-permute-done((bf16[64,512]{1,0:T(8,128)(2,1)S(1)}, bf16[64,512]{1,0:T(8,128)(2,1)S(1)}, u32[]{:S(2)}, u32[]{:S(2)}) %collective-permute-start.22) | collective-permute-done | bytes 65568 | tf_op jit(solution)/shard_map/ppermute | solution.py:63
  72.2 1.7 %collective-permute-start.34 = (bf16[64,512]{1,0:T(8,128)(2,1)S(1)}, bf16[64,512]{1,0:T(8,128)(2,1)S(1)}, u32[]{:S(2)}, u32[]{:S(2)}) collective-permute-start(bf16[64,512]{1,0:T(8,128)(2,1)S(1)} %fusion.12), channel_id=1, source_target_pairs={{0,48},{1,49},{2,50},{3,51},{4,52},{5,53},{6,54},{7,55},{8,56},{9,... | collective-permute-start | bytes 196616 | tf_op jit(solution)/shard_map/ppermute | solution.py:63
  74.4 1.4 %collective-permute-start.26 = (bf16[64,512]{1,0:T(8,128)(2,1)S(1)}, bf16[64,512]{1,0:T(8,128)(2,1)S(1)}, u32[]{:S(2)}, u32[]{:S(2)}) collective-permute-start(bf16[64,512]{1,0:T(8,128)(2,1)S(1)} %fusion.12), channel_id=1, source_target_pairs={{0,16},{1,17},{2,18},{3,19},{4,20},{5,21},{6,22},{7,23},{8,24},{9,... | collective-permute-start | bytes 196616 | tf_op jit(solution)/shard_map/ppermute | solution.py:63
  77.2 1.4 %collective-permute-done.30 = bf16[64,512]{1,0:T(8,128)(2,1)S(1)} collective-permute-done((bf16[64,512]{1,0:T(8,128)(2,1)S(1)}, bf16[64,512]{1,0:T(8,128)(2,1)S(1)}, u32[]{:S(2)}, u32[]{:S(2)}) %collective-permute-start.30) | collective-permute-done | bytes 65568 | tf_op jit(solution)/shard_map/ppermute | solution.py:63
  78.6 1.4 %collective-permute-start.31 = (bf16[1,64,512]{2,1,0:T(8,128)(2,1)S(1)}, bf16[1,64,512]{2,1,0:T(8,128)(2,1)S(1)}, u32[]{:S(2)}, u32[]{:S(2)}) collective-permute-start(bf16[1,64,512]{2,1,0:T(8,128)(2,1)S(1)} %bitcast.79), channel_id=1, source_target_pairs={{0,130},{1,13},{2,128},{3,15},{4,134},{5,9},{6,132},{7,11},{8,138}... | collective-permute-start | bytes 196616 | tf_op jit(solution)/shard_map/ppermute | solution.py:59
  80.2 1.2 collective-permute-start.24
  81.4 1.5 %collective-permute-start.36 = (bf16[2,64,512]{2,1,0:T(8,128)(2,1)S(1)}, bf16[2,64,512]{2,1,0:T(8,128)(2,1)S(1)}, u32[]{:S(2)}, u32[]{:S(2)}) collective-permute-start(bf16[2,64,512]{2,1,0:T(8,128)(2,1)S(1)} %join.21.here), channel_id=1, source_target_pairs={{0,4},{1,3},{2,6},{3,1},{4,0},{5,7},{6,2},{7,5},{8,12},{9,11},{10,... | collective-permute-start | bytes 393224 | tf_op jit(solution)/shard_map/ppermute | solution.py:59
  85.3 1.7 %collective-permute-start.25 = (bf16[4,64,512]{2,1,0:T(8,128)(2,1)S(1)}, bf16[4,64,512]{2,1,0:T(8,128)(2,1)S(1)}, u32[]{:S(2)}, u32[]{:S(2)}) collective-permute-start(bf16[4,64,512]{2,1,0:T(8,128)(2,1)S(1)} %join.13.here), channel_id=1, source_target_pairs={{0,4},{1,3},{2,6},{3,1},{4,0},{5,7},{6,2},{7,5},{8,12},{9,11},{10,... | collective-permute-start | bytes 786440 | tf_op jit(solution)/shard_map/ppermute | solution.py:59
  87.1 1.7 %collective-permute-start.37 = (bf16[4,64,512]{2,1,0:T(8,128)(2,1)S(1)}, bf16[4,64,512]{2,1,0:T(8,128)(2,1)S(1)}, u32[]{:S(2)}, u32[]{:S(2)}) collective-permute-start(bf16[4,64,512]{2,1,0:T(8,128)(2,1)S(1)} %join.22.here), channel_id=1, source_target_pairs={{0,130},{1,13},{2,128},{3,15},{4,134},{5,9},{6,132},{7,11},{8,138}... | collective-permute-start | bytes 786440 | tf_op jit(solution)/shard_map/ppermute | solution.py:59
  89.0 1.6 %collective-permute-start.29 = (bf16[4,64,512]{2,1,0:T(8,128)(2,1)S(1)}, bf16[4,64,512]{2,1,0:T(8,128)(2,1)S(1)}, u32[]{:S(2)}, u32[]{:S(2)}) collective-permute-start(bf16[4,64,512]{2,1,0:T(8,128)(2,1)S(1)} %join.16.here), channel_id=1, source_target_pairs={{0,12},{1,131},{2,14},{3,129},{4,8},{5,135},{6,10},{7,133},{8,4},{... | collective-permute-start | bytes 786440 | tf_op jit(solution)/shard_map/ppermute | solution.py:59
  92.4 1.4 %collective-permute-done.37.got = bf16[4,64,512]{2,1,0:T(8,128)(2,1)S(1)} collective-permute-done((bf16[4,64,512]{2,1,0:T(8,128)(2,1)S(1)}, bf16[4,64,512]{2,1,0:T(8,128)(2,1)S(1)}, u32[]{:S(2)}, u32[]{:S(2)}) %collective-permute-start.37) | collective-permute-done | bytes 262176 | tf_op jit(solution)/shard_map/ppermute | solution.py:59
  94.6 1.3 %collective-permute-done.33.got = bf16[4,64,512]{2,1,0:T(8,128)(2,1)S(1)} collective-permute-done((bf16[4,64,512]{2,1,0:T(8,128)(2,1)S(1)}, bf16[4,64,512]{2,1,0:T(8,128)(2,1)S(1)}, u32[]{:S(2)}, u32[]{:S(2)}) %collective-permute-start.33) | collective-permute-done | bytes 262176 | tf_op jit(solution)/shard_map/ppermute | solution.py:59
  98.9 5.5 %collective-permute-done.38.refs_1_ = bf16[8,64,512]{2,1,0:T(8,128)(2,1)S(1)} collective-permute-done((bf16[8,64,512]{2,1,0:T(8,128)(2,1)S(1)}, bf16[8,64,512]{2,1,0:T(8,128)(2,1)S(1)}, u32[]{:S(2)}, u32[]{:S(2)}) %collective-permute-start.38) | collective-permute-done | bytes 524320 | tf_op jit(solution)/shard_map/ppermute | solution.py:59
  104.5 2.8 %collective-permute-done.40.refs_5_ = bf16[8,64,512]{2,1,0:T(8,128)(2,1)S(1)} collective-permute-done((bf16[8,64,512]{2,1,0:T(8,128)(2,1)S(1)}, bf16[8,64,512]{2,1,0:T(8,128)(2,1)S(1)}, u32[]{:S(2)}, u32[]{:S(2)}) %collective-permute-start.40) | collective-permute-done | bytes 524320 | tf_op jit(solution)/shard_map/ppermute | solution.py:59
  107.3 1.9 %collective-permute-done.39.refs_3_ = bf16[8,64,512]{2,1,0:T(8,128)(2,1)S(1)} collective-permute-done((bf16[8,64,512]{2,1,0:T(8,128)(2,1)S(1)}, bf16[8,64,512]{2,1,0:T(8,128)(2,1)S(1)}, u32[]{:S(2)}, u32[]{:S(2)}) %collective-permute-start.39) | collective-permute-done | bytes 524320 | tf_op jit(solution)/shard_map/ppermute | solution.py:59
  109.2 2.6 %project.1 = (bf16[512,512]{1,0:T(8,128)(2,1)}, f32[256,512]{1,0:T(8,128)S(1)}, bf16[256,512]{1,0:T(8,128)(2,1)S(1)}) custom-call(bf16[512,4096]{1,0:T(8,128)(2,1)S(1)} %stage.1.both, bf16[8,64,512]{2,1,0:T(8,128)(2,1)S(1)} %join.14.refs_0_, bf16[8,64,512]{2,1,0:T(8,128)(2,1)S(1)} %collective-permute-done.38.refs_1_, ...), custom_call_target="tpu_custom_call" | custom-call | flops 2147483648 | bytes 9437184 | tf_op jit(solution)/shard_map/project/pallas_call | solution.py:372
  111.8 11.4 %collective-permute-start.42 = (bf16[256,512]{1,0:T(8,128)(2,1)S(1)}, bf16[256,512]{1,0:T(8,128)(2,1)S(1)}, u32[]{:S(2)}, u32[]{:S(2)}) collective-permute-start(bf16[256,512]{1,0:T(8,128)(2,1)S(1)} %get-tuple-element.86), channel_id=1, source_target_pairs={{0,1},{1,0},{2,3},{3,2},{4,5},{5,4},{6,7},{7,6},{8,9},{9,8},{10,11... | collective-permute-start | bytes 786440 | tf_op jit(solution)/shard_map/ppermute | solution.py:67
  (109 shorter events, 30.7 us)
Async XLA Ops:
  4.7 7.5 %collective-permute-start.1 = (bf16[256,4608]{1,0:T(8,128)(2,1)S(1)}, bf16[256,4608]{1,0:T(8,128)(2,1)S(1)}, u32[]{:S(2)}, u32[]{:S(2)}) collective-permute-start(bf16[256,4608]{1,0:T(8,128)(2,1)S(1)} %get-tuple-element.48), channel_id=1, source_target_pairs={{0,1},{1,0},{2,3},{3,2},{4,5},{5,4},{6,7},{7,6},{8,9},{9,8},{10,11... | collective-permute-start | bytes 7077896 | tf_op jit(solution)/shard_map/ppermute | solution.py:67
  18.7 19.3 %collective-permute-start.2 = (bf16[8,64,512]{2,1,0:T(8,128)(2,1)S(1)}, bf16[8,64,512]{2,1,0:T(8,128)(2,1)S(1)}, u32[]{:S(2)}, u32[]{:S(2)}) collective-permute-start(bf16[8,64,512]{2,1,0:T(8,128)(2,1)S(1)} %get-tuple-element.51), channel_id=1, source_target_pairs={{0,2},{1,5},{2,0},{3,7},{4,6},{5,1},{6,4},{7,3},{8,10},{9,13},{10,... | collective-permute-start | bytes 1572872 | tf_op jit(solution)/shard_map/ppermute | solution.py:59
  18.8 19.2 %collective-permute-start.3 = (bf16[8,64,512]{2,1,0:T(8,128)(2,1)S(1)}, bf16[8,64,512]{2,1,0:T(8,128)(2,1)S(1)}, u32[]{:S(2)}, u32[]{:S(2)}) collective-permute-start(bf16[8,64,512]{2,1,0:T(8,128)(2,1)S(1)} %get-tuple-element.53), channel_id=1, source_target_pairs={{0,130},{1,13},{2,128},{3,15},{4,134},{5,9},{6,132},{7,11},{8,138}... | collective-permute-start | bytes 1572872 | tf_op jit(solution)/shard_map/ppermute | solution.py:59
  20.3 17.7 %collective-permute-start.4 = (bf16[8,64,512]{2,1,0:T(8,128)(2,1)S(1)}, bf16[8,64,512]{2,1,0:T(8,128)(2,1)S(1)}, u32[]{:S(2)}, u32[]{:S(2)}) collective-permute-start(bf16[8,64,512]{2,1,0:T(8,128)(2,1)S(1)} %get-tuple-element.55), channel_id=1, source_target_pairs={{0,4},{1,3},{2,6},{3,1},{4,0},{5,7},{6,2},{7,5},{8,12},{9,11},{10,... | collective-permute-start | bytes 1572872 | tf_op jit(solution)/shard_map/ppermute | solution.py:59
  21.5 16.5 %collective-permute-start.5 = (bf16[8,64,512]{2,1,0:T(8,128)(2,1)S(1)}, bf16[8,64,512]{2,1,0:T(8,128)(2,1)S(1)}, u32[]{:S(2)}, u32[]{:S(2)}) collective-permute-start(bf16[8,64,512]{2,1,0:T(8,128)(2,1)S(1)} %get-tuple-element.57), channel_id=1, source_target_pairs={{0,12},{1,131},{2,14},{3,129},{4,8},{5,135},{6,10},{7,133},{8,4},{... | collective-permute-start | bytes 1572872 | tf_op jit(solution)/shard_map/ppermute | solution.py:59
  23.3 14.7 %collective-permute-start = (f32[3,32,512]{2,1,0:T(8,128)S(1)}, f32[3,32,512]{2,1,0:T(8,128)S(1)}, u32[]{:S(2)}, u32[]{:S(2)}) collective-permute-start(f32[3,32,512]{2,1,0:T(8,128)S(1)} %get-tuple-element.47), channel_id=1, source_target_pairs={{0,112},{1,113},{2,114},{3,115},{4,116},{5,117},{6,118},{7,119},{8... | collective-permute-start | bytes 589832 | tf_op jit(solution)/shard_map/ppermute | solution.py:63
  38.5 22.0 %collective-permute-start.8 = (bf16[256,4096]{1,0:T(8,128)(2,1)S(1)}, bf16[256,4096]{1,0:T(8,128)(2,1)S(1)}, u32[]{:S(2)}, u32[]{:S(2)}) collective-permute-start(bf16[256,4096]{1,0:T(8,128)(2,1)S(1)} %get-tuple-element.63), channel_id=1, source_target_pairs={{0,1},{1,0},{2,3},{3,2},{4,5},{5,4},{6,7},{7,6},{8,9},{9,8},{10,11... | collective-permute-start | bytes 6291464 | tf_op jit(solution)/shard_map/ppermute | solution.py:67
  39.6 7.2 %collective-permute-start.10 = (bf16[4,64,512]{2,1,0:T(8,128)(2,1)S(1)}, bf16[4,64,512]{2,1,0:T(8,128)(2,1)S(1)}, u32[]{:S(2)}, u32[]{:S(2)}) collective-permute-start(bf16[4,64,512]{2,1,0:T(8,128)(2,1)S(1)} %get-tuple-element.67), channel_id=1, source_target_pairs={{0,12},{1,131},{2,14},{3,129},{4,8},{5,135},{6,10},{7,133},{8,4},{... | collective-permute-start | bytes 786440 | tf_op jit(solution)/shard_map/ppermute | solution.py:59
  40.4 8.0 %collective-permute-start.14 = (bf16[4,64,512]{2,1,0:T(8,128)(2,1)S(1)}, bf16[4,64,512]{2,1,0:T(8,128)(2,1)S(1)}, u32[]{:S(2)}, u32[]{:S(2)}) collective-permute-start(bf16[4,64,512]{2,1,0:T(8,128)(2,1)S(1)} %get-tuple-element.73), channel_id=1, source_target_pairs={{0,2},{1,5},{2,0},{3,7},{4,6},{5,1},{6,4},{7,3},{8,10},{9,13},{10,... | collective-permute-start | bytes 786440 | tf_op jit(solution)/shard_map/ppermute | solution.py:59
  40.8 8.8 %collective-permute-start.18 = (bf16[4,64,512]{2,1,0:T(8,128)(2,1)S(1)}, bf16[4,64,512]{2,1,0:T(8,128)(2,1)S(1)}, u32[]{:S(2)}, u32[]{:S(2)}) collective-permute-start(bf16[4,64,512]{2,1,0:T(8,128)(2,1)S(1)} %get-tuple-element.79), channel_id=1, source_target_pairs={{0,130},{1,13},{2,128},{3,15},{4,134},{5,9},{6,132},{7,11},{8,138}... | collective-permute-start | bytes 786440 | tf_op jit(solution)/shard_map/ppermute | solution.py:59
  41.4 9.9 %collective-permute-start.6 = (bf16[4,64,512]{2,1,0:T(8,128)(2,1)S(1)}, bf16[4,64,512]{2,1,0:T(8,128)(2,1)S(1)}, u32[]{:S(2)}, u32[]{:S(2)}) collective-permute-start(bf16[4,64,512]{2,1,0:T(8,128)(2,1)S(1)} %get-tuple-element.60), channel_id=1, source_target_pairs={{0,4},{1,3},{2,6},{3,1},{4,0},{5,7},{6,2},{7,5},{8,12},{9,11},{10,... | collective-permute-start | bytes 786440 | tf_op jit(solution)/shard_map/ppermute | solution.py:59
  48.4 5.1 %collective-permute-start.15 = (bf16[2,64,512]{2,1,0:T(8,128)(2,1)S(1)}, bf16[2,64,512]{2,1,0:T(8,128)(2,1)S(1)}, u32[]{:S(2)}, u32[]{:S(2)}) collective-permute-start(bf16[2,64,512]{2,1,0:T(8,128)(2,1)S(1)} %get-tuple-element.75), channel_id=1, source_target_pairs={{0,12},{1,131},{2,14},{3,129},{4,8},{5,135},{6,10},{7,133},{8,4},{... | collective-permute-start | bytes 393224 | tf_op jit(solution)/shard_map/ppermute | solution.py:59
  49.7 5.2 %collective-permute-start.19 = (bf16[2,64,512]{2,1,0:T(8,128)(2,1)S(1)}, bf16[2,64,512]{2,1,0:T(8,128)(2,1)S(1)}, u32[]{:S(2)}, u32[]{:S(2)}) collective-permute-start(bf16[2,64,512]{2,1,0:T(8,128)(2,1)S(1)} %get-tuple-element.81), channel_id=1, source_target_pairs={{0,4},{1,3},{2,6},{3,1},{4,0},{5,7},{6,2},{7,5},{8,12},{9,11},{10,... | collective-permute-start | bytes 393224 | tf_op jit(solution)/shard_map/ppermute | solution.py:59
  51.4 9.2 %collective-permute-start.7 = (bf16[2,64,512]{2,1,0:T(8,128)(2,1)S(1)}, bf16[2,64,512]{2,1,0:T(8,128)(2,1)S(1)}, u32[]{:S(2)}, u32[]{:S(2)}) collective-permute-start(bf16[2,64,512]{2,1,0:T(8,128)(2,1)S(1)} %get-tuple-element.62), channel_id=1, source_target_pairs={{0,130},{1,13},{2,128},{3,15},{4,134},{5,9},{6,132},{7,11},{8,138}... | collective-permute-start | bytes 393224 | tf_op jit(solution)/shard_map/ppermute | solution.py:59
  53.6 5.0 %collective-permute-start.16 = (bf16[64,512]{1,0:T(8,128)(2,1)S(1)}, bf16[64,512]{1,0:T(8,128)(2,1)S(1)}, u32[]{:S(2)}, u32[]{:S(2)}) collective-permute-start(bf16[64,512]{1,0:T(8,128)(2,1)S(1)} %bitcast.85), channel_id=1, source_target_pairs={{0,130},{1,13},{2,128},{3,15},{4,134},{5,9},{6,132},{7,11},{8,138}... | collective-permute-start | bytes 196616 | tf_op jit(solution)/shard_map/ppermute | solution.py:59
  56.0 6.9 %collective-permute-start.13 = (bf16[64,512]{1,0:T(8,128)(2,1)S(1)}, bf16[64,512]{1,0:T(8,128)(2,1)S(1)}, u32[]{:S(2)}, u32[]{:S(2)}) collective-permute-start(bf16[64,512]{1,0:T(8,128)(2,1)S(1)} %fusion.17), channel_id=1, source_target_pairs={{0,16},{1,17},{2,18},{3,19},{4,20},{5,21},{6,22},{7,23},{8,24},{9,... | collective-permute-start | bytes 196616 | tf_op jit(solution)/shard_map/ppermute | solution.py:63
  59.5 5.3 %collective-permute-start.21 = (bf16[64,512]{1,0:T(8,128)(2,1)S(1)}, bf16[64,512]{1,0:T(8,128)(2,1)S(1)}, u32[]{:S(2)}, u32[]{:S(2)}) collective-permute-start(bf16[64,512]{1,0:T(8,128)(2,1)S(1)} %fusion.15), channel_id=1, source_target_pairs={{0,48},{1,49},{2,50},{3,51},{4,52},{5,53},{6,54},{7,55},{8,56},{9,... | collective-permute-start | bytes 196616 | tf_op jit(solution)/shard_map/ppermute | solution.py:63
  65.1 6.8 %collective-permute-start.22 = (bf16[64,512]{1,0:T(8,128)(2,1)S(1)}, bf16[64,512]{1,0:T(8,128)(2,1)S(1)}, u32[]{:S(2)}, u32[]{:S(2)}) collective-permute-start(bf16[64,512]{1,0:T(8,128)(2,1)S(1)} %fusion.21), channel_id=1, source_target_pairs={{0,112},{1,113},{2,114},{3,115},{4,116},{5,117},{6,118},{7,119},{8... | collective-permute-start | bytes 196616 | tf_op jit(solution)/shard_map/ppermute | solution.py:63
  72.2 5.0 %collective-permute-start.34 = (bf16[64,512]{1,0:T(8,128)(2,1)S(1)}, bf16[64,512]{1,0:T(8,128)(2,1)S(1)}, u32[]{:S(2)}, u32[]{:S(2)}) collective-permute-start(bf16[64,512]{1,0:T(8,128)(2,1)S(1)} %fusion.12), channel_id=1, source_target_pairs={{0,48},{1,49},{2,50},{3,51},{4,52},{5,53},{6,54},{7,55},{8,56},{9,... | collective-permute-start | bytes 196616 | tf_op jit(solution)/shard_map/ppermute | solution.py:63
  74.4 5.6 %collective-permute-start.26 = (bf16[64,512]{1,0:T(8,128)(2,1)S(1)}, bf16[64,512]{1,0:T(8,128)(2,1)S(1)}, u32[]{:S(2)}, u32[]{:S(2)}) collective-permute-start(bf16[64,512]{1,0:T(8,128)(2,1)S(1)} %fusion.12), channel_id=1, source_target_pairs={{0,16},{1,17},{2,18},{3,19},{4,20},{5,21},{6,22},{7,23},{8,24},{9,... | collective-permute-start | bytes 196616 | tf_op jit(solution)/shard_map/ppermute | solution.py:63
  80.2 5.1 %collective-permute-start.24 = (bf16[2,64,512]{2,1,0:T(8,128)(2,1)S(1)}, bf16[2,64,512]{2,1,0:T(8,128)(2,1)S(1)}, u32[]{:S(2)}, u32[]{:S(2)}) collective-permute-start(bf16[2,64,512]{2,1,0:T(8,128)(2,1)S(1)} %join.12.here), channel_id=1, source_target_pairs={{0,130},{1,13},{2,128},{3,15},{4,134},{5,9},{6,132},{7,11},{8,138}... | collective-permute-start | bytes 393224 | tf_op jit(solution)/shard_map/ppermute | solution.py:59
  81.4 5.6 %collective-permute-start.36 = (bf16[2,64,512]{2,1,0:T(8,128)(2,1)S(1)}, bf16[2,64,512]{2,1,0:T(8,128)(2,1)S(1)}, u32[]{:S(2)}, u32[]{:S(2)}) collective-permute-start(bf16[2,64,512]{2,1,0:T(8,128)(2,1)S(1)} %join.21.here), channel_id=1, source_target_pairs={{0,4},{1,3},{2,6},{3,1},{4,0},{5,7},{6,2},{7,5},{8,12},{9,11},{10,... | collective-permute-start | bytes 393224 | tf_op jit(solution)/shard_map/ppermute | solution.py:59
  83.2 5.6 %collective-permute-start.32 = (bf16[2,64,512]{2,1,0:T(8,128)(2,1)S(1)}, bf16[2,64,512]{2,1,0:T(8,128)(2,1)S(1)}, u32[]{:S(2)}, u32[]{:S(2)}) collective-permute-start(bf16[2,64,512]{2,1,0:T(8,128)(2,1)S(1)} %join.18.here), channel_id=1, source_target_pairs={{0,12},{1,131},{2,14},{3,129},{4,8},{5,135},{6,10},{7,133},{8,4},{... | collective-permute-start | bytes 393224 | tf_op jit(solution)/shard_map/ppermute | solution.py:59
  85.3 6.2 %collective-permute-start.25 = (bf16[4,64,512]{2,1,0:T(8,128)(2,1)S(1)}, bf16[4,64,512]{2,1,0:T(8,128)(2,1)S(1)}, u32[]{:S(2)}, u32[]{:S(2)}) collective-permute-start(bf16[4,64,512]{2,1,0:T(8,128)(2,1)S(1)} %join.13.here), channel_id=1, source_target_pairs={{0,4},{1,3},{2,6},{3,1},{4,0},{5,7},{6,2},{7,5},{8,12},{9,11},{10,... | collective-permute-start | bytes 786440 | tf_op jit(solution)/shard_map/ppermute | solution.py:59
  87.1 6.8 %collective-permute-start.37 = (bf16[4,64,512]{2,1,0:T(8,128)(2,1)S(1)}, bf16[4,64,512]{2,1,0:T(8,128)(2,1)S(1)}, u32[]{:S(2)}, u32[]{:S(2)}) collective-permute-start(bf16[4,64,512]{2,1,0:T(8,128)(2,1)S(1)} %join.22.here), channel_id=1, source_target_pairs={{0,130},{1,13},{2,128},{3,15},{4,134},{5,9},{6,132},{7,11},{8,138}... | collective-permute-start | bytes 786440 | tf_op jit(solution)/shard_map/ppermute | solution.py:59
  88.8 7.1 %collective-permute-start.33 = (bf16[4,64,512]{2,1,0:T(8,128)(2,1)S(1)}, bf16[4,64,512]{2,1,0:T(8,128)(2,1)S(1)}, u32[]{:S(2)}, u32[]{:S(2)}) collective-permute-start(bf16[4,64,512]{2,1,0:T(8,128)(2,1)S(1)} %join.19.here), channel_id=1, source_target_pairs={{0,2},{1,5},{2,0},{3,7},{4,6},{5,1},{6,4},{7,3},{8,10},{9,13},{10,... | collective-permute-start | bytes 786440 | tf_op jit(solution)/shard_map/ppermute | solution.py:59
  89.0 8.2 %collective-permute-start.29 = (bf16[4,64,512]{2,1,0:T(8,128)(2,1)S(1)}, bf16[4,64,512]{2,1,0:T(8,128)(2,1)S(1)}, u32[]{:S(2)}, u32[]{:S(2)}) collective-permute-start(bf16[4,64,512]{2,1,0:T(8,128)(2,1)S(1)} %join.16.here), channel_id=1, source_target_pairs={{0,12},{1,131},{2,14},{3,129},{4,8},{5,135},{6,10},{7,133},{8,4},{... | collective-permute-start | bytes 786440 | tf_op jit(solution)/shard_map/ppermute | solution.py:59
  91.5 12.9 %collective-permute-start.38 = (bf16[8,64,512]{2,1,0:T(8,128)(2,1)S(1)}, bf16[8,64,512]{2,1,0:T(8,128)(2,1)S(1)}, u32[]{:S(2)}, u32[]{:S(2)}) collective-permute-start(bf16[8,64,512]{2,1,0:T(8,128)(2,1)S(1)} %join.14.refs_0_), channel_id=1, source_target_pairs={{0,2},{1,5},{2,0},{3,7},{4,6},{5,1},{6,4},{7,3},{8,10},{9,13},{10,... | collective-permute-start | bytes 1572872 | tf_op jit(solution)/shard_map/ppermute | solution.py:59
  93.9 10.6 %collective-permute-start.41 = (bf16[8,64,512]{2,1,0:T(8,128)(2,1)S(1)}, bf16[8,64,512]{2,1,0:T(8,128)(2,1)S(1)}, u32[]{:S(2)}, u32[]{:S(2)}) collective-permute-start(bf16[8,64,512]{2,1,0:T(8,128)(2,1)S(1)} %join.23.refs_3_.refs_6_), channel_id=1, source_target_pairs={{0,12},{1,131},{2,14},{3,129},{4,8},{5,135},{6,10},{7,133},{8,4},{... | collective-permute-start | bytes 1572872 | tf_op jit(solution)/shard_map/ppermute | solution.py:59
  95.9 11.4 %collective-permute-start.40 = (bf16[8,64,512]{2,1,0:T(8,128)(2,1)S(1)}, bf16[8,64,512]{2,1,0:T(8,128)(2,1)S(1)}, u32[]{:S(2)}, u32[]{:S(2)}) collective-permute-start(bf16[8,64,512]{2,1,0:T(8,128)(2,1)S(1)} %join.20.refs_2_.refs_4_), channel_id=1, source_target_pairs={{0,4},{1,3},{2,6},{3,1},{4,0},{5,7},{6,2},{7,5},{8,12},{9,11},{10,... | collective-permute-start | bytes 1572872 | tf_op jit(solution)/shard_map/ppermute | solution.py:59
  97.2 12.0 %collective-permute-start.39 = (bf16[8,64,512]{2,1,0:T(8,128)(2,1)S(1)}, bf16[8,64,512]{2,1,0:T(8,128)(2,1)S(1)}, u32[]{:S(2)}, u32[]{:S(2)}) collective-permute-start(bf16[8,64,512]{2,1,0:T(8,128)(2,1)S(1)} %join.17.refs_1_.refs_2_), channel_id=1, source_target_pairs={{0,130},{1,13},{2,128},{3,15},{4,134},{5,9},{6,132},{7,11},{8,138}... | collective-permute-start | bytes 1572872 | tf_op jit(solution)/shard_map/ppermute | solution.py:59
  111.8 12.7 %collective-permute-start.42 = (bf16[256,512]{1,0:T(8,128)(2,1)S(1)}, bf16[256,512]{1,0:T(8,128)(2,1)S(1)}, u32[]{:S(2)}, u32[]{:S(2)}) collective-permute-start(bf16[256,512]{1,0:T(8,128)(2,1)S(1)} %get-tuple-element.86), channel_id=1, source_target_pairs={{0,1},{1,0},{2,3},{3,2},{4,5},{5,4},{6,7},{7,6},{8,9},{9,8},{10,11... | collective-permute-start | bytes 786440 | tf_op jit(solution)/shard_map/ppermute | solution.py:67
  (20 other events, 87.4 us)
